TPU v7x, 32 devices: a whole 2x2x4 slice. The times are simulated.
32 devices in a mesh: groups: 2 (over y), cells: 4 (over z), nodes: 2 (over x), sub: 2 (over core).
Axes of the slice: x: 2, y: 2, z: 4, core: 2. Of those that a mesh axis runs over, the one named last changes fastest.
Arguments:
- adjoint_start: float32 [4, 5, 16384], P('nodes', None, ('groups', 'cells', 'sub')), parts along dimension 2, may hold values from -6 to 6
- adjoint_rhs: float32 [4, 5, 16384], P('nodes', None, ('groups', 'cells', 'sub')), parts along dimension 2, may hold values from -6 to 6
- off_blocks: bfloat16 [4, 6, 25, 16384], P('nodes', None, None, ('groups', 'cells', 'sub')), parts along dimension 3, may hold values from -0.5 to 0.5
- diag_inverse: float32 [4, 25, 16384], P('nodes', None, ('groups', 'cells', 'sub')), parts along dimension 2, may hold values from -2.4 to 2.4
- neighbours: int32 [6, 8192], P(None, ('cells', 'sub')), may hold values from -1 to 8191, as said below
- node_weights: float32 [4], P('nodes'), may hold values from 0.05 to 0.5
- sens_blocks: bfloat16 [4, 15, 16384], P('nodes', None, ('groups', 'cells', 'sub')), parts along dimension 2, may hold values from -1.796875 to 1.796875
- cell_points: float32 [3, 8192], P(None, ('cells', 'sub')), may hold values from 0 to 1
- base_points: float32 [3, 4096], replicated, may hold values from 0 to 1
- ffd_index: int32 [4096, 8], replicated, may hold values from 0 to 511
- ffd_weight: float32 [4096, 8], replicated, may hold values from 0 to 1
Outputs:
- adjoint: float32 [4, 5, 16384], P('nodes', None, ('groups', 'cells', 'sub')), parts along dimension 2
- control_grad: float32 [6, 512], P('groups'), parts along dimension 0
There are 2 independent parts, one for each index of `groups`. A program takes and returns all parts, laid end to end along the dimension named above; an argument that names none is the same for every part. Nothing has to cross between parts.
Inputs may be any that keep to these rules, and one draw needn't show every extreme that they name: `neighbours`: each entry is -1 (no neighbour) or the index of a cell at most 1024 away from the cell; the distance 1024 occurs.
All inputs are finite; a program needn't handle non-finite values.
Results may differ from a plain program's by a relative error of at most 0.0003.
Values sent between devices are 32-bit elements; how exact they have to be, the bound alone decides.
No kernel may reach another device: no remote copies, remote signals or barrier semaphores. Data moves between devices by JAX's collectives and lax.ppermute only.
A program may use at most 64 MiB of HBM per device.

v0:
```python
import jax
import jax.numpy as jnp
from jax import lax
from jax.sharding import PartitionSpec as P

SWEEPS = 2
FFD = 512


support_radius = 0.3


def with_halo(array, sides, width):
    for axis, dim in sides:
        peers, length = (lax.axis_size(axis), array.shape[dim])
        up = [(i, (i + 1) % peers) for i in range(peers - 1)]
        down = [(j, i) for i, j in up]
        last = lax.slice_in_dim(array, length - width, length, axis=dim)
        initial = lax.slice_in_dim(array, 0, width, axis=dim)
        before = lax.ppermute(last, axis, up)
        after = lax.ppermute(initial, axis, down)
        array = jnp.concatenate([before, array, after], axis=dim)
    return array


def relax(adjoint, adjoint_rhs, off_blocks, diag_inverse, present, local_index):
    cell_count = adjoint.shape[2]
    node_count = adjoint.shape[0]
    widened = with_halo(adjoint, ((("cells", "sub"), 2),), cell_count)
    coupled = jnp.zeros(adjoint.shape, jnp.float32)
    for face_slot in range(off_blocks.shape[1]):
        beside = jnp.where(
            present[face_slot][None, None, :], widened[:, :, local_index[face_slot]], 0.0
        )
        coupling = (
            off_blocks[:, face_slot].astype(jnp.float32).reshape(node_count, 5, 5, cell_count)
        )
        coupled = coupled + jnp.sum(coupling * beside[:, None], axis=2)
    inverse = diag_inverse.reshape(node_count, 5, 5, cell_count)
    return jnp.sum(inverse * (adjoint_rhs - coupled)[:, None], axis=2)


def kernel_sum(sensitivity, points, base):
    squared = jnp.zeros((points.shape[1], base.shape[1]), jnp.float32)
    for axis_slot in range(3):
        squared = squared + (points[axis_slot][:, None] - base[axis_slot][None, :]) ** 2
    ratio = jnp.sqrt(squared) / support_radius
    kernel = jnp.maximum(1.0 - ratio, 0.0) ** 4 * (4.0 * ratio + 1.0)
    return jnp.dot(
        sensitivity, kernel, precision=lax.Precision.HIGHEST, preferred_element_type=jnp.float32
    )


def lattice_matrix(lattice_index, lattice_weight, columns):
    matches = lattice_index[:, :, None] == jnp.arange(columns, dtype=jnp.int32)[None, None, :]
    return jnp.sum(jnp.where(matches, lattice_weight[:, :, None], 0.0), axis=1)


def body(
    adjoint_start,
    adjoint_rhs,
    off_blocks,
    diag_inverse,
    neighbours,
    node_weights,
    sens_blocks,
    cell_points,
    base_points,
    ffd_index,
    ffd_weight,
):
    cell_count = adjoint_start.shape[2]
    first_cell = lax.axis_index(("cells", "sub")) * cell_count
    present = neighbours >= 0
    local_index = jnp.where(present, neighbours - first_cell + cell_count, 0)
    adjoint = adjoint_start
    for sweep_step in range(SWEEPS):
        adjoint = relax(adjoint, adjoint_rhs, off_blocks, diag_inverse, present, local_index)
    node_count = adjoint.shape[0]
    derive = sens_blocks.astype(jnp.float32).reshape(node_count, 5, 3, cell_count)
    per_node = jnp.sum(adjoint[:, :, None] * derive, axis=1)
    partial_sens = jnp.sum(node_weights[:, None, None] * per_node, axis=0)
    share_count = cell_count // lax.axis_size("nodes")
    share_start = lax.axis_index("nodes") * share_count
    node_sum = lax.psum(partial_sens, "nodes")
    sensitivity = lax.dynamic_slice_in_dim(node_sum, share_start, share_count, 1)
    points = lax.dynamic_slice_in_dim(cell_points, share_start, share_count, 1)
    base_count = base_points.shape[1]
    base_block = min(512, base_count)
    pieces = []
    for block_index in range(base_count // base_block):
        base_part = base_points[:, block_index * base_block : (block_index + 1) * base_block]
        pieces.append(kernel_sum(sensitivity, points, base_part))
    g_part = jnp.concatenate(pieces, axis=1)
    scale = 1.0 / jnp.sqrt(jnp.float32(cell_count * lax.axis_size(("cells", "sub"))))
    columns = FFD
    owned = base_count // lax.axis_size(("cells", "nodes", "sub"))
    owner_start = lax.axis_index(("cells", "nodes", "sub")) * owned
    base_grad = (
        lax.psum_scatter(g_part, ("cells", "nodes", "sub"), scatter_dimension=1, tiled=True) * scale
    )
    lattice_index = lax.dynamic_slice_in_dim(ffd_index, owner_start, owned, 0)
    lattice_weight = lax.dynamic_slice_in_dim(ffd_weight, owner_start, owned, 0)
    lattice = lattice_matrix(lattice_index, lattice_weight, columns)
    own_grad = jnp.dot(
        base_grad, lattice, precision=lax.Precision.HIGHEST, preferred_element_type=jnp.float32
    )
    control_grad = lax.psum(own_grad, ("cells", "nodes", "sub"))
    return (adjoint, control_grad)


def solution(mesh):
    return jax.shard_map(
        body,
        mesh=mesh,
        in_specs=(
            P("nodes", None, ("groups", "cells", "sub")),
            P("nodes", None, ("groups", "cells", "sub")),
            P("nodes", None, None, ("groups", "cells", "sub")),
            P("nodes", None, ("groups", "cells", "sub")),
            P(None, ("cells", "sub")),
            P("nodes"),
            P("nodes", None, ("groups", "cells", "sub")),
            P(None, ("cells", "sub")),
            P(),
            P(),
            P(),
        ),
        out_specs=(P("nodes", None, ("groups", "cells", "sub")), P("groups", None)),
        check_vma=False,
    )
```

profile of v0, /device:TPU:0, one launch (start us, length us, event | category | flops | bytes accessed | tf_op | source)
XLA Modules:
  0.0 309.0 jit_solution(3301898094393572463)
XLA Ops:
  7.2 2.4 collective-permute-start
  15.5 2.3 fusion.265
  20.1 3.8 %copy.58 = f32[2,5,3072]{1,0,2:T(2,128)S(1)} copy(f32[2,5,3072]{2,0,1:T(2,128)} %pad_maximum_fusion) | data formatting | bytes 245760 | tf_op jit(solution)/shard_map/concatenate | solution.py:22
  23.9 7.7 %gather_fusion = f32[1024,2,5]{2,1,0:T(2,128)} fusion(f32[2,5,3072]{1,0,2:T(2,128)S(1)} %copy.58, s32[1024]{0:T(1024)S(1)} %get-tuple-element.52), kind=kCustom, calls=%fused_computation | custom fusion | bytes 86016 | tf_op jit(solution)/shard_map/gather | solution.py:33
  31.6 5.3 %select_bitcast_fusion.11 = f32[2,5,1024]{1,0,2:T(2,128)S(1)} fusion(f32[1024,2,5]{2,1,0:T(2,128)} %gather_fusion, pred[1024]{0:T(1024)(128)(4,1)S(1)} %get-tuple-element.7), kind=kLoop, calls=%fused_computation.33 | loop fusion | flops 10240 | bytes 82944 | tf_op jit(solution)/shard_map/jit(_where)/select_n | solution.py:32
  37.4 5.4 %gather_fusion.1 = f32[1024,2,5]{2,1,0:T(2,128)S(1)} fusion(f32[2,5,3072]{1,0,2:T(2,128)} %copy-done.1, s32[1024]{0:T(1024)S(1)} %get-tuple-element.51), kind=kCustom, calls=%fused_computation.1 | custom fusion | bytes 86016 | tf_op jit(solution)/shard_map/gather | solution.py:33
  42.9 3.7 %select_bitcast_fusion.10 = f32[2,5,1024]{1,0,2:T(2,128)S(1)} fusion(f32[1024,2,5]{2,1,0:T(2,128)S(1)} %gather_fusion.1, pred[1024]{0:T(1024)(128)(4,1)S(1)} %get-tuple-element.2), kind=kLoop, calls=%fused_computation.32 | loop fusion | flops 10240 | bytes 82944 | tf_op jit(solution)/shard_map/jit(_where)/select_n | solution.py:32
  47.1 5.4 %gather_fusion.2 = f32[1024,2,5]{2,1,0:T(2,128)S(1)} fusion(f32[2,5,3072]{1,0,2:T(2,128)} %copy-done.1, s32[1024]{0:T(1024)S(1)} %get-tuple-element.50), kind=kCustom, calls=%fused_computation.2 | custom fusion | bytes 86016 | tf_op jit(solution)/shard_map/gather | solution.py:33
  52.5 3.7 %select_bitcast_fusion.9 = f32[2,5,1024]{1,0,2:T(2,128)S(1)} fusion(f32[1024,2,5]{2,1,0:T(2,128)S(1)} %gather_fusion.2, pred[1024]{0:T(1024)(128)(4,1)S(1)} %get-tuple-element.5), kind=kLoop, calls=%fused_computation.31 | loop fusion | flops 10240 | bytes 82944 | tf_op jit(solution)/shard_map/jit(_where)/select_n | solution.py:32
  56.7 5.4 %gather_fusion.3 = f32[1024,2,5]{2,1,0:T(2,128)S(1)} fusion(f32[2,5,3072]{1,0,2:T(2,128)} %copy-done.1, s32[1024]{0:T(1024)S(1)} %get-tuple-element.49), kind=kCustom, calls=%fused_computation.3 | custom fusion | bytes 86016 | tf_op jit(solution)/shard_map/gather | solution.py:33
  62.2 3.7 %select_bitcast_fusion.8 = f32[2,5,1024]{1,0,2:T(2,128)S(1)} fusion(f32[1024,2,5]{2,1,0:T(2,128)S(1)} %gather_fusion.3, pred[1024]{0:T(1024)(128)(4,1)S(1)} %get-tuple-element.4), kind=kLoop, calls=%fused_computation.30 | loop fusion | flops 10240 | bytes 82944 | tf_op jit(solution)/shard_map/jit(_where)/select_n | solution.py:32
  66.4 5.4 %gather_fusion.4 = f32[1024,2,5]{2,1,0:T(2,128)S(1)} fusion(f32[2,5,3072]{1,0,2:T(2,128)} %copy-done.1, s32[1024]{0:T(1024)S(1)} %get-tuple-element.48), kind=kCustom, calls=%fused_computation.4 | custom fusion | bytes 86016 | tf_op jit(solution)/shard_map/gather | solution.py:33
  71.9 3.7 %select_bitcast_fusion.7 = f32[2,5,1024]{1,0,2:T(2,128)S(1)} fusion(f32[1024,2,5]{2,1,0:T(2,128)S(1)} %gather_fusion.4, pred[1024]{0:T(1024)(128)(4,1)S(1)} %get-tuple-element.3), kind=kLoop, calls=%fused_computation.29 | loop fusion | flops 10240 | bytes 82944 | tf_op jit(solution)/shard_map/jit(_where)/select_n | solution.py:32
  76.1 5.4 %gather_fusion.5 = f32[1024,2,5]{2,1,0:T(2,128)S(1)} fusion(f32[2,5,3072]{1,0,2:T(2,128)} %copy-done.1, s32[1024]{0:T(1024)S(1)} %get-tuple-element.47), kind=kCustom, calls=%fused_computation.5 | custom fusion | bytes 86016 | tf_op jit(solution)/shard_map/gather | solution.py:33
  81.6 3.7 %select_bitcast_fusion.6 = f32[2,5,1024]{1,0,2:T(2,128)S(1)} fusion(f32[1024,2,5]{2,1,0:T(2,128)S(1)} %gather_fusion.5, pred[1024]{0:T(1024)(128)(4,1)S(1)} %get-tuple-element.6), kind=kLoop, calls=%fused_computation.28 | loop fusion | flops 10240 | bytes 82944 | tf_op jit(solution)/shard_map/jit(_where)/select_n | solution.py:32
  86.7 5.2 %collective-permute-start.2 = (f32[2,5,1024]{2,0,1:T(2,128)S(1)}, f32[2,5,1024]{2,0,1:T(2,128)S(1)}, u32[]{:S(2)}, u32[]{:S(2)}) collective-permute-start(f32[2,5,1024]{2,0,1:T(2,128)S(1)} %multiply_reduce_fusion.1), channel_id=1, source_target_pairs={{0,1},{1,4},{4,5},{5,8},{8,9},{9,12},{12,13},{2,3},{3,6},{6,7},{7,... | collective-permute-start | bytes 122888 | tf_op jit(solution)/shard_map/ppermute | solution.py:20
  97.2 3.8 %copy.70 = f32[2,5,3072]{1,0,2:T(2,128)S(1)} copy(f32[2,5,3072]{2,0,1:T(2,128)} %pad_maximum_fusion.1) | data formatting | bytes 245760 | tf_op jit(solution)/shard_map/concatenate | solution.py:22
  101.0 7.5 %gather_fusion.6 = f32[1024,2,5]{2,1,0:T(2,128)} fusion(f32[2,5,3072]{1,0,2:T(2,128)S(1)} %copy.70, s32[1024]{0:T(1024)S(1)} %get-tuple-element.52), kind=kCustom, calls=%fused_computation.6 | custom fusion | bytes 86016 | tf_op jit(solution)/shard_map/gather | solution.py:33
  108.5 7.5 %gather_fusion.7 = f32[1024,2,5]{2,1,0:T(2,128)} fusion(f32[2,5,3072]{1,0,2:T(2,128)S(1)} %copy.70, s32[1024]{0:T(1024)S(1)} %get-tuple-element.51), kind=kCustom, calls=%fused_computation.7 | custom fusion | bytes 86016 | tf_op jit(solution)/shard_map/gather | solution.py:33
  116.0 7.4 %gather_fusion.8 = f32[1024,2,5]{2,1,0:T(2,128)} fusion(f32[2,5,3072]{1,0,2:T(2,128)S(1)} %copy.70, s32[1024]{0:T(1024)S(1)} %get-tuple-element.50), kind=kCustom, calls=%fused_computation.8 | custom fusion | bytes 86016 | tf_op jit(solution)/shard_map/gather | solution.py:33
  123.5 7.5 %gather_fusion.9 = f32[1024,2,5]{2,1,0:T(2,128)} fusion(f32[2,5,3072]{1,0,2:T(2,128)S(1)} %copy.70, s32[1024]{0:T(1024)S(1)} %get-tuple-element.49), kind=kCustom, calls=%fused_computation.9 | custom fusion | bytes 86016 | tf_op jit(solution)/shard_map/gather | solution.py:33
  130.9 7.5 %gather_fusion.10 = f32[1024,2,5]{2,1,0:T(2,128)} fusion(f32[2,5,3072]{1,0,2:T(2,128)S(1)} %copy.70, s32[1024]{0:T(1024)S(1)} %get-tuple-element.48), kind=kCustom, calls=%fused_computation.10 | custom fusion | bytes 86016 | tf_op jit(solution)/shard_map/gather | solution.py:33
  138.4 7.5 %gather_fusion.11 = f32[1024,2,5]{2,1,0:T(2,128)} fusion(f32[2,5,3072]{1,0,2:T(2,128)S(1)} %copy.70, s32[1024]{0:T(1024)S(1)} %get-tuple-element.47), kind=kCustom, calls=%fused_computation.11 | custom fusion | bytes 86016 | tf_op jit(solution)/shard_map/gather | solution.py:33
  145.9 5.4 %select_bitcast_fusion.5 = f32[2,5,1024]{1,0,2:T(2,128)S(1)} fusion(f32[1024,2,5]{2,1,0:T(2,128)} %gather_fusion.6, pred[1024]{0:T(1024)(128)(4,1)S(1)} %get-tuple-element.7), kind=kLoop, calls=%fused_computation.27 | loop fusion | flops 10240 | bytes 82944 | tf_op jit(solution)/shard_map/jit(_where)/select_n | solution.py:32
  153.4 3.7 %select_bitcast_fusion.4 = f32[2,5,1024]{1,0,2:T(2,128)S(1)} fusion(f32[1024,2,5]{2,1,0:T(2,128)S(1)} %copy-done.5, pred[1024]{0:T(1024)(128)(4,1)S(1)} %get-tuple-element.2), kind=kLoop, calls=%fused_computation.26 | loop fusion | flops 10240 | bytes 82944 | tf_op jit(solution)/shard_map/jit(_where)/select_n | solution.py:32
  159.3 3.7 %select_bitcast_fusion.3 = f32[2,5,1024]{1,0,2:T(2,128)S(1)} fusion(f32[1024,2,5]{2,1,0:T(2,128)S(1)} %copy-done.4, pred[1024]{0:T(1024)(128)(4,1)S(1)} %get-tuple-element.5), kind=kLoop, calls=%fused_computation.25 | loop fusion | flops 10240 | bytes 82944 | tf_op jit(solution)/shard_map/jit(_where)/select_n | solution.py:32
  165.1 5.4 %select_bitcast_fusion.2 = f32[2,5,1024]{1,0,2:T(2,128)S(1)} fusion(f32[1024,2,5]{2,1,0:T(2,128)} %gather_fusion.9, pred[1024]{0:T(1024)(128)(4,1)S(1)} %get-tuple-element.4), kind=kLoop, calls=%fused_computation.24 | loop fusion | flops 10240 | bytes 82944 | tf_op jit(solution)/shard_map/jit(_where)/select_n | solution.py:32
  172.7 3.7 %select_bitcast_fusion.1 = f32[2,5,1024]{1,0,2:T(2,128)S(1)} fusion(f32[1024,2,5]{2,1,0:T(2,128)S(1)} %copy-done.3, pred[1024]{0:T(1024)(128)(4,1)S(1)} %get-tuple-element.3), kind=kLoop, calls=%fused_computation.23 | loop fusion | flops 10240 | bytes 82944 | tf_op jit(solution)/shard_map/jit(_where)/select_n | solution.py:32
  177.1 3.7 %select_bitcast_fusion = f32[2,5,1024]{1,0,2:T(2,128)S(1)} fusion(f32[1024,2,5]{2,1,0:T(2,128)S(1)} %copy-done.2, pred[1024]{0:T(1024)(128)(4,1)S(1)} %get-tuple-element.6), kind=kLoop, calls=%fused_computation.22 | loop fusion | flops 10240 | bytes 82944 | tf_op jit(solution)/shard_map/jit(_where)/select_n | solution.py:32
  183.6 8.2 %psum.14 = f32[3,1024]{1,0:T(4,128)S(1)} all-reduce(f32[3,1024]{1,0:T(4,128)S(1)} %multiply_reduce_fusion.2), channel_id=1, replica_groups=mesh['groups'=2,'cells'=4,'nodes'=2,'sub'=2] {'nodes'}, use_global_device_ids=true, to_apply=%region_16.17 | all-reduce | flops 3072 | bytes 24576 | tf_op jit(solution)/shard_map/psum | solution.py:85
  207.4 62.8 %reduce-scatter.4.cloned.1.call-done = f32[256,3]{1,0:T(8,128)} async-done(((f32[4096,3]{1,0:T(8,128)}), f32[256,3]{1,0:T(8,128)}) %reduce-scatter.4.cloned.1.call-update) | async-done | bytes 3088
  271.6 30.6 %psum.15 = f32[3,512]{1,0:T(4,128)} all-reduce(f32[3,512]{1,0:T(4,128)S(1)} %fusion.229), channel_id=1, replica_groups=mesh['groups'=2,'cells'=4,'nodes'=2,'sub'=2] {'cells','nodes','sub'}, use_global_device_ids=true, to_apply=%region_19.20 | all-reduce | flops 1536 | bytes 12288 | tf_op jit(solution)/shard_map/psum | solution.py:108
  (154 shorter events, 45.7 us)
Async XLA Ops:
  7.2 10.7 %copy-start = (s32[4096,8]{0,1:T(8,128)S(1)}, s32[4096,8]{0,1:T(8,128)}, u32[]{:S(2)}) copy-start(s32[4096,8]{0,1:T(8,128)} %param.20) | copy-start | bytes 393220
  7.2 263.1 %reduce-scatter.4.cloned.1.call-start = ((), (), s32[]{:S(2)}) async-start(), calls=%async_computation.1 | async-start | bytes 2228224
  7.2 11.4 %collective-permute-start = (f32[2,5,1024]{2,0,1:T(2,128)}, f32[2,5,1024]{2,0,1:T(2,128)S(1)}, u32[]{:S(2)}, u32[]{:S(2)}) collective-permute-start(f32[2,5,1024]{2,0,1:T(2,128)} %param.11), channel_id=1, source_target_pairs={{0,1},{1,4},{4,5},{5,8},{8,9},{9,12},{12,13},{2,3},{3,6},{6,7},{7,... | collective-permute-start | bytes 122888 | tf_op jit(solution)/shard_map/ppermute | solution.py:20
  9.6 9.0 %collective-permute-start.1 = (f32[2,5,1024]{2,0,1:T(2,128)}, f32[2,5,1024]{2,0,1:T(2,128)S(1)}, u32[]{:S(2)}, u32[]{:S(2)}) collective-permute-start(f32[2,5,1024]{2,0,1:T(2,128)} %param.11), channel_id=1, source_target_pairs={{1,0},{4,1},{5,4},{8,5},{9,8},{12,9},{13,12},{3,2},{6,3},{7,6},{10... | collective-permute-start | bytes 122888 | tf_op jit(solution)/shard_map/ppermute | solution.py:21
  23.9 7.7 %copy-start.1 = (f32[2,5,3072]{1,0,2:T(2,128)}, f32[2,5,3072]{1,0,2:T(2,128)S(1)}, u32[]{:S(2)}) copy-start(f32[2,5,3072]{1,0,2:T(2,128)S(1)} %copy.58) | copy-start | bytes 368644
  71.8 13.9 %copy-start.9 = (bf16[2,1,25,1024]{3,0,2,1:T(2,128)(2,1)S(1)}, bf16[2,1,25,1024]{3,0,2,1:T(2,128)(2,1)}, u32[]{:S(2)}) copy-start(bf16[2,1,25,1024]{3,0,2,1:T(2,128)(2,1)} %get-tuple-element.11) | copy-start | bytes 307204
  71.8 14.1 %copy-start.8 = (bf16[2,1,25,1024]{3,0,2,1:T(2,128)(2,1)S(1)}, bf16[2,1,25,1024]{3,0,2,1:T(2,128)(2,1)}, u32[]{:S(2)}) copy-start(bf16[2,1,25,1024]{3,0,2,1:T(2,128)(2,1)} %get-tuple-element.8) | copy-start | bytes 307204
  71.9 14.2 %copy-start.7 = (bf16[2,1,25,1024]{3,0,2,1:T(2,128)(2,1)S(1)}, bf16[2,1,25,1024]{3,0,2,1:T(2,128)(2,1)}, u32[]{:S(2)}) copy-start(bf16[2,1,25,1024]{3,0,2,1:T(2,128)(2,1)} %get-tuple-element.10) | copy-start | bytes 307204
  71.9 14.3 %copy-start.6 = (bf16[2,1,25,1024]{3,0,2,1:T(2,128)(2,1)S(1)}, bf16[2,1,25,1024]{3,0,2,1:T(2,128)(2,1)}, u32[]{:S(2)}) copy-start(bf16[2,1,25,1024]{3,0,2,1:T(2,128)(2,1)} %get-tuple-element.9) | copy-start | bytes 307204
  75.6 10.9 %copy-start.13 = (f32[2,5,1024]{2,0,1:T(2,128)S(1)}, f32[2,5,1024]{2,0,1:T(2,128)}, u32[]{:S(2)}) copy-start(f32[2,5,1024]{2,0,1:T(2,128)} %param.12) | copy-start | bytes 122884
  75.6 11.0 %copy-start.10 = (f32[2,25,1024]{2,0,1:T(2,128)S(1)}, f32[2,25,1024]{2,0,1:T(2,128)}, u32[]{:S(2)}) copy-start(f32[2,25,1024]{2,0,1:T(2,128)} %param.14) | copy-start | bytes 614404
  86.7 9.8 %collective-permute-start.2 = (f32[2,5,1024]{2,0,1:T(2,128)S(1)}, f32[2,5,1024]{2,0,1:T(2,128)S(1)}, u32[]{:S(2)}, u32[]{:S(2)}) collective-permute-start(f32[2,5,1024]{2,0,1:T(2,128)S(1)} %multiply_reduce_fusion.1), channel_id=1, source_target_pairs={{0,1},{1,4},{4,5},{5,8},{8,9},{9,12},{12,13},{2,3},{3,6},{6,7},{7,... | collective-permute-start | bytes 122888 | tf_op jit(solution)/shard_map/ppermute | solution.py:20
  92.0 4.5 %collective-permute-start.3 = (f32[2,5,1024]{2,0,1:T(2,128)S(1)}, f32[2,5,1024]{2,0,1:T(2,128)S(1)}, u32[]{:S(2)}, u32[]{:S(2)}) collective-permute-start(f32[2,5,1024]{2,0,1:T(2,128)S(1)} %multiply_reduce_fusion.1), channel_id=1, source_target_pairs={{1,0},{4,1},{5,4},{8,5},{9,8},{12,9},{13,12},{3,2},{6,3},{7,6},{10... | collective-permute-start | bytes 122888 | tf_op jit(solution)/shard_map/ppermute | solution.py:21
  145.9 7.6 %copy-start.5 = (f32[1024,2,5]{2,1,0:T(2,128)S(1)}, f32[1024,2,5]{2,1,0:T(2,128)}, u32[]{:S(2)}) copy-start(f32[1024,2,5]{2,1,0:T(2,128)} %gather_fusion.7) | copy-start | bytes 122884
  145.9 13.4 %copy-start.4 = (f32[1024,2,5]{2,1,0:T(2,128)S(1)}, f32[1024,2,5]{2,1,0:T(2,128)}, u32[]{:S(2)}) copy-start(f32[1024,2,5]{2,1,0:T(2,128)} %gather_fusion.8) | copy-start | bytes 122884
  159.3 13.4 %copy-start.3 = (f32[1024,2,5]{2,1,0:T(2,128)S(1)}, f32[1024,2,5]{2,1,0:T(2,128)}, u32[]{:S(2)}) copy-start(f32[1024,2,5]{2,1,0:T(2,128)} %gather_fusion.10) | copy-start | bytes 122884
  165.1 11.9 %copy-start.2 = (f32[1024,2,5]{2,1,0:T(2,128)S(1)}, f32[1024,2,5]{2,1,0:T(2,128)}, u32[]{:S(2)}) copy-start(f32[1024,2,5]{2,1,0:T(2,128)} %gather_fusion.11) | copy-start | bytes 122884
  172.7 8.8 %copy-start.14 = (f32[2,5,1024]{2,0,1:T(2,128)S(1)}, f32[2,5,1024]{2,0,1:T(2,128)}, u32[]{:S(2)}) copy-start(f32[2,5,1024]{2,0,1:T(2,128)} %param.12) | copy-start | bytes 122884
  176.4 15.4 %copy-start.31 = (f32[1,512]{1,0:T(1,128)S(1)}, f32[1,512]{1,0:T(1,128)}, u32[]{:S(2)}) copy-start(f32[1,512]{1,0:T(1,128)} %get-tuple-element.34) | copy-start | bytes 6148
  176.4 15.4 %copy-start.32 = (f32[1,512]{1,0:T(1,128)S(1)}, f32[1,512]{1,0:T(1,128)}, u32[]{:S(2)}) copy-start(f32[1,512]{1,0:T(1,128)} %get-tuple-element.35) | copy-start | bytes 6148
  176.4 15.4 %copy-start.33 = (f32[1,512]{1,0:T(1,128)S(1)}, f32[1,512]{1,0:T(1,128)}, u32[]{:S(2)}) copy-start(f32[1,512]{1,0:T(1,128)} %get-tuple-element.36) | copy-start | bytes 6148
  176.4 15.4 %copy-start.40 = (f32[1,512]{1,0:T(1,128)S(1)}, f32[1,512]{1,0:T(1,128)}, u32[]{:S(2)}) copy-start(f32[1,512]{1,0:T(1,128)} %get-tuple-element.44) | copy-start | bytes 6148
  176.9 4.6 %copy-start.16 = (f32[2,5,1024]{2,0,1:T(2,128)S(1)}, f32[2,5,1024]{2,0,1:T(2,128)}, u32[]{:S(2)}) copy-start(f32[2,5,1024]{2,0,1:T(2,128)} %fusion.223) | copy-start | bytes 122884
  176.9 6.5 %copy-start.17 = (bf16[2,15,1024]{2,0,1:T(2,128)(2,1)S(1)}, bf16[2,15,1024]{2,0,1:T(2,128)(2,1)}, u32[]{:S(2)}) copy-start(bf16[2,15,1024]{2,0,1:T(2,128)(2,1)} %param.17) | copy-start | bytes 184324
  176.9 6.6 %copy-start.43 = (f32[2]{0:T(128)S(1)}, f32[2]{0:T(128)}, u32[]{:S(2)}) copy-start(f32[2]{0:T(128)} %param.16) | copy-start | bytes 28
  176.9 14.9 %copy-start.41 = (f32[1,512]{1,0:T(1,128)S(1)}, f32[1,512]{1,0:T(1,128)}, u32[]{:S(2)}) copy-start(f32[1,512]{1,0:T(1,128)} %get-tuple-element.45) | copy-start | bytes 6148
  176.9 14.9 %copy-start.42 = (f32[1,512]{1,0:T(1,128)S(1)}, f32[1,512]{1,0:T(1,128)}, u32[]{:S(2)}) copy-start(f32[1,512]{1,0:T(1,128)} %get-tuple-element.46) | copy-start | bytes 6148
  180.8 12.5 %copy-start.37 = (f32[1,512]{1,0:T(1,128)S(1)}, f32[1,512]{1,0:T(1,128)}, u32[]{:S(2)}) copy-start(f32[1,512]{1,0:T(1,128)} %get-tuple-element.30) | copy-start | bytes 6148
  180.8 12.5 %copy-start.38 = (f32[1,512]{1,0:T(1,128)S(1)}, f32[1,512]{1,0:T(1,128)}, u32[]{:S(2)}) copy-start(f32[1,512]{1,0:T(1,128)} %get-tuple-element.31) | copy-start | bytes 6148
  180.8 12.5 %copy-start.39 = (f32[1,512]{1,0:T(1,128)S(1)}, f32[1,512]{1,0:T(1,128)}, u32[]{:S(2)}) copy-start(f32[1,512]{1,0:T(1,128)} %get-tuple-element.32) | copy-start | bytes 6148
  183.4 11.4 %copy-start.15 = (f32[2,5,1024]{2,0,1:T(2,128)}, f32[2,5,1024]{2,0,1:T(2,128)S(1)}, u32[]{:S(2)}) copy-start(f32[2,5,1024]{2,0,1:T(2,128)S(1)} %multiply_reduce_fusion) | copy-start | bytes 122884
  203.7 2.0 copy-start.12
  (17 other events, 26.2 us)
Sparse Core Ops, SparseCore 0:
  205.8 64.3 reduce-scatter.3
where the time goes:
time: 311 us; the launch traced here: 309 us
  local copies, waits for them, and re-layouts  105 us (34%)
  other arithmetic  65 us (21%)
  waiting for transfers between devices  62.9 us (20%)
  blocking collectives  38.8 us (12%)
  between operations  14.8 us (5%)
  matrix products  11.9 us (4%)
  starting transfers between devices  10.4 us (3%)
    gather x12, local copies, waits for them, and re-layouts, relax(): widened[:, :, local_index[face_slot]]  79.7 us
    unnamed x2, waiting for transfers between devices  62.8 us
    select_n x12, other arithmetic, relax(): jnp.where(present[face_slot][None, None, :], widened[:, :, local_index[fa...  49.7 us
    psum x1, blocking collectives, body(): control_grad = lax.psum(own_grad, ('cells', 'nodes', 'sub'))  30.6 us
    dot_general x8, matrix products, kernel_sum(): jnp.dot(sensitivity, kernel, precision=lax.Precision.HIGHEST, preferred_e...  11.6 us
    psum x1, blocking collectives, body(): node_sum = lax.psum(partial_sens, 'nodes')  8.16 us
    reduce_sum x12, other arithmetic, relax(): coupled = coupled + jnp.sum(coupling * beside[:, None], axis=2)  7.63 us
    ppermute x2, starting transfers between devices, with_halo(): before = lax.ppermute(last, axis, up)  7.61 us
  transfers between devices with their start and end apart: 5, of which 1 were waited for; matrix products, arithmetic and copies ran while one was open for 4% of the time, Pallas kernels for 0%

commit v1 on v0

v1 whole, which is shorter than its diff:
```python
import functools
import math

import jax
import jax.numpy as jnp
from jax import lax
from jax.experimental import pallas as pl
from jax.experimental.pallas import tpu as pltpu
from jax.sharding import PartitionSpec as P

SWEEPS = 2
FFD = 512
SUPPORT_RADIUS = 0.3
LANES = 128
VMEM_LIMIT = 48 * 1024 * 1024

CELL_AXES = ("cells", "sub")
SUM_AXES = ("cells", "nodes", "sub")


def rows_of(array):
    nodes, rows, cells = array.shape
    blocks = cells // LANES
    split = array.reshape(nodes, rows, blocks, LANES)
    return split.transpose(1, 2, 0, 3).reshape(rows * blocks * nodes, LANES)


def from_rows(array, nodes, cells):
    blocks = cells // LANES
    split = array.reshape(-1, blocks, nodes, LANES)
    return split.transpose(2, 0, 1, 3).reshape(nodes, -1, cells)


def spread_neighbours(neigh_ref, first_cell, lane_ref, step_ref, nodes):
    faces, cells = neigh_ref.shape
    blocks = cells // LANES
    per_face = blocks * nodes
    for block in range(blocks):
        index = neigh_ref[:, block * LANES : (block + 1) * LANES]
        local = index - first_cell + cells
        lane = jnp.bitwise_and(local, LANES - 1)
        step = jnp.right_shift(local, 7) - block
        step = jnp.where(index >= 0, step, -1)
        for node in range(nodes):
            rows = pl.ds(block * nodes + node, faces, stride=per_face)
            lane_ref[rows, :] = lane
            step_ref[rows, :] = step


def sweep_rows(window_ref, rhs_ref, off_ref, inverse_ref, lane_ref, step_ref, faces, per, steps, store):
    width = 3 * per
    stride = steps[1]
    for half in range(0, per, 8):
        lanes = [lane_ref[f * per + half : f * per + half + 8, :] for f in range(faces)]
        dist = [step_ref[f * per + half : f * per + half + 8, :] for f in range(faces)]
        beside = [[jnp.zeros((8, LANES), jnp.float32)] * 5 for _ in range(faces)]
        for d in range(steps[0]):
            here = [dist[f] == d for f in range(faces)]
            for b in range(5):
                first = b * width + half + d * stride
                table = window_ref[pl.ds(first, 8), :]
                for f in range(faces):
                    got = jnp.take_along_axis(
                        table, lanes[f], axis=1, mode="promise_in_bounds"
                    )
                    beside[f][b] = jnp.where(here[f], got, beside[f][b])
        remaining = []
        for a in range(5):
            total = rhs_ref[a * per + half : a * per + half + 8, :]
            for f in range(faces):
                for b in range(5):
                    row = (f * 25 + 5 * a + b) * per + half
                    total = total - off_ref[row : row + 8, :] * beside[f][b]
            remaining.append(total)
        for a in range(5):
            total = None
            for b in range(5):
                row = (5 * a + b) * per + half
                term = inverse_ref[row : row + 8, :] * remaining[b]
                total = term if total is None else total + term
            store(a, half, total)


def fill_window(window_ref, before_ref, own_ref, after_ref, per):
    for b in range(5):
        for place, ref in enumerate((before_ref, own_ref, after_ref)):
            window_ref[(3 * b + place) * per : (3 * b + place + 1) * per, :] = ref[
                b * per : (b + 1) * per, :
            ]


def sweep_kernel(
    nodes,
    before_ref,
    own_ref,
    after_ref,
    rhs_ref,
    off_ref,
    inverse_ref,
    neigh_ref,
    out_ref,
    window_ref,
    off32_ref,
    lane_ref,
    step_ref,
):
    faces, cells = neigh_ref.shape
    blocks = cells // LANES
    per = blocks * nodes
    first_cell = lax.axis_index(CELL_AXES) * cells
    spread_neighbours(neigh_ref, first_cell, lane_ref, step_ref, nodes)
    fill_window(window_ref, before_ref, own_ref, after_ref, per)
    off32_ref[...] = off_ref[...].astype(jnp.float32)

    def store(a, half, value):
        out_ref[a * per + half : a * per + half + 8, :] = value

    sweep_rows(
        window_ref, rhs_ref, off32_ref, inverse_ref, lane_ref, step_ref,
        faces, per, (2 * blocks + 1, nodes), store,
    )


def last_sweep_kernel(
    nodes,
    before_ref,
    own_ref,
    after_ref,
    rhs_ref,
    off_ref,
    inverse_ref,
    neigh_ref,
    weight_ref,
    sens_ref,
    out_ref,
    sens_out_ref,
    window_ref,
    off32_ref,
    lane_ref,
    step_ref,
    part_ref,
):
    sweep_kernel(
        nodes, before_ref, own_ref, after_ref, rhs_ref, off_ref, inverse_ref, neigh_ref,
        out_ref, window_ref, off32_ref, lane_ref, step_ref,
    )
    cells = neigh_ref.shape[1]
    blocks = cells // LANES
    per = blocks * nodes
    row_node = lax.rem(lax.broadcasted_iota(jnp.int32, (per, LANES), 0), nodes)
    weights = jnp.zeros((per, LANES), jnp.float32)
    for node in range(nodes):
        weights = jnp.where(row_node == node, weight_ref[node], weights)
    for k in range(3):
        total = None
        for a in range(5):
            row = (3 * a + k) * per
            term = out_ref[a * per : (a + 1) * per, :] * sens_ref[row : row + per, :].astype(
                jnp.float32
            )
            total = term if total is None else total + term
        part_ref[k * per : (k + 1) * per, :] = total * weights
    for block in range(blocks):
        total = None
        for node in range(nodes):
            term = part_ref[pl.ds(block * nodes + node, 3, stride=per), :]
            total = term if total is None else total + term
        sens_out_ref[:, block * LANES : (block + 1) * LANES] = total


def pieces(value, count):
    found = []
    for _ in range(count):
        piece = value.astype(jnp.bfloat16).astype(jnp.float32)
        found.append(piece)
        value = value - piece
    return found


def distance_factors(points, left):
    count = points.shape[1]
    scaled = (points - 0.5) * (1.0 / SUPPORT_RADIUS)
    scaled = jnp.concatenate([scaled, jnp.zeros((5, count), jnp.float32)], axis=0)
    norm = jnp.sum(scaled * scaled, axis=0, keepdims=True)
    norms = pieces(jnp.broadcast_to(norm, (8, count)), 3)
    row = lax.broadcasted_iota(jnp.int32, (8, count), 0)
    norm_block = jnp.zeros((8, count), jnp.float32)
    for place in range(3):
        norm_block = jnp.where(row == place, norms[place], norm_block)
    ones_block = jnp.where(row < 3, 1.0, 0.0)
    first, second, third = pieces(scaled, 3)
    if left:
        dims = [first, first, second, second, first, third]
        dims = [-2.0 * part for part in dims]
        blocks = dims + [norm_block, ones_block]
    else:
        dims = [first, second, first, second, third, first]
        blocks = dims + [ones_block, norm_block]
    return jnp.concatenate(blocks, axis=0)


def response_kernel(
    chunk, cell_ref, base_ref, index_ref, weight_ref, out_ref, left_ref, lattice_ref
):
    cells = cell_ref.shape[1]
    owned = base_ref.shape[1] // lax.axis_size("nodes")
    start = pl.multiple_of(lax.axis_index("nodes") * owned, LANES)
    left_ref[...] = distance_factors(cell_ref[...], True).T.astype(jnp.bfloat16)
    slots = index_ref.shape[0]
    columns = out_ref.shape[1]
    out_ref[...] = jnp.zeros_like(out_ref)

    @pl.loop(0, owned // chunk)
    def _(step):
        here = pl.ds(pl.multiple_of(start + step * chunk, LANES), chunk)
        index = index_ref[:, here]
        weight = weight_ref[:, here]
        combined = []
        for j in range(slots):
            total = weight[j : j + 1]
            for i in range(slots):
                if i != j:
                    total = total + jnp.where(
                        index[i : i + 1] == index[j : j + 1], weight[i : i + 1], 0.0
                    )
            combined.append(total)

        for tile in range(0, columns, 8):
            row = lax.broadcasted_iota(jnp.int32, (8, chunk), 0) + tile
            value = jnp.zeros((8, chunk), jnp.float32)
            for j in range(slots):
                value = jnp.where(index[j : j + 1] == row, combined[j], value)
            lattice_ref[tile : tile + 8, :] = value
        lattice = lattice_ref[...]
        lattice_first = lattice.astype(jnp.bfloat16)
        lattice_rest = (lattice - lattice_first.astype(jnp.float32)).astype(jnp.bfloat16)
        right = distance_factors(base_ref[:, here], False).astype(jnp.bfloat16)
        squared = jnp.dot(left_ref[...], right, preferred_element_type=jnp.float32)
        squared = jnp.maximum(squared, 1e-30)
        near = jnp.maximum(1.0 - squared * lax.rsqrt(squared), 0.0)
        power = near * near
        kernel = power * power * (1.25 - near)
        kernel_first = kernel.astype(jnp.bfloat16)
        kernel_rest = (kernel - kernel_first.astype(jnp.float32)).astype(jnp.bfloat16)
        over = (((1,), (1,)), ((), ()))
        out_ref[...] += lax.dot_general(
            jnp.concatenate([kernel_first, kernel_rest, kernel_first], axis=1),
            jnp.concatenate([lattice_first, lattice_first, lattice_rest], axis=1),
            over,
            preferred_element_type=jnp.float32,
        )


def control_kernel(scale, copies, *refs):
    sens_refs, (response_ref, out_ref) = refs[:-2], refs[-2:]
    total = sens_refs[0][...]
    for ref in sens_refs[1:]:
        total = total + ref[...]
    grad = jnp.dot(
        total * scale,
        response_ref[...],
        precision=lax.Precision.HIGHEST,
        preferred_element_type=jnp.float32,
    )
    for copy in range(copies):
        out_ref[copy] = grad


def vmem(count):
    return [pl.BlockSpec(memory_space=pltpu.VMEM)] * count


def body(
    adjoint_start,
    adjoint_rhs,
    off_blocks,
    diag_inverse,
    neighbours,
    node_weights,
    sens_blocks,
    cell_points,
    base_points,
    ffd_index,
    ffd_weight,
):
    nodes, _, cells = adjoint_start.shape
    faces = off_blocks.shape[1]
    blocks = cells // LANES
    per = blocks * nodes
    params = pltpu.CompilerParams(vmem_limit_bytes=VMEM_LIMIT)

    peers = lax.axis_size(CELL_AXES)
    up = [(i, i + 1) for i in range(peers - 1)]
    down = [(j, i) for i, j in up]
    rhs = rows_of(adjoint_rhs)
    off = rows_of(off_blocks.reshape(nodes, faces * 25, cells))
    inverse = rows_of(diag_inverse)
    sens = rows_of(sens_blocks)
    scratch = [
        pltpu.VMEM((3 * 5 * per, LANES), jnp.float32),
        pltpu.VMEM((faces * 25 * per, LANES), jnp.float32),
        pltpu.VMEM((faces * per, LANES), jnp.int32),
        pltpu.VMEM((faces * per, LANES), jnp.int32),
    ]

    base_count = base_points.shape[1]
    owned = base_count // lax.axis_size("nodes")
    chunk = min(256, owned)
    response = pl.pallas_call(
        functools.partial(response_kernel, chunk),
        out_shape=jax.ShapeDtypeStruct((cells, FFD), jnp.float32),
        in_specs=vmem(4),
        out_specs=pl.BlockSpec(memory_space=pltpu.VMEM),
        scratch_shapes=[
            pltpu.VMEM((cells, 64), jnp.bfloat16),
            pltpu.VMEM((FFD, chunk), jnp.float32),
        ],
        compiler_params=params,
        cost_estimate=pl.CostEstimate(
            flops=2 * 3 * cells * owned * FFD, bytes_accessed=4 * cells * FFD, transcendentals=0
        ),
        name="response",
    )(cell_points, base_points, ffd_index.T, ffd_weight.T)

    adjoint = rows_of(adjoint_start)
    for step in range(SWEEPS):
        before = lax.ppermute(adjoint, CELL_AXES, up)
        after = lax.ppermute(adjoint, CELL_AXES, down)
        common = (before, adjoint, after, rhs, off, inverse, neighbours)
        cost = pl.CostEstimate(
            flops=2 * 10 * 35 * cells, bytes_accessed=2 * faces * 25 * per * LANES, transcendentals=0
        )
        if step < SWEEPS - 1:
            adjoint = pl.pallas_call(
                functools.partial(sweep_kernel, nodes),
                out_shape=jax.ShapeDtypeStruct((5 * per, LANES), jnp.float32),
                in_specs=vmem(7),
                out_specs=pl.BlockSpec(memory_space=pltpu.VMEM),
                scratch_shapes=scratch,
                compiler_params=params,
                cost_estimate=cost,
                name="sweep",
            )(*common)
        else:
            adjoint, part_sens = pl.pallas_call(
                functools.partial(last_sweep_kernel, nodes),
                out_shape=(
                    jax.ShapeDtypeStruct((5 * per, LANES), jnp.float32),
                    jax.ShapeDtypeStruct((3, cells), jnp.float32),
                ),
                in_specs=vmem(7) + [pl.BlockSpec(memory_space=pltpu.SMEM)] + vmem(1),
                out_specs=tuple(vmem(2)),
                scratch_shapes=scratch + [pltpu.VMEM((3 * per, LANES), jnp.float32)],
                compiler_params=params,
                cost_estimate=cost,
                name="last_sweep",
            )(*common, node_weights, sens)

    node_peers = lax.axis_size("nodes")
    all_sens = [part_sens]
    for shift in range(1, node_peers):
        ring = [(i, (i + shift) % node_peers) for i in range(node_peers)]
        all_sens.append(lax.ppermute(part_sens, "nodes", ring))
    holders = lax.axis_size(SUM_AXES)
    scale = 4.0 / math.sqrt(cells * peers)
    copies = pl.pallas_call(
        functools.partial(control_kernel, scale, holders),
        out_shape=jax.ShapeDtypeStruct((holders, 3, FFD), jnp.float32),
        in_specs=vmem(node_peers + 1),
        out_specs=pl.BlockSpec(memory_space=pltpu.VMEM),
        compiler_params=params,
        name="control",
    )(*all_sens, response)
    gathered = lax.all_to_all(copies, SUM_AXES, 0, 0, tiled=True)
    control_grad = jnp.sum(gathered, axis=0)
    return (from_rows(adjoint, nodes, cells), control_grad)


def solution(mesh):
    return jax.shard_map(
        body,
        mesh=mesh,
        in_specs=(
            P("nodes", None, ("groups", "cells", "sub")),
            P("nodes", None, ("groups", "cells", "sub")),
            P("nodes", None, None, ("groups", "cells", "sub")),
            P("nodes", None, ("groups", "cells", "sub")),
            P(None, ("cells", "sub")),
            P("nodes"),
            P("nodes", None, ("groups", "cells", "sub")),
            P(None, ("cells", "sub")),
            P(),
            P(),
            P(),
        ),
        out_specs=(P("nodes", None, ("groups", "cells", "sub")), P("groups", None)),
        check_vma=False,
    )
```

time: 311 us -> 63.4 us (0.20)
  local copies, waits for them, and re-layouts: 105 us -> 9.35 us
  other arithmetic: 65 us -> 0.63 us
  waiting for transfers between devices: 62.9 us -> 1.9 us
  blocking collectives: 38.8 us -> 15.8 us
  Pallas kernels: 0 us -> 21.6 us
  between operations: 14.8 us -> 0.73 us
  matrix products: 11.9 us -> 0 us
    gather x12 -> x0, local copies, waits for them, and re-layouts: 79.7 us -> none  [relax(): widened[:, :, local_index[face_slot]]]
    unnamed x2 -> x0, waiting for transfers between devices: 62.8 us -> none
    select_n x14 -> x0, other arithmetic: 50.5 us -> none  [the longest x12 49.7 us: relax(): jnp.where(present[face_slot][None, None, :], widened[:, :, local_index[fa...]
    psum x2 -> x0, blocking collectives: 38.8 us -> none  [the longest x1 30.6 us: body(): control_grad = lax.psum(own_grad, ('cells', 'nodes', 'sub'))]
    pallas_call x0 -> x4, Pallas kernels: none -> 21.6 us  [the longest x1 13.3 us: body(): pl.pallas_call(functools.partial(response_kernel, chunk), out_shape=jax.S...]
    all_to_all x0 -> x1, blocking collectives: none -> 15.8 us  [body(): gathered = lax.all_to_all(copies, SUM_AXES, 0, 0, tiled=True)]
    dot_general x9 -> x0, matrix products: 11.9 us -> none  [the longest x8 11.6 us: kernel_sum(): jnp.dot(sensitivity, kernel, precision=lax.Precision.HIGHEST, preferred_e...]
    reduce_sum x17 -> x1, other arithmetic: 10.6 us -> 0.63 us  [body(): control_grad = jnp.sum(gathered, axis=0)]
  transfers between devices with their start and end apart: 5 -> 5, of which waited for: 1 -> 2; matrix products, arithmetic and copies ran while one was open for 4% -> 0% of each run, Pallas kernels for 0% -> 21%
where the time goes in v1:
time: 63.4 us; the launch traced here: 62.6 us
  Pallas kernels  21.6 us (34%)
  blocking collectives  15.8 us (25%)
  starting transfers between devices  12.6 us (20%)
  local copies, waits for them, and re-layouts  9.35 us (15%)
  waiting for transfers between devices  1.9 us (3%)
  between operations  0.73 us (1%)
    all_to_all x1, blocking collectives, body(): gathered = lax.all_to_all(copies, SUM_AXES, 0, 0, tiled=True)  15.8 us
    pallas_call x1, Pallas kernels, body(): pl.pallas_call(functools.partial(response_kernel, chunk), out_shape=jax.S...  13.3 us
    unnamed x30, local copies, waits for them, and re-layouts  9.35 us
    ppermute x2, starting transfers between devices, body(): before = lax.ppermute(adjoint, CELL_AXES, up)  8.54 us
    pallas_call x1, Pallas kernels, body(): pl.pallas_call(functools.partial(last_sweep_kernel, nodes), out_shape=(ja...  4.2 us
    pallas_call x1, Pallas kernels, body(): pl.pallas_call(functools.partial(sweep_kernel, nodes), out_shape=jax.Shap...  3.03 us
    ppermute x2, starting transfers between devices, body(): after = lax.ppermute(adjoint, CELL_AXES, down)  2.58 us
    ppermute x2, waiting for transfers between devices, body(): before = lax.ppermute(adjoint, CELL_AXES, up)  1.89 us
  transfers between devices with their start and end apart: 5, of which 2 were waited for; matrix products, arithmetic and copies ran while one was open for 0% of the time, Pallas kernels for 21%

profile of v1, /device:TPU:0, one launch (start us, length us, event | category | flops | bytes accessed | tf_op | source)
XLA Modules:
  0.0 62.6 jit_solution(2896986882953996891)
XLA Ops:
  0.6 1.3 %collective-permute-start.1 = (f32[80,128]{1,0:T(8,128)}, f32[80,128]{1,0:T(8,128)S(1)}, u32[]{:S(2)}, u32[]{:S(2)}) collective-permute-start(f32[80,128]{1,0:T(8,128)} %bitcast.39), channel_id=1, source_target_pairs={{1,0},{4,1},{5,4},{8,5},{9,8},{12,9},{13,12},{3,2},{6,3},{7,6},{10... | collective-permute-start | bytes 122888 | tf_op jit(solution)/shard_map/ppermute | solution.py:328
  1.9 3.0 %collective-permute-start = (f32[80,128]{1,0:T(8,128)}, f32[80,128]{1,0:T(8,128)S(1)}, u32[]{:S(2)}, u32[]{:S(2)}) collective-permute-start(f32[80,128]{1,0:T(8,128)} %bitcast.40), channel_id=1, source_target_pairs={{0,1},{1,4},{4,5},{5,8},{8,9},{9,12},{12,13},{2,3},{3,6},{6,7},{7,... | collective-permute-start | bytes 122888 | tf_op jit(solution)/shard_map/ppermute | solution.py:327
  5.0 0.0 collective-permute-done.1.after_ref
  5.0 1.1 %collective-permute-done.before_ref = f32[80,128]{1,0:T(8,128)S(1)} collective-permute-done((f32[80,128]{1,0:T(8,128)}, f32[80,128]{1,0:T(8,128)S(1)}, u32[]{:S(2)}, u32[]{:S(2)}) %collective-permute-start) | collective-permute-done | bytes 40992 | tf_op jit(solution)/shard_map/ppermute | solution.py:327
  6.0 0.0 copy-start
  6.0 1.1 %copy-done = bf16[2,6,25,1024]{3,0,2,1:T(2,128)(2,1)S(1)} copy-done((bf16[2,6,25,1024]{3,0,2,1:T(2,128)(2,1)S(1)}, bf16[2,6,25,1024]{3,0,2,1:T(2,128)(2,1)}, u32[]{:S(2)}) %copy-start) | copy-done | bytes 614424
  7.1 0.9 %copy-done.2 = f32[2,25,1024]{2,0,1:T(2,128)S(1)} copy-done((f32[2,25,1024]{2,0,1:T(2,128)S(1)}, f32[2,25,1024]{2,0,1:T(2,128)}, u32[]{:S(2)}) %copy-start.2) | copy-done | bytes 204824
  8.0 0.8 %copy-done.4 = f32[2,5,1024]{2,0,1:T(2,128)S(1)} copy-done((f32[2,5,1024]{2,0,1:T(2,128)S(1)}, f32[2,5,1024]{2,0,1:T(2,128)}, u32[]{:S(2)}) %copy-start.4) | copy-done | bytes 40984
  8.8 0.8 %copy-done.6 = s32[6,1024]{1,0:T(8,128)S(1)} copy-done((s32[6,1024]{1,0:T(8,128)S(1)}, s32[6,1024]{1,0:T(8,128)}, u32[]{:S(2)}) %copy-start.6) | copy-done | bytes 24600
  9.6 0.8 %copy-done.9 = f32[2,5,1024]{2,0,1:T(2,128)S(1)} copy-done((f32[2,5,1024]{2,0,1:T(2,128)S(1)}, f32[2,5,1024]{2,0,1:T(2,128)}, u32[]{:S(2)}) %copy-start.9) | copy-done | bytes 40984
  10.4 3.0 %sweep.1.own_ref = f32[80,128]{1,0:T(8,128)S(1)} custom-call(f32[80,128]{1,0:T(8,128)S(1)} %collective-permute-done.before_ref, f32[80,128]{1,0:T(8,128)S(1)} %bitcast.41, f32[80,128]{1,0:T(8,128)S(1)} %collective-permute-done.1.after_ref, f32[80,128]{1,0:T(8,128)S(1)} %bitcast.36, bf16[2400,128]{1,0:T(8,128)(2,1)S(1)} %bitcast.32, f32[400,128]{1,0:T(8,128)S(1)} %bitcast.34, ...), custom_call_target="tpu_custom_call" | custom-call | flops 716800 | bytes 614400 | tf_op jit(solution)/shard_map/sweep/pallas_call | solution.py:334
  13.4 1.3 %collective-permute-start.3 = (f32[80,128]{1,0:T(8,128)S(1)}, f32[80,128]{1,0:T(8,128)S(1)}, u32[]{:S(2)}, u32[]{:S(2)}) collective-permute-start(f32[80,128]{1,0:T(8,128)S(1)} %sweep.1.own_ref), channel_id=1, source_target_pairs={{1,0},{4,1},{5,4},{8,5},{9,8},{12,9},{13,12},{3,2},{6,3},{7,6},{10... | collective-permute-start | bytes 122888 | tf_op jit(solution)/shard_map/ppermute | solution.py:328
  14.7 5.5 %collective-permute-start.2 = (f32[80,128]{1,0:T(8,128)S(1)}, f32[80,128]{1,0:T(8,128)S(1)}, u32[]{:S(2)}, u32[]{:S(2)}) collective-permute-start(f32[80,128]{1,0:T(8,128)S(1)} %sweep.1.own_ref), channel_id=1, source_target_pairs={{0,1},{1,4},{4,5},{5,8},{8,9},{9,12},{12,13},{2,3},{3,6},{6,7},{7,... | collective-permute-start | bytes 122888 | tf_op jit(solution)/shard_map/ppermute | solution.py:327
  20.2 0.0 collective-permute-done.3.after_ref
  20.2 0.8 %collective-permute-done.2.before_ref = f32[80,128]{1,0:T(8,128)S(1)} collective-permute-done((f32[80,128]{1,0:T(8,128)S(1)}, f32[80,128]{1,0:T(8,128)S(1)}, u32[]{:S(2)}, u32[]{:S(2)}) %collective-permute-start.2) | collective-permute-done | bytes 40992 | tf_op jit(solution)/shard_map/ppermute | solution.py:327
  21.1 1.1 %copy-done.1 = bf16[2,6,25,1024]{3,0,2,1:T(2,128)(2,1)S(1)} copy-done((bf16[2,6,25,1024]{3,0,2,1:T(2,128)(2,1)S(1)}, bf16[2,6,25,1024]{3,0,2,1:T(2,128)(2,1)}, u32[]{:S(2)}) %copy-start.1) | copy-done | bytes 614424
  22.1 0.9 %copy-done.3 = f32[2,25,1024]{2,0,1:T(2,128)S(1)} copy-done((f32[2,25,1024]{2,0,1:T(2,128)S(1)}, f32[2,25,1024]{2,0,1:T(2,128)}, u32[]{:S(2)}) %copy-start.3) | copy-done | bytes 204824
  23.1 0.8 %copy-done.5 = f32[2,5,1024]{2,0,1:T(2,128)S(1)} copy-done((f32[2,5,1024]{2,0,1:T(2,128)S(1)}, f32[2,5,1024]{2,0,1:T(2,128)}, u32[]{:S(2)}) %copy-start.5) | copy-done | bytes 40984
  23.9 0.8 %copy-done.7 = s32[6,1024]{1,0:T(8,128)S(1)} copy-done((s32[6,1024]{1,0:T(8,128)S(1)}, s32[6,1024]{1,0:T(8,128)}, u32[]{:S(2)}) %copy-start.7) | copy-done | bytes 24600
  24.6 0.8 %copy-done.8 = bf16[2,15,1024]{2,0,1:T(2,128)(2,1)S(1)} copy-done((bf16[2,15,1024]{2,0,1:T(2,128)(2,1)S(1)}, bf16[2,15,1024]{2,0,1:T(2,128)(2,1)}, u32[]{:S(2)}) %copy-start.8) | copy-done | bytes 61464
  25.4 0.7 %copy-done.10 = f32[2]{0:T(128)S(1)} copy-done((f32[2]{0:T(128)S(1)}, f32[2]{0:T(128)}, u32[]{:S(2)}) %copy-start.10) | copy-done | bytes 32
  26.1 4.2 %last_sweep.1 = (f32[80,128]{1,0:T(8,128)}, f32[3,1024]{1,0:T(4,128)S(1)}) custom-call(f32[80,128]{1,0:T(8,128)S(1)} %collective-permute-done.2.before_ref, f32[80,128]{1,0:T(8,128)S(1)} %sweep.1.own_ref, f32[80,128]{1,0:T(8,128)S(1)} %collective-permute-done.3.after_ref, f32[80,128]{1,0:T(8,128)S(1)} %bitcast.37, bf16[2400,128]{1,0:T(8,128)(2,1)S(1)} %bitcast.33, ...), custom_call_target="tpu_custom_call" | custom-call | flops 716800 | bytes 614400 | tf_op jit(solution)/shard_map/last_sweep/pallas_call | solution.py:345
  30.3 1.5 %collective-permute-start.4 = (f32[3,1024]{1,0:T(4,128)S(1)}, f32[3,1024]{1,0:T(4,128)S(1)}, u32[]{:S(2)}, u32[]{:S(2)}) collective-permute-start(f32[3,1024]{1,0:T(4,128)S(1)} %get-tuple-element.5.refs_0_), channel_id=1, source_target_pairs={{0,2},{2,0},{1,3},{3,1},{4,6},{6,4},{5,7},{7,5},{8,10},{10,8},{9,1... | collective-permute-start | bytes 36872 | tf_op jit(solution)/shard_map/ppermute | solution.py:363
  31.8 0.0 copy-done.11
  31.8 0.0 copy-done.12
  31.8 0.0 copy-done.13
  31.8 0.0 copy-done.14
  31.8 13.3 %response.1.refs_2_ = f32[1024,512]{1,0:T(8,128)S(1)} custom-call(f32[3,1024]{1,0:T(4,128)S(1)} %copy-done.14, f32[3,4096]{1,0:T(4,128)S(1)} %copy-done.13, s32[8,4096]{1,0:T(8,128)S(1)} %bitcast.42, f32[8,4096]{1,0:T(8,128)S(1)} %bitcast.43), custom_call_target="tpu_custom_call" | custom-call | flops 6442450944 | bytes 2097152 | tf_op jit(solution)/shard_map/response/pallas_call | solution.py:309
  45.1 0.0 collective-permute-done.4.refs_1_
  45.2 1.0 %control.1 = f32[16,3,512]{2,1,0:T(4,128)S(1)} custom-call(f32[3,1024]{1,0:T(4,128)S(1)} %get-tuple-element.5.refs_0_, f32[3,1024]{1,0:T(4,128)S(1)} %collective-permute-done.4.refs_1_, f32[1024,512]{1,0:T(8,128)S(1)} %response.1.refs_2_), custom_call_target="tpu_custom_call" | custom-call | tf_op jit(solution)/shard_map/control/pallas_call | solution.py:366
  46.2 15.8 %all_to_all.5 = f32[16,3,512]{2,1,0:T(4,128)S(1)} all-to-all(f32[16,3,512]{2,1,0:T(4,128)S(1)} %control.1), channel_id=1, replica_groups=mesh['groups'=2,'cells'=4,'nodes'=2,'sub'=2] {'cells','nodes','sub'}, dimensions={0} | all-to-all | bytes 196608 | tf_op jit(solution)/shard_map/all_to_all | solution.py:374
  62.0 0.6 %reduce_sum.9 = f32[3,512]{1,0:T(4,128)} reduce(f32[16,3,512]{2,1,0:T(4,128)S(1)} %all_to_all.5, f32[]{:T(128)} %constant.0.clone.1), dimensions={0}, to_apply=%region_0.0 | reduce | flops 23040 | bytes 104452 | tf_op jit(solution)/shard_map/reduce_sum | solution.py:375
  (14 shorter events, 0.0 us)
Async XLA Ops:
  0.6 4.3 %collective-permute-start.1 = (f32[80,128]{1,0:T(8,128)}, f32[80,128]{1,0:T(8,128)S(1)}, u32[]{:S(2)}, u32[]{:S(2)}) collective-permute-start(f32[80,128]{1,0:T(8,128)} %bitcast.39), channel_id=1, source_target_pairs={{1,0},{4,1},{5,4},{8,5},{9,8},{12,9},{13,12},{3,2},{6,3},{7,6},{10... | collective-permute-start | bytes 122888 | tf_op jit(solution)/shard_map/ppermute | solution.py:328
  1.9 4.1 %collective-permute-start = (f32[80,128]{1,0:T(8,128)}, f32[80,128]{1,0:T(8,128)S(1)}, u32[]{:S(2)}, u32[]{:S(2)}) collective-permute-start(f32[80,128]{1,0:T(8,128)} %bitcast.40), channel_id=1, source_target_pairs={{0,1},{1,4},{4,5},{5,8},{8,9},{9,12},{12,13},{2,3},{3,6},{6,7},{7,... | collective-permute-start | bytes 122888 | tf_op jit(solution)/shard_map/ppermute | solution.py:327
  6.0 1.1 %copy-start = (bf16[2,6,25,1024]{3,0,2,1:T(2,128)(2,1)S(1)}, bf16[2,6,25,1024]{3,0,2,1:T(2,128)(2,1)}, u32[]{:S(2)}) copy-start(bf16[2,6,25,1024]{3,0,2,1:T(2,128)(2,1)} %param.13) | copy-start | bytes 1843204
  7.1 0.9 %copy-start.2 = (f32[2,25,1024]{2,0,1:T(2,128)S(1)}, f32[2,25,1024]{2,0,1:T(2,128)}, u32[]{:S(2)}) copy-start(f32[2,25,1024]{2,0,1:T(2,128)} %param.14) | copy-start | bytes 614404
  8.0 0.8 %copy-start.4 = (f32[2,5,1024]{2,0,1:T(2,128)S(1)}, f32[2,5,1024]{2,0,1:T(2,128)}, u32[]{:S(2)}) copy-start(f32[2,5,1024]{2,0,1:T(2,128)} %param.12) | copy-start | bytes 122884
  8.8 0.8 %copy-start.6 = (s32[6,1024]{1,0:T(8,128)S(1)}, s32[6,1024]{1,0:T(8,128)}, u32[]{:S(2)}) copy-start(s32[6,1024]{1,0:T(8,128)} %neigh_ref.3) | copy-start | bytes 73732
  9.6 0.8 %copy-start.9 = (f32[2,5,1024]{2,0,1:T(2,128)S(1)}, f32[2,5,1024]{2,0,1:T(2,128)}, u32[]{:S(2)}) copy-start(f32[2,5,1024]{2,0,1:T(2,128)} %param.11) | copy-start | bytes 122884
  10.4 21.4 %copy-start.11 = (s32[4096,8]{0,1:T(8,128)S(1)}, s32[4096,8]{0,1:T(8,128)}, u32[]{:S(2)}) copy-start(s32[4096,8]{0,1:T(8,128)} %param.20) | copy-start | bytes 393220
  10.4 21.4 %copy-start.12 = (f32[4096,8]{0,1:T(8,128)S(1)}, f32[4096,8]{0,1:T(8,128)}, u32[]{:S(2)}) copy-start(f32[4096,8]{0,1:T(8,128)} %param.21) | copy-start | bytes 393220
  10.4 21.4 %copy-start.13 = (f32[3,4096]{1,0:T(4,128)S(1)}, f32[3,4096]{1,0:T(4,128)}, u32[]{:S(2)}) copy-start(f32[3,4096]{1,0:T(4,128)} %base_ref.1) | copy-start | bytes 147460
  10.4 21.4 %copy-start.14 = (f32[3,1024]{1,0:T(4,128)S(1)}, f32[3,1024]{1,0:T(4,128)}, u32[]{:S(2)}) copy-start(f32[3,1024]{1,0:T(4,128)} %cell_ref.1) | copy-start | bytes 36868
  13.4 6.8 %collective-permute-start.3 = (f32[80,128]{1,0:T(8,128)S(1)}, f32[80,128]{1,0:T(8,128)S(1)}, u32[]{:S(2)}, u32[]{:S(2)}) collective-permute-start(f32[80,128]{1,0:T(8,128)S(1)} %sweep.1.own_ref), channel_id=1, source_target_pairs={{1,0},{4,1},{5,4},{8,5},{9,8},{12,9},{13,12},{3,2},{6,3},{7,6},{10... | collective-permute-start | bytes 122888 | tf_op jit(solution)/shard_map/ppermute | solution.py:328
  14.7 6.4 %collective-permute-start.2 = (f32[80,128]{1,0:T(8,128)S(1)}, f32[80,128]{1,0:T(8,128)S(1)}, u32[]{:S(2)}, u32[]{:S(2)}) collective-permute-start(f32[80,128]{1,0:T(8,128)S(1)} %sweep.1.own_ref), channel_id=1, source_target_pairs={{0,1},{1,4},{4,5},{5,8},{8,9},{9,12},{12,13},{2,3},{3,6},{6,7},{7,... | collective-permute-start | bytes 122888 | tf_op jit(solution)/shard_map/ppermute | solution.py:327
  21.1 1.1 %copy-start.1 = (bf16[2,6,25,1024]{3,0,2,1:T(2,128)(2,1)S(1)}, bf16[2,6,25,1024]{3,0,2,1:T(2,128)(2,1)}, u32[]{:S(2)}) copy-start(bf16[2,6,25,1024]{3,0,2,1:T(2,128)(2,1)} %param.13) | copy-start | bytes 1843204
  22.1 0.9 %copy-start.3 = (f32[2,25,1024]{2,0,1:T(2,128)S(1)}, f32[2,25,1024]{2,0,1:T(2,128)}, u32[]{:S(2)}) copy-start(f32[2,25,1024]{2,0,1:T(2,128)} %param.14) | copy-start | bytes 614404
  23.1 0.8 %copy-start.5 = (f32[2,5,1024]{2,0,1:T(2,128)S(1)}, f32[2,5,1024]{2,0,1:T(2,128)}, u32[]{:S(2)}) copy-start(f32[2,5,1024]{2,0,1:T(2,128)} %param.12) | copy-start | bytes 122884
  23.9 0.8 %copy-start.7 = (s32[6,1024]{1,0:T(8,128)S(1)}, s32[6,1024]{1,0:T(8,128)}, u32[]{:S(2)}) copy-start(s32[6,1024]{1,0:T(8,128)} %neigh_ref.3) | copy-start | bytes 73732
  24.6 0.8 %copy-start.8 = (bf16[2,15,1024]{2,0,1:T(2,128)(2,1)S(1)}, bf16[2,15,1024]{2,0,1:T(2,128)(2,1)}, u32[]{:S(2)}) copy-start(bf16[2,15,1024]{2,0,1:T(2,128)(2,1)} %param.17) | copy-start | bytes 184324
  25.4 0.7 %copy-start.10 = (f32[2]{0:T(128)S(1)}, f32[2]{0:T(128)}, u32[]{:S(2)}) copy-start(f32[2]{0:T(128)} %weight_ref.1) | copy-start | bytes 28
  30.3 14.8 %collective-permute-start.4 = (f32[3,1024]{1,0:T(4,128)S(1)}, f32[3,1024]{1,0:T(4,128)S(1)}, u32[]{:S(2)}, u32[]{:S(2)}) collective-permute-start(f32[3,1024]{1,0:T(4,128)S(1)} %get-tuple-element.5.refs_0_), channel_id=1, source_target_pairs={{0,2},{2,0},{1,3},{3,1},{4,6},{6,4},{5,7},{7,5},{8,10},{10,8},{9,1... | collective-permute-start | bytes 36872 | tf_op jit(solution)/shard_map/ppermute | solution.py:363

commit v2 on v0

v2 whole, which is shorter than its diff:
```python
import functools
import math

import jax
import jax.numpy as jnp
from jax import lax
from jax.experimental import pallas as pl
from jax.experimental.pallas import tpu as pltpu
from jax.sharding import PartitionSpec as P

SWEEPS = 2
FFD = 512
SUPPORT_RADIUS = 0.3
LANES = 128
CELL_AXES = ("cells", "sub")
FACTOR_ROWS = 64
PARAMS = pltpu.CompilerParams(vmem_limit_bytes=24 * 1024 * 1024)
VMEM = pl.BlockSpec(memory_space=pltpu.VMEM)
HBM = pl.BlockSpec(memory_space=pltpu.HBM)


def rows_of(array):
    nodes, rows, cells = array.shape
    blocks = cells // LANES
    split = array.reshape(nodes, rows, blocks, LANES)
    return split.transpose(1, 2, 0, 3).reshape(rows * blocks * nodes, LANES)


def from_rows(array, nodes, cells):
    blocks = cells // LANES
    split = array.reshape(-1, blocks, nodes, LANES)
    return split.transpose(2, 0, 1, 3).reshape(nodes, -1, cells)


def in_hbm(*arrays):
    return [pltpu.with_memory_space_constraint(array, pltpu.HBM) for array in arrays]


def prepare_kernel(
    nodes,
    off_in,
    inverse_in,
    rhs_in,
    sens_in,
    neigh_in,
    weight_in,
    index_in,
    spread_in,
    start_in,
    off_ref,
    inverse_ref,
    rhs_ref,
    sens_ref,
    lane_ref,
    step_ref,
    high_ref,
    spread_ref,
    one_hot_ref,
    start_ref,
    off_buf,
    sens_buf,
    neigh_buf,
    weight_buf,
    index_buf,
    sems,
):
    owned = index_buf.shape[1]
    start = pl.multiple_of(lax.axis_index("nodes") * owned, LANES)
    mine = pl.ds(start, owned)
    pairs = (
        (neigh_in, neigh_buf),
        (index_in.at[:, mine], index_buf),
        (off_in, off_buf),
        (weight_in, weight_buf),
        (sens_in, sens_buf),
        (spread_in.at[:, mine], spread_ref),
        (inverse_in, inverse_ref),
        (rhs_in, rhs_ref),
        (start_in, start_ref),
    )
    copies = [pltpu.make_async_copy(a, b, sems.at[i]) for i, (a, b) in enumerate(pairs)]
    for copy in copies:
        copy.start()

    faces, cells = neigh_buf.shape
    blocks = cells // LANES
    per = blocks * nodes
    first_cell = lax.axis_index(CELL_AXES) * cells
    copies[0].wait()
    for block in range(blocks):
        index = neigh_buf[:, block * LANES : (block + 1) * LANES]
        local = index - first_cell + cells
        lane = jnp.bitwise_and(local, LANES - 1)
        step = jnp.right_shift(local, 7) - block
        step = jnp.where(index >= 0, step, -1)
        for node in range(nodes):
            rows = pl.ds(block * nodes + node, faces, stride=per)
            lane_ref[rows, :] = lane
            step_ref[rows, :] = step

    copies[1].wait()
    high_ref[...] = jnp.right_shift(index_buf[...], 7)
    piece = min(512, owned)
    for first in range(0, owned, piece):
        here = slice(first, first + piece)
        low = jnp.bitwise_and(index_buf[:, here], LANES - 1).astype(jnp.float32)
        low = low.astype(jnp.bfloat16)
        row = lax.broadcasted_iota(jnp.int32, (LANES, piece), 0).astype(jnp.float32)
        row = row.astype(jnp.bfloat16)
        for j in range(index_buf.shape[0]):
            hit = jnp.broadcast_to(low[j : j + 1], (LANES, piece)) == row
            one_hot_ref[j * LANES : (j + 1) * LANES, here] = jnp.where(
                hit, jnp.bfloat16(1.0), jnp.bfloat16(0.0)
            )

    copies[2].wait()
    off_ref[...] = off_buf[...].astype(jnp.float32)
    copies[3].wait()
    copies[4].wait()
    row_node = lax.rem(lax.broadcasted_iota(jnp.int32, (per, LANES), 0), nodes)
    weights = jnp.zeros((per, LANES), jnp.float32)
    for node in range(nodes):
        weights = jnp.where(row_node == node, weight_buf[node], weights)
    for row in range(0, sens_buf.shape[0], per):
        here = slice(row, row + per)
        sens_ref[here, :] = sens_buf[here, :].astype(jnp.float32) * weights
    for copy in copies[5:]:
        copy.wait()


def sweep_into(
    blocks, first_ref, second_ref, own_ref, rhs_ref, off_ref, inverse_ref, lane_ref, step_ref,
    out_ref, window_ref,
):
    per = rhs_ref.shape[0] // 5
    nodes = per // blocks
    faces = lane_ref.shape[0] // per
    odd = lax.rem(lax.axis_index(CELL_AXES), 2)
    place = pl.multiple_of((1 - odd) * 2 * per, 8)
    other = pl.multiple_of(odd * 2 * per, 8)
    for b in range(5):
        rows = slice(b * per, (b + 1) * per)
        base = 3 * b * per
        window_ref[pl.ds(base + place, per), :] = first_ref[rows, :]
        window_ref[base + per : base + 2 * per, :] = own_ref[rows, :]
        window_ref[pl.ds(base + other, per), :] = second_ref[rows, :]
    for half in range(0, per, 8):
        lanes = [lane_ref[f * per + half : f * per + half + 8, :] for f in range(faces)]
        dist = [step_ref[f * per + half : f * per + half + 8, :] for f in range(faces)]
        beside = [[jnp.zeros((8, LANES), jnp.float32)] * 5 for _ in range(faces)]
        for d in range(2 * blocks + 1):
            here = [dist[f] == d for f in range(faces)]
            for b in range(5):
                table = window_ref[pl.ds(3 * b * per + half + d * nodes, 8), :]
                for f in range(faces):
                    got = jnp.take_along_axis(
                        table, lanes[f], axis=1, mode="promise_in_bounds"
                    )
                    beside[f][b] = jnp.where(here[f], got, beside[f][b])
        remaining = []
        for a in range(5):
            total = rhs_ref[a * per + half : a * per + half + 8, :]
            for f in range(faces):
                for b in range(5):
                    row = (f * 25 + 5 * a + b) * per + half
                    total = total - off_ref[row : row + 8, :] * beside[f][b]
            remaining.append(total)
        for a in range(5):
            total = None
            for b in range(5):
                row = (5 * a + b) * per + half
                term = inverse_ref[row : row + 8, :] * remaining[b]
                total = term if total is None else total + term
            out_ref[a * per + half : a * per + half + 8, :] = total


def sweep_kernel(blocks, *refs):
    sweep_into(blocks, *refs)


def last_sweep_kernel(blocks, *refs):
    ins, (sens_ref, _, out_ref, sens_out_ref, window_ref, part_ref) = refs[:8], refs[8:]
    sweep_into(blocks, *ins, out_ref, window_ref)
    per = out_ref.shape[0] // 5
    nodes = per // blocks
    for k in range(3):
        total = None
        for a in range(5):
            row = (3 * a + k) * per
            term = out_ref[a * per : (a + 1) * per, :] * sens_ref[row : row + per, :]
            total = term if total is None else total + term
        part_ref[k * per : (k + 1) * per, :] = total
    for block in range(blocks):
        total = None
        for node in range(nodes):
            term = part_ref[pl.ds(block * nodes + node, 3, stride=per), :]
            total = term if total is None else total + term
        sens_out_ref[:, block * LANES : (block + 1) * LANES] = total


def pieces(value, count):
    found = []
    for _ in range(count):
        piece = value.astype(jnp.bfloat16).astype(jnp.float32)
        found.append(piece)
        value = value - piece
    return found


def distance_factors(points, left):
    count = points.shape[1]
    scaled = (points - 0.5) * (1.0 / SUPPORT_RADIUS)
    scaled = jnp.concatenate([scaled, jnp.zeros((5, count), jnp.float32)], axis=0)
    norm = jnp.sum(scaled * scaled, axis=0, keepdims=True)
    norms = pieces(jnp.broadcast_to(norm, (8, count)), 3)
    row = lax.broadcasted_iota(jnp.int32, (8, count), 0)
    norm_block = jnp.zeros((8, count), jnp.float32)
    for place in range(3):
        norm_block = jnp.where(row == place, norms[place], norm_block)
    ones_block = jnp.where(row < 3, 1.0, 0.0)
    first, second, third = pieces(scaled, 3)
    if left:
        dims = [first, first, second, second, first, third]
        dims = [-2.0 * part for part in dims]
        blocks = dims + [norm_block, ones_block]
    else:
        dims = [first, second, first, second, third, first]
        blocks = dims + [ones_block, norm_block]
    return jnp.concatenate(blocks, axis=0)


def wendland_kernel(
    cell_in, base_in, _, kernel_ref, token_ref, cell_buf, base_buf, left_ref, right_ref, sems
):
    cells, owned = kernel_ref.shape
    start = pl.multiple_of(lax.axis_index("nodes") * owned, LANES)
    copies = [
        pltpu.make_async_copy(cell_in, cell_buf, sems.at[0]),
        pltpu.make_async_copy(base_in.at[:, pl.ds(start, owned)], base_buf, sems.at[1]),
    ]
    for copy in copies:
        copy.start()
    token_ref[...] = jnp.zeros_like(token_ref)
    copies[0].wait()
    left_ref[...] = distance_factors(cell_buf[...], True).T.astype(jnp.bfloat16)
    copies[1].wait()
    right_ref[...] = distance_factors(base_buf[...], False).astype(jnp.bfloat16)
    tile, wide = 64, min(256, owned)

    @pl.loop(0, cells // tile)
    def _(step):
        rows = pl.ds(pl.multiple_of(step * tile, tile), tile)
        left = left_ref[rows, :]
        for first in range(0, owned, wide):
            here = slice(first, first + wide)
            squared = jnp.dot(left, right_ref[:, here], preferred_element_type=jnp.float32)
            squared = jnp.maximum(squared, 1e-30)
            near = jnp.maximum(1.0 - squared * lax.rsqrt(squared), 0.0)
            power = near * near
            kernel_ref[rows, here] = power * power * (1.25 - near)


def control_kernel(scale, *refs):
    sens_refs = refs[:-7]
    kernel_ref, high_ref, spread_ref, one_hot_ref, out_ref, sens_buf, part_ref = refs[-7:]
    cells, owned = kernel_ref.shape
    slots = high_ref.shape[0]
    groups = FFD // LANES
    total = sens_refs[0][...]
    for ref in sens_refs[1:]:
        total = total + ref[...]
    total = jnp.concatenate([total * scale, jnp.zeros((5, cells), jnp.float32)], axis=0).T
    for k in range(3):
        sens_buf[k * cells : (k + 1) * cells, :] = jnp.broadcast_to(
            total[:, k : k + 1], (cells, LANES)
        )
    part_ref[...] = jnp.zeros_like(part_ref)
    wide = min(4 * LANES, owned)
    tile = 64
    for first in range(0, owned, wide):

        def add(step, sums):
            sums = list(sums)
            for inner in range(0, tile, 8):
                row = pl.multiple_of(step * tile, tile) + inner
                value = [
                    kernel_ref[pl.ds(row, 8), first + lane : first + lane + LANES]
                    for lane in range(0, wide, LANES)
                ]
                for k in range(3):
                    sens = sens_buf[pl.ds(k * cells + row, 8), :]
                    for place in range(len(value)):
                        at = k * len(value) + place
                        sums[at] = sums[at] + value[place] * sens
            return tuple(sums)

        count = wide // LANES
        zero = jnp.zeros((8, LANES), jnp.float32)
        sums = lax.fori_loop(0, cells // tile, add, (zero,) * (3 * count))
        for k in range(3):
            for place in range(count):
                lane = first + place * LANES
                grad = jnp.sum(sums[k * count + place], axis=0, keepdims=True)
                grad = grad * spread_ref[:, lane : lane + LANES]
                high = high_ref[:, lane : lane + LANES]
                for group in range(groups):
                    row = lane // LANES * slots * 16 + k * groups + group
                    part_ref[pl.ds(row, slots, stride=16), :] = jnp.where(
                        high == group, grad, 0.0
                    )
    result = jnp.zeros((32, LANES), jnp.float32)
    over = (((1,), (1,)), ((), ()))
    for j in range(slots):
        part = jnp.concatenate(
            [
                part_ref[(block * slots + j) * 16 : (block * slots + j + 1) * 16, :]
                for block in range(owned // LANES)
            ],
            axis=1,
        )
        part_first = part.astype(jnp.bfloat16)
        part_rest = (part - part_first.astype(jnp.float32)).astype(jnp.bfloat16)
        result = result + lax.dot_general(
            jnp.concatenate([part_first, part_rest], axis=0),
            one_hot_ref[j * LANES : (j + 1) * LANES, :],
            over,
            preferred_element_type=jnp.float32,
        )
    out_ref[...] = result[:16] + result[16:]


def tree(values):
    while len(values) > 1:
        values = [a + b for a, b in zip(values[::2], values[1::2])]
    return values[0]


def add_kernel(*refs):
    refs[-1][...] = tree([ref[...] for ref in refs[:-1]])


def finish_kernel(*refs):
    total = tree([ref[...] for ref in refs[:-1]])
    groups = FFD // LANES
    for k in range(3):
        for group in range(groups):
            row = k * groups + group
            refs[-1][k : k + 1, group * LANES : (group + 1) * LANES] = total[row : row + 1]


def exchanged(value, axes):
    peers = lax.axis_size(axes)
    if peers > 8 or peers & (peers - 1):
        return [lax.psum(value, axes)]
    return [value] + [
        lax.ppermute(value, axes, [(i, i ^ shift) for i in range(peers)])
        for shift in range(1, peers)
    ]


def body(
    adjoint_start,
    adjoint_rhs,
    off_blocks,
    diag_inverse,
    neighbours,
    node_weights,
    sens_blocks,
    cell_points,
    base_points,
    ffd_index,
    ffd_weight,
):
    nodes, _, cells = adjoint_start.shape
    faces = off_blocks.shape[1]
    blocks = cells // LANES
    per = blocks * nodes
    slots = ffd_index.shape[1]
    owned = base_points.shape[1] // lax.axis_size("nodes")
    peers = lax.axis_size(CELL_AXES)
    f32, i32, bf16 = jnp.float32, jnp.int32, jnp.bfloat16

    def shape(dims, dtype=f32):
        return jax.ShapeDtypeStruct(dims, dtype)

    def cost(flops, moved):
        return pl.CostEstimate(flops=flops, bytes_accessed=moved, transcendentals=0)

    def swaps(array):
        first = [(i, i ^ 1) for i in range(peers) if i ^ 1 < peers]
        second = [(i, i + 1 if i % 2 else i - 1) for i in range(peers)]
        second = [(i, j) for i, j in second if 0 <= j < peers]
        far = lax.ppermute(array, CELL_AXES, second)
        close = lax.ppermute(array, CELL_AXES, first)
        return far, close

    adjoint = rows_of(adjoint_start)
    far, close = swaps(adjoint)
    prepared = pl.pallas_call(
        functools.partial(prepare_kernel, nodes),
        out_shape=(
            shape((faces * 25 * per, LANES)),
            shape((25 * per, LANES)),
            shape((5 * per, LANES)),
            shape((15 * per, LANES)),
            shape((faces * per, LANES), i32),
            shape((faces * per, LANES), i32),
            shape((slots, owned), i32),
            shape((slots, owned)),
            shape((slots * LANES, owned), bf16),
            shape((5 * per, LANES)),
        ),
        in_specs=[HBM] * 9,
        out_specs=(VMEM,) * 10,
        scratch_shapes=[
            pltpu.VMEM((faces * 25 * per, LANES), bf16),
            pltpu.VMEM((15 * per, LANES), bf16),
            pltpu.VMEM((faces, cells), i32),
            pltpu.SMEM((nodes,), f32),
            pltpu.VMEM((slots, owned), i32),
            pltpu.SemaphoreType.DMA((9,)),
        ],
        compiler_params=PARAMS,
        cost_estimate=cost(10**9, 10**7),
        name="prepare",
    )(
        *in_hbm(
            rows_of(off_blocks.reshape(nodes, faces * 25, cells)),
            rows_of(diag_inverse),
            rows_of(adjoint_rhs),
            rows_of(sens_blocks),
            neighbours,
            node_weights,
            ffd_index.T,
            ffd_weight.T,
            adjoint,
        )
    )
    off, inverse, rhs, sens, lane, step, high, spread, one_hot, adjoint = prepared
    window = pltpu.VMEM((3 * 5 * per, LANES), f32)
    sweep_cost = cost(2 * 10 * 35 * cells, 4 * faces * 25 * per * LANES)

    for _ in range(SWEEPS - 1):
        adjoint = pl.pallas_call(
            functools.partial(sweep_kernel, blocks),
            out_shape=shape((5 * per, LANES)),
            in_specs=[VMEM] * 8,
            out_specs=VMEM,
            scratch_shapes=[window],
            compiler_params=PARAMS,
            cost_estimate=sweep_cost,
            name="sweep",
        )(close, far, adjoint, rhs, off, inverse, lane, step)
        far, close = swaps(adjoint)

    kernel, token = pl.pallas_call(
        wendland_kernel,
        out_shape=(shape((cells, owned)), shape((8, LANES))),
        in_specs=[HBM, HBM, VMEM],
        out_specs=(VMEM, VMEM),
        scratch_shapes=[
            pltpu.VMEM((3, cells), f32),
            pltpu.VMEM((3, owned), f32),
            pltpu.VMEM((cells, FACTOR_ROWS), bf16),
            pltpu.VMEM((FACTOR_ROWS, owned), bf16),
            pltpu.SemaphoreType.DMA((2,)),
        ],
        compiler_params=PARAMS,
        cost_estimate=cost(10**9, 10**7),
        name="wendland",
    )(*in_hbm(cell_points, base_points), adjoint)

    adjoint, part_sens = pl.pallas_call(
        functools.partial(last_sweep_kernel, blocks),
        out_shape=(shape((5 * per, LANES)), shape((3, cells))),
        in_specs=[VMEM] * 10,
        out_specs=(VMEM, VMEM),
        scratch_shapes=[window, pltpu.VMEM((3 * per, LANES), f32)],
        compiler_params=PARAMS,
        cost_estimate=sweep_cost,
        name="last_sweep",
    )(close, far, adjoint, rhs, off, inverse, lane, step, sens, token)

    all_sens = exchanged(part_sens, "nodes")
    scale = 4.0 / math.sqrt(cells * peers)
    partial = pl.pallas_call(
        functools.partial(control_kernel, scale),
        out_shape=shape((16, LANES)),
        in_specs=[VMEM] * (len(all_sens) + 4),
        out_specs=VMEM,
        scratch_shapes=[
            pltpu.VMEM((3 * cells, LANES), f32),
            pltpu.VMEM((owned // LANES * slots * 16, LANES), f32),
        ],
        compiler_params=PARAMS,
        name="control",
    )(*all_sens, kernel, high, spread, one_hot)

    close_parts = exchanged(partial, ("nodes", "sub"))
    partial = pl.pallas_call(
        add_kernel, out_shape=shape((16, LANES)), name="add", compiler_params=PARAMS
    )(*close_parts)
    control_grad = pl.pallas_call(
        finish_kernel, out_shape=shape((3, FFD)), name="finish", compiler_params=PARAMS
    )(*exchanged(partial, "cells"))
    return (from_rows(adjoint, nodes, cells), control_grad)


def solution(mesh):
    return jax.shard_map(
        body,
        mesh=mesh,
        in_specs=(
            P("nodes", None, ("groups", "cells", "sub")),
            P("nodes", None, ("groups", "cells", "sub")),
            P("nodes", None, None, ("groups", "cells", "sub")),
            P("nodes", None, ("groups", "cells", "sub")),
            P(None, ("cells", "sub")),
            P("nodes"),
            P("nodes", None, ("groups", "cells", "sub")),
            P(None, ("cells", "sub")),
            P(),
            P(),
            P(),
        ),
        out_specs=(P("nodes", None, ("groups", "cells", "sub")), P("groups", None)),
        check_vma=False,
    )
```

time: 311 us -> 43.7 us (0.14)
  local copies, waits for them, and re-layouts: 105 us -> 0 us
  other arithmetic: 65 us -> 0 us
  waiting for transfers between devices: 62.9 us -> 6.75 us
  blocking collectives: 38.8 us -> 0 us
  Pallas kernels: 0 us -> 19.1 us
  between operations: 14.8 us -> 0.71 us
  matrix products: 11.9 us -> 0 us
  starting transfers between devices: 10.4 us -> 16.9 us
    gather x12 -> x0, local copies, waits for them, and re-layouts: 79.7 us -> none  [relax(): widened[:, :, local_index[face_slot]]]
    unnamed x2 -> x0, waiting for transfers between devices: 62.8 us -> none
    select_n x14 -> x0, other arithmetic: 50.5 us -> none  [the longest x12 49.7 us: relax(): jnp.where(present[face_slot][None, None, :], widened[:, :, local_index[fa...]
    psum x2 -> x0, blocking collectives: 38.8 us -> none  [the longest x1 30.6 us: body(): control_grad = lax.psum(own_grad, ('cells', 'nodes', 'sub'))]
    pallas_call x0 -> x7, Pallas kernels: none -> 19.1 us  [the longest x1 6.03 us: body(): pl.pallas_call(wendland_kernel, out_shape=(shape((cells, owned)), shape((...]
    dot_general x9 -> x0, matrix products: 11.9 us -> none  [the longest x8 11.6 us: kernel_sum(): jnp.dot(sensitivity, kernel, precision=lax.Precision.HIGHEST, preferred_e...]
    reduce_sum x17 -> x0, other arithmetic: 10.6 us -> none  [the longest x12 7.63 us: relax(): coupled = coupled + jnp.sum(coupling * beside[:, None], axis=2)]
    concatenate x2 -> x0, local copies, waits for them, and re-layouts: 7.61 us -> none  [with_halo(): array = jnp.concatenate([before, array, after], axis=dim)]
  transfers between devices with their start and end apart: 5 -> 11, of which waited for: 1 -> 5; matrix products, arithmetic and copies ran while one was open for 4% -> 0% of each run, Pallas kernels for 0% -> 17%
where the time goes in v2:
time: 43.7 us; the launch traced here: 43.4 us
  Pallas kernels  19.1 us (44%)
  starting transfers between devices  16.9 us (39%)
  waiting for transfers between devices  6.75 us (15%)
  between operations  0.71 us (2%)
    ppermute x7, starting transfers between devices, exchanged(): lax.ppermute(value, axes, [(i, i ^ shift) for i in range(peers)])  7.82 us
    ppermute x2, starting transfers between devices, swaps(): close = lax.ppermute(array, CELL_AXES, first)  7.78 us
    ppermute x7, waiting for transfers between devices, exchanged(): lax.ppermute(value, axes, [(i, i ^ shift) for i in range(peers)])  6.74 us
    pallas_call x1, Pallas kernels, body(): pl.pallas_call(wendland_kernel, out_shape=(shape((cells, owned)), shape((...  6.03 us
    pallas_call x1, Pallas kernels, body(): pl.pallas_call(functools.partial(control_kernel, scale), out_shape=shape(...  4.39 us
    pallas_call x1, Pallas kernels, body(): pl.pallas_call(functools.partial(last_sweep_kernel, blocks), out_shape=(s...  3.56 us
    pallas_call x1, Pallas kernels, body(): pl.pallas_call(functools.partial(sweep_kernel, blocks), out_shape=shape((...  2.95 us
    pallas_call x1, Pallas kernels, body(): pl.pallas_call(functools.partial(prepare_kernel, nodes), out_shape=(shape...  1.5 us
  transfers between devices with their start and end apart: 11, of which 5 were waited for; matrix products, arithmetic and copies ran while one was open for 0% of the time, Pallas kernels for 17%

profile of v2, /device:TPU:0, one launch (start us, length us, event | category | flops | bytes accessed | tf_op | source)
XLA Modules:
  0.0 43.4 jit_solution(10034412740231361366)
XLA Ops:
  0.6 0.7 %collective-permute-start.1 = (f32[80,128]{1,0:T(8,128)}, f32[80,128]{1,0:T(8,128)S(1)}, u32[]{:S(2)}, u32[]{:S(2)}) collective-permute-start(f32[80,128]{1,0:T(8,128)} %bitcast.38), channel_id=1, source_target_pairs={{1,4},{4,1},{5,8},{8,5},{9,12},{12,9},{3,6},{6,3},{7,10},{10,7},{1... | collective-permute-start | bytes 122888 | tf_op jit(solution)/shard_map/ppermute | solution.py:393
  1.3 4.4 %collective-permute-start = (f32[80,128]{1,0:T(8,128)}, f32[80,128]{1,0:T(8,128)S(1)}, u32[]{:S(2)}, u32[]{:S(2)}) collective-permute-start(f32[80,128]{1,0:T(8,128)} %bitcast.39), channel_id=1, source_target_pairs={{0,1},{1,0},{4,5},{5,4},{8,9},{9,8},{12,13},{13,12},{2,3},{3,2},{6... | collective-permute-start | bytes 122888 | tf_op jit(solution)/shard_map/ppermute | solution.py:394
  5.8 1.5 %prepare.1 = (f32[2400,128]{1,0:T(8,128)S(1)}, f32[400,128]{1,0:T(8,128)S(1)}, f32[80,128]{1,0:T(8,128)S(1)}, f32[240,128]{1,0:T(8,128)S(1)}, s32[96,128]{1,0:T(...) custom-call(bf16[2400,128]{1,0:T(8,128)(2,1)} %bitcast.32, ...), custom_call_target="tpu_custom_call" | custom-call | flops 1000000000 | bytes 10000000 | tf_op jit(solution)/shard_map/prepare/pallas_call | solution.py:399
  7.3 0.0 collective-permute-done.1.refs_1_
  7.3 0.0 collective-permute-done.refs_0_
  7.3 3.0 %sweep.1._.refs_2_ = f32[80,128]{1,0:T(8,128)S(1)} custom-call(f32[80,128]{1,0:T(8,128)S(1)} %collective-permute-done.refs_0_, f32[80,128]{1,0:T(8,128)S(1)} %collective-permute-done.1.refs_1_, f32[80,128]{1,0:T(8,128)S(1)} %get-tuple-element.16.refs_2_, f32[80,128]{1,0:T(8,128)S(1)} %get-tuple-element.17.refs_3_, ...), custom_call_target="tpu_custom_call" | custom-call | flops 716800 | bytes 1228800 | tf_op jit(solution)/shard_map/sweep/pallas_call | solution.py:444
  10.2 0.7 %collective-permute-start.3 = (f32[80,128]{1,0:T(8,128)S(1)}, f32[80,128]{1,0:T(8,128)S(1)}, u32[]{:S(2)}, u32[]{:S(2)}) collective-permute-start(f32[80,128]{1,0:T(8,128)S(1)} %sweep.1._.refs_2_), channel_id=1, source_target_pairs={{1,4},{4,1},{5,8},{8,5},{9,12},{12,9},{3,6},{6,3},{7,10},{10,7},{1... | collective-permute-start | bytes 122888 | tf_op jit(solution)/shard_map/ppermute | solution.py:393
  10.9 3.3 %collective-permute-start.2 = (f32[80,128]{1,0:T(8,128)S(1)}, f32[80,128]{1,0:T(8,128)S(1)}, u32[]{:S(2)}, u32[]{:S(2)}) collective-permute-start(f32[80,128]{1,0:T(8,128)S(1)} %sweep.1._.refs_2_), channel_id=1, source_target_pairs={{0,1},{1,0},{4,5},{5,4},{8,9},{9,8},{12,13},{13,12},{2,3},{3,2},{6... | collective-permute-start | bytes 122888 | tf_op jit(solution)/shard_map/ppermute | solution.py:394
  14.2 6.0 %wendland.1 = (f32[1024,2048]{1,0:T(8,128)S(1)}, f32[8,128]{1,0:T(8,128)S(1)}) custom-call(f32[3,1024]{1,0:T(4,128)} %cell_in.1, f32[3,4096]{1,0:T(4,128)} %base_in.1, f32[80,128]{1,0:T(8,128)S(1)} %sweep.1._.refs_2_), custom_call_target="tpu_custom_call" | custom-call | flops 1000000000 | bytes 10000000 | tf_op jit(solution)/shard_map/wendland/pallas_call | solution.py:456
  20.3 0.0 collective-permute-done.3.refs_1_
  20.3 0.0 collective-permute-done.2.refs_0_
  20.3 3.6 %last_sweep.1 = (f32[80,128]{1,0:T(8,128)}, f32[3,1024]{1,0:T(4,128)S(1)}) custom-call(f32[80,128]{1,0:T(8,128)S(1)} %collective-permute-done.2.refs_0_, f32[80,128]{1,0:T(8,128)S(1)} %collective-permute-done.3.refs_1_, f32[80,128]{1,0:T(8,128)S(1)} %sweep.1._.refs_2_, f32[80,128]{1,0:T(8,128)S(1)} %get-tuple-element.17.refs_3_, ...), custom_call_target="tpu_custom_call" | custom-call | flops 716800 | bytes 1228800 | tf_op jit(solution)/shard_map/last_sweep/pallas_call | solution.py:473
  23.9 1.5 %collective-permute-start.4 = (f32[3,1024]{1,0:T(4,128)S(1)}, f32[3,1024]{1,0:T(4,128)S(1)}, u32[]{:S(2)}, u32[]{:S(2)}) collective-permute-start(f32[3,1024]{1,0:T(4,128)S(1)} %get-tuple-element.25.refs_0_), channel_id=1, source_target_pairs={{0,2},{2,0},{1,3},{3,1},{4,6},{6,4},{5,7},{7,5},{8,10},{10,8},{9,1... | collective-permute-start | bytes 36872 | tf_op jit(solution)/shard_map/ppermute | solution.py:356
  25.4 2.3 %collective-permute-done.4.refs_1_ = f32[3,1024]{1,0:T(4,128)S(1)} collective-permute-done((f32[3,1024]{1,0:T(4,128)S(1)}, f32[3,1024]{1,0:T(4,128)S(1)}, u32[]{:S(2)}, u32[]{:S(2)}) %collective-permute-start.4) | collective-permute-done | bytes 12320 | tf_op jit(solution)/shard_map/ppermute | solution.py:356
  27.6 4.4 %control.1.refs_0_ = f32[16,128]{1,0:T(8,128)S(1)} custom-call(f32[3,1024]{1,0:T(4,128)S(1)} %get-tuple-element.25.refs_0_, f32[3,1024]{1,0:T(4,128)S(1)} %collective-permute-done.4.refs_1_, f32[1024,2048]{1,0:T(8,128)S(1)} %get-tuple-element.26.refs_2_, s32[8,2048]{1,0:T(8,128)S(1)} %get-tuple-element.27.refs_3_, f32[8,2048]{1,0:T(8,128)S(1)} %get-tuple-element.28.refs_4_, ...), custom_call_target="tpu_custom_call" | custom-call | tf_op jit(solution)/shard_map/control/pallas_call | solution.py:486
  32.0 0.0 collective-permute-start.7
  32.0 1.6 %collective-permute-start.6 = (f32[16,128]{1,0:T(8,128)S(1)}, f32[16,128]{1,0:T(8,128)S(1)}, u32[]{:S(2)}, u32[]{:S(2)}) collective-permute-start(f32[16,128]{1,0:T(8,128)S(1)} %control.1.refs_0_), channel_id=1, source_target_pairs={{0,2},{1,3},{2,0},{3,1},{4,6},{5,7},{6,4},{7,5},{8,10},{9,11},{10,... | collective-permute-start | bytes 24584 | tf_op jit(solution)/shard_map/ppermute | solution.py:356
  33.6 0.3 collective-permute-start.5
  33.9 1.3 %collective-permute-done.7.refs_3_ = f32[16,128]{1,0:T(8,128)S(1)} collective-permute-done((f32[16,128]{1,0:T(8,128)S(1)}, f32[16,128]{1,0:T(8,128)S(1)}, u32[]{:S(2)}, u32[]{:S(2)}) %collective-permute-start.7) | collective-permute-done | bytes 8224 | tf_op jit(solution)/shard_map/ppermute | solution.py:356
  35.1 0.6 %collective-permute-done.6.refs_2_ = f32[16,128]{1,0:T(8,128)S(1)} collective-permute-done((f32[16,128]{1,0:T(8,128)S(1)}, f32[16,128]{1,0:T(8,128)S(1)}, u32[]{:S(2)}, u32[]{:S(2)}) %collective-permute-start.6) | collective-permute-done | bytes 8224 | tf_op jit(solution)/shard_map/ppermute | solution.py:356
  35.7 0.0 collective-permute-done.5.refs_1_
  35.7 2.5 %collective-permute-start.10 = (f32[16,128]{1,0:T(8,128)S(1)}, f32[16,128]{1,0:T(8,128)S(1)}, u32[]{:S(2)}, u32[]{:S(2)}) collective-permute-start(f32[16,128]{1,0:T(8,128)S(1)} %add.1.refs_0_), channel_id=1, source_target_pairs={{0,12},{4,8},{8,4},{12,0},{1,13},{5,9},{9,5},{13,1},{2,14},{6,10},... | collective-permute-start | bytes 24584 | tf_op jit(solution)/shard_map/ppermute | solution.py:356
  38.3 0.6 %collective-permute-start.9 = (f32[16,128]{1,0:T(8,128)S(1)}, f32[16,128]{1,0:T(8,128)S(1)}, u32[]{:S(2)}, u32[]{:S(2)}) collective-permute-start(f32[16,128]{1,0:T(8,128)S(1)} %add.1.refs_0_), channel_id=1, source_target_pairs={{0,8},{4,12},{8,0},{12,4},{1,9},{5,13},{9,1},{13,5},{2,10},{6,14},... | collective-permute-start | bytes 24584 | tf_op jit(solution)/shard_map/ppermute | solution.py:356
  38.8 1.3 %collective-permute-start.8 = (f32[16,128]{1,0:T(8,128)S(1)}, f32[16,128]{1,0:T(8,128)S(1)}, u32[]{:S(2)}, u32[]{:S(2)}) collective-permute-start(f32[16,128]{1,0:T(8,128)S(1)} %add.1.refs_0_), channel_id=1, source_target_pairs={{0,4},{4,0},{8,12},{12,8},{1,5},{5,1},{9,13},{13,9},{2,6},{6,2},{1... | collective-permute-start | bytes 24584 | tf_op jit(solution)/shard_map/ppermute | solution.py:356
  40.2 1.1 %collective-permute-done.10.refs_3_ = f32[16,128]{1,0:T(8,128)S(1)} collective-permute-done((f32[16,128]{1,0:T(8,128)S(1)}, f32[16,128]{1,0:T(8,128)S(1)}, u32[]{:S(2)}, u32[]{:S(2)}) %collective-permute-start.10) | collective-permute-done | bytes 8224 | tf_op jit(solution)/shard_map/ppermute | solution.py:356
  41.2 1.6 %collective-permute-done.9.refs_2_ = f32[16,128]{1,0:T(8,128)S(1)} collective-permute-done((f32[16,128]{1,0:T(8,128)S(1)}, f32[16,128]{1,0:T(8,128)S(1)}, u32[]{:S(2)}, u32[]{:S(2)}) %collective-permute-start.9) | collective-permute-done | bytes 8224 | tf_op jit(solution)/shard_map/ppermute | solution.py:356
  42.8 0.0 collective-permute-done.8.refs_1_
  42.8 0.6 %finish.1 = f32[3,512]{1,0:T(4,128)} custom-call(f32[16,128]{1,0:T(8,128)S(1)} %add.1.refs_0_, f32[16,128]{1,0:T(8,128)S(1)} %collective-permute-done.8.refs_1_, f32[16,128]{1,0:T(8,128)S(1)} %collective-permute-done.9.refs_2_, f32[16,128]{1,0:T(8,128)S(1)} %collective-permute-done.10.refs_3_), custom_call_target="tpu_custom_call" | custom-call | tf_op jit(solution)/shard_map/finish/pallas_call | solution.py:503
  (1 shorter events, 0.0 us)
Async XLA Ops:
  0.6 6.6 %collective-permute-start.1 = (f32[80,128]{1,0:T(8,128)}, f32[80,128]{1,0:T(8,128)S(1)}, u32[]{:S(2)}, u32[]{:S(2)}) collective-permute-start(f32[80,128]{1,0:T(8,128)} %bitcast.38), channel_id=1, source_target_pairs={{1,4},{4,1},{5,8},{8,5},{9,12},{12,9},{3,6},{6,3},{7,10},{10,7},{1... | collective-permute-start | bytes 122888 | tf_op jit(solution)/shard_map/ppermute | solution.py:393
  1.3 6.0 %collective-permute-start = (f32[80,128]{1,0:T(8,128)}, f32[80,128]{1,0:T(8,128)S(1)}, u32[]{:S(2)}, u32[]{:S(2)}) collective-permute-start(f32[80,128]{1,0:T(8,128)} %bitcast.39), channel_id=1, source_target_pairs={{0,1},{1,0},{4,5},{5,4},{8,9},{9,8},{12,13},{13,12},{2,3},{3,2},{6... | collective-permute-start | bytes 122888 | tf_op jit(solution)/shard_map/ppermute | solution.py:394
  10.2 10.0 %collective-permute-start.3 = (f32[80,128]{1,0:T(8,128)S(1)}, f32[80,128]{1,0:T(8,128)S(1)}, u32[]{:S(2)}, u32[]{:S(2)}) collective-permute-start(f32[80,128]{1,0:T(8,128)S(1)} %sweep.1._.refs_2_), channel_id=1, source_target_pairs={{1,4},{4,1},{5,8},{8,5},{9,12},{12,9},{3,6},{6,3},{7,10},{10,7},{1... | collective-permute-start | bytes 122888 | tf_op jit(solution)/shard_map/ppermute | solution.py:393
  10.9 9.4 %collective-permute-start.2 = (f32[80,128]{1,0:T(8,128)S(1)}, f32[80,128]{1,0:T(8,128)S(1)}, u32[]{:S(2)}, u32[]{:S(2)}) collective-permute-start(f32[80,128]{1,0:T(8,128)S(1)} %sweep.1._.refs_2_), channel_id=1, source_target_pairs={{0,1},{1,0},{4,5},{5,4},{8,9},{9,8},{12,13},{13,12},{2,3},{3,2},{6... | collective-permute-start | bytes 122888 | tf_op jit(solution)/shard_map/ppermute | solution.py:394
  23.9 3.7 %collective-permute-start.4 = (f32[3,1024]{1,0:T(4,128)S(1)}, f32[3,1024]{1,0:T(4,128)S(1)}, u32[]{:S(2)}, u32[]{:S(2)}) collective-permute-start(f32[3,1024]{1,0:T(4,128)S(1)} %get-tuple-element.25.refs_0_), channel_id=1, source_target_pairs={{0,2},{2,0},{1,3},{3,1},{4,6},{6,4},{5,7},{7,5},{8,10},{10,8},{9,1... | collective-permute-start | bytes 36872 | tf_op jit(solution)/shard_map/ppermute | solution.py:356
  32.0 3.1 %collective-permute-start.7 = (f32[16,128]{1,0:T(8,128)S(1)}, f32[16,128]{1,0:T(8,128)S(1)}, u32[]{:S(2)}, u32[]{:S(2)}) collective-permute-start(f32[16,128]{1,0:T(8,128)S(1)} %control.1.refs_0_), channel_id=1, source_target_pairs={{0,3},{1,2},{2,1},{3,0},{4,7},{5,6},{6,5},{7,4},{8,11},{9,10},{10,... | collective-permute-start | bytes 24584 | tf_op jit(solution)/shard_map/ppermute | solution.py:356
  32.0 3.7 %collective-permute-start.6 = (f32[16,128]{1,0:T(8,128)S(1)}, f32[16,128]{1,0:T(8,128)S(1)}, u32[]{:S(2)}, u32[]{:S(2)}) collective-permute-start(f32[16,128]{1,0:T(8,128)S(1)} %control.1.refs_0_), channel_id=1, source_target_pairs={{0,2},{1,3},{2,0},{3,1},{4,6},{5,7},{6,4},{7,5},{8,10},{9,11},{10,... | collective-permute-start | bytes 24584 | tf_op jit(solution)/shard_map/ppermute | solution.py:356
  33.6 2.2 %collective-permute-start.5 = (f32[16,128]{1,0:T(8,128)S(1)}, f32[16,128]{1,0:T(8,128)S(1)}, u32[]{:S(2)}, u32[]{:S(2)}) collective-permute-start(f32[16,128]{1,0:T(8,128)S(1)} %control.1.refs_0_), channel_id=1, source_target_pairs={{0,1},{1,0},{2,3},{3,2},{4,5},{5,4},{6,7},{7,6},{8,9},{9,8},{10,11... | collective-permute-start | bytes 24584 | tf_op jit(solution)/shard_map/ppermute | solution.py:356
  35.7 5.5 %collective-permute-start.10 = (f32[16,128]{1,0:T(8,128)S(1)}, f32[16,128]{1,0:T(8,128)S(1)}, u32[]{:S(2)}, u32[]{:S(2)}) collective-permute-start(f32[16,128]{1,0:T(8,128)S(1)} %add.1.refs_0_), channel_id=1, source_target_pairs={{0,12},{4,8},{8,4},{12,0},{1,13},{5,9},{9,5},{13,1},{2,14},{6,10},... | collective-permute-start | bytes 24584 | tf_op jit(solution)/shard_map/ppermute | solution.py:356
  38.3 4.5 %collective-permute-start.9 = (f32[16,128]{1,0:T(8,128)S(1)}, f32[16,128]{1,0:T(8,128)S(1)}, u32[]{:S(2)}, u32[]{:S(2)}) collective-permute-start(f32[16,128]{1,0:T(8,128)S(1)} %add.1.refs_0_), channel_id=1, source_target_pairs={{0,8},{4,12},{8,0},{12,4},{1,9},{5,13},{9,1},{13,5},{2,10},{6,14},... | collective-permute-start | bytes 24584 | tf_op jit(solution)/shard_map/ppermute | solution.py:356
  38.8 4.0 %collective-permute-start.8 = (f32[16,128]{1,0:T(8,128)S(1)}, f32[16,128]{1,0:T(8,128)S(1)}, u32[]{:S(2)}, u32[]{:S(2)}) collective-permute-start(f32[16,128]{1,0:T(8,128)S(1)} %add.1.refs_0_), channel_id=1, source_target_pairs={{0,4},{4,0},{8,12},{12,8},{1,5},{5,1},{9,13},{13,9},{2,6},{6,2},{1... | collective-permute-start | bytes 24584 | tf_op jit(solution)/shard_map/ppermute | solution.py:356

commit v3 on v2

--- a/solution.py
+++ b/solution.py
@@ -47,33 +47,41 @@
     index_in,
     spread_in,
     start_in,
+    cell_in,
+    base_in,
     off_ref,
     inverse_ref,
     rhs_ref,
     sens_ref,
     lane_ref,
     step_ref,
-    high_ref,
     spread_ref,
     one_hot_ref,
     start_ref,
+    left_ref,
+    right_ref,
     off_buf,
     sens_buf,
     neigh_buf,
     weight_buf,
     index_buf,
+    spread_buf,
+    cell_buf,
+    base_buf,
     sems,
 ):
-    owned = index_buf.shape[1]
+    slots, owned = index_buf.shape
     start = pl.multiple_of(lax.axis_index("nodes") * owned, LANES)
     mine = pl.ds(start, owned)
     pairs = (
         (neigh_in, neigh_buf),
         (index_in.at[:, mine], index_buf),
+        (spread_in.at[:, mine], spread_buf),
+        (cell_in, cell_buf),
+        (base_in.at[:, mine], base_buf),
         (off_in, off_buf),
         (weight_in, weight_buf),
         (sens_in, sens_buf),
-        (spread_in.at[:, mine], spread_ref),
         (inverse_in, inverse_ref),
         (rhs_in, rhs_ref),
         (start_in, start_ref),
@@ -99,24 +107,36 @@
             step_ref[rows, :] = step
 
     copies[1].wait()
-    high_ref[...] = jnp.right_shift(index_buf[...], 7)
+    copies[2].wait()
+    groups = FFD // LANES
     piece = min(512, owned)
     for first in range(0, owned, piece):
         here = slice(first, first + piece)
         low = jnp.bitwise_and(index_buf[:, here], LANES - 1).astype(jnp.float32)
         low = low.astype(jnp.bfloat16)
+        high = jnp.right_shift(index_buf[:, here], 7)
         row = lax.broadcasted_iota(jnp.int32, (LANES, piece), 0).astype(jnp.float32)
         row = row.astype(jnp.bfloat16)
-        for j in range(index_buf.shape[0]):
+        part = lax.broadcasted_iota(jnp.int32, (16, piece), 0)
+        part = jnp.where(part < 3 * groups, lax.rem(part, groups), -1)
+        for j in range(slots):
             hit = jnp.broadcast_to(low[j : j + 1], (LANES, piece)) == row
             one_hot_ref[j * LANES : (j + 1) * LANES, here] = jnp.where(
                 hit, jnp.bfloat16(1.0), jnp.bfloat16(0.0)
             )
-
-    copies[2].wait()
+            spread_ref[j * 16 : (j + 1) * 16, here] = jnp.where(
+                high[j : j + 1] == part, spread_buf[j : j + 1, here], 0.0
+            )
+
+    copies[3].wait()
+    left_ref[...] = distance_factors(cell_buf[...], True).T.astype(jnp.bfloat16)
+    copies[4].wait()
+    right_ref[...] = distance_factors(base_buf[...], False).astype(jnp.bfloat16)
+
+    copies[5].wait()
     off_ref[...] = off_buf[...].astype(jnp.float32)
-    copies[3].wait()
-    copies[4].wait()
+    copies[6].wait()
+    copies[7].wait()
     row_node = lax.rem(lax.broadcasted_iota(jnp.int32, (per, LANES), 0), nodes)
     weights = jnp.zeros((per, LANES), jnp.float32)
     for node in range(nodes):
@@ -124,13 +144,13 @@
     for row in range(0, sens_buf.shape[0], per):
         here = slice(row, row + per)
         sens_ref[here, :] = sens_buf[here, :].astype(jnp.float32) * weights
-    for copy in copies[5:]:
+    for copy in copies[8:]:
         copy.wait()
 
 
 def sweep_into(
     blocks, first_ref, second_ref, own_ref, rhs_ref, off_ref, inverse_ref, lane_ref, step_ref,
-    out_ref, window_ref,
+    out_ref, window_ref, table_ref,
 ):
     per = rhs_ref.shape[0] // 5
     nodes = per // blocks
@@ -138,33 +158,39 @@
     odd = lax.rem(lax.axis_index(CELL_AXES), 2)
     place = pl.multiple_of((1 - odd) * 2 * per, 8)
     other = pl.multiple_of(odd * 2 * per, 8)
+    width = 3 * per
     for b in range(5):
         rows = slice(b * per, (b + 1) * per)
-        base = 3 * b * per
+        base = b * width
         window_ref[pl.ds(base + place, per), :] = first_ref[rows, :]
         window_ref[base + per : base + 2 * per, :] = own_ref[rows, :]
         window_ref[pl.ds(base + other, per), :] = second_ref[rows, :]
+    for shift in range(8 // nodes):
+        for b in range(5):
+            for tile in range(0, width - (8 if shift else 0), 8):
+                to = (shift * 5 + b) * width + tile
+                table_ref[to : to + 8, :] = window_ref[
+                    pl.ds(b * width + tile + shift * nodes, 8), :
+                ]
     for half in range(0, per, 8):
-        lanes = [lane_ref[f * per + half : f * per + half + 8, :] for f in range(faces)]
-        dist = [step_ref[f * per + half : f * per + half + 8, :] for f in range(faces)]
-        beside = [[jnp.zeros((8, LANES), jnp.float32)] * 5 for _ in range(faces)]
-        for d in range(2 * blocks + 1):
-            here = [dist[f] == d for f in range(faces)]
-            for b in range(5):
-                table = window_ref[pl.ds(3 * b * per + half + d * nodes, 8), :]
-                for f in range(faces):
+        remaining = [rhs_ref[a * per + half : a * per + half + 8, :] for a in range(5)]
+        for f in range(faces):
+            lanes = lane_ref[f * per + half : f * per + half + 8, :]
+            dist = step_ref[f * per + half : f * per + half + 8, :]
+            beside = [jnp.zeros((8, LANES), jnp.float32)] * 5
+            for d in range(2 * blocks + 1):
+                here = dist == d
+                first = half + d * nodes
+                for b in range(5):
+                    at = ((first % 8) // nodes * 5 + b) * width + first // 8 * 8
                     got = jnp.take_along_axis(
-                        table, lanes[f], axis=1, mode="promise_in_bounds"
+                        table_ref[at : at + 8, :], lanes, axis=1, mode="promise_in_bounds"
                     )
-                    beside[f][b] = jnp.where(here[f], got, beside[f][b])
-        remaining = []
-        for a in range(5):
-            total = rhs_ref[a * per + half : a * per + half + 8, :]
-            for f in range(faces):
+                    beside[b] = jnp.where(here, got, beside[b])
+            for a in range(5):
                 for b in range(5):
                     row = (f * 25 + 5 * a + b) * per + half
-                    total = total - off_ref[row : row + 8, :] * beside[f][b]
-            remaining.append(total)
+                    remaining[a] = remaining[a] - off_ref[row : row + 8, :] * beside[b]
         for a in range(5):
             total = None
             for b in range(5):
@@ -179,8 +205,9 @@
 
 
 def last_sweep_kernel(blocks, *refs):
-    ins, (sens_ref, _, out_ref, sens_out_ref, window_ref, part_ref) = refs[:8], refs[8:]
-    sweep_into(blocks, *ins, out_ref, window_ref)
+    ins, rest = refs[:8], refs[8:]
+    sens_ref, _, out_ref, sens_out_ref, window_ref, table_ref, part_ref = rest
+    sweep_into(blocks, *ins, out_ref, window_ref, table_ref)
     per = out_ref.shape[0] // 5
     nodes = per // blocks
     for k in range(3):
@@ -229,103 +256,70 @@
     return jnp.concatenate(blocks, axis=0)
 
 
-def wendland_kernel(
-    cell_in, base_in, _, kernel_ref, token_ref, cell_buf, base_buf, left_ref, right_ref, sems
-):
-    cells, owned = kernel_ref.shape
-    start = pl.multiple_of(lax.axis_index("nodes") * owned, LANES)
-    copies = [
-        pltpu.make_async_copy(cell_in, cell_buf, sems.at[0]),
-        pltpu.make_async_copy(base_in.at[:, pl.ds(start, owned)], base_buf, sems.at[1]),
-    ]
-    for copy in copies:
-        copy.start()
-    token_ref[...] = jnp.zeros_like(token_ref)
-    copies[0].wait()
-    left_ref[...] = distance_factors(cell_buf[...], True).T.astype(jnp.bfloat16)
-    copies[1].wait()
-    right_ref[...] = distance_factors(base_buf[...], False).astype(jnp.bfloat16)
-    tile, wide = 64, min(256, owned)
+def wendland_kernel(first_cell, left_ref, right_ref, _, first_ref, rest_ref):
+    cells, owned = first_ref.shape
+    tile, wide = min(128, cells), min(256, owned)
 
     @pl.loop(0, cells // tile)
     def _(step):
-        rows = pl.ds(pl.multiple_of(step * tile, tile), tile)
-        left = left_ref[rows, :]
-        for first in range(0, owned, wide):
-            here = slice(first, first + wide)
+        row = pl.multiple_of(step * tile, tile)
+        left = left_ref[pl.ds(row + first_cell, tile), :]
+        for lane in range(0, owned, wide):
+            here = slice(lane, lane + wide)
             squared = jnp.dot(left, right_ref[:, here], preferred_element_type=jnp.float32)
             squared = jnp.maximum(squared, 1e-30)
             near = jnp.maximum(1.0 - squared * lax.rsqrt(squared), 0.0)
             power = near * near
-            kernel_ref[rows, here] = power * power * (1.25 - near)
+            kernel = power * power * (1.25 - near)
+            first = kernel.astype(jnp.bfloat16)
+            first_ref[pl.ds(row, tile), here] = first
+            rest_ref[pl.ds(row, tile), here] = (kernel - first.astype(jnp.float32)).astype(
+                jnp.bfloat16
+            )
 
 
 def control_kernel(scale, *refs):
-    sens_refs = refs[:-7]
-    kernel_ref, high_ref, spread_ref, one_hot_ref, out_ref, sens_buf, part_ref = refs[-7:]
-    cells, owned = kernel_ref.shape
-    slots = high_ref.shape[0]
+    (*sens_refs, near_first, near_rest, far_first, far_rest, spread_ref, one_hot_ref, out_ref) = refs
+    cells = sens_refs[0].shape[1]
+    half = near_first.shape[0]
+    slots = spread_ref.shape[0] // 16
     groups = FFD // LANES
     total = sens_refs[0][...]
     for ref in sens_refs[1:]:
         total = total + ref[...]
-    total = jnp.concatenate([total * scale, jnp.zeros((5, cells), jnp.float32)], axis=0).T
+    total = total * scale
+    row = lax.broadcasted_iota(jnp.int32, (16, cells), 0)
+    sens = jnp.zeros((16, cells), jnp.float32)
     for k in range(3):
-        sens_buf[k * cells : (k + 1) * cells, :] = jnp.broadcast_to(
-            total[:, k : k + 1], (cells, LANES)
-        )
-    part_ref[...] = jnp.zeros_like(part_ref)
-    wide = min(4 * LANES, owned)
-    tile = 64
-    for first in range(0, owned, wide):
-
-        def add(step, sums):
-            sums = list(sums)
-            for inner in range(0, tile, 8):
-                row = pl.multiple_of(step * tile, tile) + inner
-                value = [
-                    kernel_ref[pl.ds(row, 8), first + lane : first + lane + LANES]
-                    for lane in range(0, wide, LANES)
-                ]
-                for k in range(3):
-                    sens = sens_buf[pl.ds(k * cells + row, 8), :]
-                    for place in range(len(value)):
-                        at = k * len(value) + place
-                        sums[at] = sums[at] + value[place] * sens
-            return tuple(sums)
-
-        count = wide // LANES
-        zero = jnp.zeros((8, LANES), jnp.float32)
-        sums = lax.fori_loop(0, cells // tile, add, (zero,) * (3 * count))
-        for k in range(3):
-            for place in range(count):
-                lane = first + place * LANES
-                grad = jnp.sum(sums[k * count + place], axis=0, keepdims=True)
-                grad = grad * spread_ref[:, lane : lane + LANES]
-                high = high_ref[:, lane : lane + LANES]
-                for group in range(groups):
-                    row = lane // LANES * slots * 16 + k * groups + group
-                    part_ref[pl.ds(row, slots, stride=16), :] = jnp.where(
-                        high == group, grad, 0.0
-                    )
-    result = jnp.zeros((32, LANES), jnp.float32)
+        mine = jnp.logical_and(row >= k * groups, row < (k + 1) * groups)
+        sens = jnp.where(mine, total[k : k + 1], sens)
+
+    def halves(value):
+        first = value.astype(jnp.bfloat16)
+        rest = (value - first.astype(jnp.float32)).astype(jnp.bfloat16)
+        return jnp.concatenate([first, rest], axis=0)
+
+    sens = halves(sens)
+    grad = None
+    for part, ref in (
+        (sens[:, :half], near_first),
+        (sens[:, :half], near_rest),
+        (sens[:, half:], far_first),
+        (sens[:, half:], far_rest),
+    ):
+        term = jnp.dot(part, ref[...], preferred_element_type=jnp.float32)
+        grad = term if grad is None else grad + term
+    grad = grad[:16] + grad[16:]
     over = (((1,), (1,)), ((), ()))
+    result = None
     for j in range(slots):
-        part = jnp.concatenate(
-            [
-                part_ref[(block * slots + j) * 16 : (block * slots + j + 1) * 16, :]
-                for block in range(owned // LANES)
-            ],
-            axis=1,
-        )
-        part_first = part.astype(jnp.bfloat16)
-        part_rest = (part - part_first.astype(jnp.float32)).astype(jnp.bfloat16)
-        result = result + lax.dot_general(
-            jnp.concatenate([part_first, part_rest], axis=0),
+        term = lax.dot_general(
+            halves(grad * spread_ref[j * 16 : (j + 1) * 16, :]),
             one_hot_ref[j * LANES : (j + 1) * LANES, :],
             over,
             preferred_element_type=jnp.float32,
         )
+        result = term if result is None else result + term
     out_ref[...] = result[:16] + result[16:]
 
 
@@ -405,20 +399,24 @@
             shape((15 * per, LANES)),
             shape((faces * per, LANES), i32),
             shape((faces * per, LANES), i32),
-            shape((slots, owned), i32),
-            shape((slots, owned)),
+            shape((slots * 16, owned)),
             shape((slots * LANES, owned), bf16),
             shape((5 * per, LANES)),
+            shape((cells, FACTOR_ROWS), bf16),
+            shape((FACTOR_ROWS, owned), bf16),
         ),
-        in_specs=[HBM] * 9,
-        out_specs=(VMEM,) * 10,
+        in_specs=[HBM] * 11,
+        out_specs=(VMEM,) * 11,
         scratch_shapes=[
             pltpu.VMEM((faces * 25 * per, LANES), bf16),
             pltpu.VMEM((15 * per, LANES), bf16),
             pltpu.VMEM((faces, cells), i32),
             pltpu.SMEM((nodes,), f32),
             pltpu.VMEM((slots, owned), i32),
-            pltpu.SemaphoreType.DMA((9,)),
+            pltpu.VMEM((slots, owned), f32),
+            pltpu.VMEM((3, cells), f32),
+            pltpu.VMEM((3, owned), f32),
+            pltpu.SemaphoreType.DMA((11,)),
         ],
         compiler_params=PARAMS,
         cost_estimate=cost(10**9, 10**7),
@@ -434,10 +432,15 @@
             ffd_index.T,
             ffd_weight.T,
             adjoint,
+            cell_points,
+            base_points,
         )
     )
-    off, inverse, rhs, sens, lane, step, high, spread, one_hot, adjoint = prepared
-    window = pltpu.VMEM((3 * 5 * per, LANES), f32)
+    off, inverse, rhs, sens, lane, step, spread, one_hot, adjoint, left, right = prepared
+    scratch = [
+        pltpu.VMEM((3 * 5 * per, LANES), f32),
+        pltpu.VMEM((8 // nodes * 3 * 5 * per, LANES), f32),
+    ]
     sweep_cost = cost(2 * 10 * 35 * cells, 4 * faces * 25 * per * LANES)
 
     for _ in range(SWEEPS - 1):
@@ -446,55 +449,48 @@
             out_shape=shape((5 * per, LANES)),
             in_specs=[VMEM] * 8,
             out_specs=VMEM,
-            scratch_shapes=[window],
+            scratch_shapes=scratch,
             compiler_params=PARAMS,
             cost_estimate=sweep_cost,
             name="sweep",
         )(close, far, adjoint, rhs, off, inverse, lane, step)
         far, close = swaps(adjoint)
 
-    kernel, token = pl.pallas_call(
-        wendland_kernel,
-        out_shape=(shape((cells, owned)), shape((8, LANES))),
-        in_specs=[HBM, HBM, VMEM],
-        out_specs=(VMEM, VMEM),
-        scratch_shapes=[
-            pltpu.VMEM((3, cells), f32),
-            pltpu.VMEM((3, owned), f32),
-            pltpu.VMEM((cells, FACTOR_ROWS), bf16),
-            pltpu.VMEM((FACTOR_ROWS, owned), bf16),
-            pltpu.SemaphoreType.DMA((2,)),
-        ],
-        compiler_params=PARAMS,
-        cost_estimate=cost(10**9, 10**7),
-        name="wendland",
-    )(*in_hbm(cell_points, base_points), adjoint)
-
+    def wendland(first_cell, count, behind):
+        return pl.pallas_call(
+            functools.partial(wendland_kernel, first_cell),
+            out_shape=(shape((count, owned), bf16), shape((count, owned), bf16)),
+            in_specs=[VMEM] * 3,
+            out_specs=(VMEM, VMEM),
+            compiler_params=PARAMS,
+            cost_estimate=cost(10**9, 10**7),
+            name="wendland",
+        )(left, right, behind)
+
+    half = cells // 2
+    near_first, near_rest = wendland(0, half, adjoint)
     adjoint, part_sens = pl.pallas_call(
         functools.partial(last_sweep_kernel, blocks),
         out_shape=(shape((5 * per, LANES)), shape((3, cells))),
-        in_specs=[VMEM] * 10,
+        in_specs=[VMEM] * 9 + [pl.BlockSpec(memory_space=pl.ANY)],
         out_specs=(VMEM, VMEM),
-        scratch_shapes=[window, pltpu.VMEM((3 * per, LANES), f32)],
+        scratch_shapes=scratch + [pltpu.VMEM((3 * per, LANES), f32)],
         compiler_params=PARAMS,
         cost_estimate=sweep_cost,
         name="last_sweep",
-    )(close, far, adjoint, rhs, off, inverse, lane, step, sens, token)
+    )(close, far, adjoint, rhs, off, inverse, lane, step, sens, near_first)
 
     all_sens = exchanged(part_sens, "nodes")
+    far_first, far_rest = wendland(half, cells - half, part_sens)
     scale = 4.0 / math.sqrt(cells * peers)
     partial = pl.pallas_call(
         functools.partial(control_kernel, scale),
         out_shape=shape((16, LANES)),
-        in_specs=[VMEM] * (len(all_sens) + 4),
+        in_specs=[VMEM] * (len(all_sens) + 6),
         out_specs=VMEM,
-        scratch_shapes=[
-            pltpu.VMEM((3 * cells, LANES), f32),
-            pltpu.VMEM((owned // LANES * slots * 16, LANES), f32),
-        ],
         compiler_params=PARAMS,
         name="control",
-    )(*all_sens, kernel, high, spread, one_hot)
+    )(*all_sens, near_first, near_rest, far_first, far_rest, spread, one_hot)
 
     close_parts = exchanged(partial, ("nodes", "sub"))
     partial = pl.pallas_call(

time: 43.7 us -> 37.8 us (0.86)
  Pallas kernels: 19.1 us -> 14.8 us
  waiting for transfers between devices: 6.75 us -> 5.75 us
  starting transfers between devices: 16.9 us -> 16.3 us
    ppermute x2, starting transfers between devices: 7.78 us -> 4.54 us  [swaps(): close = lax.ppermute(array, CELL_AXES, first)]
    ppermute x7, starting transfers between devices: 7.82 us -> 10.5 us  [exchanged(): lax.ppermute(value, axes, [(i, i ^ shift) for i in range(peers)])]
    pallas_call x1, Pallas kernels: 2.95 us -> 1.24 us  [body(): pl.pallas_call(functools.partial(sweep_kernel, blocks), out_shape=shape((...]
    pallas_call x1, Pallas kernels: 3.56 us -> 1.87 us  [body(): pl.pallas_call(functools.partial(last_sweep_kernel, blocks), out_shape=(s...]
    pallas_call x1 -> x2, Pallas kernels: 6.03 us -> 4.91 us  [wendland(): pl.pallas_call(functools.partial(wendland_kernel, first_cell), out_shape=...]
    ppermute x7, waiting for transfers between devices: 6.74 us -> 5.74 us  [exchanged(): lax.ppermute(value, axes, [(i, i ^ shift) for i in range(peers)])]
  transfers between devices with their start and end apart: 11 -> 11, of which waited for: 5 -> 4; matrix products, arithmetic and copies ran while one was open for 0% -> 0% of each run, Pallas kernels for 17% -> 18%
where the time goes in v3:
time: 37.8 us; the launch traced here: 37.6 us
  starting transfers between devices  16.3 us (43%)
  Pallas kernels  14.8 us (39%)
  waiting for transfers between devices  5.75 us (15%)
  between operations  0.73 us (2%)
    ppermute x7, starting transfers between devices, exchanged(): lax.ppermute(value, axes, [(i, i ^ shift) for i in range(peers)])  10.5 us
    ppermute x7, waiting for transfers between devices, exchanged(): lax.ppermute(value, axes, [(i, i ^ shift) for i in range(peers)])  5.74 us
    pallas_call x2, Pallas kernels, wendland(): pl.pallas_call(functools.partial(wendland_kernel, first_cell), out_shape=...  4.91 us
    ppermute x2, starting transfers between devices, swaps(): close = lax.ppermute(array, CELL_AXES, first)  4.54 us
    pallas_call x1, Pallas kernels, body(): pl.pallas_call(functools.partial(control_kernel, scale), out_shape=shape(...  4.29 us
    pallas_call x1, Pallas kernels, body(): pl.pallas_call(functools.partial(last_sweep_kernel, blocks), out_shape=(s...  1.87 us
    pallas_call x1, Pallas kernels, body(): pl.pallas_call(functools.partial(prepare_kernel, nodes), out_shape=(shape...  1.86 us
    ppermute x2, starting transfers between devices, swaps(): far = lax.ppermute(array, CELL_AXES, second)  1.3 us
  transfers between devices with their start and end apart: 11, of which 4 were waited for; matrix products, arithmetic and copies ran while one was open for 0% of the time, Pallas kernels for 18%

profile of v3, /device:TPU:0, one launch (start us, length us, event | category | flops | bytes accessed | tf_op | source)
XLA Modules:
  0.0 37.6 jit_solution(11680143268707125998)
XLA Ops:
  0.6 0.5 %collective-permute-start = (f32[80,128]{1,0:T(8,128)}, f32[80,128]{1,0:T(8,128)S(1)}, u32[]{:S(2)}, u32[]{:S(2)}) collective-permute-start(f32[80,128]{1,0:T(8,128)} %bitcast.38), channel_id=1, source_target_pairs={{0,1},{1,0},{4,5},{5,4},{8,9},{9,8},{12,13},{13,12},{2,3},{3,2},{6... | collective-permute-start | bytes 122888 | tf_op jit(solution)/shard_map/ppermute | solution.py:388
  1.2 0.7 %collective-permute-start.1 = (f32[80,128]{1,0:T(8,128)}, f32[80,128]{1,0:T(8,128)S(1)}, u32[]{:S(2)}, u32[]{:S(2)}) collective-permute-start(f32[80,128]{1,0:T(8,128)} %bitcast.39), channel_id=1, source_target_pairs={{1,4},{4,1},{5,8},{8,5},{9,12},{12,9},{3,6},{6,3},{7,10},{10,7},{1... | collective-permute-start | bytes 122888 | tf_op jit(solution)/shard_map/ppermute | solution.py:387
  1.8 1.9 %prepare.1 = (f32[2400,128]{1,0:T(8,128)S(1)}, f32[400,128]{1,0:T(8,128)S(1)}, f32[80,128]{1,0:T(8,128)S(1)}, f32[240,128]{1,0:T(8,128)S(1)}, s32[96,128]{1,0:T(...) custom-call(bf16[2400,128]{1,0:T(8,128)(2,1)} %bitcast.32, ...), custom_call_target="tpu_custom_call" | custom-call | flops 1000000000 | bytes 10000000 | tf_op jit(solution)/shard_map/prepare/pallas_call | solution.py:393
  3.7 0.0 collective-permute-done.refs_0_
  3.7 0.0 collective-permute-done.1.refs_1_
  3.7 1.2 %sweep.1._.refs_2_ = f32[80,128]{1,0:T(8,128)S(1)} custom-call(f32[80,128]{1,0:T(8,128)S(1)} %collective-permute-done.refs_0_, f32[80,128]{1,0:T(8,128)S(1)} %collective-permute-done.1.refs_1_, f32[80,128]{1,0:T(8,128)S(1)} %get-tuple-element.19.refs_2_, f32[80,128]{1,0:T(8,128)S(1)} %get-tuple-element.20.refs_3_, ...), custom_call_target="tpu_custom_call" | custom-call | flops 716800 | bytes 1228800 | tf_op jit(solution)/shard_map/sweep/pallas_call | solution.py:447
  4.9 4.0 %collective-permute-start.2 = (f32[80,128]{1,0:T(8,128)S(1)}, f32[80,128]{1,0:T(8,128)S(1)}, u32[]{:S(2)}, u32[]{:S(2)}) collective-permute-start(f32[80,128]{1,0:T(8,128)S(1)} %sweep.1._.refs_2_), channel_id=1, source_target_pairs={{0,1},{1,0},{4,5},{5,4},{8,9},{9,8},{12,13},{13,12},{2,3},{3,2},{6... | collective-permute-start | bytes 122888 | tf_op jit(solution)/shard_map/ppermute | solution.py:388
  9.0 0.7 %collective-permute-start.3 = (f32[80,128]{1,0:T(8,128)S(1)}, f32[80,128]{1,0:T(8,128)S(1)}, u32[]{:S(2)}, u32[]{:S(2)}) collective-permute-start(f32[80,128]{1,0:T(8,128)S(1)} %sweep.1._.refs_2_), channel_id=1, source_target_pairs={{1,4},{4,1},{5,8},{8,5},{9,12},{12,9},{3,6},{6,3},{7,10},{10,7},{1... | collective-permute-start | bytes 122888 | tf_op jit(solution)/shard_map/ppermute | solution.py:387
  9.6 2.5 %wendland.2 = (bf16[512,2048]{1,0:T(8,128)(2,1)S(1)}, bf16[512,2048]{1,0:T(8,128)(2,1)S(1)}) custom-call(bf16[1024,64]{1,0:T(8,128)(2,1)S(1)} %get-tuple-element.26.left_ref, bf16[64,2048]{1,0:T(8,128)(2,1)S(1)} %get-tuple-element.27.right_ref, f32[80,128]{1,0:T(8,128)S(1)} %sweep.1._.refs_2_), custom_call_target="tpu_custom_call" | custom-call | flops 1000000000 | bytes 10000000 | tf_op jit(solution)/shard_map/wendland/pallas_call | solution.py:460
  12.1 0.0 collective-permute-done.2.refs_0_
  12.1 0.0 collective-permute-done.3.refs_1_
  12.1 1.9 %last_sweep.1 = (f32[80,128]{1,0:T(8,128)}, f32[3,1024]{1,0:T(4,128)S(1)}) custom-call(f32[80,128]{1,0:T(8,128)S(1)} %collective-permute-done.2.refs_0_, f32[80,128]{1,0:T(8,128)S(1)} %collective-permute-done.3.refs_1_, f32[80,128]{1,0:T(8,128)S(1)} %sweep.1._.refs_2_, f32[80,128]{1,0:T(8,128)S(1)} %get-tuple-element.20.refs_3_, ...), custom_call_target="tpu_custom_call" | custom-call | flops 716800 | bytes 1228800 | tf_op jit(solution)/shard_map/last_sweep/pallas_call | solution.py:472
  14.0 2.0 %collective-permute-start.4 = (f32[3,1024]{1,0:T(4,128)S(1)}, f32[3,1024]{1,0:T(4,128)S(1)}, u32[]{:S(2)}, u32[]{:S(2)}) collective-permute-start(f32[3,1024]{1,0:T(4,128)S(1)} %get-tuple-element.30._.refs_0_), channel_id=1, source_target_pairs={{0,2},{2,0},{1,3},{3,1},{4,6},{6,4},{5,7},{7,5},{8,10},{10,8},{9,1... | collective-permute-start | bytes 36872 | tf_op jit(solution)/shard_map/ppermute | solution.py:350
  16.0 2.5 %wendland.3 = (bf16[512,2048]{1,0:T(8,128)(2,1)S(1)}, bf16[512,2048]{1,0:T(8,128)(2,1)S(1)}) custom-call(bf16[1024,64]{1,0:T(8,128)(2,1)S(1)} %get-tuple-element.26.left_ref, bf16[64,2048]{1,0:T(8,128)(2,1)S(1)} %get-tuple-element.27.right_ref, f32[3,1024]{1,0:T(4,128)S(1)} %get-tuple-element.30._.refs_0_), custom_call_target="tpu_custom_call" | custom-call | flops 1000000000 | bytes 10000000 | tf_op jit(solution)/shard_map/wendland/pallas_call | solution.py:460
  18.5 0.0 collective-permute-done.4.refs_1_
  18.5 4.3 %control.1.refs_0_ = f32[16,128]{1,0:T(8,128)S(1)} custom-call(f32[3,1024]{1,0:T(4,128)S(1)} %get-tuple-element.30._.refs_0_, f32[3,1024]{1,0:T(4,128)S(1)} %collective-permute-done.4.refs_1_, bf16[512,2048]{1,0:T(8,128)(2,1)S(1)} %get-tuple-element.28.refs_9_.refs_2_, bf16[512,2048]{1,0:T(8,128)(2,1)S(1)} %get-tuple-element.31.refs_3_, ...), custom_call_target="tpu_custom_call" | custom-call | tf_op jit(solution)/shard_map/control/pallas_call | solution.py:486
  22.8 2.7 %collective-permute-start.5 = (f32[16,128]{1,0:T(8,128)S(1)}, f32[16,128]{1,0:T(8,128)S(1)}, u32[]{:S(2)}, u32[]{:S(2)}) collective-permute-start(f32[16,128]{1,0:T(8,128)S(1)} %control.1.refs_0_), channel_id=1, source_target_pairs={{0,1},{1,0},{2,3},{3,2},{4,5},{5,4},{6,7},{7,6},{8,9},{9,8},{10,11... | collective-permute-start | bytes 24584 | tf_op jit(solution)/shard_map/ppermute | solution.py:350
  25.4 0.5 %collective-permute-start.6 = (f32[16,128]{1,0:T(8,128)S(1)}, f32[16,128]{1,0:T(8,128)S(1)}, u32[]{:S(2)}, u32[]{:S(2)}) collective-permute-start(f32[16,128]{1,0:T(8,128)S(1)} %control.1.refs_0_), channel_id=1, source_target_pairs={{0,2},{1,3},{2,0},{3,1},{4,6},{5,7},{6,4},{7,5},{8,10},{9,11},{10,... | collective-permute-start | bytes 24584 | tf_op jit(solution)/shard_map/ppermute | solution.py:350
  26.0 0.8 %collective-permute-start.7 = (f32[16,128]{1,0:T(8,128)S(1)}, f32[16,128]{1,0:T(8,128)S(1)}, u32[]{:S(2)}, u32[]{:S(2)}) collective-permute-start(f32[16,128]{1,0:T(8,128)S(1)} %control.1.refs_0_), channel_id=1, source_target_pairs={{0,3},{1,2},{2,1},{3,0},{4,7},{5,6},{6,5},{7,4},{8,11},{9,10},{10,... | collective-permute-start | bytes 24584 | tf_op jit(solution)/shard_map/ppermute | solution.py:350
  26.8 0.0 collective-permute-done.5.refs_1_
  26.8 2.3 %collective-permute-done.6.refs_2_ = f32[16,128]{1,0:T(8,128)S(1)} collective-permute-done((f32[16,128]{1,0:T(8,128)S(1)}, f32[16,128]{1,0:T(8,128)S(1)}, u32[]{:S(2)}, u32[]{:S(2)}) %collective-permute-start.6) | collective-permute-done | bytes 8224 | tf_op jit(solution)/shard_map/ppermute | solution.py:350
  29.1 0.0 collective-permute-done.7.refs_3_
  29.2 3.3 %collective-permute-start.10 = (f32[16,128]{1,0:T(8,128)S(1)}, f32[16,128]{1,0:T(8,128)S(1)}, u32[]{:S(2)}, u32[]{:S(2)}) collective-permute-start(f32[16,128]{1,0:T(8,128)S(1)} %add.1.refs_0_), channel_id=1, source_target_pairs={{0,12},{4,8},{8,4},{12,0},{1,13},{5,9},{9,5},{13,1},{2,14},{6,10},... | collective-permute-start | bytes 24584 | tf_op jit(solution)/shard_map/ppermute | solution.py:350
  32.4 0.0 collective-permute-start.8
  32.4 1.2 %collective-permute-start.9 = (f32[16,128]{1,0:T(8,128)S(1)}, f32[16,128]{1,0:T(8,128)S(1)}, u32[]{:S(2)}, u32[]{:S(2)}) collective-permute-start(f32[16,128]{1,0:T(8,128)S(1)} %add.1.refs_0_), channel_id=1, source_target_pairs={{0,8},{4,12},{8,0},{12,4},{1,9},{5,13},{9,1},{13,5},{2,10},{6,14},... | collective-permute-start | bytes 24584 | tf_op jit(solution)/shard_map/ppermute | solution.py:350
  33.6 1.1 %collective-permute-done.10.refs_3_ = f32[16,128]{1,0:T(8,128)S(1)} collective-permute-done((f32[16,128]{1,0:T(8,128)S(1)}, f32[16,128]{1,0:T(8,128)S(1)}, u32[]{:S(2)}, u32[]{:S(2)}) %collective-permute-start.10) | collective-permute-done | bytes 8224 | tf_op jit(solution)/shard_map/ppermute | solution.py:350
  34.7 1.4 %collective-permute-done.8.refs_1_ = f32[16,128]{1,0:T(8,128)S(1)} collective-permute-done((f32[16,128]{1,0:T(8,128)S(1)}, f32[16,128]{1,0:T(8,128)S(1)}, u32[]{:S(2)}, u32[]{:S(2)}) %collective-permute-start.8) | collective-permute-done | bytes 8224 | tf_op jit(solution)/shard_map/ppermute | solution.py:350
  36.1 0.9 %collective-permute-done.9.refs_2_ = f32[16,128]{1,0:T(8,128)S(1)} collective-permute-done((f32[16,128]{1,0:T(8,128)S(1)}, f32[16,128]{1,0:T(8,128)S(1)}, u32[]{:S(2)}, u32[]{:S(2)}) %collective-permute-start.9) | collective-permute-done | bytes 8224 | tf_op jit(solution)/shard_map/ppermute | solution.py:350
  37.0 0.6 %finish.1 = f32[3,512]{1,0:T(4,128)} custom-call(f32[16,128]{1,0:T(8,128)S(1)} %add.1.refs_0_, f32[16,128]{1,0:T(8,128)S(1)} %collective-permute-done.8.refs_1_, f32[16,128]{1,0:T(8,128)S(1)} %collective-permute-done.9.refs_2_, f32[16,128]{1,0:T(8,128)S(1)} %collective-permute-done.10.refs_3_), custom_call_target="tpu_custom_call" | custom-call | tf_op jit(solution)/shard_map/finish/pallas_call | solution.py:499
  (1 shorter events, 0.0 us)
Async XLA Ops:
  0.6 3.0 %collective-permute-start = (f32[80,128]{1,0:T(8,128)}, f32[80,128]{1,0:T(8,128)S(1)}, u32[]{:S(2)}, u32[]{:S(2)}) collective-permute-start(f32[80,128]{1,0:T(8,128)} %bitcast.38), channel_id=1, source_target_pairs={{0,1},{1,0},{4,5},{5,4},{8,9},{9,8},{12,13},{13,12},{2,3},{3,2},{6... | collective-permute-start | bytes 122888 | tf_op jit(solution)/shard_map/ppermute | solution.py:388
  1.2 2.5 %collective-permute-start.1 = (f32[80,128]{1,0:T(8,128)}, f32[80,128]{1,0:T(8,128)S(1)}, u32[]{:S(2)}, u32[]{:S(2)}) collective-permute-start(f32[80,128]{1,0:T(8,128)} %bitcast.39), channel_id=1, source_target_pairs={{1,4},{4,1},{5,8},{8,5},{9,12},{12,9},{3,6},{6,3},{7,10},{10,7},{1... | collective-permute-start | bytes 122888 | tf_op jit(solution)/shard_map/ppermute | solution.py:387
  4.9 7.1 %collective-permute-start.2 = (f32[80,128]{1,0:T(8,128)S(1)}, f32[80,128]{1,0:T(8,128)S(1)}, u32[]{:S(2)}, u32[]{:S(2)}) collective-permute-start(f32[80,128]{1,0:T(8,128)S(1)} %sweep.1._.refs_2_), channel_id=1, source_target_pairs={{0,1},{1,0},{4,5},{5,4},{8,9},{9,8},{12,13},{13,12},{2,3},{3,2},{6... | collective-permute-start | bytes 122888 | tf_op jit(solution)/shard_map/ppermute | solution.py:388
  9.0 3.1 %collective-permute-start.3 = (f32[80,128]{1,0:T(8,128)S(1)}, f32[80,128]{1,0:T(8,128)S(1)}, u32[]{:S(2)}, u32[]{:S(2)}) collective-permute-start(f32[80,128]{1,0:T(8,128)S(1)} %sweep.1._.refs_2_), channel_id=1, source_target_pairs={{1,4},{4,1},{5,8},{8,5},{9,12},{12,9},{3,6},{6,3},{7,10},{10,7},{1... | collective-permute-start | bytes 122888 | tf_op jit(solution)/shard_map/ppermute | solution.py:387
  14.0 4.5 %collective-permute-start.4 = (f32[3,1024]{1,0:T(4,128)S(1)}, f32[3,1024]{1,0:T(4,128)S(1)}, u32[]{:S(2)}, u32[]{:S(2)}) collective-permute-start(f32[3,1024]{1,0:T(4,128)S(1)} %get-tuple-element.30._.refs_0_), channel_id=1, source_target_pairs={{0,2},{2,0},{1,3},{3,1},{4,6},{6,4},{5,7},{7,5},{8,10},{10,8},{9,1... | collective-permute-start | bytes 36872 | tf_op jit(solution)/shard_map/ppermute | solution.py:350
  22.8 4.0 %collective-permute-start.5 = (f32[16,128]{1,0:T(8,128)S(1)}, f32[16,128]{1,0:T(8,128)S(1)}, u32[]{:S(2)}, u32[]{:S(2)}) collective-permute-start(f32[16,128]{1,0:T(8,128)S(1)} %control.1.refs_0_), channel_id=1, source_target_pairs={{0,1},{1,0},{2,3},{3,2},{4,5},{5,4},{6,7},{7,6},{8,9},{9,8},{10,11... | collective-permute-start | bytes 24584 | tf_op jit(solution)/shard_map/ppermute | solution.py:350
  25.4 3.7 %collective-permute-start.6 = (f32[16,128]{1,0:T(8,128)S(1)}, f32[16,128]{1,0:T(8,128)S(1)}, u32[]{:S(2)}, u32[]{:S(2)}) collective-permute-start(f32[16,128]{1,0:T(8,128)S(1)} %control.1.refs_0_), channel_id=1, source_target_pairs={{0,2},{1,3},{2,0},{3,1},{4,6},{5,7},{6,4},{7,5},{8,10},{9,11},{10,... | collective-permute-start | bytes 24584 | tf_op jit(solution)/shard_map/ppermute | solution.py:350
  26.0 3.2 %collective-permute-start.7 = (f32[16,128]{1,0:T(8,128)S(1)}, f32[16,128]{1,0:T(8,128)S(1)}, u32[]{:S(2)}, u32[]{:S(2)}) collective-permute-start(f32[16,128]{1,0:T(8,128)S(1)} %control.1.refs_0_), channel_id=1, source_target_pairs={{0,3},{1,2},{2,1},{3,0},{4,7},{5,6},{6,5},{7,4},{8,11},{9,10},{10,... | collective-permute-start | bytes 24584 | tf_op jit(solution)/shard_map/ppermute | solution.py:350
  29.2 5.5 %collective-permute-start.10 = (f32[16,128]{1,0:T(8,128)S(1)}, f32[16,128]{1,0:T(8,128)S(1)}, u32[]{:S(2)}, u32[]{:S(2)}) collective-permute-start(f32[16,128]{1,0:T(8,128)S(1)} %add.1.refs_0_), channel_id=1, source_target_pairs={{0,12},{4,8},{8,4},{12,0},{1,13},{5,9},{9,5},{13,1},{2,14},{6,10},... | collective-permute-start | bytes 24584 | tf_op jit(solution)/shard_map/ppermute | solution.py:350
  32.4 3.7 %collective-permute-start.8 = (f32[16,128]{1,0:T(8,128)S(1)}, f32[16,128]{1,0:T(8,128)S(1)}, u32[]{:S(2)}, u32[]{:S(2)}) collective-permute-start(f32[16,128]{1,0:T(8,128)S(1)} %add.1.refs_0_), channel_id=1, source_target_pairs={{0,4},{4,0},{8,12},{12,8},{1,5},{5,1},{9,13},{13,9},{2,6},{6,2},{1... | collective-permute-start | bytes 24584 | tf_op jit(solution)/shard_map/ppermute | solution.py:350
  32.4 4.5 %collective-permute-start.9 = (f32[16,128]{1,0:T(8,128)S(1)}, f32[16,128]{1,0:T(8,128)S(1)}, u32[]{:S(2)}, u32[]{:S(2)}) collective-permute-start(f32[16,128]{1,0:T(8,128)S(1)} %add.1.refs_0_), channel_id=1, source_target_pairs={{0,8},{4,12},{8,0},{12,4},{1,9},{5,13},{9,1},{13,5},{2,10},{6,14},... | collective-permute-start | bytes 24584 | tf_op jit(solution)/shard_map/ppermute | solution.py:350

commit v4 on v3

--- a/solution.py
+++ b/solution.py
@@ -112,16 +112,16 @@
     piece = min(512, owned)
     for first in range(0, owned, piece):
         here = slice(first, first + piece)
-        low = jnp.bitwise_and(index_buf[:, here], LANES - 1).astype(jnp.float32)
+        low = jnp.bitwise_and(index_buf[:, here], LANES - 1).astype(jnp.float32).T
         low = low.astype(jnp.bfloat16)
         high = jnp.right_shift(index_buf[:, here], 7)
-        row = lax.broadcasted_iota(jnp.int32, (LANES, piece), 0).astype(jnp.float32)
-        row = row.astype(jnp.bfloat16)
+        lane = lax.broadcasted_iota(jnp.int32, (piece, LANES), 1).astype(jnp.float32)
+        lane = lane.astype(jnp.bfloat16)
         part = lax.broadcasted_iota(jnp.int32, (16, piece), 0)
         part = jnp.where(part < 3 * groups, lax.rem(part, groups), -1)
         for j in range(slots):
-            hit = jnp.broadcast_to(low[j : j + 1], (LANES, piece)) == row
-            one_hot_ref[j * LANES : (j + 1) * LANES, here] = jnp.where(
+            hit = jnp.broadcast_to(low[:, j : j + 1], (piece, LANES)) == lane
+            one_hot_ref[j * owned + first : j * owned + first + piece, :] = jnp.where(
                 hit, jnp.bfloat16(1.0), jnp.bfloat16(0.0)
             )
             spread_ref[j * 16 : (j + 1) * 16, here] = jnp.where(
@@ -310,36 +310,39 @@
         term = jnp.dot(part, ref[...], preferred_element_type=jnp.float32)
         grad = term if grad is None else grad + term
     grad = grad[:16] + grad[16:]
-    over = (((1,), (1,)), ((), ()))
+    owned = grad.shape[1]
     result = None
     for j in range(slots):
-        term = lax.dot_general(
+        term = jnp.dot(
             halves(grad * spread_ref[j * 16 : (j + 1) * 16, :]),
-            one_hot_ref[j * LANES : (j + 1) * LANES, :],
-            over,
+            one_hot_ref[j * owned : (j + 1) * owned, :],
             preferred_element_type=jnp.float32,
         )
         result = term if result is None else result + term
-    out_ref[...] = result[:16] + result[16:]
+    result = result[:16] + result[16:]
+    for copy in range(out_ref.shape[0]):
+        out_ref[copy] = result
 
 
 def tree(values):
     while len(values) > 1:
-        values = [a + b for a, b in zip(values[::2], values[1::2])]
+        values = [sum(values[i : i + 2]) for i in range(0, len(values), 2)]
     return values[0]
 
 
-def add_kernel(*refs):
-    refs[-1][...] = tree([ref[...] for ref in refs[:-1]])
-
-
-def finish_kernel(*refs):
-    total = tree([ref[...] for ref in refs[:-1]])
+def add_kernel(in_ref, out_ref):
+    total = tree([in_ref[i] for i in range(in_ref.shape[0])])
+    for copy in range(out_ref.shape[0]):
+        out_ref[copy] = total
+
+
+def finish_kernel(in_ref, out_ref):
+    total = tree([in_ref[i] for i in range(in_ref.shape[0])])
     groups = FFD // LANES
     for k in range(3):
         for group in range(groups):
             row = k * groups + group
-            refs[-1][k : k + 1, group * LANES : (group + 1) * LANES] = total[row : row + 1]
+            out_ref[k : k + 1, group * LANES : (group + 1) * LANES] = total[row : row + 1]
 
 
 def exchanged(value, axes):
@@ -400,7 +403,7 @@
             shape((faces * per, LANES), i32),
             shape((faces * per, LANES), i32),
             shape((slots * 16, owned)),
-            shape((slots * LANES, owned), bf16),
+            shape((slots * owned, LANES), bf16),
             shape((5 * per, LANES)),
             shape((cells, FACTOR_ROWS), bf16),
             shape((FACTOR_ROWS, owned), bf16),
@@ -483,22 +486,25 @@
     all_sens = exchanged(part_sens, "nodes")
     far_first, far_rest = wendland(half, cells - half, part_sens)
     scale = 4.0 / math.sqrt(cells * peers)
-    partial = pl.pallas_call(
+    chip_peers = lax.axis_size(("nodes", "sub"))
+    row_peers = lax.axis_size("cells")
+    copies = pl.pallas_call(
         functools.partial(control_kernel, scale),
-        out_shape=shape((16, LANES)),
+        out_shape=shape((chip_peers, 16, LANES)),
         in_specs=[VMEM] * (len(all_sens) + 6),
         out_specs=VMEM,
         compiler_params=PARAMS,
         name="control",
     )(*all_sens, near_first, near_rest, far_first, far_rest, spread, one_hot)
 
-    close_parts = exchanged(partial, ("nodes", "sub"))
-    partial = pl.pallas_call(
-        add_kernel, out_shape=shape((16, LANES)), name="add", compiler_params=PARAMS
-    )(*close_parts)
+    gathered = lax.all_to_all(copies, ("nodes", "sub"), 0, 0, tiled=True)
+    copies = pl.pallas_call(
+        add_kernel, out_shape=shape((row_peers, 16, LANES)), name="add", compiler_params=PARAMS
+    )(gathered)
+    gathered = lax.all_to_all(copies, "cells", 0, 0, tiled=True)
     control_grad = pl.pallas_call(
         finish_kernel, out_shape=shape((3, FFD)), name="finish", compiler_params=PARAMS
-    )(*exchanged(partial, "cells"))
+    )(gathered)
     return (from_rows(adjoint, nodes, cells), control_grad)
 
 

time: 37.8 us -> 39.7 us (1.050)
  blocking collectives: 0 us -> 17.9 us
  starting transfers between devices: 16.3 us -> 7.34 us
  waiting for transfers between devices: 5.75 us -> 0.01 us
  Pallas kernels: 14.8 us -> 13.5 us
    all_to_all x0 -> x2, blocking collectives: none -> 17.9 us  [the longest x1 10.1 us: body(): gathered = lax.all_to_all(copies, 'cells', 0, 0, tiled=True)]
    ppermute x7 -> x1, starting transfers between devices: 10.5 us -> 1.5 us  [exchanged(): lax.ppermute(value, axes, [(i, i ^ shift) for i in range(peers)])]
    ppermute x7 -> x1, waiting for transfers between devices: 5.74 us -> 0.01 us  [exchanged(): lax.ppermute(value, axes, [(i, i ^ shift) for i in range(peers)])]
    pallas_call x1, Pallas kernels: 4.29 us -> 2.09 us  [body(): pl.pallas_call(functools.partial(control_kernel, scale), out_shape=shape(...]
    pallas_call x1, Pallas kernels: 1.86 us -> 2.74 us  [body(): pl.pallas_call(functools.partial(prepare_kernel, nodes), out_shape=(shape...]
  transfers between devices with their start and end apart: 11 -> 5, of which waited for: 4 -> 0; matrix products, arithmetic and copies ran while one was open for 0% -> 0% of each run, Pallas kernels for 18% -> 19%
where the time goes in v4:
time: 39.7 us; the launch traced here: 39.5 us
  blocking collectives  17.9 us (45%)
  Pallas kernels  13.5 us (34%)
  starting transfers between devices  7.34 us (18%)
  between operations  0.73 us (2%)
    all_to_all x1, blocking collectives, body(): gathered = lax.all_to_all(copies, 'cells', 0, 0, tiled=True)  10.1 us
    all_to_all x1, blocking collectives, body(): gathered = lax.all_to_all(copies, ('nodes', 'sub'), 0, 0, tiled=True)  7.81 us
    pallas_call x2, Pallas kernels, wendland(): pl.pallas_call(functools.partial(wendland_kernel, first_cell), out_shape=...  4.91 us
    ppermute x2, starting transfers between devices, swaps(): close = lax.ppermute(array, CELL_AXES, first)  4.54 us
    pallas_call x1, Pallas kernels, body(): pl.pallas_call(functools.partial(prepare_kernel, nodes), out_shape=(shape...  2.74 us
    pallas_call x1, Pallas kernels, body(): pl.pallas_call(functools.partial(control_kernel, scale), out_shape=shape(...  2.09 us
    pallas_call x1, Pallas kernels, body(): pl.pallas_call(functools.partial(last_sweep_kernel, blocks), out_shape=(s...  1.87 us
    ppermute x1, starting transfers between devices, exchanged(): lax.ppermute(value, axes, [(i, i ^ shift) for i in range(peers)])  1.5 us
  transfers between devices with their start and end apart: 5, of which 0 were waited for; matrix products, arithmetic and copies ran while one was open for 0% of the time, Pallas kernels for 19%

profile of v4, /device:TPU:0, one launch (start us, length us, event | category | flops | bytes accessed | tf_op | source)
XLA Modules:
  0.0 39.5 jit_solution(2403878330167202063)
XLA Ops:
  0.6 0.5 %collective-permute-start = (f32[80,128]{1,0:T(8,128)}, f32[80,128]{1,0:T(8,128)S(1)}, u32[]{:S(2)}, u32[]{:S(2)}) collective-permute-start(f32[80,128]{1,0:T(8,128)} %bitcast.38), channel_id=1, source_target_pairs={{0,1},{1,0},{4,5},{5,4},{8,9},{9,8},{12,13},{13,12},{2,3},{3,2},{6... | collective-permute-start | bytes 122888 | tf_op jit(solution)/shard_map/ppermute | solution.py:391
  1.2 0.7 %collective-permute-start.1 = (f32[80,128]{1,0:T(8,128)}, f32[80,128]{1,0:T(8,128)S(1)}, u32[]{:S(2)}, u32[]{:S(2)}) collective-permute-start(f32[80,128]{1,0:T(8,128)} %bitcast.39), channel_id=1, source_target_pairs={{1,4},{4,1},{5,8},{8,5},{9,12},{12,9},{3,6},{6,3},{7,10},{10,7},{1... | collective-permute-start | bytes 122888 | tf_op jit(solution)/shard_map/ppermute | solution.py:390
  1.8 2.7 %prepare.1 = (f32[2400,128]{1,0:T(8,128)S(1)}, f32[400,128]{1,0:T(8,128)S(1)}, f32[80,128]{1,0:T(8,128)S(1)}, f32[240,128]{1,0:T(8,128)S(1)}, s32[96,128]{1,0:T(...) custom-call(bf16[2400,128]{1,0:T(8,128)(2,1)} %bitcast.32, ...), custom_call_target="tpu_custom_call" | custom-call | flops 1000000000 | bytes 10000000 | tf_op jit(solution)/shard_map/prepare/pallas_call | solution.py:396
  4.6 0.0 collective-permute-done.refs_0_
  4.6 0.0 collective-permute-done.1.refs_1_
  4.6 1.2 %sweep.1._.refs_2_ = f32[80,128]{1,0:T(8,128)S(1)} custom-call(f32[80,128]{1,0:T(8,128)S(1)} %collective-permute-done.refs_0_, f32[80,128]{1,0:T(8,128)S(1)} %collective-permute-done.1.refs_1_, f32[80,128]{1,0:T(8,128)S(1)} %get-tuple-element.19.refs_2_, f32[80,128]{1,0:T(8,128)S(1)} %get-tuple-element.20.refs_3_, ...), custom_call_target="tpu_custom_call" | custom-call | flops 716800 | bytes 1228800 | tf_op jit(solution)/shard_map/sweep/pallas_call | solution.py:450
  5.8 4.0 %collective-permute-start.2 = (f32[80,128]{1,0:T(8,128)S(1)}, f32[80,128]{1,0:T(8,128)S(1)}, u32[]{:S(2)}, u32[]{:S(2)}) collective-permute-start(f32[80,128]{1,0:T(8,128)S(1)} %sweep.1._.refs_2_), channel_id=1, source_target_pairs={{0,1},{1,0},{4,5},{5,4},{8,9},{9,8},{12,13},{13,12},{2,3},{3,2},{6... | collective-permute-start | bytes 122888 | tf_op jit(solution)/shard_map/ppermute | solution.py:391
  9.8 0.7 %collective-permute-start.3 = (f32[80,128]{1,0:T(8,128)S(1)}, f32[80,128]{1,0:T(8,128)S(1)}, u32[]{:S(2)}, u32[]{:S(2)}) collective-permute-start(f32[80,128]{1,0:T(8,128)S(1)} %sweep.1._.refs_2_), channel_id=1, source_target_pairs={{1,4},{4,1},{5,8},{8,5},{9,12},{12,9},{3,6},{6,3},{7,10},{10,7},{1... | collective-permute-start | bytes 122888 | tf_op jit(solution)/shard_map/ppermute | solution.py:390
  10.5 2.5 %wendland.2 = (bf16[512,2048]{1,0:T(8,128)(2,1)S(1)}, bf16[512,2048]{1,0:T(8,128)(2,1)S(1)}) custom-call(bf16[1024,64]{1,0:T(8,128)(2,1)S(1)} %get-tuple-element.26.left_ref, bf16[64,2048]{1,0:T(8,128)(2,1)S(1)} %get-tuple-element.27.right_ref, f32[80,128]{1,0:T(8,128)S(1)} %sweep.1._.refs_2_), custom_call_target="tpu_custom_call" | custom-call | flops 1000000000 | bytes 10000000 | tf_op jit(solution)/shard_map/wendland/pallas_call | solution.py:463
  13.0 0.0 collective-permute-done.2.refs_0_
  13.0 0.0 collective-permute-done.3.refs_1_
  13.0 1.9 %last_sweep.1 = (f32[80,128]{1,0:T(8,128)}, f32[3,1024]{1,0:T(4,128)S(1)}) custom-call(f32[80,128]{1,0:T(8,128)S(1)} %collective-permute-done.2.refs_0_, f32[80,128]{1,0:T(8,128)S(1)} %collective-permute-done.3.refs_1_, f32[80,128]{1,0:T(8,128)S(1)} %sweep.1._.refs_2_, f32[80,128]{1,0:T(8,128)S(1)} %get-tuple-element.20.refs_3_, ...), custom_call_target="tpu_custom_call" | custom-call | flops 716800 | bytes 1228800 | tf_op jit(solution)/shard_map/last_sweep/pallas_call | solution.py:475
  14.9 1.5 %collective-permute-start.4 = (f32[3,1024]{1,0:T(4,128)S(1)}, f32[3,1024]{1,0:T(4,128)S(1)}, u32[]{:S(2)}, u32[]{:S(2)}) collective-permute-start(f32[3,1024]{1,0:T(4,128)S(1)} %get-tuple-element.30._.refs_0_), channel_id=1, source_target_pairs={{0,2},{2,0},{1,3},{3,1},{4,6},{6,4},{5,7},{7,5},{8,10},{10,8},{9,1... | collective-permute-start | bytes 36872 | tf_op jit(solution)/shard_map/ppermute | solution.py:353
  16.4 2.5 %wendland.3 = (bf16[512,2048]{1,0:T(8,128)(2,1)S(1)}, bf16[512,2048]{1,0:T(8,128)(2,1)S(1)}) custom-call(bf16[1024,64]{1,0:T(8,128)(2,1)S(1)} %get-tuple-element.26.left_ref, bf16[64,2048]{1,0:T(8,128)(2,1)S(1)} %get-tuple-element.27.right_ref, f32[3,1024]{1,0:T(4,128)S(1)} %get-tuple-element.30._.refs_0_), custom_call_target="tpu_custom_call" | custom-call | flops 1000000000 | bytes 10000000 | tf_op jit(solution)/shard_map/wendland/pallas_call | solution.py:463
  18.8 0.0 collective-permute-done.4.refs_1_
  18.8 2.1 %control.1 = f32[4,16,128]{2,1,0:T(8,128)S(1)} custom-call(f32[3,1024]{1,0:T(4,128)S(1)} %get-tuple-element.30._.refs_0_, f32[3,1024]{1,0:T(4,128)S(1)} %collective-permute-done.4.refs_1_, bf16[512,2048]{1,0:T(8,128)(2,1)S(1)} %get-tuple-element.28.refs_9_.refs_2_, bf16[512,2048]{1,0:T(8,128)(2,1)S(1)} %get-tuple-element.31.refs_3_, ...), custom_call_target="tpu_custom_call" | custom-call | tf_op jit(solution)/shard_map/control/pallas_call | solution.py:491
  20.9 7.8 %all_to_all.10.in_ref = f32[4,16,128]{2,1,0:T(8,128)S(1)} all-to-all(f32[4,16,128]{2,1,0:T(8,128)S(1)} %control.1), channel_id=1, replica_groups=mesh['groups'=2,'cells'=4,'nodes'=2,'sub'=2] {'nodes','sub'}, dimensions={0} | all-to-all | bytes 65536 | tf_op jit(solution)/shard_map/all_to_all | solution.py:500
  28.7 10.1 %all_to_all.11.in_ref = f32[4,16,128]{2,1,0:T(8,128)S(1)} all-to-all(f32[4,16,128]{2,1,0:T(8,128)S(1)} %add.1), channel_id=1, replica_groups=mesh['groups'=2,'cells'=4,'nodes'=2,'sub'=2] {'cells'}, dimensions={0} | all-to-all | bytes 65536 | tf_op jit(solution)/shard_map/all_to_all | solution.py:504
  38.9 0.6 %finish.1 = f32[3,512]{1,0:T(4,128)} custom-call(f32[4,16,128]{2,1,0:T(8,128)S(1)} %all_to_all.11.in_ref), custom_call_target="tpu_custom_call" | custom-call | tf_op jit(solution)/shard_map/finish/pallas_call | solution.py:505
  (1 shorter events, 0.0 us)
Async XLA Ops:
  0.6 3.9 %collective-permute-start = (f32[80,128]{1,0:T(8,128)}, f32[80,128]{1,0:T(8,128)S(1)}, u32[]{:S(2)}, u32[]{:S(2)}) collective-permute-start(f32[80,128]{1,0:T(8,128)} %bitcast.38), channel_id=1, source_target_pairs={{0,1},{1,0},{4,5},{5,4},{8,9},{9,8},{12,13},{13,12},{2,3},{3,2},{6... | collective-permute-start | bytes 122888 | tf_op jit(solution)/shard_map/ppermute | solution.py:391
  1.2 3.4 %collective-permute-start.1 = (f32[80,128]{1,0:T(8,128)}, f32[80,128]{1,0:T(8,128)S(1)}, u32[]{:S(2)}, u32[]{:S(2)}) collective-permute-start(f32[80,128]{1,0:T(8,128)} %bitcast.39), channel_id=1, source_target_pairs={{1,4},{4,1},{5,8},{8,5},{9,12},{12,9},{3,6},{6,3},{7,10},{10,7},{1... | collective-permute-start | bytes 122888 | tf_op jit(solution)/shard_map/ppermute | solution.py:390
  5.8 7.1 %collective-permute-start.2 = (f32[80,128]{1,0:T(8,128)S(1)}, f32[80,128]{1,0:T(8,128)S(1)}, u32[]{:S(2)}, u32[]{:S(2)}) collective-permute-start(f32[80,128]{1,0:T(8,128)S(1)} %sweep.1._.refs_2_), channel_id=1, source_target_pairs={{0,1},{1,0},{4,5},{5,4},{8,9},{9,8},{12,13},{13,12},{2,3},{3,2},{6... | collective-permute-start | bytes 122888 | tf_op jit(solution)/shard_map/ppermute | solution.py:391
  9.8 3.1 %collective-permute-start.3 = (f32[80,128]{1,0:T(8,128)S(1)}, f32[80,128]{1,0:T(8,128)S(1)}, u32[]{:S(2)}, u32[]{:S(2)}) collective-permute-start(f32[80,128]{1,0:T(8,128)S(1)} %sweep.1._.refs_2_), channel_id=1, source_target_pairs={{1,4},{4,1},{5,8},{8,5},{9,12},{12,9},{3,6},{6,3},{7,10},{10,7},{1... | collective-permute-start | bytes 122888 | tf_op jit(solution)/shard_map/ppermute | solution.py:390
  14.9 4.0 %collective-permute-start.4 = (f32[3,1024]{1,0:T(4,128)S(1)}, f32[3,1024]{1,0:T(4,128)S(1)}, u32[]{:S(2)}, u32[]{:S(2)}) collective-permute-start(f32[3,1024]{1,0:T(4,128)S(1)} %get-tuple-element.30._.refs_0_), channel_id=1, source_target_pairs={{0,2},{2,0},{1,3},{3,1},{4,6},{6,4},{5,7},{7,5},{8,10},{10,8},{9,1... | collective-permute-start | bytes 36872 | tf_op jit(solution)/shard_map/ppermute | solution.py:353

commit v5 on v4

--- a/solution.py
+++ b/solution.py
@@ -258,12 +258,9 @@
 
 def wendland_kernel(first_cell, left_ref, right_ref, _, first_ref, rest_ref):
     cells, owned = first_ref.shape
-    tile, wide = min(128, cells), min(256, owned)
-
-    @pl.loop(0, cells // tile)
-    def _(step):
-        row = pl.multiple_of(step * tile, tile)
-        left = left_ref[pl.ds(row + first_cell, tile), :]
+    tile, wide = min(64, cells), min(256, owned)
+    for row in range(0, cells, tile):
+        left = left_ref[first_cell + row : first_cell + row + tile, :]
         for lane in range(0, owned, wide):
             here = slice(lane, lane + wide)
             squared = jnp.dot(left, right_ref[:, here], preferred_element_type=jnp.float32)
@@ -272,10 +269,18 @@
             power = near * near
             kernel = power * power * (1.25 - near)
             first = kernel.astype(jnp.bfloat16)
-            first_ref[pl.ds(row, tile), here] = first
-            rest_ref[pl.ds(row, tile), here] = (kernel - first.astype(jnp.float32)).astype(
+            first_ref[row : row + tile, here] = first
+            rest_ref[row : row + tile, here] = (kernel - first.astype(jnp.float32)).astype(
                 jnp.bfloat16
             )
+
+
+def wendland_and_write_kernel(first_cell, left_ref, right_ref, after, adjoint_ref, *rest):
+    first_ref, rest_ref, result_ref, sem = rest
+    copy = pltpu.make_async_copy(adjoint_ref, result_ref, sem)
+    copy.start()
+    wendland_kernel(first_cell, left_ref, right_ref, after, first_ref, rest_ref)
+    copy.wait()
 
 
 def control_kernel(scale, *refs):
@@ -320,39 +325,29 @@
         )
         result = term if result is None else result + term
     result = result[:16] + result[16:]
-    for copy in range(out_ref.shape[0]):
-        out_ref[copy] = result
-
-
-def tree(values):
-    while len(values) > 1:
-        values = [sum(values[i : i + 2]) for i in range(0, len(values), 2)]
-    return values[0]
-
-
-def add_kernel(in_ref, out_ref):
-    total = tree([in_ref[i] for i in range(in_ref.shape[0])])
-    for copy in range(out_ref.shape[0]):
-        out_ref[copy] = total
-
-
-def finish_kernel(in_ref, out_ref):
-    total = tree([in_ref[i] for i in range(in_ref.shape[0])])
+    out_ref[...] = result
+
+
+def add_kernel(own_ref, other_ref, out_ref):
+    out_ref[...] = own_ref[...] + other_ref[...]
+
+
+def finish_kernel(*refs):
+    total = sum(ref[...] for ref in refs[:-1])
     groups = FFD // LANES
     for k in range(3):
         for group in range(groups):
             row = k * groups + group
-            out_ref[k : k + 1, group * LANES : (group + 1) * LANES] = total[row : row + 1]
-
-
-def exchanged(value, axes):
-    peers = lax.axis_size(axes)
-    if peers > 8 or peers & (peers - 1):
-        return [lax.psum(value, axes)]
-    return [value] + [
-        lax.ppermute(value, axes, [(i, i ^ shift) for i in range(peers)])
-        for shift in range(1, peers)
-    ]
+            refs[-1][k : k + 1, group * LANES : (group + 1) * LANES] = total[row : row + 1]
+
+
+def steps_of_sum(axes):
+    for axis in axes:
+        peers = lax.axis_size(axis)
+        shift = 1
+        while shift < peers:
+            yield axis, [(i, i ^ shift) for i in range(peers)]
+            shift *= 2
 
 
 def body(
@@ -384,9 +379,9 @@
         return pl.CostEstimate(flops=flops, bytes_accessed=moved, transcendentals=0)
 
     def swaps(array):
-        first = [(i, i ^ 1) for i in range(peers) if i ^ 1 < peers]
+        first = [(i, i ^ 1) for i in range(peers)]
         second = [(i, i + 1 if i % 2 else i - 1) for i in range(peers)]
-        second = [(i, j) for i, j in second if 0 <= j < peers]
+        second = [(i, j if 0 <= j < peers else i) for i, j in second]
         far = lax.ppermute(array, CELL_AXES, second)
         close = lax.ppermute(array, CELL_AXES, first)
         return far, close
@@ -459,19 +454,18 @@
         )(close, far, adjoint, rhs, off, inverse, lane, step)
         far, close = swaps(adjoint)
 
-    def wendland(first_cell, count, behind):
-        return pl.pallas_call(
-            functools.partial(wendland_kernel, first_cell),
-            out_shape=(shape((count, owned), bf16), shape((count, owned), bf16)),
-            in_specs=[VMEM] * 3,
-            out_specs=(VMEM, VMEM),
-            compiler_params=PARAMS,
-            cost_estimate=cost(10**9, 10**7),
-            name="wendland",
-        )(left, right, behind)
-
     half = cells // 2
-    near_first, near_rest = wendland(0, half, adjoint)
+    wendland_cost = cost(10**9, 10**7)
+    kernel_shape = shape((half, owned), bf16)
+    near_first, near_rest = pl.pallas_call(
+        functools.partial(wendland_kernel, 0),
+        out_shape=(kernel_shape, kernel_shape),
+        in_specs=[VMEM] * 3,
+        out_specs=(VMEM, VMEM),
+        compiler_params=PARAMS,
+        cost_estimate=wendland_cost,
+        name="near_wendland",
+    )(left, right, adjoint)
     adjoint, part_sens = pl.pallas_call(
         functools.partial(last_sweep_kernel, blocks),
         out_shape=(shape((5 * per, LANES)), shape((3, cells))),
@@ -483,28 +477,42 @@
         name="last_sweep",
     )(close, far, adjoint, rhs, off, inverse, lane, step, sens, near_first)
 
-    all_sens = exchanged(part_sens, "nodes")
-    far_first, far_rest = wendland(half, cells - half, part_sens)
+    all_sens = [part_sens]
+    node_peers = lax.axis_size("nodes")
+    for shift in range(1, node_peers):
+        ring = [(i, (i + shift) % node_peers) for i in range(node_peers)]
+        all_sens.append(lax.ppermute(part_sens, "nodes", ring))
+    far_first, far_rest, adjoint = pl.pallas_call(
+        functools.partial(wendland_and_write_kernel, half),
+        out_shape=(kernel_shape, kernel_shape, shape((5 * per, LANES))),
+        in_specs=[VMEM] * 4,
+        out_specs=(VMEM, VMEM, HBM),
+        scratch_shapes=[pltpu.SemaphoreType.DMA],
+        compiler_params=PARAMS,
+        cost_estimate=wendland_cost,
+        name="far_wendland",
+    )(left, right, part_sens, adjoint)
     scale = 4.0 / math.sqrt(cells * peers)
-    chip_peers = lax.axis_size(("nodes", "sub"))
-    row_peers = lax.axis_size("cells")
-    copies = pl.pallas_call(
-        functools.partial(control_kernel, scale),
-        out_shape=shape((chip_peers, 16, LANES)),
-        in_specs=[VMEM] * (len(all_sens) + 6),
-        out_specs=VMEM,
-        compiler_params=PARAMS,
-        name="control",
-    )(*all_sens, near_first, near_rest, far_first, far_rest, spread, one_hot)
-
-    gathered = lax.all_to_all(copies, ("nodes", "sub"), 0, 0, tiled=True)
-    copies = pl.pallas_call(
-        add_kernel, out_shape=shape((row_peers, 16, LANES)), name="add", compiler_params=PARAMS
-    )(gathered)
-    gathered = lax.all_to_all(copies, "cells", 0, 0, tiled=True)
+    terms = [
+        pl.pallas_call(
+            functools.partial(control_kernel, scale),
+            out_shape=shape((16, LANES)),
+            in_specs=[VMEM] * (len(all_sens) + 6),
+            out_specs=VMEM,
+            compiler_params=PARAMS,
+            name="control",
+        )(*all_sens, near_first, near_rest, far_first, far_rest, spread, one_hot)
+    ]
+    for axis, partners in steps_of_sum(("sub", "nodes", "cells")):
+        partial = terms[0]
+        if len(terms) > 1:
+            partial = pl.pallas_call(
+                add_kernel, out_shape=shape((16, LANES)), name="add", compiler_params=PARAMS
+            )(*terms)
+        terms = [partial, lax.ppermute(partial, axis, partners)]
     control_grad = pl.pallas_call(
         finish_kernel, out_shape=shape((3, FFD)), name="finish", compiler_params=PARAMS
-    )(gathered)
+    )(*terms)
     return (from_rows(adjoint, nodes, cells), control_grad)
 
 

time: 39.7 us -> 36.4 us (0.917)
  blocking collectives: 17.9 us -> 0 us
  waiting for transfers between devices: 0.01 us -> 7.98 us
  starting transfers between devices: 7.34 us -> 14.8 us
  Pallas kernels: 13.5 us -> 12.6 us
    all_to_all x2 -> x0, blocking collectives: 17.9 us -> none  [the longest x1 10.1 us: body(): gathered = lax.all_to_all(copies, 'cells', 0, 0, tiled=True)]
    ppermute x1 -> x5, waiting for transfers between devices: 0.01 us -> 7.97 us  [the longest x4 7.97 us: body(): terms = [partial, lax.ppermute(partial, axis, partners)]]
    ppermute x1 -> x5, starting transfers between devices: 1.5 us -> 8.97 us  [the longest x4 7.41 us: body(): terms = [partial, lax.ppermute(partial, axis, partners)]]
    ppermute x2, starting transfers between devices: 1.3 us -> 2.08 us  [swaps(): far = lax.ppermute(array, CELL_AXES, second)]
    ppermute x2, starting transfers between devices: 4.54 us -> 3.78 us  [swaps(): close = lax.ppermute(array, CELL_AXES, first)]
    pallas_call x1, Pallas kernels: 1.87 us -> 1.27 us  [body(): pl.pallas_call(functools.partial(last_sweep_kernel, blocks), out_shape=(s...]
    pallas_call x3 -> x5, Pallas kernels: 4.92 us -> 4.66 us  [the longest x1 2.33 us: body(): pl.pallas_call(functools.partial(wendland_and_write_kernel, half), out_sh...]
  transfers between devices with their start and end apart: 5 -> 9, of which waited for: 0 -> 4; matrix products, arithmetic and copies ran while one was open for 0% -> 0% of each run, Pallas kernels for 19% -> 20%
where the time goes in v5:
time: 36.4 us; the launch traced here: 36.2 us
  starting transfers between devices  14.8 us (41%)
  Pallas kernels  12.6 us (35%)
  waiting for transfers between devices  7.98 us (22%)
  between operations  0.73 us (2%)
    ppermute x4, waiting for transfers between devices, body(): terms = [partial, lax.ppermute(partial, axis, partners)]  7.97 us
    ppermute x4, starting transfers between devices, body(): terms = [partial, lax.ppermute(partial, axis, partners)]  7.41 us
    ppermute x2, starting transfers between devices, swaps(): close = lax.ppermute(array, CELL_AXES, first)  3.78 us
    pallas_call x1, Pallas kernels, body(): pl.pallas_call(functools.partial(prepare_kernel, nodes), out_shape=(shape...  2.73 us
    pallas_call x1, Pallas kernels, body(): pl.pallas_call(functools.partial(wendland_and_write_kernel, half), out_sh...  2.33 us
    pallas_call x1, Pallas kernels, body(): pl.pallas_call(functools.partial(wendland_kernel, 0), out_shape=(kernel_s...  2.32 us
    pallas_call x1, Pallas kernels, body(): pl.pallas_call(functools.partial(control_kernel, scale), out_shape=shape(...  2.14 us
    ppermute x2, starting transfers between devices, swaps(): far = lax.ppermute(array, CELL_AXES, second)  2.08 us
  transfers between devices with their start and end apart: 9, of which 4 were waited for; matrix products, arithmetic and copies ran while one was open for 0% of the time, Pallas kernels for 20%

profile of v5, /device:TPU:0, one launch (start us, length us, event | category | flops | bytes accessed | tf_op | source)
XLA Modules:
  0.0 36.2 jit_solution(7045677321856248264)
XLA Ops:
  0.6 0.5 %collective-permute-start = (f32[80,128]{1,0:T(8,128)}, f32[80,128]{1,0:T(8,128)S(1)}, u32[]{:S(2)}, u32[]{:S(2)}) collective-permute-start(f32[80,128]{1,0:T(8,128)} %bitcast.38), channel_id=1, source_target_pairs={{0,1},{1,0},{4,5},{5,4},{8,9},{9,8},{12,13},{13,12},{2,3},{3,2},{6... | collective-permute-start | bytes 122888 | tf_op jit(solution)/shard_map/ppermute | solution.py:386
  1.2 1.4 %collective-permute-start.1 = (f32[80,128]{1,0:T(8,128)}, f32[80,128]{1,0:T(8,128)S(1)}, u32[]{:S(2)}, u32[]{:S(2)}) collective-permute-start(f32[80,128]{1,0:T(8,128)} %bitcast.39), channel_id=1, source_target_pairs={{0,0},{1,4},{4,1},{5,8},{8,5},{9,12},{12,9},{13,13},{2,2},{3,6},{6... | collective-permute-start | bytes 122888 | tf_op jit(solution)/shard_map/ppermute | solution.py:385
  2.6 2.7 %prepare.1 = (f32[2400,128]{1,0:T(8,128)S(1)}, f32[400,128]{1,0:T(8,128)S(1)}, f32[80,128]{1,0:T(8,128)S(1)}, f32[240,128]{1,0:T(8,128)S(1)}, s32[96,128]{1,0:T(...) custom-call(bf16[2400,128]{1,0:T(8,128)(2,1)} %bitcast.32, ...), custom_call_target="tpu_custom_call" | custom-call | flops 1000000000 | bytes 10000000 | tf_op jit(solution)/shard_map/prepare/pallas_call | solution.py:391
  5.3 0.0 collective-permute-done.refs_0_
  5.3 0.0 collective-permute-done.1.refs_1_
  5.3 1.2 %sweep.1._.refs_2_ = f32[80,128]{1,0:T(8,128)S(1)} custom-call(f32[80,128]{1,0:T(8,128)S(1)} %collective-permute-done.refs_0_, f32[80,128]{1,0:T(8,128)S(1)} %collective-permute-done.1.refs_1_, f32[80,128]{1,0:T(8,128)S(1)} %get-tuple-element.22.refs_2_, f32[80,128]{1,0:T(8,128)S(1)} %get-tuple-element.23.refs_3_, ...), custom_call_target="tpu_custom_call" | custom-call | flops 716800 | bytes 1228800 | tf_op jit(solution)/shard_map/sweep/pallas_call | solution.py:445
  6.6 3.3 %collective-permute-start.2 = (f32[80,128]{1,0:T(8,128)S(1)}, f32[80,128]{1,0:T(8,128)S(1)}, u32[]{:S(2)}, u32[]{:S(2)}) collective-permute-start(f32[80,128]{1,0:T(8,128)S(1)} %sweep.1._.refs_2_), channel_id=1, source_target_pairs={{0,1},{1,0},{4,5},{5,4},{8,9},{9,8},{12,13},{13,12},{2,3},{3,2},{6... | collective-permute-start | bytes 122888 | tf_op jit(solution)/shard_map/ppermute | solution.py:386
  9.8 0.7 %collective-permute-start.3 = (f32[80,128]{1,0:T(8,128)S(1)}, f32[80,128]{1,0:T(8,128)S(1)}, u32[]{:S(2)}, u32[]{:S(2)}) collective-permute-start(f32[80,128]{1,0:T(8,128)S(1)} %sweep.1._.refs_2_), channel_id=1, source_target_pairs={{0,0},{1,4},{4,1},{5,8},{8,5},{9,12},{12,9},{13,13},{2,2},{3,6},{6... | collective-permute-start | bytes 122888 | tf_op jit(solution)/shard_map/ppermute | solution.py:385
  10.5 2.3 %near_wendland.1 = (bf16[512,2048]{1,0:T(8,128)(2,1)S(1)}, bf16[512,2048]{1,0:T(8,128)(2,1)S(1)}) custom-call(bf16[1024,64]{1,0:T(8,128)(2,1)S(1)} %get-tuple-element.20.left_ref, bf16[64,2048]{1,0:T(8,128)(2,1)S(1)} %get-tuple-element.21.right_ref, f32[80,128]{1,0:T(8,128)S(1)} %sweep.1._.refs_2_), custom_call_target="tpu_custom_call" | custom-call | flops 1000000000 | bytes 10000000 | tf_op jit(solution)/shard_map/near_wendland/pallas_call | solution.py:460
  12.8 0.0 collective-permute-done.2.refs_0_
  12.8 0.0 collective-permute-done.3.refs_1_
  12.9 1.3 %last_sweep.1 = (f32[80,128]{1,0:T(8,128)S(1)}, f32[3,1024]{1,0:T(4,128)S(1)}) custom-call(f32[80,128]{1,0:T(8,128)S(1)} %collective-permute-done.2.refs_0_, f32[80,128]{1,0:T(8,128)S(1)} %collective-permute-done.3.refs_1_, f32[80,128]{1,0:T(8,128)S(1)} %sweep.1._.refs_2_, f32[80,128]{1,0:T(8,128)S(1)} %get-tuple-element.23.refs_3_, ...), custom_call_target="tpu_custom_call" | custom-call | flops 716800 | bytes 1228800 | tf_op jit(solution)/shard_map/last_sweep/pallas_call | solution.py:469
  14.1 1.6 %collective-permute-start.4 = (f32[3,1024]{1,0:T(4,128)S(1)}, f32[3,1024]{1,0:T(4,128)S(1)}, u32[]{:S(2)}, u32[]{:S(2)}) collective-permute-start(f32[3,1024]{1,0:T(4,128)S(1)} %get-tuple-element.30.after.refs_0_), channel_id=1, source_target_pairs={{0,2},{2,0},{1,3},{3,1},{4,6},{6,4},{5,7},{7,5},{8,10},{10,8},{9,1... | collective-permute-start | bytes 36872 | tf_op jit(solution)/shard_map/ppermute | solution.py:484
  15.7 2.3 %far_wendland.1 = (bf16[512,2048]{1,0:T(8,128)(2,1)S(1)}, bf16[512,2048]{1,0:T(8,128)(2,1)S(1)}, f32[80,128]{1,0:T(8,128)}) custom-call(bf16[1024,64]{1,0:T(8,128)(2,1)S(1)} %get-tuple-element.20.left_ref, bf16[64,2048]{1,0:T(8,128)(2,1)S(1)} %get-tuple-element.21.right_ref, f32[3,1024]{1,0:T(4,128)S(1)} %get-tuple-element.30.after.refs_0_, ...), custom_call_target="tpu_custom_call" | custom-call | flops 1000000000 | bytes 10000000 | tf_op jit(solution)/shard_map/far_wendland/pallas_call | solution.py:485
  18.0 0.0 collective-permute-done.4.refs_1_
  18.0 2.1 %control.1.own_ref = f32[16,128]{1,0:T(8,128)S(1)} custom-call(f32[3,1024]{1,0:T(4,128)S(1)} %get-tuple-element.30.after.refs_0_, f32[3,1024]{1,0:T(4,128)S(1)} %collective-permute-done.4.refs_1_, bf16[512,2048]{1,0:T(8,128)(2,1)S(1)} %get-tuple-element.29.refs_9_.refs_2_, bf16[512,2048]{1,0:T(8,128)(2,1)S(1)} %get-tuple-element.33.refs_3_, ...), custom_call_target="tpu_custom_call" | custom-call | tf_op jit(solution)/shard_map/control/pallas_call | solution.py:497
  20.2 2.7 %collective-permute-start.5 = (f32[16,128]{1,0:T(8,128)S(1)}, f32[16,128]{1,0:T(8,128)S(1)}, u32[]{:S(2)}, u32[]{:S(2)}) collective-permute-start(f32[16,128]{1,0:T(8,128)S(1)} %control.1.own_ref), channel_id=1, source_target_pairs={{0,1},{1,0},{2,3},{3,2},{4,5},{5,4},{6,7},{7,6},{8,9},{9,8},{10,11... | collective-permute-start | bytes 24584 | tf_op jit(solution)/shard_map/ppermute | solution.py:512
  22.9 0.8 %collective-permute-done.5.other_ref = f32[16,128]{1,0:T(8,128)S(1)} collective-permute-done((f32[16,128]{1,0:T(8,128)S(1)}, f32[16,128]{1,0:T(8,128)S(1)}, u32[]{:S(2)}, u32[]{:S(2)}) %collective-permute-start.5) | collective-permute-done | bytes 8224 | tf_op jit(solution)/shard_map/ppermute | solution.py:512
  23.7 0.5 %collective-permute-start.6 = (f32[16,128]{1,0:T(8,128)S(1)}, f32[16,128]{1,0:T(8,128)S(1)}, u32[]{:S(2)}, u32[]{:S(2)}) collective-permute-start(f32[16,128]{1,0:T(8,128)S(1)} %add.3.own_ref), channel_id=1, source_target_pairs={{0,2},{2,0},{1,3},{3,1},{4,6},{6,4},{5,7},{7,5},{8,10},{10,8},{9,1... | collective-permute-start | bytes 24584 | tf_op jit(solution)/shard_map/ppermute | solution.py:512
  24.3 3.1 %collective-permute-done.6.other_ref = f32[16,128]{1,0:T(8,128)S(1)} collective-permute-done((f32[16,128]{1,0:T(8,128)S(1)}, f32[16,128]{1,0:T(8,128)S(1)}, u32[]{:S(2)}, u32[]{:S(2)}) %collective-permute-start.6) | collective-permute-done | bytes 8224 | tf_op jit(solution)/shard_map/ppermute | solution.py:512
  27.4 1.6 %collective-permute-start.7 = (f32[16,128]{1,0:T(8,128)S(1)}, f32[16,128]{1,0:T(8,128)S(1)}, u32[]{:S(2)}, u32[]{:S(2)}) collective-permute-start(f32[16,128]{1,0:T(8,128)S(1)} %add.4.own_ref), channel_id=1, source_target_pairs={{0,4},{4,0},{8,12},{12,8},{1,5},{5,1},{9,13},{13,9},{2,6},{6,2},{1... | collective-permute-start | bytes 24584 | tf_op jit(solution)/shard_map/ppermute | solution.py:512
  29.0 2.1 %collective-permute-done.7.other_ref = f32[16,128]{1,0:T(8,128)S(1)} collective-permute-done((f32[16,128]{1,0:T(8,128)S(1)}, f32[16,128]{1,0:T(8,128)S(1)}, u32[]{:S(2)}, u32[]{:S(2)}) %collective-permute-start.7) | collective-permute-done | bytes 8224 | tf_op jit(solution)/shard_map/ppermute | solution.py:512
  31.0 2.6 %collective-permute-start.8 = (f32[16,128]{1,0:T(8,128)S(1)}, f32[16,128]{1,0:T(8,128)S(1)}, u32[]{:S(2)}, u32[]{:S(2)}) collective-permute-start(f32[16,128]{1,0:T(8,128)S(1)} %add.5.refs_0_), channel_id=1, source_target_pairs={{0,8},{4,12},{8,0},{12,4},{1,9},{5,13},{9,1},{13,5},{2,10},{6,14},... | collective-permute-start | bytes 24584 | tf_op jit(solution)/shard_map/ppermute | solution.py:512
  33.6 2.0 %collective-permute-done.8.refs_1_ = f32[16,128]{1,0:T(8,128)S(1)} collective-permute-done((f32[16,128]{1,0:T(8,128)S(1)}, f32[16,128]{1,0:T(8,128)S(1)}, u32[]{:S(2)}, u32[]{:S(2)}) %collective-permute-start.8) | collective-permute-done | bytes 8224 | tf_op jit(solution)/shard_map/ppermute | solution.py:512
  35.6 0.6 %finish.1 = f32[3,512]{1,0:T(4,128)} custom-call(f32[16,128]{1,0:T(8,128)S(1)} %add.5.refs_0_, f32[16,128]{1,0:T(8,128)S(1)} %collective-permute-done.8.refs_1_), custom_call_target="tpu_custom_call" | custom-call | tf_op jit(solution)/shard_map/finish/pallas_call | solution.py:513
  (3 shorter events, 0.0 us)
Async XLA Ops:
  0.6 4.7 %collective-permute-start = (f32[80,128]{1,0:T(8,128)}, f32[80,128]{1,0:T(8,128)S(1)}, u32[]{:S(2)}, u32[]{:S(2)}) collective-permute-start(f32[80,128]{1,0:T(8,128)} %bitcast.38), channel_id=1, source_target_pairs={{0,1},{1,0},{4,5},{5,4},{8,9},{9,8},{12,13},{13,12},{2,3},{3,2},{6... | collective-permute-start | bytes 122888 | tf_op jit(solution)/shard_map/ppermute | solution.py:386
  1.2 4.2 %collective-permute-start.1 = (f32[80,128]{1,0:T(8,128)}, f32[80,128]{1,0:T(8,128)S(1)}, u32[]{:S(2)}, u32[]{:S(2)}) collective-permute-start(f32[80,128]{1,0:T(8,128)} %bitcast.39), channel_id=1, source_target_pairs={{0,0},{1,4},{4,1},{5,8},{8,5},{9,12},{12,9},{13,13},{2,2},{3,6},{6... | collective-permute-start | bytes 122888 | tf_op jit(solution)/shard_map/ppermute | solution.py:385
  6.6 6.3 %collective-permute-start.2 = (f32[80,128]{1,0:T(8,128)S(1)}, f32[80,128]{1,0:T(8,128)S(1)}, u32[]{:S(2)}, u32[]{:S(2)}) collective-permute-start(f32[80,128]{1,0:T(8,128)S(1)} %sweep.1._.refs_2_), channel_id=1, source_target_pairs={{0,1},{1,0},{4,5},{5,4},{8,9},{9,8},{12,13},{13,12},{2,3},{3,2},{6... | collective-permute-start | bytes 122888 | tf_op jit(solution)/shard_map/ppermute | solution.py:386
  9.8 3.0 %collective-permute-start.3 = (f32[80,128]{1,0:T(8,128)S(1)}, f32[80,128]{1,0:T(8,128)S(1)}, u32[]{:S(2)}, u32[]{:S(2)}) collective-permute-start(f32[80,128]{1,0:T(8,128)S(1)} %sweep.1._.refs_2_), channel_id=1, source_target_pairs={{0,0},{1,4},{4,1},{5,8},{8,5},{9,12},{12,9},{13,13},{2,2},{3,6},{6... | collective-permute-start | bytes 122888 | tf_op jit(solution)/shard_map/ppermute | solution.py:385
  14.1 3.9 %collective-permute-start.4 = (f32[3,1024]{1,0:T(4,128)S(1)}, f32[3,1024]{1,0:T(4,128)S(1)}, u32[]{:S(2)}, u32[]{:S(2)}) collective-permute-start(f32[3,1024]{1,0:T(4,128)S(1)} %get-tuple-element.30.after.refs_0_), channel_id=1, source_target_pairs={{0,2},{2,0},{1,3},{3,1},{4,6},{6,4},{5,7},{7,5},{8,10},{10,8},{9,1... | collective-permute-start | bytes 36872 | tf_op jit(solution)/shard_map/ppermute | solution.py:484
  20.2 3.5 %collective-permute-start.5 = (f32[16,128]{1,0:T(8,128)S(1)}, f32[16,128]{1,0:T(8,128)S(1)}, u32[]{:S(2)}, u32[]{:S(2)}) collective-permute-start(f32[16,128]{1,0:T(8,128)S(1)} %control.1.own_ref), channel_id=1, source_target_pairs={{0,1},{1,0},{2,3},{3,2},{4,5},{5,4},{6,7},{7,6},{8,9},{9,8},{10,11... | collective-permute-start | bytes 24584 | tf_op jit(solution)/shard_map/ppermute | solution.py:512
  23.7 3.7 %collective-permute-start.6 = (f32[16,128]{1,0:T(8,128)S(1)}, f32[16,128]{1,0:T(8,128)S(1)}, u32[]{:S(2)}, u32[]{:S(2)}) collective-permute-start(f32[16,128]{1,0:T(8,128)S(1)} %add.3.own_ref), channel_id=1, source_target_pairs={{0,2},{2,0},{1,3},{3,1},{4,6},{6,4},{5,7},{7,5},{8,10},{10,8},{9,1... | collective-permute-start | bytes 24584 | tf_op jit(solution)/shard_map/ppermute | solution.py:512
  27.4 3.7 %collective-permute-start.7 = (f32[16,128]{1,0:T(8,128)S(1)}, f32[16,128]{1,0:T(8,128)S(1)}, u32[]{:S(2)}, u32[]{:S(2)}) collective-permute-start(f32[16,128]{1,0:T(8,128)S(1)} %add.4.own_ref), channel_id=1, source_target_pairs={{0,4},{4,0},{8,12},{12,8},{1,5},{5,1},{9,13},{13,9},{2,6},{6,2},{1... | collective-permute-start | bytes 24584 | tf_op jit(solution)/shard_map/ppermute | solution.py:512
  31.0 4.5 %collective-permute-start.8 = (f32[16,128]{1,0:T(8,128)S(1)}, f32[16,128]{1,0:T(8,128)S(1)}, u32[]{:S(2)}, u32[]{:S(2)}) collective-permute-start(f32[16,128]{1,0:T(8,128)S(1)} %add.5.refs_0_), channel_id=1, source_target_pairs={{0,8},{4,12},{8,0},{12,4},{1,9},{5,13},{9,1},{13,5},{2,10},{6,14},... | collective-permute-start | bytes 24584 | tf_op jit(solution)/shard_map/ppermute | solution.py:512

commit v6 on v5

--- a/solution.py
+++ b/solution.py
@@ -13,6 +13,7 @@
 SUPPORT_RADIUS = 0.3
 LANES = 128
 CELL_AXES = ("cells", "sub")
+SUM_AXES = ("cells", "nodes", "sub")
 FACTOR_ROWS = 64
 PARAMS = pltpu.CompilerParams(vmem_limit_bytes=24 * 1024 * 1024)
 VMEM = pl.BlockSpec(memory_space=pltpu.VMEM)
@@ -49,6 +50,7 @@
     start_in,
     cell_in,
     base_in,
+    _,
     off_ref,
     inverse_ref,
     rhs_ref,
@@ -332,22 +334,63 @@
     out_ref[...] = own_ref[...] + other_ref[...]
 
 
-def finish_kernel(*refs):
-    total = sum(ref[...] for ref in refs[:-1])
+def line_kernel(own_ref, *refs):
+    received, out_ref = [ref[...] for ref in refs[:-1]], refs[-1]
+    core = lax.axis_index("sub")
+    values = [jnp.where(core == 0, own_ref[...], received[0])] + received[1:]
+    while len(values) > 1:
+        values = [a + b for a, b in zip(values[::2], values[1::2])]
+    out_ref[...] = values[0]
+
+
+def finish_kernel(own_ref, other_ref, out_ref):
+    total = own_ref[...] + other_ref[...]
     groups = FFD // LANES
     for k in range(3):
         for group in range(groups):
             row = k * groups + group
-            refs[-1][k : k + 1, group * LANES : (group + 1) * LANES] = total[row : row + 1]
-
-
-def steps_of_sum(axes):
-    for axis in axes:
-        peers = lax.axis_size(axis)
+            out_ref[k : k + 1, group * LANES : (group + 1) * LANES] = total[row : row + 1]
+
+
+def small_call(kernel, name, *arrays):
+    shape = jax.ShapeDtypeStruct(arrays[0].shape, arrays[0].dtype)
+    return pl.pallas_call(kernel, out_shape=shape, name=name, compiler_params=PARAMS)(*arrays)
+
+
+def last_terms(value):
+    lines, nodes, cores = (lax.axis_size(axis) for axis in SUM_AXES)
+
+    def swap(array, axis, shift):
+        pairs = [(i, i ^ shift) for i in range(lax.axis_size(axis))]
+        return lax.ppermute(array, axis, pairs)
+
+    if (nodes, cores) == (2, 2) and lines in (2, 4):
+        chip = small_call(add_kernel, "add", value, swap(value, "sub", 1))
+        received = []
+        for shift in range(lines):
+            pairs = []
+            for line in range(lines):
+                for node in range(2):
+                    for core in range(2):
+                        other = node ^ 1 if core or not shift else node
+                        pairs.append(
+                            (
+                                (line * 2 + node) * 2 + core,
+                                ((line ^ shift) * 2 + other) * 2 + core,
+                            )
+                        )
+            received.append(lax.ppermute(chip, SUM_AXES, pairs))
+        total = small_call(line_kernel, "line", chip, *received)
+        return total, swap(total, "sub", 1)
+
+    terms = (value,)
+    for axis in ("sub", "nodes", "cells"):
         shift = 1
-        while shift < peers:
-            yield axis, [(i, i ^ shift) for i in range(peers)]
+        while shift < lax.axis_size(axis):
+            total = small_call(add_kernel, "add", *terms) if len(terms) > 1 else value
+            terms = (total, swap(total, axis, shift))
             shift *= 2
+    return terms
 
 
 def body(
@@ -378,16 +421,14 @@
     def cost(flops, moved):
         return pl.CostEstimate(flops=flops, bytes_accessed=moved, transcendentals=0)
 
-    def swaps(array):
-        first = [(i, i ^ 1) for i in range(peers)]
-        second = [(i, i + 1 if i % 2 else i - 1) for i in range(peers)]
-        second = [(i, j if 0 <= j < peers else i) for i, j in second]
-        far = lax.ppermute(array, CELL_AXES, second)
-        close = lax.ppermute(array, CELL_AXES, first)
-        return far, close
+    def halo(array):
+        close = lax.ppermute(array, CELL_AXES, [(i, i ^ 1) for i in range(peers)])
+        onward = [(i, i - 2 if i % 2 else i + 2) for i in range(peers)]
+        onward = [(i, j) for i, j in onward if 0 <= j < peers]
+        return lax.ppermute(close, CELL_AXES, onward), close
 
     adjoint = rows_of(adjoint_start)
-    far, close = swaps(adjoint)
+    far, close = halo(adjoint)
     prepared = pl.pallas_call(
         functools.partial(prepare_kernel, nodes),
         out_shape=(
@@ -403,7 +444,7 @@
             shape((cells, FACTOR_ROWS), bf16),
             shape((FACTOR_ROWS, owned), bf16),
         ),
-        in_specs=[HBM] * 11,
+        in_specs=[HBM] * 11 + [VMEM],
         out_specs=(VMEM,) * 11,
         scratch_shapes=[
             pltpu.VMEM((faces * 25 * per, LANES), bf16),
@@ -432,7 +473,8 @@
             adjoint,
             cell_points,
             base_points,
-        )
+        ),
+        close,
     )
     off, inverse, rhs, sens, lane, step, spread, one_hot, adjoint, left, right = prepared
     scratch = [
@@ -452,7 +494,7 @@
             cost_estimate=sweep_cost,
             name="sweep",
         )(close, far, adjoint, rhs, off, inverse, lane, step)
-        far, close = swaps(adjoint)
+        far, close = halo(adjoint)
 
     half = cells // 2
     wendland_cost = cost(10**9, 10**7)
@@ -465,7 +507,7 @@
         compiler_params=PARAMS,
         cost_estimate=wendland_cost,
         name="near_wendland",
-    )(left, right, adjoint)
+    )(left, right, close)
     adjoint, part_sens = pl.pallas_call(
         functools.partial(last_sweep_kernel, blocks),
         out_shape=(shape((5 * per, LANES)), shape((3, cells))),
@@ -493,26 +535,17 @@
         name="far_wendland",
     )(left, right, part_sens, adjoint)
     scale = 4.0 / math.sqrt(cells * peers)
-    terms = [
-        pl.pallas_call(
-            functools.partial(control_kernel, scale),
-            out_shape=shape((16, LANES)),
-            in_specs=[VMEM] * (len(all_sens) + 6),
-            out_specs=VMEM,
-            compiler_params=PARAMS,
-            name="control",
-        )(*all_sens, near_first, near_rest, far_first, far_rest, spread, one_hot)
-    ]
-    for axis, partners in steps_of_sum(("sub", "nodes", "cells")):
-        partial = terms[0]
-        if len(terms) > 1:
-            partial = pl.pallas_call(
-                add_kernel, out_shape=shape((16, LANES)), name="add", compiler_params=PARAMS
-            )(*terms)
-        terms = [partial, lax.ppermute(partial, axis, partners)]
+    partial = pl.pallas_call(
+        functools.partial(control_kernel, scale),
+        out_shape=shape((16, LANES)),
+        in_specs=[VMEM] * (len(all_sens) + 6),
+        out_specs=VMEM,
+        compiler_params=PARAMS,
+        name="control",
+    )(*all_sens, near_first, near_rest, far_first, far_rest, spread, one_hot)
     control_grad = pl.pallas_call(
         finish_kernel, out_shape=shape((3, FFD)), name="finish", compiler_params=PARAMS
-    )(*terms)
+    )(*last_terms(partial))
     return (from_rows(adjoint, nodes, cells), control_grad)
 
 

time: 36.4 us -> 39.5 us (1.085)
  waiting for transfers between devices: 7.98 us -> 9.53 us
  starting transfers between devices: 14.8 us -> 16.3 us
    ppermute x8 -> x10, waiting for transfers between devices: 7.98 us -> 9.52 us  [the longest x4 4.91 us: last_terms(): received.append(lax.ppermute(chip, SUM_AXES, pairs))]
    ppermute x8 -> x10, starting transfers between devices: 13.3 us -> 14.7 us  [the longest x2 8.29 us: halo(): return (lax.ppermute(close, CELL_AXES, onward), close)]
  transfers between devices with their start and end apart: 9 -> 11, of which waited for: 4 -> 6; matrix products, arithmetic and copies ran while one was open for 0% -> 0% of each run, Pallas kernels for 20% -> 19%
where the time goes in v6:
time: 39.5 us; the launch traced here: 39.3 us
  starting transfers between devices  16.3 us (41%)
  Pallas kernels  12.8 us (32%)
  waiting for transfers between devices  9.53 us (24%)
  between operations  0.74 us (2%)
    ppermute x2, starting transfers between devices, halo(): return (lax.ppermute(close, CELL_AXES, onward), close)  8.29 us
    ppermute x4, starting transfers between devices, last_terms(): received.append(lax.ppermute(chip, SUM_AXES, pairs))  5.76 us
    ppermute x4, waiting for transfers between devices, last_terms(): received.append(lax.ppermute(chip, SUM_AXES, pairs))  4.91 us
    pallas_call x1, Pallas kernels, body(): pl.pallas_call(functools.partial(prepare_kernel, nodes), out_shape=(shape...  2.74 us
    pallas_call x1, Pallas kernels, body(): pl.pallas_call(functools.partial(wendland_and_write_kernel, half), out_sh...  2.34 us
    pallas_call x1, Pallas kernels, body(): pl.pallas_call(functools.partial(wendland_kernel, 0), out_shape=(kernel_s...  2.33 us
    ppermute x2, waiting for transfers between devices, swap(): return lax.ppermute(array, axis, pairs)  2.32 us
    ppermute x2, waiting for transfers between devices, halo(): close = lax.ppermute(array, CELL_AXES, [(i, i ^ 1) for i in range(peers)])  2.29 us
  transfers between devices with their start and end apart: 11, of which 6 were waited for; matrix products, arithmetic and copies ran while one was open for 0% of the time, Pallas kernels for 19%

profile of v6, /device:TPU:0, one launch (start us, length us, event | category | flops | bytes accessed | tf_op | source)
XLA Modules:
  0.0 39.3 jit_solution(8387471118304374555)
XLA Ops:
  0.6 0.5 %collective-permute-start = (f32[80,128]{1,0:T(8,128)}, f32[80,128]{1,0:T(8,128)S(1)}, u32[]{:S(2)}, u32[]{:S(2)}) collective-permute-start(f32[80,128]{1,0:T(8,128)} %bitcast.38), channel_id=1, source_target_pairs={{0,1},{1,0},{4,5},{5,4},{8,9},{9,8},{12,13},{13,12},{2,3},{3,2},{6... | collective-permute-start | bytes 122888 | tf_op jit(solution)/shard_map/ppermute | solution.py:425
  1.2 1.1 %collective-permute-done._.refs_0_ = f32[80,128]{1,0:T(8,128)S(1)} collective-permute-done((f32[80,128]{1,0:T(8,128)}, f32[80,128]{1,0:T(8,128)S(1)}, u32[]{:S(2)}, u32[]{:S(2)}) %collective-permute-start) | collective-permute-done | bytes 40992 | tf_op jit(solution)/shard_map/ppermute | solution.py:425
  2.2 4.8 %collective-permute-start.1 = (f32[80,128]{1,0:T(8,128)S(1)}, f32[80,128]{1,0:T(8,128)S(1)}, u32[]{:S(2)}, u32[]{:S(2)}) collective-permute-start(f32[80,128]{1,0:T(8,128)S(1)} %collective-permute-done._.refs_0_), channel_id=1, source_target_pairs={{0,4},{4,8},{5,1},{8,12},{9,5},{13,9},{2,6},{6,10},{7,3},{10,14},{... | collective-permute-start | bytes 122888 | tf_op jit(solution)/shard_map/ppermute | solution.py:428
  7.1 2.7 %prepare.1 = (f32[2400,128]{1,0:T(8,128)S(1)}, f32[400,128]{1,0:T(8,128)S(1)}, f32[80,128]{1,0:T(8,128)S(1)}, f32[240,128]{1,0:T(8,128)S(1)}, s32[96,128]{1,0:T(...) custom-call(bf16[2400,128]{1,0:T(8,128)(2,1)} %bitcast.32, ...), custom_call_target="tpu_custom_call" | custom-call | flops 1000000000 | bytes 10000000 | tf_op jit(solution)/shard_map/prepare/pallas_call | solution.py:432
  9.8 0.0 collective-permute-done.1.refs_1_
  9.8 1.3 %sweep.1.refs_2_ = f32[80,128]{1,0:T(8,128)S(1)} custom-call(f32[80,128]{1,0:T(8,128)S(1)} %collective-permute-done._.refs_0_, f32[80,128]{1,0:T(8,128)S(1)} %collective-permute-done.1.refs_1_, f32[80,128]{1,0:T(8,128)S(1)} %get-tuple-element.22.refs_2_, f32[80,128]{1,0:T(8,128)S(1)} %get-tuple-element.23.refs_3_, ...), custom_call_target="tpu_custom_call" | custom-call | flops 716800 | bytes 1228800 | tf_op jit(solution)/shard_map/sweep/pallas_call | solution.py:487
  11.1 0.1 collective-permute-start.2
  11.2 1.2 %collective-permute-done.2._.refs_0_ = f32[80,128]{1,0:T(8,128)S(1)} collective-permute-done((f32[80,128]{1,0:T(8,128)S(1)}, f32[80,128]{1,0:T(8,128)S(1)}, u32[]{:S(2)}, u32[]{:S(2)}) %collective-permute-start.2) | collective-permute-done | bytes 40992 | tf_op jit(solution)/shard_map/ppermute | solution.py:425
  12.4 3.5 %collective-permute-start.3 = (f32[80,128]{1,0:T(8,128)S(1)}, f32[80,128]{1,0:T(8,128)S(1)}, u32[]{:S(2)}, u32[]{:S(2)}) collective-permute-start(f32[80,128]{1,0:T(8,128)S(1)} %collective-permute-done.2._.refs_0_), channel_id=1, source_target_pairs={{0,4},{4,8},{5,1},{8,12},{9,5},{13,9},{2,6},{6,10},{7,3},{10,14},{... | collective-permute-start | bytes 122888 | tf_op jit(solution)/shard_map/ppermute | solution.py:428
  15.9 2.3 %near_wendland.1 = (bf16[512,2048]{1,0:T(8,128)(2,1)S(1)}, bf16[512,2048]{1,0:T(8,128)(2,1)S(1)}) custom-call(bf16[1024,64]{1,0:T(8,128)(2,1)S(1)} %get-tuple-element.20.left_ref, bf16[64,2048]{1,0:T(8,128)(2,1)S(1)} %get-tuple-element.21.right_ref, f32[80,128]{1,0:T(8,128)S(1)} %collective-permute-done.2._.refs_0_), custom_call_target="tpu_custom_call" | custom-call | flops 1000000000 | bytes 10000000 | tf_op jit(solution)/shard_map/near_wendland/pallas_call | solution.py:502
  18.2 0.0 collective-permute-done.3.refs_1_
  18.2 1.3 %last_sweep.1 = (f32[80,128]{1,0:T(8,128)S(1)}, f32[3,1024]{1,0:T(4,128)S(1)}) custom-call(f32[80,128]{1,0:T(8,128)S(1)} %collective-permute-done.2._.refs_0_, f32[80,128]{1,0:T(8,128)S(1)} %collective-permute-done.3.refs_1_, f32[80,128]{1,0:T(8,128)S(1)} %sweep.1.refs_2_, f32[80,128]{1,0:T(8,128)S(1)} %get-tuple-element.23.refs_3_, ...), custom_call_target="tpu_custom_call" | custom-call | flops 716800 | bytes 1228800 | tf_op jit(solution)/shard_map/last_sweep/pallas_call | solution.py:511
  19.6 1.6 %collective-permute-start.4 = (f32[3,1024]{1,0:T(4,128)S(1)}, f32[3,1024]{1,0:T(4,128)S(1)}, u32[]{:S(2)}, u32[]{:S(2)}) collective-permute-start(f32[3,1024]{1,0:T(4,128)S(1)} %get-tuple-element.30.after.refs_0_), channel_id=1, source_target_pairs={{0,2},{2,0},{1,3},{3,1},{4,6},{6,4},{5,7},{7,5},{8,10},{10,8},{9,1... | collective-permute-start | bytes 36872 | tf_op jit(solution)/shard_map/ppermute | solution.py:526
  21.1 2.3 %far_wendland.1 = (bf16[512,2048]{1,0:T(8,128)(2,1)S(1)}, bf16[512,2048]{1,0:T(8,128)(2,1)S(1)}, f32[80,128]{1,0:T(8,128)}) custom-call(bf16[1024,64]{1,0:T(8,128)(2,1)S(1)} %get-tuple-element.20.left_ref, bf16[64,2048]{1,0:T(8,128)(2,1)S(1)} %get-tuple-element.21.right_ref, f32[3,1024]{1,0:T(4,128)S(1)} %get-tuple-element.30.after.refs_0_, ...), custom_call_target="tpu_custom_call" | custom-call | flops 1000000000 | bytes 10000000 | tf_op jit(solution)/shard_map/far_wendland/pallas_call | solution.py:527
  23.5 0.0 collective-permute-done.4.refs_1_
  23.5 2.1 %control.1.own_ref = f32[16,128]{1,0:T(8,128)S(1)} custom-call(f32[3,1024]{1,0:T(4,128)S(1)} %get-tuple-element.30.after.refs_0_, f32[3,1024]{1,0:T(4,128)S(1)} %collective-permute-done.4.refs_1_, bf16[512,2048]{1,0:T(8,128)(2,1)S(1)} %get-tuple-element.29.refs_9_.refs_2_, bf16[512,2048]{1,0:T(8,128)(2,1)S(1)} %get-tuple-element.33.refs_3_, ...), custom_call_target="tpu_custom_call" | custom-call | tf_op jit(solution)/shard_map/control/pallas_call | solution.py:538
  25.6 0.1 collective-permute-start.5
  25.7 1.2 %collective-permute-done.5.other_ref = f32[16,128]{1,0:T(8,128)S(1)} collective-permute-done((f32[16,128]{1,0:T(8,128)S(1)}, f32[16,128]{1,0:T(8,128)S(1)}, u32[]{:S(2)}, u32[]{:S(2)}) %collective-permute-start.5) | collective-permute-done | bytes 8224 | tf_op jit(solution)/shard_map/ppermute | solution.py:365
  26.9 1.4 %collective-permute-start.6 = (f32[16,128]{1,0:T(8,128)S(1)}, f32[16,128]{1,0:T(8,128)S(1)}, u32[]{:S(2)}, u32[]{:S(2)}) collective-permute-start(f32[16,128]{1,0:T(8,128)S(1)} %add.1.own_ref), channel_id=1, source_target_pairs={{0,2},{1,3},{2,0},{3,1},{4,6},{5,7},{6,4},{7,5},{8,10},{9,11},{10,... | collective-permute-start | bytes 24584 | tf_op jit(solution)/shard_map/ppermute | solution.py:382
  28.3 1.6 %collective-permute-start.7 = (f32[16,128]{1,0:T(8,128)S(1)}, f32[16,128]{1,0:T(8,128)S(1)}, u32[]{:S(2)}, u32[]{:S(2)}) collective-permute-start(f32[16,128]{1,0:T(8,128)S(1)} %add.1.own_ref), channel_id=1, source_target_pairs={{0,4},{1,7},{2,6},{3,5},{4,0},{5,3},{6,2},{7,1},{8,12},{9,15},{10,... | collective-permute-start | bytes 24584 | tf_op jit(solution)/shard_map/ppermute | solution.py:382
  29.9 2.2 %collective-permute-start.8 = (f32[16,128]{1,0:T(8,128)S(1)}, f32[16,128]{1,0:T(8,128)S(1)}, u32[]{:S(2)}, u32[]{:S(2)}) collective-permute-start(f32[16,128]{1,0:T(8,128)S(1)} %add.1.own_ref), channel_id=1, source_target_pairs={{0,8},{1,11},{2,10},{3,9},{4,12},{5,15},{6,14},{7,13},{8,0},{9,3},... | collective-permute-start | bytes 24584 | tf_op jit(solution)/shard_map/ppermute | solution.py:382
  32.1 0.5 %collective-permute-start.9 = (f32[16,128]{1,0:T(8,128)S(1)}, f32[16,128]{1,0:T(8,128)S(1)}, u32[]{:S(2)}, u32[]{:S(2)}) collective-permute-start(f32[16,128]{1,0:T(8,128)S(1)} %add.1.own_ref), channel_id=1, source_target_pairs={{0,12},{1,15},{2,14},{3,13},{4,8},{5,11},{6,10},{7,9},{8,4},{9,7},... | collective-permute-start | bytes 24584 | tf_op jit(solution)/shard_map/ppermute | solution.py:382
  32.6 0.0 collective-permute-done.6.refs_0_
  32.6 0.0 collective-permute-done.7.refs_1_
  32.6 1.8 %collective-permute-done.8.refs_2_ = f32[16,128]{1,0:T(8,128)S(1)} collective-permute-done((f32[16,128]{1,0:T(8,128)S(1)}, f32[16,128]{1,0:T(8,128)S(1)}, u32[]{:S(2)}, u32[]{:S(2)}) %collective-permute-start.8) | collective-permute-done | bytes 8224 | tf_op jit(solution)/shard_map/ppermute | solution.py:382
  34.4 3.1 %collective-permute-done.9.refs_3_ = f32[16,128]{1,0:T(8,128)S(1)} collective-permute-done((f32[16,128]{1,0:T(8,128)S(1)}, f32[16,128]{1,0:T(8,128)S(1)}, u32[]{:S(2)}, u32[]{:S(2)}) %collective-permute-start.9) | collective-permute-done | bytes 8224 | tf_op jit(solution)/shard_map/ppermute | solution.py:382
  37.6 0.0 collective-permute-start.10
  37.6 1.2 %collective-permute-done.10.other_ref = f32[16,128]{1,0:T(8,128)S(1)} collective-permute-done((f32[16,128]{1,0:T(8,128)S(1)}, f32[16,128]{1,0:T(8,128)S(1)}, u32[]{:S(2)}, u32[]{:S(2)}) %collective-permute-start.10) | collective-permute-done | bytes 8224 | tf_op jit(solution)/shard_map/ppermute | solution.py:365
  38.7 0.6 %finish.1 = f32[3,512]{1,0:T(4,128)} custom-call(f32[16,128]{1,0:T(8,128)S(1)} %line.1.own_ref, f32[16,128]{1,0:T(8,128)S(1)} %collective-permute-done.10.other_ref), custom_call_target="tpu_custom_call" | custom-call | tf_op jit(solution)/shard_map/finish/pallas_call | solution.py:546
  (2 shorter events, 0.0 us)
Async XLA Ops:
  0.6 1.6 %collective-permute-start = (f32[80,128]{1,0:T(8,128)}, f32[80,128]{1,0:T(8,128)S(1)}, u32[]{:S(2)}, u32[]{:S(2)}) collective-permute-start(f32[80,128]{1,0:T(8,128)} %bitcast.38), channel_id=1, source_target_pairs={{0,1},{1,0},{4,5},{5,4},{8,9},{9,8},{12,13},{13,12},{2,3},{3,2},{6... | collective-permute-start | bytes 122888 | tf_op jit(solution)/shard_map/ppermute | solution.py:425
  2.2 7.6 %collective-permute-start.1 = (f32[80,128]{1,0:T(8,128)S(1)}, f32[80,128]{1,0:T(8,128)S(1)}, u32[]{:S(2)}, u32[]{:S(2)}) collective-permute-start(f32[80,128]{1,0:T(8,128)S(1)} %collective-permute-done._.refs_0_), channel_id=1, source_target_pairs={{0,4},{4,8},{5,1},{8,12},{9,5},{13,9},{2,6},{6,10},{7,3},{10,14},{... | collective-permute-start | bytes 122888 | tf_op jit(solution)/shard_map/ppermute | solution.py:428
  11.1 1.3 %collective-permute-start.2 = (f32[80,128]{1,0:T(8,128)S(1)}, f32[80,128]{1,0:T(8,128)S(1)}, u32[]{:S(2)}, u32[]{:S(2)}) collective-permute-start(f32[80,128]{1,0:T(8,128)S(1)} %sweep.1.refs_2_), channel_id=1, source_target_pairs={{0,1},{1,0},{4,5},{5,4},{8,9},{9,8},{12,13},{13,12},{2,3},{3,2},{6... | collective-permute-start | bytes 122888 | tf_op jit(solution)/shard_map/ppermute | solution.py:425
  12.4 5.8 %collective-permute-start.3 = (f32[80,128]{1,0:T(8,128)S(1)}, f32[80,128]{1,0:T(8,128)S(1)}, u32[]{:S(2)}, u32[]{:S(2)}) collective-permute-start(f32[80,128]{1,0:T(8,128)S(1)} %collective-permute-done.2._.refs_0_), channel_id=1, source_target_pairs={{0,4},{4,8},{5,1},{8,12},{9,5},{13,9},{2,6},{6,10},{7,3},{10,14},{... | collective-permute-start | bytes 122888 | tf_op jit(solution)/shard_map/ppermute | solution.py:428
  19.6 3.9 %collective-permute-start.4 = (f32[3,1024]{1,0:T(4,128)S(1)}, f32[3,1024]{1,0:T(4,128)S(1)}, u32[]{:S(2)}, u32[]{:S(2)}) collective-permute-start(f32[3,1024]{1,0:T(4,128)S(1)} %get-tuple-element.30.after.refs_0_), channel_id=1, source_target_pairs={{0,2},{2,0},{1,3},{3,1},{4,6},{6,4},{5,7},{7,5},{8,10},{10,8},{9,1... | collective-permute-start | bytes 36872 | tf_op jit(solution)/shard_map/ppermute | solution.py:526
  25.6 1.2 %collective-permute-start.5 = (f32[16,128]{1,0:T(8,128)S(1)}, f32[16,128]{1,0:T(8,128)S(1)}, u32[]{:S(2)}, u32[]{:S(2)}) collective-permute-start(f32[16,128]{1,0:T(8,128)S(1)} %control.1.own_ref), channel_id=1, source_target_pairs={{0,1},{1,0},{2,3},{3,2},{4,5},{5,4},{6,7},{7,6},{8,9},{9,8},{10,11... | collective-permute-start | bytes 24584 | tf_op jit(solution)/shard_map/ppermute | solution.py:365
  26.9 5.8 %collective-permute-start.6 = (f32[16,128]{1,0:T(8,128)S(1)}, f32[16,128]{1,0:T(8,128)S(1)}, u32[]{:S(2)}, u32[]{:S(2)}) collective-permute-start(f32[16,128]{1,0:T(8,128)S(1)} %add.1.own_ref), channel_id=1, source_target_pairs={{0,2},{1,3},{2,0},{3,1},{4,6},{5,7},{6,4},{7,5},{8,10},{9,11},{10,... | collective-permute-start | bytes 24584 | tf_op jit(solution)/shard_map/ppermute | solution.py:382
  28.3 4.4 %collective-permute-start.7 = (f32[16,128]{1,0:T(8,128)S(1)}, f32[16,128]{1,0:T(8,128)S(1)}, u32[]{:S(2)}, u32[]{:S(2)}) collective-permute-start(f32[16,128]{1,0:T(8,128)S(1)} %add.1.own_ref), channel_id=1, source_target_pairs={{0,4},{1,7},{2,6},{3,5},{4,0},{5,3},{6,2},{7,1},{8,12},{9,15},{10,... | collective-permute-start | bytes 24584 | tf_op jit(solution)/shard_map/ppermute | solution.py:382
  29.9 4.5 %collective-permute-start.8 = (f32[16,128]{1,0:T(8,128)S(1)}, f32[16,128]{1,0:T(8,128)S(1)}, u32[]{:S(2)}, u32[]{:S(2)}) collective-permute-start(f32[16,128]{1,0:T(8,128)S(1)} %add.1.own_ref), channel_id=1, source_target_pairs={{0,8},{1,11},{2,10},{3,9},{4,12},{5,15},{6,14},{7,13},{8,0},{9,3},... | collective-permute-start | bytes 24584 | tf_op jit(solution)/shard_map/ppermute | solution.py:382
  32.1 5.4 %collective-permute-start.9 = (f32[16,128]{1,0:T(8,128)S(1)}, f32[16,128]{1,0:T(8,128)S(1)}, u32[]{:S(2)}, u32[]{:S(2)}) collective-permute-start(f32[16,128]{1,0:T(8,128)S(1)} %add.1.own_ref), channel_id=1, source_target_pairs={{0,12},{1,15},{2,14},{3,13},{4,8},{5,11},{6,10},{7,9},{8,4},{9,7},... | collective-permute-start | bytes 24584 | tf_op jit(solution)/shard_map/ppermute | solution.py:382
  37.6 1.2 %collective-permute-start.10 = (f32[16,128]{1,0:T(8,128)S(1)}, f32[16,128]{1,0:T(8,128)S(1)}, u32[]{:S(2)}, u32[]{:S(2)}) collective-permute-start(f32[16,128]{1,0:T(8,128)S(1)} %line.1.own_ref), channel_id=1, source_target_pairs={{0,1},{1,0},{2,3},{3,2},{4,5},{5,4},{6,7},{7,6},{8,9},{9,8},{10,11... | collective-permute-start | bytes 24584 | tf_op jit(solution)/shard_map/ppermute | solution.py:365

commit v7 on v5

--- a/solution.py
+++ b/solution.py
@@ -222,7 +222,7 @@
         for node in range(nodes):
             term = part_ref[pl.ds(block * nodes + node, 3, stride=per), :]
             total = term if total is None else total + term
-        sens_out_ref[:, block * LANES : (block + 1) * LANES] = total
+        sens_out_ref[pl.ds(block, 3, stride=blocks), :] = total
 
 
 def pieces(value, count):
@@ -285,7 +285,8 @@
 
 def control_kernel(scale, *refs):
     (*sens_refs, near_first, near_rest, far_first, far_rest, spread_ref, one_hot_ref, out_ref) = refs
-    cells = sens_refs[0].shape[1]
+    blocks = sens_refs[0].shape[0] // 3
+    cells = blocks * LANES
     half = near_first.shape[0]
     slots = spread_ref.shape[0] // 16
     groups = FFD // LANES
@@ -293,11 +294,15 @@
     for ref in sens_refs[1:]:
         total = total + ref[...]
     total = total * scale
-    row = lax.broadcasted_iota(jnp.int32, (16, cells), 0)
-    sens = jnp.zeros((16, cells), jnp.float32)
-    for k in range(3):
-        mine = jnp.logical_and(row >= k * groups, row < (k + 1) * groups)
-        sens = jnp.where(mine, total[k : k + 1], sens)
+    row = lax.broadcasted_iota(jnp.int32, (16, LANES), 0)
+    wide = []
+    for block in range(blocks):
+        sens = jnp.zeros((16, LANES), jnp.float32)
+        for k in range(3):
+            mine = jnp.logical_and(row >= k * groups, row < (k + 1) * groups)
+            sens = jnp.where(mine, total[k * blocks + block : k * blocks + block + 1], sens)
+        wide.append(sens)
+    sens = jnp.concatenate(wide, axis=1)
 
     def halves(value):
         first = value.astype(jnp.bfloat16)
@@ -325,29 +330,24 @@
         )
         result = term if result is None else result + term
     result = result[:16] + result[16:]
-    out_ref[...] = result
-
-
-def add_kernel(own_ref, other_ref, out_ref):
-    out_ref[...] = own_ref[...] + other_ref[...]
-
-
-def finish_kernel(*refs):
-    total = sum(ref[...] for ref in refs[:-1])
-    groups = FFD // LANES
+    out_ref[...] = result[: 3 * groups]
+
+
+def chip_kernel(own_ref, other_ref, out_ref):
+    total = own_ref[...] + other_ref[...]
+    for copy in range(out_ref.shape[0]):
+        out_ref[copy] = total
+
+
+def finish_kernel(in_ref, out_ref):
+    values = [in_ref[i] for i in range(in_ref.shape[0])]
+    while len(values) > 1:
+        values = [sum(values[i : i + 2]) for i in range(0, len(values), 2)]
+    groups = out_ref.shape[1] // LANES
     for k in range(3):
         for group in range(groups):
             row = k * groups + group
-            refs[-1][k : k + 1, group * LANES : (group + 1) * LANES] = total[row : row + 1]
-
-
-def steps_of_sum(axes):
-    for axis in axes:
-        peers = lax.axis_size(axis)
-        shift = 1
-        while shift < peers:
-            yield axis, [(i, i ^ shift) for i in range(peers)]
-            shift *= 2
+            out_ref[k : k + 1, group * LANES : (group + 1) * LANES] = values[0][row : row + 1]
 
 
 def body(
@@ -454,12 +454,12 @@
         )(close, far, adjoint, rhs, off, inverse, lane, step)
         far, close = swaps(adjoint)
 
-    half = cells // 2
+    half = cells * 5 // 8 // LANES * LANES
     wendland_cost = cost(10**9, 10**7)
-    kernel_shape = shape((half, owned), bf16)
+    near_shape, far_shape = shape((half, owned), bf16), shape((cells - half, owned), bf16)
     near_first, near_rest = pl.pallas_call(
         functools.partial(wendland_kernel, 0),
-        out_shape=(kernel_shape, kernel_shape),
+        out_shape=(near_shape, near_shape),
         in_specs=[VMEM] * 3,
         out_specs=(VMEM, VMEM),
         compiler_params=PARAMS,
@@ -468,7 +468,7 @@
     )(left, right, adjoint)
     adjoint, part_sens = pl.pallas_call(
         functools.partial(last_sweep_kernel, blocks),
-        out_shape=(shape((5 * per, LANES)), shape((3, cells))),
+        out_shape=(shape((5 * per, LANES)), shape((3 * blocks, LANES))),
         in_specs=[VMEM] * 9 + [pl.BlockSpec(memory_space=pl.ANY)],
         out_specs=(VMEM, VMEM),
         scratch_shapes=scratch + [pltpu.VMEM((3 * per, LANES), f32)],
@@ -484,7 +484,7 @@
         all_sens.append(lax.ppermute(part_sens, "nodes", ring))
     far_first, far_rest, adjoint = pl.pallas_call(
         functools.partial(wendland_and_write_kernel, half),
-        out_shape=(kernel_shape, kernel_shape, shape((5 * per, LANES))),
+        out_shape=(far_shape, far_shape, shape((5 * per, LANES))),
         in_specs=[VMEM] * 4,
         out_specs=(VMEM, VMEM, HBM),
         scratch_shapes=[pltpu.SemaphoreType.DMA],
@@ -493,26 +493,29 @@
         name="far_wendland",
     )(left, right, part_sens, adjoint)
     scale = 4.0 / math.sqrt(cells * peers)
-    terms = [
-        pl.pallas_call(
-            functools.partial(control_kernel, scale),
-            out_shape=shape((16, LANES)),
-            in_specs=[VMEM] * (len(all_sens) + 6),
-            out_specs=VMEM,
-            compiler_params=PARAMS,
-            name="control",
-        )(*all_sens, near_first, near_rest, far_first, far_rest, spread, one_hot)
-    ]
-    for axis, partners in steps_of_sum(("sub", "nodes", "cells")):
-        partial = terms[0]
-        if len(terms) > 1:
-            partial = pl.pallas_call(
-                add_kernel, out_shape=shape((16, LANES)), name="add", compiler_params=PARAMS
-            )(*terms)
-        terms = [partial, lax.ppermute(partial, axis, partners)]
+    rows = 3 * FFD // LANES
+    partial = pl.pallas_call(
+        functools.partial(control_kernel, scale),
+        out_shape=shape((rows, LANES)),
+        in_specs=[VMEM] * (len(all_sens) + 6),
+        out_specs=VMEM,
+        compiler_params=PARAMS,
+        name="control",
+    )(*all_sens, near_first, near_rest, far_first, far_rest, spread, one_hot)
+    cores = lax.axis_size("sub")
+    other = lax.ppermute(partial, "sub", [(i, cores - 1 - i) for i in range(cores)])
+    copies = pl.pallas_call(
+        chip_kernel,
+        out_shape=shape((lax.axis_size(("cells", "nodes")), rows, LANES)),
+        in_specs=[VMEM] * 2,
+        out_specs=VMEM,
+        name="chip",
+        compiler_params=PARAMS,
+    )(partial, other)
+    gathered = lax.all_to_all(copies, ("cells", "nodes"), 0, 0, tiled=True)
     control_grad = pl.pallas_call(
         finish_kernel, out_shape=shape((3, FFD)), name="finish", compiler_params=PARAMS
-    )(*terms)
+    )(gathered)
     return (from_rows(adjoint, nodes, cells), control_grad)
 
 

time: 36.4 us -> 36.4 us (level)
  blocking collectives: 0 us -> 11.9 us
  waiting for transfers between devices: 7.98 us -> 1.27 us
  starting transfers between devices: 14.8 us -> 9.72 us
    all_to_all x0 -> x1, blocking collectives: none -> 11.9 us  [body(): gathered = lax.all_to_all(copies, ('cells', 'nodes'), 0, 0, tiled=True)]
    ppermute x4 -> x1, waiting for transfers between devices: 7.97 us -> 0.83 us  [body(): lax.ppermute(partial, 'sub', [(i, cores - 1 - i) for i in range(cores)])]
    ppermute x4 -> x1, starting transfers between devices: 7.41 us -> 2.3 us  [body(): lax.ppermute(partial, 'sub', [(i, cores - 1 - i) for i in range(cores)])]
    pallas_call x1, Pallas kernels: 2.33 us -> 1.76 us  [body(): pl.pallas_call(functools.partial(wendland_and_write_kernel, half), out_sh...]
    pallas_call x4 -> x2, Pallas kernels: 2.33 us -> 2.9 us  [the longest x1 2.89 us: body(): pl.pallas_call(functools.partial(wendland_kernel, 0), out_shape=(near_sha...]
    ppermute x1, waiting for transfers between devices: 0.01 us -> 0.43 us  [body(): all_sens.append(lax.ppermute(part_sens, 'nodes', ring))]
  transfers between devices with their start and end apart: 9 -> 6, of which waited for: 4 -> 2; matrix products, arithmetic and copies ran while one was open for 0% -> 0% of each run, Pallas kernels for 20% -> 20%
where the time goes in v7:
time: 36.4 us; the launch traced here: 36.2 us
  Pallas kernels  12.5 us (34%)
  blocking collectives  11.9 us (33%)
  starting transfers between devices  9.72 us (27%)
  waiting for transfers between devices  1.27 us (3%)
  between operations  0.72 us (2%)
    all_to_all x1, blocking collectives, body(): gathered = lax.all_to_all(copies, ('cells', 'nodes'), 0, 0, tiled=True)  11.9 us
    ppermute x2, starting transfers between devices, swaps(): close = lax.ppermute(array, CELL_AXES, first)  3.78 us
    pallas_call x1, Pallas kernels, body(): pl.pallas_call(functools.partial(wendland_kernel, 0), out_shape=(near_sha...  2.89 us
    pallas_call x1, Pallas kernels, body(): pl.pallas_call(functools.partial(prepare_kernel, nodes), out_shape=(shape...  2.73 us
    ppermute x1, starting transfers between devices, body(): lax.ppermute(partial, 'sub', [(i, cores - 1 - i) for i in range(cores)])  2.3 us
    ppermute x2, starting transfers between devices, swaps(): far = lax.ppermute(array, CELL_AXES, second)  2.08 us
    pallas_call x1, Pallas kernels, body(): pl.pallas_call(functools.partial(control_kernel, scale), out_shape=shape(...  2.04 us
    pallas_call x1, Pallas kernels, body(): pl.pallas_call(functools.partial(wendland_and_write_kernel, half), out_sh...  1.76 us
  transfers between devices with their start and end apart: 6, of which 2 were waited for; matrix products, arithmetic and copies ran while one was open for 0% of the time, Pallas kernels for 20%

profile of v7, /device:TPU:0, one launch (start us, length us, event | category | flops | bytes accessed | tf_op | source)
XLA Modules:
  0.0 36.2 jit_solution(17410742734943741396)
XLA Ops:
  0.6 0.5 %collective-permute-start = (f32[80,128]{1,0:T(8,128)}, f32[80,128]{1,0:T(8,128)S(1)}, u32[]{:S(2)}, u32[]{:S(2)}) collective-permute-start(f32[80,128]{1,0:T(8,128)} %bitcast.38), channel_id=1, source_target_pairs={{0,1},{1,0},{4,5},{5,4},{8,9},{9,8},{12,13},{13,12},{2,3},{3,2},{6... | collective-permute-start | bytes 122888 | tf_op jit(solution)/shard_map/ppermute | solution.py:386
  1.2 1.4 %collective-permute-start.1 = (f32[80,128]{1,0:T(8,128)}, f32[80,128]{1,0:T(8,128)S(1)}, u32[]{:S(2)}, u32[]{:S(2)}) collective-permute-start(f32[80,128]{1,0:T(8,128)} %bitcast.39), channel_id=1, source_target_pairs={{0,0},{1,4},{4,1},{5,8},{8,5},{9,12},{12,9},{13,13},{2,2},{3,6},{6... | collective-permute-start | bytes 122888 | tf_op jit(solution)/shard_map/ppermute | solution.py:385
  2.6 2.7 %prepare.1 = (f32[2400,128]{1,0:T(8,128)S(1)}, f32[400,128]{1,0:T(8,128)S(1)}, f32[80,128]{1,0:T(8,128)S(1)}, f32[240,128]{1,0:T(8,128)S(1)}, s32[96,128]{1,0:T(...) custom-call(bf16[2400,128]{1,0:T(8,128)(2,1)} %bitcast.32, ...), custom_call_target="tpu_custom_call" | custom-call | flops 1000000000 | bytes 10000000 | tf_op jit(solution)/shard_map/prepare/pallas_call | solution.py:391
  5.3 0.0 collective-permute-done.refs_0_
  5.3 0.0 collective-permute-done.1.refs_1_
  5.3 1.2 %sweep.1._.refs_2_ = f32[80,128]{1,0:T(8,128)S(1)} custom-call(f32[80,128]{1,0:T(8,128)S(1)} %collective-permute-done.refs_0_, f32[80,128]{1,0:T(8,128)S(1)} %collective-permute-done.1.refs_1_, f32[80,128]{1,0:T(8,128)S(1)} %get-tuple-element.22.refs_2_, f32[80,128]{1,0:T(8,128)S(1)} %get-tuple-element.23.refs_3_, ...), custom_call_target="tpu_custom_call" | custom-call | flops 716800 | bytes 1228800 | tf_op jit(solution)/shard_map/sweep/pallas_call | solution.py:445
  6.6 3.3 %collective-permute-start.2 = (f32[80,128]{1,0:T(8,128)S(1)}, f32[80,128]{1,0:T(8,128)S(1)}, u32[]{:S(2)}, u32[]{:S(2)}) collective-permute-start(f32[80,128]{1,0:T(8,128)S(1)} %sweep.1._.refs_2_), channel_id=1, source_target_pairs={{0,1},{1,0},{4,5},{5,4},{8,9},{9,8},{12,13},{13,12},{2,3},{3,2},{6... | collective-permute-start | bytes 122888 | tf_op jit(solution)/shard_map/ppermute | solution.py:386
  9.8 0.7 %collective-permute-start.3 = (f32[80,128]{1,0:T(8,128)S(1)}, f32[80,128]{1,0:T(8,128)S(1)}, u32[]{:S(2)}, u32[]{:S(2)}) collective-permute-start(f32[80,128]{1,0:T(8,128)S(1)} %sweep.1._.refs_2_), channel_id=1, source_target_pairs={{0,0},{1,4},{4,1},{5,8},{8,5},{9,12},{12,9},{13,13},{2,2},{3,6},{6... | collective-permute-start | bytes 122888 | tf_op jit(solution)/shard_map/ppermute | solution.py:385
  10.5 2.9 %near_wendland.1 = (bf16[640,2048]{1,0:T(8,128)(2,1)S(1)}, bf16[640,2048]{1,0:T(8,128)(2,1)S(1)}) custom-call(bf16[1024,64]{1,0:T(8,128)(2,1)S(1)} %get-tuple-element.20.left_ref, bf16[64,2048]{1,0:T(8,128)(2,1)S(1)} %get-tuple-element.21.right_ref, f32[80,128]{1,0:T(8,128)S(1)} %sweep.1._.refs_2_), custom_call_target="tpu_custom_call" | custom-call | flops 1000000000 | bytes 10000000 | tf_op jit(solution)/shard_map/near_wendland/pallas_call | solution.py:460
  13.4 0.0 collective-permute-done.2.refs_0_
  13.4 0.0 collective-permute-done.3.refs_1_
  13.4 1.3 %last_sweep.1 = (f32[80,128]{1,0:T(8,128)S(1)}, f32[24,128]{1,0:T(8,128)S(1)}) custom-call(f32[80,128]{1,0:T(8,128)S(1)} %collective-permute-done.2.refs_0_, f32[80,128]{1,0:T(8,128)S(1)} %collective-permute-done.3.refs_1_, f32[80,128]{1,0:T(8,128)S(1)} %sweep.1._.refs_2_, f32[80,128]{1,0:T(8,128)S(1)} %get-tuple-element.23.refs_3_, ...), custom_call_target="tpu_custom_call" | custom-call | flops 716800 | bytes 1228800 | tf_op jit(solution)/shard_map/last_sweep/pallas_call | solution.py:469
  14.7 1.6 %collective-permute-start.4 = (f32[24,128]{1,0:T(8,128)S(1)}, f32[24,128]{1,0:T(8,128)S(1)}, u32[]{:S(2)}, u32[]{:S(2)}) collective-permute-start(f32[24,128]{1,0:T(8,128)S(1)} %get-tuple-element.30.after.refs_0_), channel_id=1, source_target_pairs={{0,2},{2,0},{1,3},{3,1},{4,6},{6,4},{5,7},{7,5},{8,10},{10,8},{9,1... | collective-permute-start | bytes 36872 | tf_op jit(solution)/shard_map/ppermute | solution.py:484
  16.3 1.8 %far_wendland.1 = (bf16[384,2048]{1,0:T(8,128)(2,1)S(1)}, bf16[384,2048]{1,0:T(8,128)(2,1)S(1)}, f32[80,128]{1,0:T(8,128)}) custom-call(bf16[1024,64]{1,0:T(8,128)(2,1)S(1)} %get-tuple-element.20.left_ref, bf16[64,2048]{1,0:T(8,128)(2,1)S(1)} %get-tuple-element.21.right_ref, f32[24,128]{1,0:T(8,128)S(1)} %get-tuple-element.30.after.refs_0_, ...), custom_call_target="tpu_custom_call" | custom-call | flops 1000000000 | bytes 10000000 | tf_op jit(solution)/shard_map/far_wendland/pallas_call | solution.py:485
  18.0 0.4 %collective-permute-done.4.refs_1_ = f32[24,128]{1,0:T(8,128)S(1)} collective-permute-done((f32[24,128]{1,0:T(8,128)S(1)}, f32[24,128]{1,0:T(8,128)S(1)}, u32[]{:S(2)}, u32[]{:S(2)}) %collective-permute-start.4) | collective-permute-done | bytes 12320 | tf_op jit(solution)/shard_map/ppermute | solution.py:484
  18.5 2.0 %control.1.own_ref = f32[12,128]{1,0:T(8,128)S(1)} custom-call(f32[24,128]{1,0:T(8,128)S(1)} %get-tuple-element.30.after.refs_0_, f32[24,128]{1,0:T(8,128)S(1)} %collective-permute-done.4.refs_1_, bf16[640,2048]{1,0:T(8,128)(2,1)S(1)} %get-tuple-element.29.refs_9_.refs_2_, bf16[640,2048]{1,0:T(8,128)(2,1)S(1)} %get-tuple-element.33.refs_3_, ...), custom_call_target="tpu_custom_call" | custom-call | tf_op jit(solution)/shard_map/control/pallas_call | solution.py:497
  20.5 2.3 %collective-permute-start.5 = (f32[12,128]{1,0:T(8,128)S(1)}, f32[12,128]{1,0:T(8,128)S(1)}, u32[]{:S(2)}, u32[]{:S(2)}) collective-permute-start(f32[12,128]{1,0:T(8,128)S(1)} %control.1.own_ref), channel_id=1, source_target_pairs={{0,1},{1,0},{2,3},{3,2},{4,5},{5,4},{6,7},{7,6},{8,9},{9,8},{10,11... | collective-permute-start | bytes 18440 | tf_op jit(solution)/shard_map/ppermute | solution.py:506
  22.8 0.8 %collective-permute-done.5.other_ref = f32[12,128]{1,0:T(8,128)S(1)} collective-permute-done((f32[12,128]{1,0:T(8,128)S(1)}, f32[12,128]{1,0:T(8,128)S(1)}, u32[]{:S(2)}, u32[]{:S(2)}) %collective-permute-start.5) | collective-permute-done | bytes 6176 | tf_op jit(solution)/shard_map/ppermute | solution.py:506
  23.6 11.9 %all_to_all.5.in_ref = f32[8,12,128]{2,1,0:T(8,128)S(1)} all-to-all(f32[8,12,128]{2,1,0:T(8,128)S(1)} %chip.1), channel_id=1, replica_groups=mesh['groups'=2,'cells'=4,'nodes'=2,'sub'=2] {'cells','nodes'}, dimensions={0} | all-to-all | bytes 98304 | tf_op jit(solution)/shard_map/all_to_all | solution.py:515
  35.6 0.6 %finish.1 = f32[3,512]{1,0:T(4,128)} custom-call(f32[8,12,128]{2,1,0:T(8,128)S(1)} %all_to_all.5.in_ref), custom_call_target="tpu_custom_call" | custom-call | tf_op jit(solution)/shard_map/finish/pallas_call | solution.py:516
  (1 shorter events, 0.0 us)
Async XLA Ops:
  0.6 4.7 %collective-permute-start = (f32[80,128]{1,0:T(8,128)}, f32[80,128]{1,0:T(8,128)S(1)}, u32[]{:S(2)}, u32[]{:S(2)}) collective-permute-start(f32[80,128]{1,0:T(8,128)} %bitcast.38), channel_id=1, source_target_pairs={{0,1},{1,0},{4,5},{5,4},{8,9},{9,8},{12,13},{13,12},{2,3},{3,2},{6... | collective-permute-start | bytes 122888 | tf_op jit(solution)/shard_map/ppermute | solution.py:386
  1.2 4.2 %collective-permute-start.1 = (f32[80,128]{1,0:T(8,128)}, f32[80,128]{1,0:T(8,128)S(1)}, u32[]{:S(2)}, u32[]{:S(2)}) collective-permute-start(f32[80,128]{1,0:T(8,128)} %bitcast.39), channel_id=1, source_target_pairs={{0,0},{1,4},{4,1},{5,8},{8,5},{9,12},{12,9},{13,13},{2,2},{3,6},{6... | collective-permute-start | bytes 122888 | tf_op jit(solution)/shard_map/ppermute | solution.py:385
  6.6 6.8 %collective-permute-start.2 = (f32[80,128]{1,0:T(8,128)S(1)}, f32[80,128]{1,0:T(8,128)S(1)}, u32[]{:S(2)}, u32[]{:S(2)}) collective-permute-start(f32[80,128]{1,0:T(8,128)S(1)} %sweep.1._.refs_2_), channel_id=1, source_target_pairs={{0,1},{1,0},{4,5},{5,4},{8,9},{9,8},{12,13},{13,12},{2,3},{3,2},{6... | collective-permute-start | bytes 122888 | tf_op jit(solution)/shard_map/ppermute | solution.py:386
  9.8 3.6 %collective-permute-start.3 = (f32[80,128]{1,0:T(8,128)S(1)}, f32[80,128]{1,0:T(8,128)S(1)}, u32[]{:S(2)}, u32[]{:S(2)}) collective-permute-start(f32[80,128]{1,0:T(8,128)S(1)} %sweep.1._.refs_2_), channel_id=1, source_target_pairs={{0,0},{1,4},{4,1},{5,8},{8,5},{9,12},{12,9},{13,13},{2,2},{3,6},{6... | collective-permute-start | bytes 122888 | tf_op jit(solution)/shard_map/ppermute | solution.py:385
  14.7 3.8 %collective-permute-start.4 = (f32[24,128]{1,0:T(8,128)S(1)}, f32[24,128]{1,0:T(8,128)S(1)}, u32[]{:S(2)}, u32[]{:S(2)}) collective-permute-start(f32[24,128]{1,0:T(8,128)S(1)} %get-tuple-element.30.after.refs_0_), channel_id=1, source_target_pairs={{0,2},{2,0},{1,3},{3,1},{4,6},{6,4},{5,7},{7,5},{8,10},{10,8},{9,1... | collective-permute-start | bytes 36872 | tf_op jit(solution)/shard_map/ppermute | solution.py:484
  20.5 3.1 %collective-permute-start.5 = (f32[12,128]{1,0:T(8,128)S(1)}, f32[12,128]{1,0:T(8,128)S(1)}, u32[]{:S(2)}, u32[]{:S(2)}) collective-permute-start(f32[12,128]{1,0:T(8,128)S(1)} %control.1.own_ref), channel_id=1, source_target_pairs={{0,1},{1,0},{2,3},{3,2},{4,5},{5,4},{6,7},{7,6},{8,9},{9,8},{10,11... | collective-permute-start | bytes 18440 | tf_op jit(solution)/shard_map/ppermute | solution.py:506

commit v8 on v7

--- a/solution.py
+++ b/solution.py
@@ -34,6 +34,21 @@
 
 def in_hbm(*arrays):
     return [pltpu.with_memory_space_constraint(array, pltpu.HBM) for array in arrays]
+
+
+def write_one_hot(low_ref, one_hot_ref, first_slot):
+    owned = low_ref.shape[1]
+    piece = min(512, owned)
+    lane = lax.broadcasted_iota(jnp.int32, (piece, LANES), 1).astype(jnp.float32)
+    lane = lane.astype(jnp.bfloat16)
+    for first in range(0, owned, piece):
+        low = low_ref[:, first : first + piece].T.astype(jnp.bfloat16)
+        for j in range(one_hot_ref.shape[0] // owned):
+            column = low[:, first_slot + j : first_slot + j + 1]
+            hit = jnp.broadcast_to(column, (piece, LANES)) == lane
+            one_hot_ref[j * owned + first : j * owned + first + piece, :] = jnp.where(
+                hit, jnp.bfloat16(1.0), jnp.bfloat16(0.0)
+            )
 
 
 def prepare_kernel(
@@ -56,6 +71,7 @@
     lane_ref,
     step_ref,
     spread_ref,
+    low_ref,
     one_hot_ref,
     start_ref,
     left_ref,
@@ -112,21 +128,16 @@
     piece = min(512, owned)
     for first in range(0, owned, piece):
         here = slice(first, first + piece)
-        low = jnp.bitwise_and(index_buf[:, here], LANES - 1).astype(jnp.float32).T
-        low = low.astype(jnp.bfloat16)
         high = jnp.right_shift(index_buf[:, here], 7)
-        lane = lax.broadcasted_iota(jnp.int32, (piece, LANES), 1).astype(jnp.float32)
-        lane = lane.astype(jnp.bfloat16)
         part = lax.broadcasted_iota(jnp.int32, (16, piece), 0)
         part = jnp.where(part < 3 * groups, lax.rem(part, groups), -1)
         for j in range(slots):
-            hit = jnp.broadcast_to(low[:, j : j + 1], (piece, LANES)) == lane
-            one_hot_ref[j * owned + first : j * owned + first + piece, :] = jnp.where(
-                hit, jnp.bfloat16(1.0), jnp.bfloat16(0.0)
-            )
             spread_ref[j * 16 : (j + 1) * 16, here] = jnp.where(
                 high[j : j + 1] == part, spread_buf[j : j + 1, here], 0.0
             )
+
+    low_ref[...] = jnp.bitwise_and(index_buf[...], LANES - 1).astype(jnp.float32)
+    write_one_hot(low_ref, one_hot_ref, 0)
 
     copies[3].wait()
     left_ref[...] = distance_factors(cell_buf[...], True).T.astype(jnp.bfloat16)
@@ -275,20 +286,24 @@
             )
 
 
-def wendland_and_write_kernel(first_cell, left_ref, right_ref, after, adjoint_ref, *rest):
-    first_ref, rest_ref, result_ref, sem = rest
+def far_wendland_kernel(
+    first_cell, left_ref, right_ref, after, adjoint_ref, low_ref, *rest
+):
+    first_ref, rest_ref, one_hot_ref, result_ref, sem = rest
     copy = pltpu.make_async_copy(adjoint_ref, result_ref, sem)
     copy.start()
+    owned = low_ref.shape[1]
+    write_one_hot(low_ref, one_hot_ref, low_ref.shape[0] - one_hot_ref.shape[0] // owned)
     wendland_kernel(first_cell, left_ref, right_ref, after, first_ref, rest_ref)
     copy.wait()
 
 
 def control_kernel(scale, *refs):
-    (*sens_refs, near_first, near_rest, far_first, far_rest, spread_ref, one_hot_ref, out_ref) = refs
+    *sens_refs, near_first, near_rest, far_first, far_rest = refs[:-4]
+    spread_ref, near_hot, far_hot, out_ref = refs[-4:]
     blocks = sens_refs[0].shape[0] // 3
     cells = blocks * LANES
     half = near_first.shape[0]
-    slots = spread_ref.shape[0] // 16
     groups = FFD // LANES
     total = sens_refs[0][...]
     for ref in sens_refs[1:]:
@@ -322,10 +337,13 @@
     grad = grad[:16] + grad[16:]
     owned = grad.shape[1]
     result = None
-    for j in range(slots):
+    places = [
+        (ref, first) for ref in (near_hot, far_hot) for first in range(0, ref.shape[0], owned)
+    ]
+    for j, (ref, first) in enumerate(places):
         term = jnp.dot(
             halves(grad * spread_ref[j * 16 : (j + 1) * 16, :]),
-            one_hot_ref[j * owned : (j + 1) * owned, :],
+            ref[first : first + owned, :],
             preferred_element_type=jnp.float32,
         )
         result = term if result is None else result + term
@@ -333,21 +351,33 @@
     out_ref[...] = result[: 3 * groups]
 
 
-def chip_kernel(own_ref, other_ref, out_ref):
-    total = own_ref[...] + other_ref[...]
-    for copy in range(out_ref.shape[0]):
-        out_ref[copy] = total
-
-
-def finish_kernel(in_ref, out_ref):
-    values = [in_ref[i] for i in range(in_ref.shape[0])]
+def tree(values):
     while len(values) > 1:
         values = [sum(values[i : i + 2]) for i in range(0, len(values), 2)]
+    return values[0]
+
+
+def add_kernel(*refs):
+    refs[-1][...] = tree([ref[...] for ref in refs[:-1]])
+
+
+def finish_kernel(*refs):
+    total, out_ref = tree([ref[...] for ref in refs[:-1]]), refs[-1]
     groups = out_ref.shape[1] // LANES
     for k in range(3):
         for group in range(groups):
             row = k * groups + group
-            out_ref[k : k + 1, group * LANES : (group + 1) * LANES] = values[0][row : row + 1]
+            out_ref[k : k + 1, group * LANES : (group + 1) * LANES] = total[row : row + 1]
+
+
+def exchanged(value, axes):
+    peers = lax.axis_size(axes)
+    if peers > 8 or peers & (peers - 1):
+        return [lax.psum(value, axes)]
+    return [value] + [
+        lax.ppermute(value, axes, [(i, i ^ shift) for i in range(peers)])
+        for shift in range(1, peers)
+    ]
 
 
 def body(
@@ -398,13 +428,14 @@
             shape((faces * per, LANES), i32),
             shape((faces * per, LANES), i32),
             shape((slots * 16, owned)),
-            shape((slots * owned, LANES), bf16),
+            shape((slots, owned)),
+            shape((slots // 2 * owned, LANES), bf16),
             shape((5 * per, LANES)),
             shape((cells, FACTOR_ROWS), bf16),
             shape((FACTOR_ROWS, owned), bf16),
         ),
         in_specs=[HBM] * 11,
-        out_specs=(VMEM,) * 11,
+        out_specs=(VMEM,) * 12,
         scratch_shapes=[
             pltpu.VMEM((faces * 25 * per, LANES), bf16),
             pltpu.VMEM((15 * per, LANES), bf16),
@@ -434,7 +465,7 @@
             base_points,
         )
     )
-    off, inverse, rhs, sens, lane, step, spread, one_hot, adjoint, left, right = prepared
+    off, inverse, rhs, sens, lane, step, spread, low, near_hot, adjoint, left, right = prepared
     scratch = [
         pltpu.VMEM((3 * 5 * per, LANES), f32),
         pltpu.VMEM((8 // nodes * 3 * 5 * per, LANES), f32),
@@ -482,40 +513,33 @@
     for shift in range(1, node_peers):
         ring = [(i, (i + shift) % node_peers) for i in range(node_peers)]
         all_sens.append(lax.ppermute(part_sens, "nodes", ring))
-    far_first, far_rest, adjoint = pl.pallas_call(
-        functools.partial(wendland_and_write_kernel, half),
-        out_shape=(far_shape, far_shape, shape((5 * per, LANES))),
-        in_specs=[VMEM] * 4,
-        out_specs=(VMEM, VMEM, HBM),
+    hot_shape = shape(((slots - slots // 2) * owned, LANES), bf16)
+    far_first, far_rest, far_hot, adjoint = pl.pallas_call(
+        functools.partial(far_wendland_kernel, half),
+        out_shape=(far_shape, far_shape, hot_shape, shape((5 * per, LANES))),
+        in_specs=[VMEM] * 5,
+        out_specs=(VMEM, VMEM, VMEM, HBM),
         scratch_shapes=[pltpu.SemaphoreType.DMA],
         compiler_params=PARAMS,
         cost_estimate=wendland_cost,
         name="far_wendland",
-    )(left, right, part_sens, adjoint)
+    )(left, right, part_sens, adjoint, low)
     scale = 4.0 / math.sqrt(cells * peers)
     rows = 3 * FFD // LANES
     partial = pl.pallas_call(
         functools.partial(control_kernel, scale),
         out_shape=shape((rows, LANES)),
-        in_specs=[VMEM] * (len(all_sens) + 6),
+        in_specs=[VMEM] * (len(all_sens) + 7),
         out_specs=VMEM,
         compiler_params=PARAMS,
         name="control",
-    )(*all_sens, near_first, near_rest, far_first, far_rest, spread, one_hot)
-    cores = lax.axis_size("sub")
-    other = lax.ppermute(partial, "sub", [(i, cores - 1 - i) for i in range(cores)])
-    copies = pl.pallas_call(
-        chip_kernel,
-        out_shape=shape((lax.axis_size(("cells", "nodes")), rows, LANES)),
-        in_specs=[VMEM] * 2,
-        out_specs=VMEM,
-        name="chip",
-        compiler_params=PARAMS,
-    )(partial, other)
-    gathered = lax.all_to_all(copies, ("cells", "nodes"), 0, 0, tiled=True)
+    )(*all_sens, near_first, near_rest, far_first, far_rest, spread, near_hot, far_hot)
+    partial = pl.pallas_call(
+        add_kernel, out_shape=shape((rows, LANES)), name="add", compiler_params=PARAMS
+    )(*exchanged(partial, ("nodes", "sub")))
     control_grad = pl.pallas_call(
         finish_kernel, out_shape=shape((3, FFD)), name="finish", compiler_params=PARAMS
-    )(gathered)
+    )(*exchanged(partial, "cells"))
     return (from_rows(adjoint, nodes, cells), control_grad)
 
 

time: 36.4 us -> 35.3 us (0.970)
  blocking collectives: 11.9 us -> 0 us
  starting transfers between devices: 9.72 us -> 16.2 us
  waiting for transfers between devices: 1.27 us -> 5.57 us
    all_to_all x1 -> x0, blocking collectives: 11.9 us -> none  [body(): gathered = lax.all_to_all(copies, ('cells', 'nodes'), 0, 0, tiled=True)]
    ppermute x1 -> x6, starting transfers between devices: 2.3 us -> 8.6 us  [exchanged(): lax.ppermute(value, axes, [(i, i ^ shift) for i in range(peers)])]
    ppermute x1 -> x6, waiting for transfers between devices: 0.83 us -> 5.55 us  [exchanged(): lax.ppermute(value, axes, [(i, i ^ shift) for i in range(peers)])]
    pallas_call x1, Pallas kernels: 2.73 us -> 2.18 us  [body(): pl.pallas_call(functools.partial(prepare_kernel, nodes), out_shape=(shape...]
    pallas_call x2, Pallas kernels: 1.77 us -> 2.23 us  [the longest x1 2.22 us: body(): pl.pallas_call(functools.partial(far_wendland_kernel, half), out_shape=(f...]
    ppermute x1, waiting for transfers between devices: 0.43 us -> 0.01 us  [body(): all_sens.append(lax.ppermute(part_sens, 'nodes', ring))]
  transfers between devices with their start and end apart: 6 -> 11, of which waited for: 2 -> 4; matrix products, arithmetic and copies ran while one was open for 0% -> 0% of each run, Pallas kernels for 20% -> 21%
where the time goes in v8:
time: 35.3 us; the launch traced here: 35.1 us
  starting transfers between devices  16.2 us (46%)
  Pallas kernels  12.6 us (36%)
  waiting for transfers between devices  5.57 us (16%)
  between operations  0.73 us (2%)
    ppermute x6, starting transfers between devices, exchanged(): lax.ppermute(value, axes, [(i, i ^ shift) for i in range(peers)])  8.6 us
    ppermute x6, waiting for transfers between devices, exchanged(): lax.ppermute(value, axes, [(i, i ^ shift) for i in range(peers)])  5.55 us
    ppermute x2, starting transfers between devices, swaps(): close = lax.ppermute(array, CELL_AXES, first)  3.78 us
    pallas_call x1, Pallas kernels, body(): pl.pallas_call(functools.partial(wendland_kernel, 0), out_shape=(near_sha...  2.9 us
    pallas_call x1, Pallas kernels, body(): pl.pallas_call(functools.partial(far_wendland_kernel, half), out_shape=(f...  2.22 us
    pallas_call x1, Pallas kernels, body(): pl.pallas_call(functools.partial(prepare_kernel, nodes), out_shape=(shape...  2.18 us
    ppermute x2, starting transfers between devices, swaps(): far = lax.ppermute(array, CELL_AXES, second)  2.08 us
    pallas_call x1, Pallas kernels, body(): pl.pallas_call(functools.partial(control_kernel, scale), out_shape=shape(...  2.08 us
  transfers between devices with their start and end apart: 11, of which 4 were waited for; matrix products, arithmetic and copies ran while one was open for 0% of the time, Pallas kernels for 21%

profile of v8, /device:TPU:0, one launch (start us, length us, event | category | flops | bytes accessed | tf_op | source)
XLA Modules:
  0.0 35.1 jit_solution(7177813707580855069)
XLA Ops:
  0.6 0.5 %collective-permute-start = (f32[80,128]{1,0:T(8,128)}, f32[80,128]{1,0:T(8,128)S(1)}, u32[]{:S(2)}, u32[]{:S(2)}) collective-permute-start(f32[80,128]{1,0:T(8,128)} %bitcast.38), channel_id=1, source_target_pairs={{0,1},{1,0},{4,5},{5,4},{8,9},{9,8},{12,13},{13,12},{2,3},{3,2},{6... | collective-permute-start | bytes 122888 | tf_op jit(solution)/shard_map/ppermute | solution.py:416
  1.2 1.4 %collective-permute-start.1 = (f32[80,128]{1,0:T(8,128)}, f32[80,128]{1,0:T(8,128)S(1)}, u32[]{:S(2)}, u32[]{:S(2)}) collective-permute-start(f32[80,128]{1,0:T(8,128)} %bitcast.39), channel_id=1, source_target_pairs={{0,0},{1,4},{4,1},{5,8},{8,5},{9,12},{12,9},{13,13},{2,2},{3,6},{6... | collective-permute-start | bytes 122888 | tf_op jit(solution)/shard_map/ppermute | solution.py:415
  2.6 2.2 %prepare.1 = (f32[2400,128]{1,0:T(8,128)S(1)}, f32[400,128]{1,0:T(8,128)S(1)}, f32[80,128]{1,0:T(8,128)S(1)}, f32[240,128]{1,0:T(8,128)S(1)}, s32[96,128]{1,0:T(...) custom-call(bf16[2400,128]{1,0:T(8,128)(2,1)} %bitcast.32, ...), custom_call_target="tpu_custom_call" | custom-call | flops 1000000000 | bytes 10000000 | tf_op jit(solution)/shard_map/prepare/pallas_call | solution.py:421
  4.8 0.0 collective-permute-done.refs_0_
  4.8 0.0 collective-permute-done.1.refs_1_
  4.8 1.3 %sweep.1._.refs_2_ = f32[80,128]{1,0:T(8,128)S(1)} custom-call(f32[80,128]{1,0:T(8,128)S(1)} %collective-permute-done.refs_0_, f32[80,128]{1,0:T(8,128)S(1)} %collective-permute-done.1.refs_1_, f32[80,128]{1,0:T(8,128)S(1)} %get-tuple-element.24.refs_2_, f32[80,128]{1,0:T(8,128)S(1)} %get-tuple-element.25.refs_3_, ...), custom_call_target="tpu_custom_call" | custom-call | flops 716800 | bytes 1228800 | tf_op jit(solution)/shard_map/sweep/pallas_call | solution.py:476
  6.1 3.3 %collective-permute-start.2 = (f32[80,128]{1,0:T(8,128)S(1)}, f32[80,128]{1,0:T(8,128)S(1)}, u32[]{:S(2)}, u32[]{:S(2)}) collective-permute-start(f32[80,128]{1,0:T(8,128)S(1)} %sweep.1._.refs_2_), channel_id=1, source_target_pairs={{0,1},{1,0},{4,5},{5,4},{8,9},{9,8},{12,13},{13,12},{2,3},{3,2},{6... | collective-permute-start | bytes 122888 | tf_op jit(solution)/shard_map/ppermute | solution.py:416
  9.4 0.7 %collective-permute-start.3 = (f32[80,128]{1,0:T(8,128)S(1)}, f32[80,128]{1,0:T(8,128)S(1)}, u32[]{:S(2)}, u32[]{:S(2)}) collective-permute-start(f32[80,128]{1,0:T(8,128)S(1)} %sweep.1._.refs_2_), channel_id=1, source_target_pairs={{0,0},{1,4},{4,1},{5,8},{8,5},{9,12},{12,9},{13,13},{2,2},{3,6},{6... | collective-permute-start | bytes 122888 | tf_op jit(solution)/shard_map/ppermute | solution.py:415
  10.0 2.9 %near_wendland.1 = (bf16[640,2048]{1,0:T(8,128)(2,1)S(1)}, bf16[640,2048]{1,0:T(8,128)(2,1)S(1)}) custom-call(bf16[1024,64]{1,0:T(8,128)(2,1)S(1)} %get-tuple-element.22.left_ref, bf16[64,2048]{1,0:T(8,128)(2,1)S(1)} %get-tuple-element.23.right_ref, f32[80,128]{1,0:T(8,128)S(1)} %sweep.1._.refs_2_), custom_call_target="tpu_custom_call" | custom-call | flops 1000000000 | bytes 10000000 | tf_op jit(solution)/shard_map/near_wendland/pallas_call | solution.py:491
  12.9 0.0 collective-permute-done.2.refs_0_
  12.9 0.0 collective-permute-done.3.refs_1_
  13.0 1.3 %last_sweep.1 = (f32[80,128]{1,0:T(8,128)S(1)}, f32[24,128]{1,0:T(8,128)S(1)}) custom-call(f32[80,128]{1,0:T(8,128)S(1)} %collective-permute-done.2.refs_0_, f32[80,128]{1,0:T(8,128)S(1)} %collective-permute-done.3.refs_1_, f32[80,128]{1,0:T(8,128)S(1)} %sweep.1._.refs_2_, f32[80,128]{1,0:T(8,128)S(1)} %get-tuple-element.25.refs_3_, ...), custom_call_target="tpu_custom_call" | custom-call | flops 716800 | bytes 1228800 | tf_op jit(solution)/shard_map/last_sweep/pallas_call | solution.py:500
  14.3 1.7 %collective-permute-start.4 = (f32[24,128]{1,0:T(8,128)S(1)}, f32[24,128]{1,0:T(8,128)S(1)}, u32[]{:S(2)}, u32[]{:S(2)}) collective-permute-start(f32[24,128]{1,0:T(8,128)S(1)} %get-tuple-element.32.after.refs_0_), channel_id=1, source_target_pairs={{0,2},{2,0},{1,3},{3,1},{4,6},{6,4},{5,7},{7,5},{8,10},{10,8},{9,1... | collective-permute-start | bytes 36872 | tf_op jit(solution)/shard_map/ppermute | solution.py:515
  16.0 2.2 %far_wendland.1 = (bf16[384,2048]{1,0:T(8,128)(2,1)S(1)}, bf16[384,2048]{1,0:T(8,128)(2,1)S(1)}, bf16[8192,128]{1,0:T(8,128)(2,1)S(1)}, f32[80,128]{1,0:T(8,128)}) custom-call(bf16[1024,64]{1,0:T(8,128)(2,1)S(1)} %get-tuple-element.22.left_ref, bf16[64,2048]{1,0:T(8,128)(2,1)S(1)} %get-tuple-element.23.right_ref, ...), custom_call_target="tpu_custom_call" | custom-call | flops 1000000000 | bytes 10000000 | tf_op jit(solution)/shard_map/far_wendland/pallas_call | solution.py:517
  18.3 0.0 collective-permute-done.4.refs_1_
  18.3 2.1 %control.1.refs_0_ = f32[12,128]{1,0:T(8,128)S(1)} custom-call(f32[24,128]{1,0:T(8,128)S(1)} %get-tuple-element.32.after.refs_0_, f32[24,128]{1,0:T(8,128)S(1)} %collective-permute-done.4.refs_1_, bf16[640,2048]{1,0:T(8,128)(2,1)S(1)} %get-tuple-element.31.refs_9_.refs_2_, bf16[640,2048]{1,0:T(8,128)(2,1)S(1)} %get-tuple-element.36.refs_3_, ...), custom_call_target="tpu_custom_call" | custom-call | tf_op jit(solution)/shard_map/control/pallas_call | solution.py:529
  20.3 2.7 %collective-permute-start.5 = (f32[12,128]{1,0:T(8,128)S(1)}, f32[12,128]{1,0:T(8,128)S(1)}, u32[]{:S(2)}, u32[]{:S(2)}) collective-permute-start(f32[12,128]{1,0:T(8,128)S(1)} %control.1.refs_0_), channel_id=1, source_target_pairs={{0,1},{1,0},{2,3},{3,2},{4,5},{5,4},{6,7},{7,6},{8,9},{9,8},{10,11... | collective-permute-start | bytes 18440 | tf_op jit(solution)/shard_map/ppermute | solution.py:378
  23.1 0.6 %collective-permute-start.6 = (f32[12,128]{1,0:T(8,128)S(1)}, f32[12,128]{1,0:T(8,128)S(1)}, u32[]{:S(2)}, u32[]{:S(2)}) collective-permute-start(f32[12,128]{1,0:T(8,128)S(1)} %control.1.refs_0_), channel_id=1, source_target_pairs={{0,2},{1,3},{2,0},{3,1},{4,6},{5,7},{6,4},{7,5},{8,10},{9,11},{10,... | collective-permute-start | bytes 18440 | tf_op jit(solution)/shard_map/ppermute | solution.py:378
  23.6 0.8 %collective-permute-start.7 = (f32[12,128]{1,0:T(8,128)S(1)}, f32[12,128]{1,0:T(8,128)S(1)}, u32[]{:S(2)}, u32[]{:S(2)}) collective-permute-start(f32[12,128]{1,0:T(8,128)S(1)} %control.1.refs_0_), channel_id=1, source_target_pairs={{0,3},{1,2},{2,1},{3,0},{4,7},{5,6},{6,5},{7,4},{8,11},{9,10},{10,... | collective-permute-start | bytes 18440 | tf_op jit(solution)/shard_map/ppermute | solution.py:378
  24.5 0.0 collective-permute-done.5.refs_1_
  24.5 2.3 %collective-permute-done.6.refs_2_ = f32[12,128]{1,0:T(8,128)S(1)} collective-permute-done((f32[12,128]{1,0:T(8,128)S(1)}, f32[12,128]{1,0:T(8,128)S(1)}, u32[]{:S(2)}, u32[]{:S(2)}) %collective-permute-start.6) | collective-permute-done | bytes 6176 | tf_op jit(solution)/shard_map/ppermute | solution.py:378
  26.8 0.0 collective-permute-done.7.refs_3_
  26.8 3.1 %collective-permute-start.10 = (f32[12,128]{1,0:T(8,128)S(1)}, f32[12,128]{1,0:T(8,128)S(1)}, u32[]{:S(2)}, u32[]{:S(2)}) collective-permute-start(f32[12,128]{1,0:T(8,128)S(1)} %add.1.refs_0_), channel_id=1, source_target_pairs={{0,12},{4,8},{8,4},{12,0},{1,13},{5,9},{9,5},{13,1},{2,14},{6,10},... | collective-permute-start | bytes 18440 | tf_op jit(solution)/shard_map/ppermute | solution.py:378
  30.0 0.0 collective-permute-start.8
  30.0 1.3 %collective-permute-start.9 = (f32[12,128]{1,0:T(8,128)S(1)}, f32[12,128]{1,0:T(8,128)S(1)}, u32[]{:S(2)}, u32[]{:S(2)}) collective-permute-start(f32[12,128]{1,0:T(8,128)S(1)} %add.1.refs_0_), channel_id=1, source_target_pairs={{0,8},{4,12},{8,0},{12,4},{1,9},{5,13},{9,1},{13,5},{2,10},{6,14},... | collective-permute-start | bytes 18440 | tf_op jit(solution)/shard_map/ppermute | solution.py:378
  31.3 1.1 %collective-permute-done.10.refs_3_ = f32[12,128]{1,0:T(8,128)S(1)} collective-permute-done((f32[12,128]{1,0:T(8,128)S(1)}, f32[12,128]{1,0:T(8,128)S(1)}, u32[]{:S(2)}, u32[]{:S(2)}) %collective-permute-start.10) | collective-permute-done | bytes 6176 | tf_op jit(solution)/shard_map/ppermute | solution.py:378
  32.3 1.3 %collective-permute-done.8.refs_1_ = f32[12,128]{1,0:T(8,128)S(1)} collective-permute-done((f32[12,128]{1,0:T(8,128)S(1)}, f32[12,128]{1,0:T(8,128)S(1)}, u32[]{:S(2)}, u32[]{:S(2)}) %collective-permute-start.8) | collective-permute-done | bytes 6176 | tf_op jit(solution)/shard_map/ppermute | solution.py:378
  33.6 0.9 %collective-permute-done.9.refs_2_ = f32[12,128]{1,0:T(8,128)S(1)} collective-permute-done((f32[12,128]{1,0:T(8,128)S(1)}, f32[12,128]{1,0:T(8,128)S(1)}, u32[]{:S(2)}, u32[]{:S(2)}) %collective-permute-start.9) | collective-permute-done | bytes 6176 | tf_op jit(solution)/shard_map/ppermute | solution.py:378
  34.5 0.6 %finish.1 = f32[3,512]{1,0:T(4,128)} custom-call(f32[12,128]{1,0:T(8,128)S(1)} %add.1.refs_0_, f32[12,128]{1,0:T(8,128)S(1)} %collective-permute-done.8.refs_1_, f32[12,128]{1,0:T(8,128)S(1)} %collective-permute-done.9.refs_2_, f32[12,128]{1,0:T(8,128)S(1)} %collective-permute-done.10.refs_3_), custom_call_target="tpu_custom_call" | custom-call | tf_op jit(solution)/shard_map/finish/pallas_call | solution.py:540
  (1 shorter events, 0.0 us)
Async XLA Ops:
  0.6 4.1 %collective-permute-start = (f32[80,128]{1,0:T(8,128)}, f32[80,128]{1,0:T(8,128)S(1)}, u32[]{:S(2)}, u32[]{:S(2)}) collective-permute-start(f32[80,128]{1,0:T(8,128)} %bitcast.38), channel_id=1, source_target_pairs={{0,1},{1,0},{4,5},{5,4},{8,9},{9,8},{12,13},{13,12},{2,3},{3,2},{6... | collective-permute-start | bytes 122888 | tf_op jit(solution)/shard_map/ppermute | solution.py:416
  1.2 3.6 %collective-permute-start.1 = (f32[80,128]{1,0:T(8,128)}, f32[80,128]{1,0:T(8,128)S(1)}, u32[]{:S(2)}, u32[]{:S(2)}) collective-permute-start(f32[80,128]{1,0:T(8,128)} %bitcast.39), channel_id=1, source_target_pairs={{0,0},{1,4},{4,1},{5,8},{8,5},{9,12},{12,9},{13,13},{2,2},{3,6},{6... | collective-permute-start | bytes 122888 | tf_op jit(solution)/shard_map/ppermute | solution.py:415
  6.1 6.8 %collective-permute-start.2 = (f32[80,128]{1,0:T(8,128)S(1)}, f32[80,128]{1,0:T(8,128)S(1)}, u32[]{:S(2)}, u32[]{:S(2)}) collective-permute-start(f32[80,128]{1,0:T(8,128)S(1)} %sweep.1._.refs_2_), channel_id=1, source_target_pairs={{0,1},{1,0},{4,5},{5,4},{8,9},{9,8},{12,13},{13,12},{2,3},{3,2},{6... | collective-permute-start | bytes 122888 | tf_op jit(solution)/shard_map/ppermute | solution.py:416
  9.4 3.6 %collective-permute-start.3 = (f32[80,128]{1,0:T(8,128)S(1)}, f32[80,128]{1,0:T(8,128)S(1)}, u32[]{:S(2)}, u32[]{:S(2)}) collective-permute-start(f32[80,128]{1,0:T(8,128)S(1)} %sweep.1._.refs_2_), channel_id=1, source_target_pairs={{0,0},{1,4},{4,1},{5,8},{8,5},{9,12},{12,9},{13,13},{2,2},{3,6},{6... | collective-permute-start | bytes 122888 | tf_op jit(solution)/shard_map/ppermute | solution.py:415
  14.3 4.0 %collective-permute-start.4 = (f32[24,128]{1,0:T(8,128)S(1)}, f32[24,128]{1,0:T(8,128)S(1)}, u32[]{:S(2)}, u32[]{:S(2)}) collective-permute-start(f32[24,128]{1,0:T(8,128)S(1)} %get-tuple-element.32.after.refs_0_), channel_id=1, source_target_pairs={{0,2},{2,0},{1,3},{3,1},{4,6},{6,4},{5,7},{7,5},{8,10},{10,8},{9,1... | collective-permute-start | bytes 36872 | tf_op jit(solution)/shard_map/ppermute | solution.py:515
  20.3 4.1 %collective-permute-start.5 = (f32[12,128]{1,0:T(8,128)S(1)}, f32[12,128]{1,0:T(8,128)S(1)}, u32[]{:S(2)}, u32[]{:S(2)}) collective-permute-start(f32[12,128]{1,0:T(8,128)S(1)} %control.1.refs_0_), channel_id=1, source_target_pairs={{0,1},{1,0},{2,3},{3,2},{4,5},{5,4},{6,7},{7,6},{8,9},{9,8},{10,11... | collective-permute-start | bytes 18440 | tf_op jit(solution)/shard_map/ppermute | solution.py:378
  23.1 3.7 %collective-permute-start.6 = (f32[12,128]{1,0:T(8,128)S(1)}, f32[12,128]{1,0:T(8,128)S(1)}, u32[]{:S(2)}, u32[]{:S(2)}) collective-permute-start(f32[12,128]{1,0:T(8,128)S(1)} %control.1.refs_0_), channel_id=1, source_target_pairs={{0,2},{1,3},{2,0},{3,1},{4,6},{5,7},{6,4},{7,5},{8,10},{9,11},{10,... | collective-permute-start | bytes 18440 | tf_op jit(solution)/shard_map/ppermute | solution.py:378
  23.6 3.2 %collective-permute-start.7 = (f32[12,128]{1,0:T(8,128)S(1)}, f32[12,128]{1,0:T(8,128)S(1)}, u32[]{:S(2)}, u32[]{:S(2)}) collective-permute-start(f32[12,128]{1,0:T(8,128)S(1)} %control.1.refs_0_), channel_id=1, source_target_pairs={{0,3},{1,2},{2,1},{3,0},{4,7},{5,6},{6,5},{7,4},{8,11},{9,10},{10,... | collective-permute-start | bytes 18440 | tf_op jit(solution)/shard_map/ppermute | solution.py:378
  26.8 5.5 %collective-permute-start.10 = (f32[12,128]{1,0:T(8,128)S(1)}, f32[12,128]{1,0:T(8,128)S(1)}, u32[]{:S(2)}, u32[]{:S(2)}) collective-permute-start(f32[12,128]{1,0:T(8,128)S(1)} %add.1.refs_0_), channel_id=1, source_target_pairs={{0,12},{4,8},{8,4},{12,0},{1,13},{5,9},{9,5},{13,1},{2,14},{6,10},... | collective-permute-start | bytes 18440 | tf_op jit(solution)/shard_map/ppermute | solution.py:378
  30.0 3.7 %collective-permute-start.8 = (f32[12,128]{1,0:T(8,128)S(1)}, f32[12,128]{1,0:T(8,128)S(1)}, u32[]{:S(2)}, u32[]{:S(2)}) collective-permute-start(f32[12,128]{1,0:T(8,128)S(1)} %add.1.refs_0_), channel_id=1, source_target_pairs={{0,4},{4,0},{8,12},{12,8},{1,5},{5,1},{9,13},{13,9},{2,6},{6,2},{1... | collective-permute-start | bytes 18440 | tf_op jit(solution)/shard_map/ppermute | solution.py:378
  30.0 4.5 %collective-permute-start.9 = (f32[12,128]{1,0:T(8,128)S(1)}, f32[12,128]{1,0:T(8,128)S(1)}, u32[]{:S(2)}, u32[]{:S(2)}) collective-permute-start(f32[12,128]{1,0:T(8,128)S(1)} %add.1.refs_0_), channel_id=1, source_target_pairs={{0,8},{4,12},{8,0},{12,4},{1,9},{5,13},{9,1},{13,5},{2,10},{6,14},... | collective-permute-start | bytes 18440 | tf_op jit(solution)/shard_map/ppermute | solution.py:378

commit v9 on v8

--- a/solution.py
+++ b/solution.py
@@ -13,6 +13,7 @@
 SUPPORT_RADIUS = 0.3
 LANES = 128
 CELL_AXES = ("cells", "sub")
+SUM_AXES = ("cells", "nodes", "sub")
 FACTOR_ROWS = 64
 PARAMS = pltpu.CompilerParams(vmem_limit_bytes=24 * 1024 * 1024)
 VMEM = pl.BlockSpec(memory_space=pltpu.VMEM)
@@ -267,8 +268,8 @@
     return jnp.concatenate(blocks, axis=0)
 
 
-def wendland_kernel(first_cell, left_ref, right_ref, _, first_ref, rest_ref):
-    cells, owned = first_ref.shape
+def wendland_kernel(first_cell, left_ref, right_ref, _, kernel_ref):
+    cells, owned = kernel_ref.shape[0] // 2, kernel_ref.shape[1]
     tile, wide = min(64, cells), min(256, owned)
     for row in range(0, cells, tile):
         left = left_ref[first_cell + row : first_cell + row + tile, :]
@@ -280,61 +281,60 @@
             power = near * near
             kernel = power * power * (1.25 - near)
             first = kernel.astype(jnp.bfloat16)
-            first_ref[row : row + tile, here] = first
-            rest_ref[row : row + tile, here] = (kernel - first.astype(jnp.float32)).astype(
-                jnp.bfloat16
-            )
+            rest = (kernel - first.astype(jnp.float32)).astype(jnp.bfloat16)
+            kernel_ref[row : row + tile, here] = first
+            kernel_ref[cells + row : cells + row + tile, here] = rest
 
 
 def far_wendland_kernel(
     first_cell, left_ref, right_ref, after, adjoint_ref, low_ref, *rest
 ):
-    first_ref, rest_ref, one_hot_ref, result_ref, sem = rest
+    kernel_ref, one_hot_ref, result_ref, sem = rest
     copy = pltpu.make_async_copy(adjoint_ref, result_ref, sem)
     copy.start()
     owned = low_ref.shape[1]
     write_one_hot(low_ref, one_hot_ref, low_ref.shape[0] - one_hot_ref.shape[0] // owned)
-    wendland_kernel(first_cell, left_ref, right_ref, after, first_ref, rest_ref)
+    wendland_kernel(first_cell, left_ref, right_ref, after, kernel_ref)
     copy.wait()
 
 
 def control_kernel(scale, *refs):
-    *sens_refs, near_first, near_rest, far_first, far_rest = refs[:-4]
+    *sens_refs, near_ref, far_ref = refs[:-4]
     spread_ref, near_hot, far_hot, out_ref = refs[-4:]
     blocks = sens_refs[0].shape[0] // 3
-    cells = blocks * LANES
-    half = near_first.shape[0]
+    half = near_ref.shape[0] // 2
     groups = FFD // LANES
     total = sens_refs[0][...]
     for ref in sens_refs[1:]:
         total = total + ref[...]
     total = total * scale
-    row = lax.broadcasted_iota(jnp.int32, (16, LANES), 0)
-    wide = []
-    for block in range(blocks):
-        sens = jnp.zeros((16, LANES), jnp.float32)
-        for k in range(3):
-            mine = jnp.logical_and(row >= k * groups, row < (k + 1) * groups)
-            sens = jnp.where(mine, total[k * blocks + block : k * blocks + block + 1], sens)
-        wide.append(sens)
-    sens = jnp.concatenate(wide, axis=1)
 
     def halves(value):
         first = value.astype(jnp.bfloat16)
         rest = (value - first.astype(jnp.float32)).astype(jnp.bfloat16)
-        return jnp.concatenate([first, rest], axis=0)
-
-    sens = halves(sens)
+        return first, rest
+
+    row = lax.broadcasted_iota(jnp.int32, (8, LANES), 0)
+    wide = []
+    for block in range(blocks):
+        sens = jnp.zeros((8, LANES), jnp.float32)
+        for k in range(3):
+            sens = jnp.where(row == k, total[k * blocks + block : k * blocks + block + 1], sens)
+        first = sens.astype(jnp.bfloat16).astype(jnp.float32)
+        wide.append(jnp.concatenate([first, sens - first], axis=0))
+    sens = jnp.concatenate(wide, axis=1).astype(jnp.bfloat16)
     grad = None
-    for part, ref in (
-        (sens[:, :half], near_first),
-        (sens[:, :half], near_rest),
-        (sens[:, half:], far_first),
-        (sens[:, half:], far_rest),
-    ):
-        term = jnp.dot(part, ref[...], preferred_element_type=jnp.float32)
+    for part, ref in ((sens[:, :half], near_ref), (sens[:, half:], far_ref)):
+        both = jnp.concatenate([part, part], axis=1)
+        term = jnp.dot(both, ref[...], preferred_element_type=jnp.float32)
         grad = term if grad is None else grad + term
-    grad = grad[:16] + grad[16:]
+    grad = grad[:8] + grad[8:]
+    row = lax.broadcasted_iota(jnp.int32, (16, grad.shape[1]), 0)
+    wide = jnp.zeros(row.shape, jnp.float32)
+    for k in range(3):
+        mine = jnp.logical_and(row >= k * groups, row < (k + 1) * groups)
+        wide = jnp.where(mine, grad[k : k + 1], wide)
+    grad = wide
     owned = grad.shape[1]
     result = None
     places = [
@@ -342,7 +342,7 @@
     ]
     for j, (ref, first) in enumerate(places):
         term = jnp.dot(
-            halves(grad * spread_ref[j * 16 : (j + 1) * 16, :]),
+            jnp.concatenate(halves(grad * spread_ref[j * 16 : (j + 1) * 16, :]), axis=0),
             ref[first : first + owned, :],
             preferred_element_type=jnp.float32,
         )
@@ -361,8 +361,9 @@
     refs[-1][...] = tree([ref[...] for ref in refs[:-1]])
 
 
-def finish_kernel(*refs):
-    total, out_ref = tree([ref[...] for ref in refs[:-1]]), refs[-1]
+def finish_kernel(own_ref, other_ref, out_ref):
+    last = lax.axis_size("sub") - 1
+    total = jnp.where(lax.axis_index("sub") == last, own_ref[...], other_ref[...])
     groups = out_ref.shape[1] // LANES
     for k in range(3):
         for group in range(groups):
@@ -370,14 +371,40 @@
             out_ref[k : k + 1, group * LANES : (group + 1) * LANES] = total[row : row + 1]
 
 
-def exchanged(value, axes):
-    peers = lax.axis_size(axes)
-    if peers > 8 or peers & (peers - 1):
-        return [lax.psum(value, axes)]
-    return [value] + [
-        lax.ppermute(value, axes, [(i, i ^ shift) for i in range(peers)])
-        for shift in range(1, peers)
+def add(*arrays):
+    shape = jax.ShapeDtypeStruct(arrays[0].shape, arrays[0].dtype)
+    return pl.pallas_call(add_kernel, out_shape=shape, name="add", compiler_params=PARAMS)(*arrays)
+
+
+def sum_on_last_cores(value):
+    cores = lax.axis_size("sub")
+    received = [
+        lax.ppermute(value, "sub", [(i, (i + shift) % cores) for i in range(cores)])
+        for shift in range(1, cores)
     ]
+    value = add(value, *received)
+    for axis, other, major in (("nodes", "cells", False), ("cells", "nodes", True)):
+        peers, others = lax.axis_size(axis), lax.axis_size(other)
+
+        def swap(array, shift):
+            pairs = []
+            for mine in range(peers):
+                for beside in range(others):
+                    ends = [
+                        at * others + beside if major else beside * peers + at
+                        for at in (mine, mine ^ shift)
+                    ]
+                    pairs.append(tuple(end * cores + cores - 1 for end in ends))
+            return lax.ppermute(array, SUM_AXES, pairs)
+
+        if peers <= 4:
+            value = add(value, *[swap(value, shift) for shift in range(1, peers)])
+        else:
+            shift = 1
+            while shift < peers:
+                value = add(value, swap(value, shift))
+                shift *= 2
+    return value
 
 
 def body(
@@ -487,12 +514,13 @@
 
     half = cells * 5 // 8 // LANES * LANES
     wendland_cost = cost(10**9, 10**7)
-    near_shape, far_shape = shape((half, owned), bf16), shape((cells - half, owned), bf16)
-    near_first, near_rest = pl.pallas_call(
+    near_shape = shape((2 * half, owned), bf16)
+    far_shape = shape((2 * (cells - half), owned), bf16)
+    near_kernel = pl.pallas_call(
         functools.partial(wendland_kernel, 0),
-        out_shape=(near_shape, near_shape),
+        out_shape=near_shape,
         in_specs=[VMEM] * 3,
-        out_specs=(VMEM, VMEM),
+        out_specs=VMEM,
         compiler_params=PARAMS,
         cost_estimate=wendland_cost,
         name="near_wendland",
@@ -506,7 +534,7 @@
         compiler_params=PARAMS,
         cost_estimate=sweep_cost,
         name="last_sweep",
-    )(close, far, adjoint, rhs, off, inverse, lane, step, sens, near_first)
+    )(close, far, adjoint, rhs, off, inverse, lane, step, sens, near_kernel)
 
     all_sens = [part_sens]
     node_peers = lax.axis_size("nodes")
@@ -514,11 +542,11 @@
         ring = [(i, (i + shift) % node_peers) for i in range(node_peers)]
         all_sens.append(lax.ppermute(part_sens, "nodes", ring))
     hot_shape = shape(((slots - slots // 2) * owned, LANES), bf16)
-    far_first, far_rest, far_hot, adjoint = pl.pallas_call(
+    far_kernel, far_hot, adjoint = pl.pallas_call(
         functools.partial(far_wendland_kernel, half),
-        out_shape=(far_shape, far_shape, hot_shape, shape((5 * per, LANES))),
+        out_shape=(far_shape, hot_shape, shape((5 * per, LANES))),
         in_specs=[VMEM] * 5,
-        out_specs=(VMEM, VMEM, VMEM, HBM),
+        out_specs=(VMEM, VMEM, HBM),
         scratch_shapes=[pltpu.SemaphoreType.DMA],
         compiler_params=PARAMS,
         cost_estimate=wendland_cost,
@@ -529,17 +557,16 @@
     partial = pl.pallas_call(
         functools.partial(control_kernel, scale),
         out_shape=shape((rows, LANES)),
-        in_specs=[VMEM] * (len(all_sens) + 7),
+        in_specs=[VMEM] * (len(all_sens) + 5),
         out_specs=VMEM,
         compiler_params=PARAMS,
         name="control",
-    )(*all_sens, near_first, near_rest, far_first, far_rest, spread, near_hot, far_hot)
-    partial = pl.pallas_call(
-        add_kernel, out_shape=shape((rows, LANES)), name="add", compiler_params=PARAMS
-    )(*exchanged(partial, ("nodes", "sub")))
+    )(*all_sens, near_kernel, far_kernel, spread, near_hot, far_hot)
+    total = sum_on_last_cores(partial)
+    last = lax.axis_size("sub") - 1
     control_grad = pl.pallas_call(
         finish_kernel, out_shape=shape((3, FFD)), name="finish", compiler_params=PARAMS
-    )(*exchanged(partial, "cells"))
+    )(total, lax.ppermute(total, "sub", [(last, i) for i in range(1)]))
     return (from_rows(adjoint, nodes, cells), control_grad)
 
 

time: 35.3 us -> 43.6 us (1.24)
  waiting for transfers between devices: 5.57 us -> 15.9 us
  starting transfers between devices: 16.2 us -> 14.2 us
    ppermute x6, waiting for transfers between devices: 5.55 us -> 15.9 us  [the longest x1 15.1 us: body(): lax.ppermute(total, 'sub', [(last, i) for i in range(1)])]
    ppermute x6, starting transfers between devices: 8.6 us -> 6.65 us  [the longest x1 2.72 us: sum_on_last_cores(): lax.ppermute(value, 'sub', [(i, (i + shift) % cores) for i in range(cores)])]
    pallas_call x2 -> x4, Pallas kernels: 2.91 us -> 2.92 us  [the longest x1 2.9 us: body(): pl.pallas_call(functools.partial(wendland_kernel, 0), out_shape=near_shap...]
  transfers between devices with their start and end apart: 11 -> 11, of which waited for: 4 -> 2; matrix products, arithmetic and copies ran while one was open for 0% -> 0% of each run, Pallas kernels for 21% -> 17%
where the time goes in v9:
time: 43.6 us; the launch traced here: 43.3 us
  waiting for transfers between devices  15.9 us (36%)
  starting transfers between devices  14.2 us (33%)
  Pallas kernels  12.3 us (28%)
  between operations  0.81 us (2%)
    ppermute x1, waiting for transfers between devices, body(): lax.ppermute(total, 'sub', [(last, i) for i in range(1)])  15.1 us
    ppermute x2, starting transfers between devices, swaps(): close = lax.ppermute(array, CELL_AXES, first)  3.78 us
    pallas_call x1, Pallas kernels, body(): pl.pallas_call(functools.partial(wendland_kernel, 0), out_shape=near_shap...  2.9 us
    ppermute x1, starting transfers between devices, sum_on_last_cores(): lax.ppermute(value, 'sub', [(i, (i + shift) % cores) for i in range(cores)])  2.72 us
    ppermute x4, starting transfers between devices, swap(): return lax.ppermute(array, SUM_AXES, pairs)  2.63 us
    pallas_call x1, Pallas kernels, body(): pl.pallas_call(functools.partial(far_wendland_kernel, half), out_shape=(f...  2.22 us
    pallas_call x1, Pallas kernels, body(): pl.pallas_call(functools.partial(prepare_kernel, nodes), out_shape=(shape...  2.18 us
    ppermute x2, starting transfers between devices, swaps(): far = lax.ppermute(array, CELL_AXES, second)  2.08 us
  transfers between devices with their start and end apart: 11, of which 2 were waited for; matrix products, arithmetic and copies ran while one was open for 0% of the time, Pallas kernels for 17%

profile of v9, /device:TPU:0, one launch (start us, length us, event | category | flops | bytes accessed | tf_op | source)
XLA Modules:
  0.0 43.3 jit_solution(12955209258368791369)
XLA Ops:
  0.6 0.5 %collective-permute-start = (f32[80,128]{1,0:T(8,128)}, f32[80,128]{1,0:T(8,128)S(1)}, u32[]{:S(2)}, u32[]{:S(2)}) collective-permute-start(f32[80,128]{1,0:T(8,128)} %bitcast.38), channel_id=1, source_target_pairs={{0,1},{1,0},{4,5},{5,4},{8,9},{9,8},{12,13},{13,12},{2,3},{3,2},{6... | collective-permute-start | bytes 122888 | tf_op jit(solution)/shard_map/ppermute | solution.py:443
  1.2 1.4 %collective-permute-start.1 = (f32[80,128]{1,0:T(8,128)}, f32[80,128]{1,0:T(8,128)S(1)}, u32[]{:S(2)}, u32[]{:S(2)}) collective-permute-start(f32[80,128]{1,0:T(8,128)} %bitcast.39), channel_id=1, source_target_pairs={{0,0},{1,4},{4,1},{5,8},{8,5},{9,12},{12,9},{13,13},{2,2},{3,6},{6... | collective-permute-start | bytes 122888 | tf_op jit(solution)/shard_map/ppermute | solution.py:442
  2.6 2.2 %prepare.1 = (f32[2400,128]{1,0:T(8,128)S(1)}, f32[400,128]{1,0:T(8,128)S(1)}, f32[80,128]{1,0:T(8,128)S(1)}, f32[240,128]{1,0:T(8,128)S(1)}, s32[96,128]{1,0:T(...) custom-call(bf16[2400,128]{1,0:T(8,128)(2,1)} %bitcast.32, ...), custom_call_target="tpu_custom_call" | custom-call | flops 1000000000 | bytes 10000000 | tf_op jit(solution)/shard_map/prepare/pallas_call | solution.py:448
  4.8 0.0 collective-permute-done.refs_0_
  4.8 0.0 collective-permute-done.1.refs_1_
  4.8 1.2 %sweep.1._.refs_2_ = f32[80,128]{1,0:T(8,128)S(1)} custom-call(f32[80,128]{1,0:T(8,128)S(1)} %collective-permute-done.refs_0_, f32[80,128]{1,0:T(8,128)S(1)} %collective-permute-done.1.refs_1_, f32[80,128]{1,0:T(8,128)S(1)} %get-tuple-element.21.refs_2_, f32[80,128]{1,0:T(8,128)S(1)} %get-tuple-element.22.refs_3_, ...), custom_call_target="tpu_custom_call" | custom-call | flops 716800 | bytes 1228800 | tf_op jit(solution)/shard_map/sweep/pallas_call | solution.py:503
  6.0 3.3 %collective-permute-start.2 = (f32[80,128]{1,0:T(8,128)S(1)}, f32[80,128]{1,0:T(8,128)S(1)}, u32[]{:S(2)}, u32[]{:S(2)}) collective-permute-start(f32[80,128]{1,0:T(8,128)S(1)} %sweep.1._.refs_2_), channel_id=1, source_target_pairs={{0,1},{1,0},{4,5},{5,4},{8,9},{9,8},{12,13},{13,12},{2,3},{3,2},{6... | collective-permute-start | bytes 122888 | tf_op jit(solution)/shard_map/ppermute | solution.py:443
  9.3 0.7 %collective-permute-start.3 = (f32[80,128]{1,0:T(8,128)S(1)}, f32[80,128]{1,0:T(8,128)S(1)}, u32[]{:S(2)}, u32[]{:S(2)}) collective-permute-start(f32[80,128]{1,0:T(8,128)S(1)} %sweep.1._.refs_2_), channel_id=1, source_target_pairs={{0,0},{1,4},{4,1},{5,8},{8,5},{9,12},{12,9},{13,13},{2,2},{3,6},{6... | collective-permute-start | bytes 122888 | tf_op jit(solution)/shard_map/ppermute | solution.py:442
  10.0 2.9 %near_wendland.1.refs_9_.refs_2_ = bf16[1280,2048]{1,0:T(8,128)(2,1)S(1)} custom-call(bf16[1024,64]{1,0:T(8,128)(2,1)S(1)} %get-tuple-element.19.left_ref, bf16[64,2048]{1,0:T(8,128)(2,1)S(1)} %get-tuple-element.20.right_ref, f32[80,128]{1,0:T(8,128)S(1)} %sweep.1._.refs_2_), custom_call_target="tpu_custom_call" | custom-call | flops 1000000000 | bytes 10000000 | tf_op jit(solution)/shard_map/near_wendland/pallas_call | solution.py:519
  12.9 0.0 collective-permute-done.2.refs_0_
  12.9 0.0 collective-permute-done.3.refs_1_
  12.9 1.3 %last_sweep.1 = (f32[80,128]{1,0:T(8,128)S(1)}, f32[24,128]{1,0:T(8,128)S(1)}) custom-call(f32[80,128]{1,0:T(8,128)S(1)} %collective-permute-done.2.refs_0_, f32[80,128]{1,0:T(8,128)S(1)} %collective-permute-done.3.refs_1_, f32[80,128]{1,0:T(8,128)S(1)} %sweep.1._.refs_2_, f32[80,128]{1,0:T(8,128)S(1)} %get-tuple-element.22.refs_3_, ...), custom_call_target="tpu_custom_call" | custom-call | flops 716800 | bytes 1228800 | tf_op jit(solution)/shard_map/last_sweep/pallas_call | solution.py:528
  14.2 1.7 %collective-permute-start.4 = (f32[24,128]{1,0:T(8,128)S(1)}, f32[24,128]{1,0:T(8,128)S(1)}, u32[]{:S(2)}, u32[]{:S(2)}) collective-permute-start(f32[24,128]{1,0:T(8,128)S(1)} %get-tuple-element.28.after.refs_0_), channel_id=1, source_target_pairs={{0,2},{2,0},{1,3},{3,1},{4,6},{6,4},{5,7},{7,5},{8,10},{10,8},{9,1... | collective-permute-start | bytes 36872 | tf_op jit(solution)/shard_map/ppermute | solution.py:543
  15.9 2.2 %far_wendland.1 = (bf16[768,2048]{1,0:T(8,128)(2,1)S(1)}, bf16[8192,128]{1,0:T(8,128)(2,1)S(1)}, f32[80,128]{1,0:T(8,128)}) custom-call(bf16[1024,64]{1,0:T(8,128)(2,1)S(1)} %get-tuple-element.19.left_ref, bf16[64,2048]{1,0:T(8,128)(2,1)S(1)} %get-tuple-element.20.right_ref, f32[24,128]{1,0:T(8,128)S(1)} %get-tuple-element.28.after.refs_0_, ...), custom_call_target="tpu_custom_call" | custom-call | flops 1000000000 | bytes 10000000 | tf_op jit(solution)/shard_map/far_wendland/pallas_call | solution.py:545
  18.1 0.0 collective-permute-done.4.refs_1_
  18.1 1.8 %control.1.refs_0_ = f32[12,128]{1,0:T(8,128)S(1)} custom-call(f32[24,128]{1,0:T(8,128)S(1)} %get-tuple-element.28.after.refs_0_, f32[24,128]{1,0:T(8,128)S(1)} %collective-permute-done.4.refs_1_, bf16[1280,2048]{1,0:T(8,128)(2,1)S(1)} %near_wendland.1.refs_9_.refs_2_, bf16[768,2048]{1,0:T(8,128)(2,1)S(1)} %get-tuple-element.32.refs_3_, ...), custom_call_target="tpu_custom_call" | custom-call | tf_op jit(solution)/shard_map/control/pallas_call | solution.py:557
  20.0 2.7 %collective-permute-start.5 = (f32[12,128]{1,0:T(8,128)S(1)}, f32[12,128]{1,0:T(8,128)S(1)}, u32[]{:S(2)}, u32[]{:S(2)}) collective-permute-start(f32[12,128]{1,0:T(8,128)S(1)} %control.1.refs_0_), channel_id=1, source_target_pairs={{0,1},{1,0},{2,3},{3,2},{4,5},{5,4},{6,7},{7,6},{8,9},{9,8},{10,11... | collective-permute-start | bytes 18440 | tf_op jit(solution)/shard_map/ppermute | solution.py:382
  22.7 0.8 %collective-permute-done.5.refs_1_ = f32[12,128]{1,0:T(8,128)S(1)} collective-permute-done((f32[12,128]{1,0:T(8,128)S(1)}, f32[12,128]{1,0:T(8,128)S(1)}, u32[]{:S(2)}, u32[]{:S(2)}) %collective-permute-start.5) | collective-permute-done | bytes 6176 | tf_op jit(solution)/shard_map/ppermute | solution.py:382
  23.5 0.6 %collective-permute-start.6 = (f32[12,128]{1,0:T(8,128)S(1)}, f32[12,128]{1,0:T(8,128)S(1)}, u32[]{:S(2)}, u32[]{:S(2)}) collective-permute-start(f32[12,128]{1,0:T(8,128)S(1)} %add.3.refs_0_), channel_id=1, source_target_pairs={{1,3},{5,7},{9,11},{13,15},{3,1},{7,5},{11,9},{15,13},{17,19},{21,... | collective-permute-start | bytes 18440 | tf_op jit(solution)/shard_map/ppermute | solution.py:398
  24.2 0.0 collective-permute-done.6.refs_1_
  24.2 0.7 %collective-permute-start.7 = (f32[12,128]{1,0:T(8,128)S(1)}, f32[12,128]{1,0:T(8,128)S(1)}, u32[]{:S(2)}, u32[]{:S(2)}) collective-permute-start(f32[12,128]{1,0:T(8,128)S(1)} %add.4.refs_0_), channel_id=1, source_target_pairs={{1,5},{3,7},{5,1},{7,3},{9,13},{11,15},{13,9},{15,11},{17,21},{19,... | collective-permute-start | bytes 18440 | tf_op jit(solution)/shard_map/ppermute | solution.py:398
  24.9 0.7 %collective-permute-start.8 = (f32[12,128]{1,0:T(8,128)S(1)}, f32[12,128]{1,0:T(8,128)S(1)}, u32[]{:S(2)}, u32[]{:S(2)}) collective-permute-start(f32[12,128]{1,0:T(8,128)S(1)} %add.4.refs_0_), channel_id=1, source_target_pairs={{1,9},{3,11},{5,13},{7,15},{9,1},{11,3},{13,5},{15,7},{17,25},{19,... | collective-permute-start | bytes 18440 | tf_op jit(solution)/shard_map/ppermute | solution.py:398
  25.5 0.7 %collective-permute-start.9 = (f32[12,128]{1,0:T(8,128)S(1)}, f32[12,128]{1,0:T(8,128)S(1)}, u32[]{:S(2)}, u32[]{:S(2)}) collective-permute-start(f32[12,128]{1,0:T(8,128)S(1)} %add.4.refs_0_), channel_id=1, source_target_pairs={{1,13},{3,15},{5,9},{7,11},{9,5},{11,7},{13,1},{15,3},{17,29},{19,... | collective-permute-start | bytes 18440 | tf_op jit(solution)/shard_map/ppermute | solution.py:398
  26.2 0.0 collective-permute-done.7.refs_1_
  26.2 0.0 collective-permute-done.8.refs_2_
  26.2 0.0 collective-permute-done.9.refs_3_
  26.3 1.3 %collective-permute-start.10 = (f32[12,128]{1,0:T(8,128)S(1)}, f32[12,128]{1,0:T(8,128)S(1)}, u32[]{:S(2)}, u32[]{:S(2)}) collective-permute-start(f32[12,128]{1,0:T(8,128)S(1)} %add.5.own_ref), channel_id=1, source_target_pairs={{1,0},{3,2},{5,4},{7,6},{9,8},{11,10},{13,12},{15,14},{17,16},{19,... | collective-permute-start | bytes 18440 | tf_op jit(solution)/shard_map/ppermute | solution.py:569
  27.6 15.1 %collective-permute-done.10.other_ref = f32[12,128]{1,0:T(8,128)S(1)} collective-permute-done((f32[12,128]{1,0:T(8,128)S(1)}, f32[12,128]{1,0:T(8,128)S(1)}, u32[]{:S(2)}, u32[]{:S(2)}) %collective-permute-start.10) | collective-permute-done | bytes 6176 | tf_op jit(solution)/shard_map/ppermute | solution.py:569
  42.6 0.6 %finish.1 = f32[3,512]{1,0:T(4,128)} custom-call(f32[12,128]{1,0:T(8,128)S(1)} %add.5.own_ref, f32[12,128]{1,0:T(8,128)S(1)} %collective-permute-done.10.other_ref), custom_call_target="tpu_custom_call" | custom-call | tf_op jit(solution)/shard_map/finish/pallas_call | solution.py:567
  (3 shorter events, 0.0 us)
Async XLA Ops:
  0.6 4.1 %collective-permute-start = (f32[80,128]{1,0:T(8,128)}, f32[80,128]{1,0:T(8,128)S(1)}, u32[]{:S(2)}, u32[]{:S(2)}) collective-permute-start(f32[80,128]{1,0:T(8,128)} %bitcast.38), channel_id=1, source_target_pairs={{0,1},{1,0},{4,5},{5,4},{8,9},{9,8},{12,13},{13,12},{2,3},{3,2},{6... | collective-permute-start | bytes 122888 | tf_op jit(solution)/shard_map/ppermute | solution.py:443
  1.2 3.6 %collective-permute-start.1 = (f32[80,128]{1,0:T(8,128)}, f32[80,128]{1,0:T(8,128)S(1)}, u32[]{:S(2)}, u32[]{:S(2)}) collective-permute-start(f32[80,128]{1,0:T(8,128)} %bitcast.39), channel_id=1, source_target_pairs={{0,0},{1,4},{4,1},{5,8},{8,5},{9,12},{12,9},{13,13},{2,2},{3,6},{6... | collective-permute-start | bytes 122888 | tf_op jit(solution)/shard_map/ppermute | solution.py:442
  6.0 6.8 %collective-permute-start.2 = (f32[80,128]{1,0:T(8,128)S(1)}, f32[80,128]{1,0:T(8,128)S(1)}, u32[]{:S(2)}, u32[]{:S(2)}) collective-permute-start(f32[80,128]{1,0:T(8,128)S(1)} %sweep.1._.refs_2_), channel_id=1, source_target_pairs={{0,1},{1,0},{4,5},{5,4},{8,9},{9,8},{12,13},{13,12},{2,3},{3,2},{6... | collective-permute-start | bytes 122888 | tf_op jit(solution)/shard_map/ppermute | solution.py:443
  9.3 3.6 %collective-permute-start.3 = (f32[80,128]{1,0:T(8,128)S(1)}, f32[80,128]{1,0:T(8,128)S(1)}, u32[]{:S(2)}, u32[]{:S(2)}) collective-permute-start(f32[80,128]{1,0:T(8,128)S(1)} %sweep.1._.refs_2_), channel_id=1, source_target_pairs={{0,0},{1,4},{4,1},{5,8},{8,5},{9,12},{12,9},{13,13},{2,2},{3,6},{6... | collective-permute-start | bytes 122888 | tf_op jit(solution)/shard_map/ppermute | solution.py:442
  14.2 4.0 %collective-permute-start.4 = (f32[24,128]{1,0:T(8,128)S(1)}, f32[24,128]{1,0:T(8,128)S(1)}, u32[]{:S(2)}, u32[]{:S(2)}) collective-permute-start(f32[24,128]{1,0:T(8,128)S(1)} %get-tuple-element.28.after.refs_0_), channel_id=1, source_target_pairs={{0,2},{2,0},{1,3},{3,1},{4,6},{6,4},{5,7},{7,5},{8,10},{10,8},{9,1... | collective-permute-start | bytes 36872 | tf_op jit(solution)/shard_map/ppermute | solution.py:543
  20.0 3.6 %collective-permute-start.5 = (f32[12,128]{1,0:T(8,128)S(1)}, f32[12,128]{1,0:T(8,128)S(1)}, u32[]{:S(2)}, u32[]{:S(2)}) collective-permute-start(f32[12,128]{1,0:T(8,128)S(1)} %control.1.refs_0_), channel_id=1, source_target_pairs={{0,1},{1,0},{2,3},{3,2},{4,5},{5,4},{6,7},{7,6},{8,9},{9,8},{10,11... | collective-permute-start | bytes 18440 | tf_op jit(solution)/shard_map/ppermute | solution.py:382
  23.5 0.7 %collective-permute-start.6 = (f32[12,128]{1,0:T(8,128)S(1)}, f32[12,128]{1,0:T(8,128)S(1)}, u32[]{:S(2)}, u32[]{:S(2)}) collective-permute-start(f32[12,128]{1,0:T(8,128)S(1)} %add.3.refs_0_), channel_id=1, source_target_pairs={{1,3},{5,7},{9,11},{13,15},{3,1},{7,5},{11,9},{15,13},{17,19},{21,... | collective-permute-start | bytes 18440 | tf_op jit(solution)/shard_map/ppermute | solution.py:398
  24.2 2.0 %collective-permute-start.7 = (f32[12,128]{1,0:T(8,128)S(1)}, f32[12,128]{1,0:T(8,128)S(1)}, u32[]{:S(2)}, u32[]{:S(2)}) collective-permute-start(f32[12,128]{1,0:T(8,128)S(1)} %add.4.refs_0_), channel_id=1, source_target_pairs={{1,5},{3,7},{5,1},{7,3},{9,13},{11,15},{13,9},{15,11},{17,21},{19,... | collective-permute-start | bytes 18440 | tf_op jit(solution)/shard_map/ppermute | solution.py:398
  24.9 1.4 %collective-permute-start.8 = (f32[12,128]{1,0:T(8,128)S(1)}, f32[12,128]{1,0:T(8,128)S(1)}, u32[]{:S(2)}, u32[]{:S(2)}) collective-permute-start(f32[12,128]{1,0:T(8,128)S(1)} %add.4.refs_0_), channel_id=1, source_target_pairs={{1,9},{3,11},{5,13},{7,15},{9,1},{11,3},{13,5},{15,7},{17,25},{19,... | collective-permute-start | bytes 18440 | tf_op jit(solution)/shard_map/ppermute | solution.py:398
  25.5 0.7 %collective-permute-start.9 = (f32[12,128]{1,0:T(8,128)S(1)}, f32[12,128]{1,0:T(8,128)S(1)}, u32[]{:S(2)}, u32[]{:S(2)}) collective-permute-start(f32[12,128]{1,0:T(8,128)S(1)} %add.4.refs_0_), channel_id=1, source_target_pairs={{1,13},{3,15},{5,9},{7,11},{9,5},{11,7},{13,1},{15,3},{17,29},{19,... | collective-permute-start | bytes 18440 | tf_op jit(solution)/shard_map/ppermute | solution.py:398
  26.3 16.4 %collective-permute-start.10 = (f32[12,128]{1,0:T(8,128)S(1)}, f32[12,128]{1,0:T(8,128)S(1)}, u32[]{:S(2)}, u32[]{:S(2)}) collective-permute-start(f32[12,128]{1,0:T(8,128)S(1)} %add.5.own_ref), channel_id=1, source_target_pairs={{1,0},{3,2},{5,4},{7,6},{9,8},{11,10},{13,12},{15,14},{17,16},{19,... | collective-permute-start | bytes 18440 | tf_op jit(solution)/shard_map/ppermute | solution.py:569

commit v10 on v9

--- a/solution.py
+++ b/solution.py
@@ -361,9 +361,8 @@
     refs[-1][...] = tree([ref[...] for ref in refs[:-1]])
 
 
-def finish_kernel(own_ref, other_ref, out_ref):
-    last = lax.axis_size("sub") - 1
-    total = jnp.where(lax.axis_index("sub") == last, own_ref[...], other_ref[...])
+def finish_kernel(*refs):
+    total, out_ref = tree([ref[...] for ref in refs[:-1]]), refs[-1]
     groups = out_ref.shape[1] // LANES
     for k in range(3):
         for group in range(groups):
@@ -371,40 +370,14 @@
             out_ref[k : k + 1, group * LANES : (group + 1) * LANES] = total[row : row + 1]
 
 
-def add(*arrays):
-    shape = jax.ShapeDtypeStruct(arrays[0].shape, arrays[0].dtype)
-    return pl.pallas_call(add_kernel, out_shape=shape, name="add", compiler_params=PARAMS)(*arrays)
-
-
-def sum_on_last_cores(value):
-    cores = lax.axis_size("sub")
-    received = [
-        lax.ppermute(value, "sub", [(i, (i + shift) % cores) for i in range(cores)])
-        for shift in range(1, cores)
+def exchanged(value, axes):
+    peers = lax.axis_size(axes)
+    if peers > 8 or peers & (peers - 1):
+        return [lax.psum(value, axes)]
+    return [value] + [
+        lax.ppermute(value, axes, [(i, i ^ shift) for i in range(peers)])
+        for shift in range(1, peers)
     ]
-    value = add(value, *received)
-    for axis, other, major in (("nodes", "cells", False), ("cells", "nodes", True)):
-        peers, others = lax.axis_size(axis), lax.axis_size(other)
-
-        def swap(array, shift):
-            pairs = []
-            for mine in range(peers):
-                for beside in range(others):
-                    ends = [
-                        at * others + beside if major else beside * peers + at
-                        for at in (mine, mine ^ shift)
-                    ]
-                    pairs.append(tuple(end * cores + cores - 1 for end in ends))
-            return lax.ppermute(array, SUM_AXES, pairs)
-
-        if peers <= 4:
-            value = add(value, *[swap(value, shift) for shift in range(1, peers)])
-        else:
-            shift = 1
-            while shift < peers:
-                value = add(value, swap(value, shift))
-                shift *= 2
-    return value
 
 
 def body(
@@ -427,6 +400,8 @@
     slots = ffd_index.shape[1]
     owned = base_points.shape[1] // lax.axis_size("nodes")
     peers = lax.axis_size(CELL_AXES)
+    cores = lax.axis_size("sub")
+    node_peers = lax.axis_size("nodes")
     f32, i32, bf16 = jnp.float32, jnp.int32, jnp.bfloat16
 
     def shape(dims, dtype=f32):
@@ -436,12 +411,22 @@
         return pl.CostEstimate(flops=flops, bytes_accessed=moved, transcendentals=0)
 
     def swaps(array):
-        first = [(i, i ^ 1) for i in range(peers)]
-        second = [(i, i + 1 if i % 2 else i - 1) for i in range(peers)]
-        second = [(i, j if 0 <= j < peers else i) for i, j in second]
-        far = lax.ppermute(array, CELL_AXES, second)
-        close = lax.ppermute(array, CELL_AXES, first)
-        return far, close
+        close = lax.ppermute(array, CELL_AXES, [(i, i ^ 1) for i in range(peers)])
+        pairs = []
+        for i in range(peers):
+            line, core = divmod(i, cores)
+            for node in range(node_peers):
+                j, beside = (i + 1 if i % 2 else i - 1), node
+                if not 0 <= j < peers:
+                    j, beside = i, (node ^ 1 if node_peers % 2 == 0 else node)
+                to_line, to_core = divmod(j, cores)
+                pairs.append(
+                    (
+                        (line * node_peers + node) * cores + core,
+                        (to_line * node_peers + beside) * cores + to_core,
+                    )
+                )
+        return lax.ppermute(array, SUM_AXES, pairs), close
 
     adjoint = rows_of(adjoint_start)
     far, close = swaps(adjoint)
@@ -537,7 +522,6 @@
     )(close, far, adjoint, rhs, off, inverse, lane, step, sens, near_kernel)
 
     all_sens = [part_sens]
-    node_peers = lax.axis_size("nodes")
     for shift in range(1, node_peers):
         ring = [(i, (i + shift) % node_peers) for i in range(node_peers)]
         all_sens.append(lax.ppermute(part_sens, "nodes", ring))
@@ -562,11 +546,12 @@
         compiler_params=PARAMS,
         name="control",
     )(*all_sens, near_kernel, far_kernel, spread, near_hot, far_hot)
-    total = sum_on_last_cores(partial)
-    last = lax.axis_size("sub") - 1
+    partial = pl.pallas_call(
+        add_kernel, out_shape=shape((rows, LANES)), name="add", compiler_params=PARAMS
+    )(*exchanged(partial, ("nodes", "sub")))
     control_grad = pl.pallas_call(
         finish_kernel, out_shape=shape((3, FFD)), name="finish", compiler_params=PARAMS
-    )(total, lax.ppermute(total, "sub", [(last, i) for i in range(1)]))
+    )(*exchanged(partial, "cells"))
     return (from_rows(adjoint, nodes, cells), control_grad)
 
 

time: 43.6 us -> 31.2 us (0.72)
  waiting for transfers between devices: 15.9 us -> 5.36 us
  starting transfers between devices: 14.2 us -> 12.7 us
    ppermute x10, waiting for transfers between devices: 15.9 us -> 4.97 us  [the longest x6 4.96 us: exchanged(): lax.ppermute(value, axes, [(i, i ^ shift) for i in range(peers)])]
    ppermute x10, starting transfers between devices: 12.5 us -> 11.6 us  [the longest x6 6.32 us: exchanged(): lax.ppermute(value, axes, [(i, i ^ shift) for i in range(peers)])]
    ppermute x1, starting transfers between devices: 1.72 us -> 1.14 us  [body(): all_sens.append(lax.ppermute(part_sens, 'nodes', ring))]
  transfers between devices with their start and end apart: 11 -> 11, of which waited for: 2 -> 6; matrix products, arithmetic and copies ran while one was open for 0% -> 0% of each run, Pallas kernels for 17% -> 23%
where the time goes in v10:
time: 31.2 us; the launch traced here: 31.1 us
  starting transfers between devices  12.7 us (41%)
  Pallas kernels  12.3 us (39%)
  waiting for transfers between devices  5.36 us (17%)
  between operations  0.72 us (2%)
    ppermute x6, starting transfers between devices, exchanged(): lax.ppermute(value, axes, [(i, i ^ shift) for i in range(peers)])  6.32 us
    ppermute x6, waiting for transfers between devices, exchanged(): lax.ppermute(value, axes, [(i, i ^ shift) for i in range(peers)])  4.96 us
    ppermute x2, starting transfers between devices, swaps(): return (lax.ppermute(array, SUM_AXES, pairs), close)  4.47 us
    pallas_call x1, Pallas kernels, body(): pl.pallas_call(functools.partial(wendland_kernel, 0), out_shape=near_shap...  2.9 us
    pallas_call x1, Pallas kernels, body(): pl.pallas_call(functools.partial(far_wendland_kernel, half), out_shape=(f...  2.21 us
    pallas_call x1, Pallas kernels, body(): pl.pallas_call(functools.partial(prepare_kernel, nodes), out_shape=(shape...  2.18 us
    pallas_call x1, Pallas kernels, body(): pl.pallas_call(functools.partial(control_kernel, scale), out_shape=shape(...  1.84 us
    pallas_call x1, Pallas kernels, body(): pl.pallas_call(functools.partial(last_sweep_kernel, blocks), out_shape=(s...  1.26 us
  transfers between devices with their start and end apart: 11, of which 6 were waited for; matrix products, arithmetic and copies ran while one was open for 0% of the time, Pallas kernels for 23%

profile of v10, /device:TPU:0, one launch (start us, length us, event | category | flops | bytes accessed | tf_op | source)
XLA Modules:
  0.0 31.1 jit_solution(5020998162433020796)
XLA Ops:
  0.6 0.5 %collective-permute-start = (f32[80,128]{1,0:T(8,128)}, f32[80,128]{1,0:T(8,128)S(1)}, u32[]{:S(2)}, u32[]{:S(2)}) collective-permute-start(f32[80,128]{1,0:T(8,128)} %bitcast.38), channel_id=1, source_target_pairs={{0,1},{1,0},{4,5},{5,4},{8,9},{9,8},{12,13},{13,12},{2,3},{3,2},{6... | collective-permute-start | bytes 122888 | tf_op jit(solution)/shard_map/ppermute | solution.py:414
  1.2 2.6 %collective-permute-start.1 = (f32[80,128]{1,0:T(8,128)}, f32[80,128]{1,0:T(8,128)S(1)}, u32[]{:S(2)}, u32[]{:S(2)}) collective-permute-start(f32[80,128]{1,0:T(8,128)} %bitcast.39), channel_id=1, source_target_pairs={{0,2},{2,0},{1,4},{3,6},{4,1},{6,3},{5,8},{7,10},{8,5},{10,7},{9,1... | collective-permute-start | bytes 122888 | tf_op jit(solution)/shard_map/ppermute | solution.py:429
  3.7 2.2 %prepare.1 = (f32[2400,128]{1,0:T(8,128)S(1)}, f32[400,128]{1,0:T(8,128)S(1)}, f32[80,128]{1,0:T(8,128)S(1)}, f32[240,128]{1,0:T(8,128)S(1)}, s32[96,128]{1,0:T(...) custom-call(bf16[2400,128]{1,0:T(8,128)(2,1)} %bitcast.32, ...), custom_call_target="tpu_custom_call" | custom-call | flops 1000000000 | bytes 10000000 | tf_op jit(solution)/shard_map/prepare/pallas_call | solution.py:433
  5.9 0.0 collective-permute-done.refs_0_
  5.9 0.0 collective-permute-done.1.refs_1_
  5.9 1.2 %sweep.1._.refs_2_ = f32[80,128]{1,0:T(8,128)S(1)} custom-call(f32[80,128]{1,0:T(8,128)S(1)} %collective-permute-done.refs_0_, f32[80,128]{1,0:T(8,128)S(1)} %collective-permute-done.1.refs_1_, f32[80,128]{1,0:T(8,128)S(1)} %get-tuple-element.21.refs_2_, f32[80,128]{1,0:T(8,128)S(1)} %get-tuple-element.22.refs_3_, ...), custom_call_target="tpu_custom_call" | custom-call | flops 716800 | bytes 1228800 | tf_op jit(solution)/shard_map/sweep/pallas_call | solution.py:488
  7.2 0.3 collective-permute-start.2
  7.4 1.9 %collective-permute-start.3 = (f32[80,128]{1,0:T(8,128)S(1)}, f32[80,128]{1,0:T(8,128)S(1)}, u32[]{:S(2)}, u32[]{:S(2)}) collective-permute-start(f32[80,128]{1,0:T(8,128)S(1)} %sweep.1._.refs_2_), channel_id=1, source_target_pairs={{0,2},{2,0},{1,4},{3,6},{4,1},{6,3},{5,8},{7,10},{8,5},{10,7},{9,1... | collective-permute-start | bytes 122888 | tf_op jit(solution)/shard_map/ppermute | solution.py:429
  9.3 2.9 %near_wendland.1.refs_9_.refs_2_ = bf16[1280,2048]{1,0:T(8,128)(2,1)S(1)} custom-call(bf16[1024,64]{1,0:T(8,128)(2,1)S(1)} %get-tuple-element.19.left_ref, bf16[64,2048]{1,0:T(8,128)(2,1)S(1)} %get-tuple-element.20.right_ref, f32[80,128]{1,0:T(8,128)S(1)} %sweep.1._.refs_2_), custom_call_target="tpu_custom_call" | custom-call | flops 1000000000 | bytes 10000000 | tf_op jit(solution)/shard_map/near_wendland/pallas_call | solution.py:504
  12.2 0.0 collective-permute-done.2.refs_0_
  12.3 0.0 collective-permute-done.3.refs_1_
  12.3 1.3 %last_sweep.1 = (f32[80,128]{1,0:T(8,128)S(1)}, f32[24,128]{1,0:T(8,128)S(1)}) custom-call(f32[80,128]{1,0:T(8,128)S(1)} %collective-permute-done.2.refs_0_, f32[80,128]{1,0:T(8,128)S(1)} %collective-permute-done.3.refs_1_, f32[80,128]{1,0:T(8,128)S(1)} %sweep.1._.refs_2_, f32[80,128]{1,0:T(8,128)S(1)} %get-tuple-element.22.refs_3_, ...), custom_call_target="tpu_custom_call" | custom-call | flops 716800 | bytes 1228800 | tf_op jit(solution)/shard_map/last_sweep/pallas_call | solution.py:513
  13.5 1.1 %collective-permute-start.4 = (f32[24,128]{1,0:T(8,128)S(1)}, f32[24,128]{1,0:T(8,128)S(1)}, u32[]{:S(2)}, u32[]{:S(2)}) collective-permute-start(f32[24,128]{1,0:T(8,128)S(1)} %get-tuple-element.28.after.refs_0_), channel_id=1, source_target_pairs={{0,2},{2,0},{1,3},{3,1},{4,6},{6,4},{5,7},{7,5},{8,10},{10,8},{9,1... | collective-permute-start | bytes 36872 | tf_op jit(solution)/shard_map/ppermute | solution.py:527
  14.7 2.2 %far_wendland.1 = (bf16[768,2048]{1,0:T(8,128)(2,1)S(1)}, bf16[8192,128]{1,0:T(8,128)(2,1)S(1)}, f32[80,128]{1,0:T(8,128)}) custom-call(bf16[1024,64]{1,0:T(8,128)(2,1)S(1)} %get-tuple-element.19.left_ref, bf16[64,2048]{1,0:T(8,128)(2,1)S(1)} %get-tuple-element.20.right_ref, f32[24,128]{1,0:T(8,128)S(1)} %get-tuple-element.28.after.refs_0_, ...), custom_call_target="tpu_custom_call" | custom-call | flops 1000000000 | bytes 10000000 | tf_op jit(solution)/shard_map/far_wendland/pallas_call | solution.py:529
  16.9 0.4 %collective-permute-done.4.refs_1_ = f32[24,128]{1,0:T(8,128)S(1)} collective-permute-done((f32[24,128]{1,0:T(8,128)S(1)}, f32[24,128]{1,0:T(8,128)S(1)}, u32[]{:S(2)}, u32[]{:S(2)}) %collective-permute-start.4) | collective-permute-done | bytes 12320 | tf_op jit(solution)/shard_map/ppermute | solution.py:527
  17.3 1.8 %control.1.refs_0_ = f32[12,128]{1,0:T(8,128)S(1)} custom-call(f32[24,128]{1,0:T(8,128)S(1)} %get-tuple-element.28.after.refs_0_, f32[24,128]{1,0:T(8,128)S(1)} %collective-permute-done.4.refs_1_, bf16[1280,2048]{1,0:T(8,128)(2,1)S(1)} %near_wendland.1.refs_9_.refs_2_, bf16[768,2048]{1,0:T(8,128)(2,1)S(1)} %get-tuple-element.32.refs_3_, ...), custom_call_target="tpu_custom_call" | custom-call | tf_op jit(solution)/shard_map/control/pallas_call | solution.py:541
  19.1 0.1 collective-permute-start.5
  19.2 1.1 %collective-permute-start.6 = (f32[12,128]{1,0:T(8,128)S(1)}, f32[12,128]{1,0:T(8,128)S(1)}, u32[]{:S(2)}, u32[]{:S(2)}) collective-permute-start(f32[12,128]{1,0:T(8,128)S(1)} %control.1.refs_0_), channel_id=1, source_target_pairs={{0,2},{1,3},{2,0},{3,1},{4,6},{5,7},{6,4},{7,5},{8,10},{9,11},{10,... | collective-permute-start | bytes 18440 | tf_op jit(solution)/shard_map/ppermute | solution.py:378
  20.4 0.7 %collective-permute-start.7 = (f32[12,128]{1,0:T(8,128)S(1)}, f32[12,128]{1,0:T(8,128)S(1)}, u32[]{:S(2)}, u32[]{:S(2)}) collective-permute-start(f32[12,128]{1,0:T(8,128)S(1)} %control.1.refs_0_), channel_id=1, source_target_pairs={{0,3},{1,2},{2,1},{3,0},{4,7},{5,6},{6,5},{7,4},{8,11},{9,10},{10,... | collective-permute-start | bytes 18440 | tf_op jit(solution)/shard_map/ppermute | solution.py:378
  21.1 0.0 collective-permute-done.5.refs_1_
  21.1 1.9 %collective-permute-done.6.refs_2_ = f32[12,128]{1,0:T(8,128)S(1)} collective-permute-done((f32[12,128]{1,0:T(8,128)S(1)}, f32[12,128]{1,0:T(8,128)S(1)}, u32[]{:S(2)}, u32[]{:S(2)}) %collective-permute-start.6) | collective-permute-done | bytes 6176 | tf_op jit(solution)/shard_map/ppermute | solution.py:378
  22.9 0.5 %collective-permute-done.7.refs_3_ = f32[12,128]{1,0:T(8,128)S(1)} collective-permute-done((f32[12,128]{1,0:T(8,128)S(1)}, f32[12,128]{1,0:T(8,128)S(1)}, u32[]{:S(2)}, u32[]{:S(2)}) %collective-permute-start.7) | collective-permute-done | bytes 6176 | tf_op jit(solution)/shard_map/ppermute | solution.py:378
  23.5 2.4 %collective-permute-start.10 = (f32[12,128]{1,0:T(8,128)S(1)}, f32[12,128]{1,0:T(8,128)S(1)}, u32[]{:S(2)}, u32[]{:S(2)}) collective-permute-start(f32[12,128]{1,0:T(8,128)S(1)} %add.1.refs_0_), channel_id=1, source_target_pairs={{0,12},{4,8},{8,4},{12,0},{1,13},{5,9},{9,5},{13,1},{2,14},{6,10},... | collective-permute-start | bytes 18440 | tf_op jit(solution)/shard_map/ppermute | solution.py:378
  25.9 0.0 collective-permute-start.8
  25.9 1.9 %collective-permute-start.9 = (f32[12,128]{1,0:T(8,128)S(1)}, f32[12,128]{1,0:T(8,128)S(1)}, u32[]{:S(2)}, u32[]{:S(2)}) collective-permute-start(f32[12,128]{1,0:T(8,128)S(1)} %add.1.refs_0_), channel_id=1, source_target_pairs={{0,8},{4,12},{8,0},{12,4},{1,9},{5,13},{9,1},{13,5},{2,10},{6,14},... | collective-permute-start | bytes 18440 | tf_op jit(solution)/shard_map/ppermute | solution.py:378
  27.8 1.1 %collective-permute-done.10.refs_3_ = f32[12,128]{1,0:T(8,128)S(1)} collective-permute-done((f32[12,128]{1,0:T(8,128)S(1)}, f32[12,128]{1,0:T(8,128)S(1)}, u32[]{:S(2)}, u32[]{:S(2)}) %collective-permute-start.10) | collective-permute-done | bytes 6176 | tf_op jit(solution)/shard_map/ppermute | solution.py:378
  28.9 0.6 %collective-permute-done.8.refs_1_ = f32[12,128]{1,0:T(8,128)S(1)} collective-permute-done((f32[12,128]{1,0:T(8,128)S(1)}, f32[12,128]{1,0:T(8,128)S(1)}, u32[]{:S(2)}, u32[]{:S(2)}) %collective-permute-start.8) | collective-permute-done | bytes 6176 | tf_op jit(solution)/shard_map/ppermute | solution.py:378
  29.5 0.9 %collective-permute-done.9.refs_2_ = f32[12,128]{1,0:T(8,128)S(1)} collective-permute-done((f32[12,128]{1,0:T(8,128)S(1)}, f32[12,128]{1,0:T(8,128)S(1)}, u32[]{:S(2)}, u32[]{:S(2)}) %collective-permute-start.9) | collective-permute-done | bytes 6176 | tf_op jit(solution)/shard_map/ppermute | solution.py:378
  30.4 0.6 %finish.1 = f32[3,512]{1,0:T(4,128)} custom-call(f32[12,128]{1,0:T(8,128)S(1)} %add.1.refs_0_, f32[12,128]{1,0:T(8,128)S(1)} %collective-permute-done.8.refs_1_, f32[12,128]{1,0:T(8,128)S(1)} %collective-permute-done.9.refs_2_, f32[12,128]{1,0:T(8,128)S(1)} %collective-permute-done.10.refs_3_), custom_call_target="tpu_custom_call" | custom-call | tf_op jit(solution)/shard_map/finish/pallas_call | solution.py:552
  (1 shorter events, 0.0 us)
Async XLA Ops:
  0.6 5.3 %collective-permute-start = (f32[80,128]{1,0:T(8,128)}, f32[80,128]{1,0:T(8,128)S(1)}, u32[]{:S(2)}, u32[]{:S(2)}) collective-permute-start(f32[80,128]{1,0:T(8,128)} %bitcast.38), channel_id=1, source_target_pairs={{0,1},{1,0},{4,5},{5,4},{8,9},{9,8},{12,13},{13,12},{2,3},{3,2},{6... | collective-permute-start | bytes 122888 | tf_op jit(solution)/shard_map/ppermute | solution.py:414
  1.2 4.8 %collective-permute-start.1 = (f32[80,128]{1,0:T(8,128)}, f32[80,128]{1,0:T(8,128)S(1)}, u32[]{:S(2)}, u32[]{:S(2)}) collective-permute-start(f32[80,128]{1,0:T(8,128)} %bitcast.39), channel_id=1, source_target_pairs={{0,2},{2,0},{1,4},{3,6},{4,1},{6,3},{5,8},{7,10},{8,5},{10,7},{9,1... | collective-permute-start | bytes 122888 | tf_op jit(solution)/shard_map/ppermute | solution.py:429
  7.2 5.1 %collective-permute-start.2 = (f32[80,128]{1,0:T(8,128)S(1)}, f32[80,128]{1,0:T(8,128)S(1)}, u32[]{:S(2)}, u32[]{:S(2)}) collective-permute-start(f32[80,128]{1,0:T(8,128)S(1)} %sweep.1._.refs_2_), channel_id=1, source_target_pairs={{0,1},{1,0},{4,5},{5,4},{8,9},{9,8},{12,13},{13,12},{2,3},{3,2},{6... | collective-permute-start | bytes 122888 | tf_op jit(solution)/shard_map/ppermute | solution.py:414
  7.4 4.8 %collective-permute-start.3 = (f32[80,128]{1,0:T(8,128)S(1)}, f32[80,128]{1,0:T(8,128)S(1)}, u32[]{:S(2)}, u32[]{:S(2)}) collective-permute-start(f32[80,128]{1,0:T(8,128)S(1)} %sweep.1._.refs_2_), channel_id=1, source_target_pairs={{0,2},{2,0},{1,4},{3,6},{4,1},{6,3},{5,8},{7,10},{8,5},{10,7},{9,1... | collective-permute-start | bytes 122888 | tf_op jit(solution)/shard_map/ppermute | solution.py:429
  13.5 3.8 %collective-permute-start.4 = (f32[24,128]{1,0:T(8,128)S(1)}, f32[24,128]{1,0:T(8,128)S(1)}, u32[]{:S(2)}, u32[]{:S(2)}) collective-permute-start(f32[24,128]{1,0:T(8,128)S(1)} %get-tuple-element.28.after.refs_0_), channel_id=1, source_target_pairs={{0,2},{2,0},{1,3},{3,1},{4,6},{6,4},{5,7},{7,5},{8,10},{10,8},{9,1... | collective-permute-start | bytes 36872 | tf_op jit(solution)/shard_map/ppermute | solution.py:527
  19.1 1.9 %collective-permute-start.5 = (f32[12,128]{1,0:T(8,128)S(1)}, f32[12,128]{1,0:T(8,128)S(1)}, u32[]{:S(2)}, u32[]{:S(2)}) collective-permute-start(f32[12,128]{1,0:T(8,128)S(1)} %control.1.refs_0_), channel_id=1, source_target_pairs={{0,1},{1,0},{2,3},{3,2},{4,5},{5,4},{6,7},{7,6},{8,9},{9,8},{10,11... | collective-permute-start | bytes 18440 | tf_op jit(solution)/shard_map/ppermute | solution.py:378
  19.2 3.7 %collective-permute-start.6 = (f32[12,128]{1,0:T(8,128)S(1)}, f32[12,128]{1,0:T(8,128)S(1)}, u32[]{:S(2)}, u32[]{:S(2)}) collective-permute-start(f32[12,128]{1,0:T(8,128)S(1)} %control.1.refs_0_), channel_id=1, source_target_pairs={{0,2},{1,3},{2,0},{3,1},{4,6},{5,7},{6,4},{7,5},{8,10},{9,11},{10,... | collective-permute-start | bytes 18440 | tf_op jit(solution)/shard_map/ppermute | solution.py:378
  20.4 3.1 %collective-permute-start.7 = (f32[12,128]{1,0:T(8,128)S(1)}, f32[12,128]{1,0:T(8,128)S(1)}, u32[]{:S(2)}, u32[]{:S(2)}) collective-permute-start(f32[12,128]{1,0:T(8,128)S(1)} %control.1.refs_0_), channel_id=1, source_target_pairs={{0,3},{1,2},{2,1},{3,0},{4,7},{5,6},{6,5},{7,4},{8,11},{9,10},{10,... | collective-permute-start | bytes 18440 | tf_op jit(solution)/shard_map/ppermute | solution.py:378
  23.5 5.4 %collective-permute-start.10 = (f32[12,128]{1,0:T(8,128)S(1)}, f32[12,128]{1,0:T(8,128)S(1)}, u32[]{:S(2)}, u32[]{:S(2)}) collective-permute-start(f32[12,128]{1,0:T(8,128)S(1)} %add.1.refs_0_), channel_id=1, source_target_pairs={{0,12},{4,8},{8,4},{12,0},{1,13},{5,9},{9,5},{13,1},{2,14},{6,10},... | collective-permute-start | bytes 18440 | tf_op jit(solution)/shard_map/ppermute | solution.py:378
  25.9 3.7 %collective-permute-start.8 = (f32[12,128]{1,0:T(8,128)S(1)}, f32[12,128]{1,0:T(8,128)S(1)}, u32[]{:S(2)}, u32[]{:S(2)}) collective-permute-start(f32[12,128]{1,0:T(8,128)S(1)} %add.1.refs_0_), channel_id=1, source_target_pairs={{0,4},{4,0},{8,12},{12,8},{1,5},{5,1},{9,13},{13,9},{2,6},{6,2},{1... | collective-permute-start | bytes 18440 | tf_op jit(solution)/shard_map/ppermute | solution.py:378
  25.9 4.5 %collective-permute-start.9 = (f32[12,128]{1,0:T(8,128)S(1)}, f32[12,128]{1,0:T(8,128)S(1)}, u32[]{:S(2)}, u32[]{:S(2)}) collective-permute-start(f32[12,128]{1,0:T(8,128)S(1)} %add.1.refs_0_), channel_id=1, source_target_pairs={{0,8},{4,12},{8,0},{12,4},{1,9},{5,13},{9,1},{13,5},{2,10},{6,14},... | collective-permute-start | bytes 18440 | tf_op jit(solution)/shard_map/ppermute | solution.py:378

commit v11 on v10

--- a/solution.py
+++ b/solution.py
@@ -177,10 +177,10 @@
         window_ref[pl.ds(base + place, per), :] = first_ref[rows, :]
         window_ref[base + per : base + 2 * per, :] = own_ref[rows, :]
         window_ref[pl.ds(base + other, per), :] = second_ref[rows, :]
-    for shift in range(8 // nodes):
+    for shift in range(1, 8 // nodes):
         for b in range(5):
-            for tile in range(0, width - (8 if shift else 0), 8):
-                to = (shift * 5 + b) * width + tile
+            for tile in range(0, width - 8, 8):
+                to = ((shift - 1) * 5 + b) * width + tile
                 table_ref[to : to + 8, :] = window_ref[
                     pl.ds(b * width + tile + shift * nodes, 8), :
                 ]
@@ -194,9 +194,14 @@
                 here = dist == d
                 first = half + d * nodes
                 for b in range(5):
-                    at = ((first % 8) // nodes * 5 + b) * width + first // 8 * 8
+                    shift, at = first % 8 // nodes, b * width + first // 8 * 8
+                    if shift:
+                        at = at + (shift - 1) * 5 * width
+                        table = table_ref[at : at + 8, :]
+                    else:
+                        table = window_ref[at : at + 8, :]
                     got = jnp.take_along_axis(
-                        table_ref[at : at + 8, :], lanes, axis=1, mode="promise_in_bounds"
+                        table, lanes, axis=1, mode="promise_in_bounds"
                     )
                     beside[b] = jnp.where(here, got, beside[b])
             for a in range(5):
@@ -370,13 +375,27 @@
             out_ref[k : k + 1, group * LANES : (group + 1) * LANES] = total[row : row + 1]
 
 
-def exchanged(value, axes):
-    peers = lax.axis_size(axes)
-    if peers > 8 or peers & (peers - 1):
-        return [lax.psum(value, axes)]
+def sum_rounds():
+    lines, nodes, cores = (lax.axis_size(axis) for axis in SUM_AXES)
+    if any(size & (size - 1) for size in (lines, nodes, cores)):
+        return None
+    near = [cores >> 1 >> i for i in range(cores.bit_length() - 1)]
+    node_bits = [cores << i for i in range(nodes.bit_length() - 1)]
+    line_bits = [cores * nodes << i for i in range(lines.bit_length() - 1)]
+    bits = near + line_bits[:1] + node_bits[:1] + line_bits[1:] + node_bits[1:]
+    rounds = []
+    for first in range(0, len(bits), 2):
+        masks = bits[first : first + 2]
+        if len(masks) == 2:
+            masks = masks + [masks[0] | masks[1]]
+        rounds.append([mask | (cores - 1) for mask in masks] if first else masks)
+    return rounds
+
+
+def exchanged(value, masks):
+    peers = lax.axis_size(SUM_AXES)
     return [value] + [
-        lax.ppermute(value, axes, [(i, i ^ shift) for i in range(peers)])
-        for shift in range(1, peers)
+        lax.ppermute(value, SUM_AXES, [(i, i ^ mask) for i in range(peers)]) for mask in masks
     ]
 
 
@@ -480,7 +499,7 @@
     off, inverse, rhs, sens, lane, step, spread, low, near_hot, adjoint, left, right = prepared
     scratch = [
         pltpu.VMEM((3 * 5 * per, LANES), f32),
-        pltpu.VMEM((8 // nodes * 3 * 5 * per, LANES), f32),
+        pltpu.VMEM((max(8 // nodes - 1, 1) * 3 * 5 * per, LANES), f32),
     ]
     sweep_cost = cost(2 * 10 * 35 * cells, 4 * faces * 25 * per * LANES)
 
@@ -546,12 +565,17 @@
         compiler_params=PARAMS,
         name="control",
     )(*all_sens, near_kernel, far_kernel, spread, near_hot, far_hot)
-    partial = pl.pallas_call(
-        add_kernel, out_shape=shape((rows, LANES)), name="add", compiler_params=PARAMS
-    )(*exchanged(partial, ("nodes", "sub")))
+    rounds = sum_rounds()
+    terms = [partial] if rounds else [lax.psum(partial, SUM_AXES)]
+    for masks in rounds or ():
+        if len(terms) > 1:
+            partial = pl.pallas_call(
+                add_kernel, out_shape=shape((rows, LANES)), name="add", compiler_params=PARAMS
+            )(*terms)
+        terms = exchanged(partial, masks)
     control_grad = pl.pallas_call(
         finish_kernel, out_shape=shape((3, FFD)), name="finish", compiler_params=PARAMS
-    )(*exchanged(partial, "cells"))
+    )(*terms)
     return (from_rows(adjoint, nodes, cells), control_grad)
 
 

time: 31.2 us -> 31.2 us (level)
  starting transfers between devices: 12.7 us -> 12.1 us
  waiting for transfers between devices: 5.36 us -> 5.93 us
    ppermute x6, starting transfers between devices: 6.32 us -> 5.73 us  [exchanged(): lax.ppermute(value, SUM_AXES, [(i, i ^ mask) for i in range(peers)])]
    ppermute x6, waiting for transfers between devices: 4.96 us -> 5.53 us  [exchanged(): lax.ppermute(value, SUM_AXES, [(i, i ^ mask) for i in range(peers)])]
  transfers between devices with their start and end apart: 11 -> 11, of which waited for: 6 -> 6; matrix products, arithmetic and copies ran while one was open for 0% -> 0% of each run, Pallas kernels for 23% -> 24%
where the time goes in v11:
time: 31.2 us; the launch traced here: 31 us
  Pallas kernels  12.2 us (39%)
  starting transfers between devices  12.1 us (39%)
  waiting for transfers between devices  5.93 us (19%)
  between operations  0.72 us (2%)
    ppermute x6, starting transfers between devices, exchanged(): lax.ppermute(value, SUM_AXES, [(i, i ^ mask) for i in range(peers)])  5.73 us
    ppermute x6, waiting for transfers between devices, exchanged(): lax.ppermute(value, SUM_AXES, [(i, i ^ mask) for i in range(peers)])  5.53 us
    ppermute x2, starting transfers between devices, swaps(): return (lax.ppermute(array, SUM_AXES, pairs), close)  4.47 us
    pallas_call x1, Pallas kernels, body(): pl.pallas_call(functools.partial(wendland_kernel, 0), out_shape=near_shap...  2.9 us
    pallas_call x1, Pallas kernels, body(): pl.pallas_call(functools.partial(far_wendland_kernel, half), out_shape=(f...  2.22 us
    pallas_call x1, Pallas kernels, body(): pl.pallas_call(functools.partial(prepare_kernel, nodes), out_shape=(shape...  2.18 us
    pallas_call x1, Pallas kernels, body(): pl.pallas_call(functools.partial(control_kernel, scale), out_shape=shape(...  1.84 us
    pallas_call x1, Pallas kernels, body(): pl.pallas_call(functools.partial(last_sweep_kernel, blocks), out_shape=(s...  1.26 us
  transfers between devices with their start and end apart: 11, of which 6 were waited for; matrix products, arithmetic and copies ran while one was open for 0% of the time, Pallas kernels for 24%

profile of v11, /device:TPU:0, one launch (start us, length us, event | category | flops | bytes accessed | tf_op | source)
XLA Modules:
  0.0 31.0 jit_solution(605270354135159826)
XLA Ops:
  0.6 0.5 %collective-permute-start = (f32[80,128]{1,0:T(8,128)}, f32[80,128]{1,0:T(8,128)S(1)}, u32[]{:S(2)}, u32[]{:S(2)}) collective-permute-start(f32[80,128]{1,0:T(8,128)} %bitcast.38), channel_id=1, source_target_pairs={{0,1},{1,0},{4,5},{5,4},{8,9},{9,8},{12,13},{13,12},{2,3},{3,2},{6... | collective-permute-start | bytes 122888 | tf_op jit(solution)/shard_map/ppermute | solution.py:433
  1.2 2.6 %collective-permute-start.1 = (f32[80,128]{1,0:T(8,128)}, f32[80,128]{1,0:T(8,128)S(1)}, u32[]{:S(2)}, u32[]{:S(2)}) collective-permute-start(f32[80,128]{1,0:T(8,128)} %bitcast.39), channel_id=1, source_target_pairs={{0,2},{2,0},{1,4},{3,6},{4,1},{6,3},{5,8},{7,10},{8,5},{10,7},{9,1... | collective-permute-start | bytes 122888 | tf_op jit(solution)/shard_map/ppermute | solution.py:448
  3.7 2.2 %prepare.1 = (f32[2400,128]{1,0:T(8,128)S(1)}, f32[400,128]{1,0:T(8,128)S(1)}, f32[80,128]{1,0:T(8,128)S(1)}, f32[240,128]{1,0:T(8,128)S(1)}, s32[96,128]{1,0:T(...) custom-call(bf16[2400,128]{1,0:T(8,128)(2,1)} %bitcast.32, ...), custom_call_target="tpu_custom_call" | custom-call | flops 1000000000 | bytes 10000000 | tf_op jit(solution)/shard_map/prepare/pallas_call | solution.py:452
  5.9 0.0 collective-permute-done.refs_0_
  5.9 0.0 collective-permute-done.1.refs_1_
  5.9 1.2 %sweep.1._.refs_2_ = f32[80,128]{1,0:T(8,128)S(1)} custom-call(f32[80,128]{1,0:T(8,128)S(1)} %collective-permute-done.refs_0_, f32[80,128]{1,0:T(8,128)S(1)} %collective-permute-done.1.refs_1_, f32[80,128]{1,0:T(8,128)S(1)} %get-tuple-element.21.refs_2_, f32[80,128]{1,0:T(8,128)S(1)} %get-tuple-element.22.refs_3_, ...), custom_call_target="tpu_custom_call" | custom-call | flops 716800 | bytes 1228800 | tf_op jit(solution)/shard_map/sweep/pallas_call | solution.py:507
  7.2 0.3 collective-permute-start.2
  7.4 1.9 %collective-permute-start.3 = (f32[80,128]{1,0:T(8,128)S(1)}, f32[80,128]{1,0:T(8,128)S(1)}, u32[]{:S(2)}, u32[]{:S(2)}) collective-permute-start(f32[80,128]{1,0:T(8,128)S(1)} %sweep.1._.refs_2_), channel_id=1, source_target_pairs={{0,2},{2,0},{1,4},{3,6},{4,1},{6,3},{5,8},{7,10},{8,5},{10,7},{9,1... | collective-permute-start | bytes 122888 | tf_op jit(solution)/shard_map/ppermute | solution.py:448
  9.3 2.9 %near_wendland.1.refs_9_.refs_2_ = bf16[1280,2048]{1,0:T(8,128)(2,1)S(1)} custom-call(bf16[1024,64]{1,0:T(8,128)(2,1)S(1)} %get-tuple-element.19.left_ref, bf16[64,2048]{1,0:T(8,128)(2,1)S(1)} %get-tuple-element.20.right_ref, f32[80,128]{1,0:T(8,128)S(1)} %sweep.1._.refs_2_), custom_call_target="tpu_custom_call" | custom-call | flops 1000000000 | bytes 10000000 | tf_op jit(solution)/shard_map/near_wendland/pallas_call | solution.py:523
  12.2 0.0 collective-permute-done.2.refs_0_
  12.3 0.0 collective-permute-done.3.refs_1_
  12.3 1.3 %last_sweep.1 = (f32[80,128]{1,0:T(8,128)S(1)}, f32[24,128]{1,0:T(8,128)S(1)}) custom-call(f32[80,128]{1,0:T(8,128)S(1)} %collective-permute-done.2.refs_0_, f32[80,128]{1,0:T(8,128)S(1)} %collective-permute-done.3.refs_1_, f32[80,128]{1,0:T(8,128)S(1)} %sweep.1._.refs_2_, f32[80,128]{1,0:T(8,128)S(1)} %get-tuple-element.22.refs_3_, ...), custom_call_target="tpu_custom_call" | custom-call | flops 716800 | bytes 1228800 | tf_op jit(solution)/shard_map/last_sweep/pallas_call | solution.py:532
  13.5 1.1 %collective-permute-start.4 = (f32[24,128]{1,0:T(8,128)S(1)}, f32[24,128]{1,0:T(8,128)S(1)}, u32[]{:S(2)}, u32[]{:S(2)}) collective-permute-start(f32[24,128]{1,0:T(8,128)S(1)} %get-tuple-element.28.after.refs_0_), channel_id=1, source_target_pairs={{0,2},{2,0},{1,3},{3,1},{4,6},{6,4},{5,7},{7,5},{8,10},{10,8},{9,1... | collective-permute-start | bytes 36872 | tf_op jit(solution)/shard_map/ppermute | solution.py:546
  14.7 2.2 %far_wendland.1 = (bf16[768,2048]{1,0:T(8,128)(2,1)S(1)}, bf16[8192,128]{1,0:T(8,128)(2,1)S(1)}, f32[80,128]{1,0:T(8,128)}) custom-call(bf16[1024,64]{1,0:T(8,128)(2,1)S(1)} %get-tuple-element.19.left_ref, bf16[64,2048]{1,0:T(8,128)(2,1)S(1)} %get-tuple-element.20.right_ref, f32[24,128]{1,0:T(8,128)S(1)} %get-tuple-element.28.after.refs_0_, ...), custom_call_target="tpu_custom_call" | custom-call | flops 1000000000 | bytes 10000000 | tf_op jit(solution)/shard_map/far_wendland/pallas_call | solution.py:548
  16.9 0.4 %collective-permute-done.4.refs_1_ = f32[24,128]{1,0:T(8,128)S(1)} collective-permute-done((f32[24,128]{1,0:T(8,128)S(1)}, f32[24,128]{1,0:T(8,128)S(1)}, u32[]{:S(2)}, u32[]{:S(2)}) %collective-permute-start.4) | collective-permute-done | bytes 12320 | tf_op jit(solution)/shard_map/ppermute | solution.py:546
  17.3 1.8 %control.1.refs_0_ = f32[12,128]{1,0:T(8,128)S(1)} custom-call(f32[24,128]{1,0:T(8,128)S(1)} %get-tuple-element.28.after.refs_0_, f32[24,128]{1,0:T(8,128)S(1)} %collective-permute-done.4.refs_1_, bf16[1280,2048]{1,0:T(8,128)(2,1)S(1)} %near_wendland.1.refs_9_.refs_2_, bf16[768,2048]{1,0:T(8,128)(2,1)S(1)} %get-tuple-element.32.refs_3_, ...), custom_call_target="tpu_custom_call" | custom-call | tf_op jit(solution)/shard_map/control/pallas_call | solution.py:560
  19.1 0.1 collective-permute-start.5
  19.2 1.3 %collective-permute-start.6 = (f32[12,128]{1,0:T(8,128)S(1)}, f32[12,128]{1,0:T(8,128)S(1)}, u32[]{:S(2)}, u32[]{:S(2)}) collective-permute-start(f32[12,128]{1,0:T(8,128)S(1)} %control.1.refs_0_), channel_id=1, source_target_pairs={{0,4},{1,5},{2,6},{3,7},{4,0},{5,1},{6,2},{7,3},{8,12},{9,13},{10,... | collective-permute-start | bytes 18440 | tf_op jit(solution)/shard_map/ppermute | solution.py:398
  20.5 0.6 %collective-permute-start.7 = (f32[12,128]{1,0:T(8,128)S(1)}, f32[12,128]{1,0:T(8,128)S(1)}, u32[]{:S(2)}, u32[]{:S(2)}) collective-permute-start(f32[12,128]{1,0:T(8,128)S(1)} %control.1.refs_0_), channel_id=1, source_target_pairs={{0,5},{1,4},{2,7},{3,6},{4,1},{5,0},{6,3},{7,2},{8,13},{9,12},{10,... | collective-permute-start | bytes 18440 | tf_op jit(solution)/shard_map/ppermute | solution.py:398
  21.1 0.0 collective-permute-done.5.refs_1_
  21.1 1.9 %collective-permute-done.6.refs_2_ = f32[12,128]{1,0:T(8,128)S(1)} collective-permute-done((f32[12,128]{1,0:T(8,128)S(1)}, f32[12,128]{1,0:T(8,128)S(1)}, u32[]{:S(2)}, u32[]{:S(2)}) %collective-permute-start.6) | collective-permute-done | bytes 6176 | tf_op jit(solution)/shard_map/ppermute | solution.py:398
  22.9 0.7 %collective-permute-done.7.refs_3_ = f32[12,128]{1,0:T(8,128)S(1)} collective-permute-done((f32[12,128]{1,0:T(8,128)S(1)}, f32[12,128]{1,0:T(8,128)S(1)}, u32[]{:S(2)}, u32[]{:S(2)}) %collective-permute-start.7) | collective-permute-done | bytes 6176 | tf_op jit(solution)/shard_map/ppermute | solution.py:398
  23.6 2.0 %collective-permute-start.10 = (f32[12,128]{1,0:T(8,128)S(1)}, f32[12,128]{1,0:T(8,128)S(1)}, u32[]{:S(2)}, u32[]{:S(2)}) collective-permute-start(f32[12,128]{1,0:T(8,128)S(1)} %add.1.refs_0_), channel_id=1, source_target_pairs={{0,11},{1,10},{2,9},{3,8},{4,15},{5,14},{6,13},{7,12},{8,3},{9,2},... | collective-permute-start | bytes 18440 | tf_op jit(solution)/shard_map/ppermute | solution.py:398
  25.7 0.8 %collective-permute-start.8 = (f32[12,128]{1,0:T(8,128)S(1)}, f32[12,128]{1,0:T(8,128)S(1)}, u32[]{:S(2)}, u32[]{:S(2)}) collective-permute-start(f32[12,128]{1,0:T(8,128)S(1)} %add.1.refs_0_), channel_id=1, source_target_pairs={{0,3},{1,2},{2,1},{3,0},{4,7},{5,6},{6,5},{7,4},{8,11},{9,10},{10,... | collective-permute-start | bytes 18440 | tf_op jit(solution)/shard_map/ppermute | solution.py:398
  26.5 1.0 %collective-permute-start.9 = (f32[12,128]{1,0:T(8,128)S(1)}, f32[12,128]{1,0:T(8,128)S(1)}, u32[]{:S(2)}, u32[]{:S(2)}) collective-permute-start(f32[12,128]{1,0:T(8,128)S(1)} %add.1.refs_0_), channel_id=1, source_target_pairs={{0,9},{1,8},{2,11},{3,10},{4,13},{5,12},{6,15},{7,14},{8,1},{9,0},... | collective-permute-start | bytes 18440 | tf_op jit(solution)/shard_map/ppermute | solution.py:398
  27.4 1.1 %collective-permute-done.10.refs_3_ = f32[12,128]{1,0:T(8,128)S(1)} collective-permute-done((f32[12,128]{1,0:T(8,128)S(1)}, f32[12,128]{1,0:T(8,128)S(1)}, u32[]{:S(2)}, u32[]{:S(2)}) %collective-permute-start.10) | collective-permute-done | bytes 6176 | tf_op jit(solution)/shard_map/ppermute | solution.py:398
  28.5 0.2 collective-permute-done.8.refs_1_
  28.8 1.7 %collective-permute-done.9.refs_2_ = f32[12,128]{1,0:T(8,128)S(1)} collective-permute-done((f32[12,128]{1,0:T(8,128)S(1)}, f32[12,128]{1,0:T(8,128)S(1)}, u32[]{:S(2)}, u32[]{:S(2)}) %collective-permute-start.9) | collective-permute-done | bytes 6176 | tf_op jit(solution)/shard_map/ppermute | solution.py:398
  30.4 0.6 %finish.1 = f32[3,512]{1,0:T(4,128)} custom-call(f32[12,128]{1,0:T(8,128)S(1)} %add.1.refs_0_, f32[12,128]{1,0:T(8,128)S(1)} %collective-permute-done.8.refs_1_, f32[12,128]{1,0:T(8,128)S(1)} %collective-permute-done.9.refs_2_, f32[12,128]{1,0:T(8,128)S(1)} %collective-permute-done.10.refs_3_), custom_call_target="tpu_custom_call" | custom-call | tf_op jit(solution)/shard_map/finish/pallas_call | solution.py:576
  (1 shorter events, 0.0 us)
Async XLA Ops:
  0.6 5.3 %collective-permute-start = (f32[80,128]{1,0:T(8,128)}, f32[80,128]{1,0:T(8,128)S(1)}, u32[]{:S(2)}, u32[]{:S(2)}) collective-permute-start(f32[80,128]{1,0:T(8,128)} %bitcast.38), channel_id=1, source_target_pairs={{0,1},{1,0},{4,5},{5,4},{8,9},{9,8},{12,13},{13,12},{2,3},{3,2},{6... | collective-permute-start | bytes 122888 | tf_op jit(solution)/shard_map/ppermute | solution.py:433
  1.2 4.8 %collective-permute-start.1 = (f32[80,128]{1,0:T(8,128)}, f32[80,128]{1,0:T(8,128)S(1)}, u32[]{:S(2)}, u32[]{:S(2)}) collective-permute-start(f32[80,128]{1,0:T(8,128)} %bitcast.39), channel_id=1, source_target_pairs={{0,2},{2,0},{1,4},{3,6},{4,1},{6,3},{5,8},{7,10},{8,5},{10,7},{9,1... | collective-permute-start | bytes 122888 | tf_op jit(solution)/shard_map/ppermute | solution.py:448
  7.2 5.1 %collective-permute-start.2 = (f32[80,128]{1,0:T(8,128)S(1)}, f32[80,128]{1,0:T(8,128)S(1)}, u32[]{:S(2)}, u32[]{:S(2)}) collective-permute-start(f32[80,128]{1,0:T(8,128)S(1)} %sweep.1._.refs_2_), channel_id=1, source_target_pairs={{0,1},{1,0},{4,5},{5,4},{8,9},{9,8},{12,13},{13,12},{2,3},{3,2},{6... | collective-permute-start | bytes 122888 | tf_op jit(solution)/shard_map/ppermute | solution.py:433
  7.4 4.8 %collective-permute-start.3 = (f32[80,128]{1,0:T(8,128)S(1)}, f32[80,128]{1,0:T(8,128)S(1)}, u32[]{:S(2)}, u32[]{:S(2)}) collective-permute-start(f32[80,128]{1,0:T(8,128)S(1)} %sweep.1._.refs_2_), channel_id=1, source_target_pairs={{0,2},{2,0},{1,4},{3,6},{4,1},{6,3},{5,8},{7,10},{8,5},{10,7},{9,1... | collective-permute-start | bytes 122888 | tf_op jit(solution)/shard_map/ppermute | solution.py:448
  13.5 3.8 %collective-permute-start.4 = (f32[24,128]{1,0:T(8,128)S(1)}, f32[24,128]{1,0:T(8,128)S(1)}, u32[]{:S(2)}, u32[]{:S(2)}) collective-permute-start(f32[24,128]{1,0:T(8,128)S(1)} %get-tuple-element.28.after.refs_0_), channel_id=1, source_target_pairs={{0,2},{2,0},{1,3},{3,1},{4,6},{6,4},{5,7},{7,5},{8,10},{10,8},{9,1... | collective-permute-start | bytes 36872 | tf_op jit(solution)/shard_map/ppermute | solution.py:546
  19.1 1.9 %collective-permute-start.5 = (f32[12,128]{1,0:T(8,128)S(1)}, f32[12,128]{1,0:T(8,128)S(1)}, u32[]{:S(2)}, u32[]{:S(2)}) collective-permute-start(f32[12,128]{1,0:T(8,128)S(1)} %control.1.refs_0_), channel_id=1, source_target_pairs={{0,1},{1,0},{2,3},{3,2},{4,5},{5,4},{6,7},{7,6},{8,9},{9,8},{10,11... | collective-permute-start | bytes 18440 | tf_op jit(solution)/shard_map/ppermute | solution.py:398
  19.2 3.7 %collective-permute-start.6 = (f32[12,128]{1,0:T(8,128)S(1)}, f32[12,128]{1,0:T(8,128)S(1)}, u32[]{:S(2)}, u32[]{:S(2)}) collective-permute-start(f32[12,128]{1,0:T(8,128)S(1)} %control.1.refs_0_), channel_id=1, source_target_pairs={{0,4},{1,5},{2,6},{3,7},{4,0},{5,1},{6,2},{7,3},{8,12},{9,13},{10,... | collective-permute-start | bytes 18440 | tf_op jit(solution)/shard_map/ppermute | solution.py:398
  20.5 3.1 %collective-permute-start.7 = (f32[12,128]{1,0:T(8,128)S(1)}, f32[12,128]{1,0:T(8,128)S(1)}, u32[]{:S(2)}, u32[]{:S(2)}) collective-permute-start(f32[12,128]{1,0:T(8,128)S(1)} %control.1.refs_0_), channel_id=1, source_target_pairs={{0,5},{1,4},{2,7},{3,6},{4,1},{5,0},{6,3},{7,2},{8,13},{9,12},{10,... | collective-permute-start | bytes 18440 | tf_op jit(solution)/shard_map/ppermute | solution.py:398
  23.6 4.9 %collective-permute-start.10 = (f32[12,128]{1,0:T(8,128)S(1)}, f32[12,128]{1,0:T(8,128)S(1)}, u32[]{:S(2)}, u32[]{:S(2)}) collective-permute-start(f32[12,128]{1,0:T(8,128)S(1)} %add.1.refs_0_), channel_id=1, source_target_pairs={{0,11},{1,10},{2,9},{3,8},{4,15},{5,14},{6,13},{7,12},{8,3},{9,2},... | collective-permute-start | bytes 18440 | tf_op jit(solution)/shard_map/ppermute | solution.py:398
  25.7 3.1 %collective-permute-start.8 = (f32[12,128]{1,0:T(8,128)S(1)}, f32[12,128]{1,0:T(8,128)S(1)}, u32[]{:S(2)}, u32[]{:S(2)}) collective-permute-start(f32[12,128]{1,0:T(8,128)S(1)} %add.1.refs_0_), channel_id=1, source_target_pairs={{0,3},{1,2},{2,1},{3,0},{4,7},{5,6},{6,5},{7,4},{8,11},{9,10},{10,... | collective-permute-start | bytes 18440 | tf_op jit(solution)/shard_map/ppermute | solution.py:398
  26.5 4.0 %collective-permute-start.9 = (f32[12,128]{1,0:T(8,128)S(1)}, f32[12,128]{1,0:T(8,128)S(1)}, u32[]{:S(2)}, u32[]{:S(2)}) collective-permute-start(f32[12,128]{1,0:T(8,128)S(1)} %add.1.refs_0_), channel_id=1, source_target_pairs={{0,9},{1,8},{2,11},{3,10},{4,13},{5,12},{6,15},{7,14},{8,1},{9,0},... | collective-permute-start | bytes 18440 | tf_op jit(solution)/shard_map/ppermute | solution.py:398

commit v12 on v11

--- a/solution.py
+++ b/solution.py
@@ -160,6 +160,23 @@
         copy.wait()
 
 
+def take_lanes(table, lanes):
+    numbers = lax.GatherDimensionNumbers(
+        offset_dims=(),
+        collapsed_slice_dims=(1,),
+        start_index_map=(1,),
+        operand_batching_dims=(0,),
+        start_indices_batching_dims=(0,),
+    )
+    return lax.gather(
+        table,
+        lanes[..., None],
+        numbers,
+        slice_sizes=(1, 1),
+        mode=lax.GatherScatterMode.PROMISE_IN_BOUNDS,
+    )
+
+
 def sweep_into(
     blocks, first_ref, second_ref, own_ref, rhs_ref, off_ref, inverse_ref, lane_ref, step_ref,
     out_ref, window_ref, table_ref,
@@ -200,10 +217,7 @@
                         table = table_ref[at : at + 8, :]
                     else:
                         table = window_ref[at : at + 8, :]
-                    got = jnp.take_along_axis(
-                        table, lanes, axis=1, mode="promise_in_bounds"
-                    )
-                    beside[b] = jnp.where(here, got, beside[b])
+                    beside[b] = jnp.where(here, take_lanes(table, lanes), beside[b])
             for a in range(5):
                 for b in range(5):
                     row = (f * 25 + 5 * a + b) * per + half
@@ -275,7 +289,7 @@
 
 def wendland_kernel(first_cell, left_ref, right_ref, _, kernel_ref):
     cells, owned = kernel_ref.shape[0] // 2, kernel_ref.shape[1]
-    tile, wide = min(64, cells), min(256, owned)
+    tile, wide = min(128, cells), min(256, owned)
     for row in range(0, cells, tile):
         left = left_ref[first_cell + row : first_cell + row + tile, :]
         for lane in range(0, owned, wide):

time: 31.2 us -> 31.1 us (level)
  transfers between devices with their start and end apart: 11 -> 11, of which waited for: 6 -> 6; matrix products, arithmetic and copies ran while one was open for 0% -> 0% of each run, Pallas kernels for 24% -> 23%
where the time goes in v12:
time: 31.1 us; the launch traced here: 30.9 us
  starting transfers between devices  12.2 us (39%)
  Pallas kernels  12.1 us (39%)
  waiting for transfers between devices  5.9 us (19%)
  between operations  0.72 us (2%)
    ppermute x6, starting transfers between devices, exchanged(): lax.ppermute(value, SUM_AXES, [(i, i ^ mask) for i in range(peers)])  5.73 us
    ppermute x6, waiting for transfers between devices, exchanged(): lax.ppermute(value, SUM_AXES, [(i, i ^ mask) for i in range(peers)])  5.51 us
    ppermute x2, starting transfers between devices, swaps(): return (lax.ppermute(array, SUM_AXES, pairs), close)  4.47 us
    pallas_call x1, Pallas kernels, body(): pl.pallas_call(functools.partial(wendland_kernel, 0), out_shape=near_shap...  2.82 us
    pallas_call x1, Pallas kernels, body(): pl.pallas_call(functools.partial(prepare_kernel, nodes), out_shape=(shape...  2.18 us
    pallas_call x1, Pallas kernels, body(): pl.pallas_call(functools.partial(far_wendland_kernel, half), out_shape=(f...  2.15 us
    pallas_call x1, Pallas kernels, body(): pl.pallas_call(functools.partial(control_kernel, scale), out_shape=shape(...  1.84 us
    pallas_call x1, Pallas kernels, body(): pl.pallas_call(functools.partial(last_sweep_kernel, blocks), out_shape=(s...  1.26 us
  transfers between devices with their start and end apart: 11, of which 6 were waited for; matrix products, arithmetic and copies ran while one was open for 0% of the time, Pallas kernels for 23%

profile of v12, /device:TPU:0, one launch (start us, length us, event | category | flops | bytes accessed | tf_op | source)
XLA Modules:
  0.0 30.9 jit_solution(14350970468873143476)
XLA Ops:
  0.6 0.5 %collective-permute-start = (f32[80,128]{1,0:T(8,128)}, f32[80,128]{1,0:T(8,128)S(1)}, u32[]{:S(2)}, u32[]{:S(2)}) collective-permute-start(f32[80,128]{1,0:T(8,128)} %bitcast.38), channel_id=1, source_target_pairs={{0,1},{1,0},{4,5},{5,4},{8,9},{9,8},{12,13},{13,12},{2,3},{3,2},{6... | collective-permute-start | bytes 122888 | tf_op jit(solution)/shard_map/ppermute | solution.py:447
  1.2 2.6 %collective-permute-start.1 = (f32[80,128]{1,0:T(8,128)}, f32[80,128]{1,0:T(8,128)S(1)}, u32[]{:S(2)}, u32[]{:S(2)}) collective-permute-start(f32[80,128]{1,0:T(8,128)} %bitcast.39), channel_id=1, source_target_pairs={{0,2},{2,0},{1,4},{3,6},{4,1},{6,3},{5,8},{7,10},{8,5},{10,7},{9,1... | collective-permute-start | bytes 122888 | tf_op jit(solution)/shard_map/ppermute | solution.py:462
  3.7 2.2 %prepare.1 = (f32[2400,128]{1,0:T(8,128)S(1)}, f32[400,128]{1,0:T(8,128)S(1)}, f32[80,128]{1,0:T(8,128)S(1)}, f32[240,128]{1,0:T(8,128)S(1)}, s32[96,128]{1,0:T(...) custom-call(bf16[2400,128]{1,0:T(8,128)(2,1)} %bitcast.32, ...), custom_call_target="tpu_custom_call" | custom-call | flops 1000000000 | bytes 10000000 | tf_op jit(solution)/shard_map/prepare/pallas_call | solution.py:466
  5.9 0.0 collective-permute-done.refs_0_
  5.9 0.0 collective-permute-done.1.refs_1_
  5.9 1.2 %sweep.1._.refs_2_ = f32[80,128]{1,0:T(8,128)S(1)} custom-call(f32[80,128]{1,0:T(8,128)S(1)} %collective-permute-done.refs_0_, f32[80,128]{1,0:T(8,128)S(1)} %collective-permute-done.1.refs_1_, f32[80,128]{1,0:T(8,128)S(1)} %get-tuple-element.21.refs_2_, f32[80,128]{1,0:T(8,128)S(1)} %get-tuple-element.22.refs_3_, ...), custom_call_target="tpu_custom_call" | custom-call | flops 716800 | bytes 1228800 | tf_op jit(solution)/shard_map/sweep/pallas_call | solution.py:521
  7.2 0.3 collective-permute-start.2
  7.4 1.9 %collective-permute-start.3 = (f32[80,128]{1,0:T(8,128)S(1)}, f32[80,128]{1,0:T(8,128)S(1)}, u32[]{:S(2)}, u32[]{:S(2)}) collective-permute-start(f32[80,128]{1,0:T(8,128)S(1)} %sweep.1._.refs_2_), channel_id=1, source_target_pairs={{0,2},{2,0},{1,4},{3,6},{4,1},{6,3},{5,8},{7,10},{8,5},{10,7},{9,1... | collective-permute-start | bytes 122888 | tf_op jit(solution)/shard_map/ppermute | solution.py:462
  9.3 2.8 %near_wendland.1.refs_9_.refs_2_ = bf16[1280,2048]{1,0:T(8,128)(2,1)S(1)} custom-call(bf16[1024,64]{1,0:T(8,128)(2,1)S(1)} %get-tuple-element.19.left_ref, bf16[64,2048]{1,0:T(8,128)(2,1)S(1)} %get-tuple-element.20.right_ref, f32[80,128]{1,0:T(8,128)S(1)} %sweep.1._.refs_2_), custom_call_target="tpu_custom_call" | custom-call | flops 1000000000 | bytes 10000000 | tf_op jit(solution)/shard_map/near_wendland/pallas_call | solution.py:537
  12.2 0.0 collective-permute-done.2.refs_0_
  12.2 0.0 collective-permute-done.3.refs_1_
  12.2 1.3 %last_sweep.1 = (f32[80,128]{1,0:T(8,128)S(1)}, f32[24,128]{1,0:T(8,128)S(1)}) custom-call(f32[80,128]{1,0:T(8,128)S(1)} %collective-permute-done.2.refs_0_, f32[80,128]{1,0:T(8,128)S(1)} %collective-permute-done.3.refs_1_, f32[80,128]{1,0:T(8,128)S(1)} %sweep.1._.refs_2_, f32[80,128]{1,0:T(8,128)S(1)} %get-tuple-element.22.refs_3_, ...), custom_call_target="tpu_custom_call" | custom-call | flops 716800 | bytes 1228800 | tf_op jit(solution)/shard_map/last_sweep/pallas_call | solution.py:546
  13.5 1.2 %collective-permute-start.4 = (f32[24,128]{1,0:T(8,128)S(1)}, f32[24,128]{1,0:T(8,128)S(1)}, u32[]{:S(2)}, u32[]{:S(2)}) collective-permute-start(f32[24,128]{1,0:T(8,128)S(1)} %get-tuple-element.28.after.refs_0_), channel_id=1, source_target_pairs={{0,2},{2,0},{1,3},{3,1},{4,6},{6,4},{5,7},{7,5},{8,10},{10,8},{9,1... | collective-permute-start | bytes 36872 | tf_op jit(solution)/shard_map/ppermute | solution.py:560
  14.7 2.2 %far_wendland.1 = (bf16[768,2048]{1,0:T(8,128)(2,1)S(1)}, bf16[8192,128]{1,0:T(8,128)(2,1)S(1)}, f32[80,128]{1,0:T(8,128)}) custom-call(bf16[1024,64]{1,0:T(8,128)(2,1)S(1)} %get-tuple-element.19.left_ref, bf16[64,2048]{1,0:T(8,128)(2,1)S(1)} %get-tuple-element.20.right_ref, f32[24,128]{1,0:T(8,128)S(1)} %get-tuple-element.28.after.refs_0_, ...), custom_call_target="tpu_custom_call" | custom-call | flops 1000000000 | bytes 10000000 | tf_op jit(solution)/shard_map/far_wendland/pallas_call | solution.py:562
  16.8 0.4 %collective-permute-done.4.refs_1_ = f32[24,128]{1,0:T(8,128)S(1)} collective-permute-done((f32[24,128]{1,0:T(8,128)S(1)}, f32[24,128]{1,0:T(8,128)S(1)}, u32[]{:S(2)}, u32[]{:S(2)}) %collective-permute-start.4) | collective-permute-done | bytes 12320 | tf_op jit(solution)/shard_map/ppermute | solution.py:560
  17.2 1.8 %control.1.refs_0_ = f32[12,128]{1,0:T(8,128)S(1)} custom-call(f32[24,128]{1,0:T(8,128)S(1)} %get-tuple-element.28.after.refs_0_, f32[24,128]{1,0:T(8,128)S(1)} %collective-permute-done.4.refs_1_, bf16[1280,2048]{1,0:T(8,128)(2,1)S(1)} %near_wendland.1.refs_9_.refs_2_, bf16[768,2048]{1,0:T(8,128)(2,1)S(1)} %get-tuple-element.32.refs_3_, ...), custom_call_target="tpu_custom_call" | custom-call | tf_op jit(solution)/shard_map/control/pallas_call | solution.py:574
  19.1 0.1 collective-permute-start.5
  19.1 1.2 %collective-permute-start.6 = (f32[12,128]{1,0:T(8,128)S(1)}, f32[12,128]{1,0:T(8,128)S(1)}, u32[]{:S(2)}, u32[]{:S(2)}) collective-permute-start(f32[12,128]{1,0:T(8,128)S(1)} %control.1.refs_0_), channel_id=1, source_target_pairs={{0,4},{1,5},{2,6},{3,7},{4,0},{5,1},{6,2},{7,3},{8,12},{9,13},{10,... | collective-permute-start | bytes 18440 | tf_op jit(solution)/shard_map/ppermute | solution.py:412
  20.4 0.7 %collective-permute-start.7 = (f32[12,128]{1,0:T(8,128)S(1)}, f32[12,128]{1,0:T(8,128)S(1)}, u32[]{:S(2)}, u32[]{:S(2)}) collective-permute-start(f32[12,128]{1,0:T(8,128)S(1)} %control.1.refs_0_), channel_id=1, source_target_pairs={{0,5},{1,4},{2,7},{3,6},{4,1},{5,0},{6,3},{7,2},{8,13},{9,12},{10,... | collective-permute-start | bytes 18440 | tf_op jit(solution)/shard_map/ppermute | solution.py:412
  21.0 0.0 collective-permute-done.5.refs_1_
  21.0 1.9 %collective-permute-done.6.refs_2_ = f32[12,128]{1,0:T(8,128)S(1)} collective-permute-done((f32[12,128]{1,0:T(8,128)S(1)}, f32[12,128]{1,0:T(8,128)S(1)}, u32[]{:S(2)}, u32[]{:S(2)}) %collective-permute-start.6) | collective-permute-done | bytes 6176 | tf_op jit(solution)/shard_map/ppermute | solution.py:412
  22.9 0.6 %collective-permute-done.7.refs_3_ = f32[12,128]{1,0:T(8,128)S(1)} collective-permute-done((f32[12,128]{1,0:T(8,128)S(1)}, f32[12,128]{1,0:T(8,128)S(1)}, u32[]{:S(2)}, u32[]{:S(2)}) %collective-permute-start.7) | collective-permute-done | bytes 6176 | tf_op jit(solution)/shard_map/ppermute | solution.py:412
  23.5 2.2 %collective-permute-start.10 = (f32[12,128]{1,0:T(8,128)S(1)}, f32[12,128]{1,0:T(8,128)S(1)}, u32[]{:S(2)}, u32[]{:S(2)}) collective-permute-start(f32[12,128]{1,0:T(8,128)S(1)} %add.1.refs_0_), channel_id=1, source_target_pairs={{0,11},{1,10},{2,9},{3,8},{4,15},{5,14},{6,13},{7,12},{8,3},{9,2},... | collective-permute-start | bytes 18440 | tf_op jit(solution)/shard_map/ppermute | solution.py:412
  25.7 0.7 %collective-permute-start.8 = (f32[12,128]{1,0:T(8,128)S(1)}, f32[12,128]{1,0:T(8,128)S(1)}, u32[]{:S(2)}, u32[]{:S(2)}) collective-permute-start(f32[12,128]{1,0:T(8,128)S(1)} %add.1.refs_0_), channel_id=1, source_target_pairs={{0,3},{1,2},{2,1},{3,0},{4,7},{5,6},{6,5},{7,4},{8,11},{9,10},{10,... | collective-permute-start | bytes 18440 | tf_op jit(solution)/shard_map/ppermute | solution.py:412
  26.4 0.9 %collective-permute-start.9 = (f32[12,128]{1,0:T(8,128)S(1)}, f32[12,128]{1,0:T(8,128)S(1)}, u32[]{:S(2)}, u32[]{:S(2)}) collective-permute-start(f32[12,128]{1,0:T(8,128)S(1)} %add.1.refs_0_), channel_id=1, source_target_pairs={{0,9},{1,8},{2,11},{3,10},{4,13},{5,12},{6,15},{7,14},{8,1},{9,0},... | collective-permute-start | bytes 18440 | tf_op jit(solution)/shard_map/ppermute | solution.py:412
  27.3 1.1 %collective-permute-done.10.refs_3_ = f32[12,128]{1,0:T(8,128)S(1)} collective-permute-done((f32[12,128]{1,0:T(8,128)S(1)}, f32[12,128]{1,0:T(8,128)S(1)}, u32[]{:S(2)}, u32[]{:S(2)}) %collective-permute-start.10) | collective-permute-done | bytes 6176 | tf_op jit(solution)/shard_map/ppermute | solution.py:412
  28.4 0.4 %collective-permute-done.8.refs_1_ = f32[12,128]{1,0:T(8,128)S(1)} collective-permute-done((f32[12,128]{1,0:T(8,128)S(1)}, f32[12,128]{1,0:T(8,128)S(1)}, u32[]{:S(2)}, u32[]{:S(2)}) %collective-permute-start.8) | collective-permute-done | bytes 6176 | tf_op jit(solution)/shard_map/ppermute | solution.py:412
  28.8 1.5 %collective-permute-done.9.refs_2_ = f32[12,128]{1,0:T(8,128)S(1)} collective-permute-done((f32[12,128]{1,0:T(8,128)S(1)}, f32[12,128]{1,0:T(8,128)S(1)}, u32[]{:S(2)}, u32[]{:S(2)}) %collective-permute-start.9) | collective-permute-done | bytes 6176 | tf_op jit(solution)/shard_map/ppermute | solution.py:412
  30.3 0.6 %finish.1 = f32[3,512]{1,0:T(4,128)} custom-call(f32[12,128]{1,0:T(8,128)S(1)} %add.1.refs_0_, f32[12,128]{1,0:T(8,128)S(1)} %collective-permute-done.8.refs_1_, f32[12,128]{1,0:T(8,128)S(1)} %collective-permute-done.9.refs_2_, f32[12,128]{1,0:T(8,128)S(1)} %collective-permute-done.10.refs_3_), custom_call_target="tpu_custom_call" | custom-call | tf_op jit(solution)/shard_map/finish/pallas_call | solution.py:590
  (1 shorter events, 0.0 us)
Async XLA Ops:
  0.6 5.3 %collective-permute-start = (f32[80,128]{1,0:T(8,128)}, f32[80,128]{1,0:T(8,128)S(1)}, u32[]{:S(2)}, u32[]{:S(2)}) collective-permute-start(f32[80,128]{1,0:T(8,128)} %bitcast.38), channel_id=1, source_target_pairs={{0,1},{1,0},{4,5},{5,4},{8,9},{9,8},{12,13},{13,12},{2,3},{3,2},{6... | collective-permute-start | bytes 122888 | tf_op jit(solution)/shard_map/ppermute | solution.py:447
  1.2 4.8 %collective-permute-start.1 = (f32[80,128]{1,0:T(8,128)}, f32[80,128]{1,0:T(8,128)S(1)}, u32[]{:S(2)}, u32[]{:S(2)}) collective-permute-start(f32[80,128]{1,0:T(8,128)} %bitcast.39), channel_id=1, source_target_pairs={{0,2},{2,0},{1,4},{3,6},{4,1},{6,3},{5,8},{7,10},{8,5},{10,7},{9,1... | collective-permute-start | bytes 122888 | tf_op jit(solution)/shard_map/ppermute | solution.py:462
  7.2 5.0 %collective-permute-start.2 = (f32[80,128]{1,0:T(8,128)S(1)}, f32[80,128]{1,0:T(8,128)S(1)}, u32[]{:S(2)}, u32[]{:S(2)}) collective-permute-start(f32[80,128]{1,0:T(8,128)S(1)} %sweep.1._.refs_2_), channel_id=1, source_target_pairs={{0,1},{1,0},{4,5},{5,4},{8,9},{9,8},{12,13},{13,12},{2,3},{3,2},{6... | collective-permute-start | bytes 122888 | tf_op jit(solution)/shard_map/ppermute | solution.py:447
  7.4 4.8 %collective-permute-start.3 = (f32[80,128]{1,0:T(8,128)S(1)}, f32[80,128]{1,0:T(8,128)S(1)}, u32[]{:S(2)}, u32[]{:S(2)}) collective-permute-start(f32[80,128]{1,0:T(8,128)S(1)} %sweep.1._.refs_2_), channel_id=1, source_target_pairs={{0,2},{2,0},{1,4},{3,6},{4,1},{6,3},{5,8},{7,10},{8,5},{10,7},{9,1... | collective-permute-start | bytes 122888 | tf_op jit(solution)/shard_map/ppermute | solution.py:462
  13.5 3.8 %collective-permute-start.4 = (f32[24,128]{1,0:T(8,128)S(1)}, f32[24,128]{1,0:T(8,128)S(1)}, u32[]{:S(2)}, u32[]{:S(2)}) collective-permute-start(f32[24,128]{1,0:T(8,128)S(1)} %get-tuple-element.28.after.refs_0_), channel_id=1, source_target_pairs={{0,2},{2,0},{1,3},{3,1},{4,6},{6,4},{5,7},{7,5},{8,10},{10,8},{9,1... | collective-permute-start | bytes 36872 | tf_op jit(solution)/shard_map/ppermute | solution.py:560
  19.1 1.9 %collective-permute-start.5 = (f32[12,128]{1,0:T(8,128)S(1)}, f32[12,128]{1,0:T(8,128)S(1)}, u32[]{:S(2)}, u32[]{:S(2)}) collective-permute-start(f32[12,128]{1,0:T(8,128)S(1)} %control.1.refs_0_), channel_id=1, source_target_pairs={{0,1},{1,0},{2,3},{3,2},{4,5},{5,4},{6,7},{7,6},{8,9},{9,8},{10,11... | collective-permute-start | bytes 18440 | tf_op jit(solution)/shard_map/ppermute | solution.py:412
  19.1 3.7 %collective-permute-start.6 = (f32[12,128]{1,0:T(8,128)S(1)}, f32[12,128]{1,0:T(8,128)S(1)}, u32[]{:S(2)}, u32[]{:S(2)}) collective-permute-start(f32[12,128]{1,0:T(8,128)S(1)} %control.1.refs_0_), channel_id=1, source_target_pairs={{0,4},{1,5},{2,6},{3,7},{4,0},{5,1},{6,2},{7,3},{8,12},{9,13},{10,... | collective-permute-start | bytes 18440 | tf_op jit(solution)/shard_map/ppermute | solution.py:412
  20.4 3.1 %collective-permute-start.7 = (f32[12,128]{1,0:T(8,128)S(1)}, f32[12,128]{1,0:T(8,128)S(1)}, u32[]{:S(2)}, u32[]{:S(2)}) collective-permute-start(f32[12,128]{1,0:T(8,128)S(1)} %control.1.refs_0_), channel_id=1, source_target_pairs={{0,5},{1,4},{2,7},{3,6},{4,1},{5,0},{6,3},{7,2},{8,13},{9,12},{10,... | collective-permute-start | bytes 18440 | tf_op jit(solution)/shard_map/ppermute | solution.py:412
  23.5 4.9 %collective-permute-start.10 = (f32[12,128]{1,0:T(8,128)S(1)}, f32[12,128]{1,0:T(8,128)S(1)}, u32[]{:S(2)}, u32[]{:S(2)}) collective-permute-start(f32[12,128]{1,0:T(8,128)S(1)} %add.1.refs_0_), channel_id=1, source_target_pairs={{0,11},{1,10},{2,9},{3,8},{4,15},{5,14},{6,13},{7,12},{8,3},{9,2},... | collective-permute-start | bytes 18440 | tf_op jit(solution)/shard_map/ppermute | solution.py:412
  25.7 3.1 %collective-permute-start.8 = (f32[12,128]{1,0:T(8,128)S(1)}, f32[12,128]{1,0:T(8,128)S(1)}, u32[]{:S(2)}, u32[]{:S(2)}) collective-permute-start(f32[12,128]{1,0:T(8,128)S(1)} %add.1.refs_0_), channel_id=1, source_target_pairs={{0,3},{1,2},{2,1},{3,0},{4,7},{5,6},{6,5},{7,4},{8,11},{9,10},{10,... | collective-permute-start | bytes 18440 | tf_op jit(solution)/shard_map/ppermute | solution.py:412
  26.4 4.0 %collective-permute-start.9 = (f32[12,128]{1,0:T(8,128)S(1)}, f32[12,128]{1,0:T(8,128)S(1)}, u32[]{:S(2)}, u32[]{:S(2)}) collective-permute-start(f32[12,128]{1,0:T(8,128)S(1)} %add.1.refs_0_), channel_id=1, source_target_pairs={{0,9},{1,8},{2,11},{3,10},{4,13},{5,12},{6,15},{7,14},{8,1},{9,0},... | collective-permute-start | bytes 18440 | tf_op jit(solution)/shard_map/ppermute | solution.py:412

commit v13 on v12

--- a/solution.py
+++ b/solution.py
@@ -290,19 +290,26 @@
 def wendland_kernel(first_cell, left_ref, right_ref, _, kernel_ref):
     cells, owned = kernel_ref.shape[0] // 2, kernel_ref.shape[1]
     tile, wide = min(128, cells), min(256, owned)
-    for row in range(0, cells, tile):
+
+    def squares(row, lane):
         left = left_ref[first_cell + row : first_cell + row + tile, :]
-        for lane in range(0, owned, wide):
-            here = slice(lane, lane + wide)
-            squared = jnp.dot(left, right_ref[:, here], preferred_element_type=jnp.float32)
-            squared = jnp.maximum(squared, 1e-30)
-            near = jnp.maximum(1.0 - squared * lax.rsqrt(squared), 0.0)
-            power = near * near
-            kernel = power * power * (1.25 - near)
-            first = kernel.astype(jnp.bfloat16)
-            rest = (kernel - first.astype(jnp.float32)).astype(jnp.bfloat16)
-            kernel_ref[row : row + tile, here] = first
-            kernel_ref[cells + row : cells + row + tile, here] = rest
+        right = right_ref[:, lane : lane + wide]
+        return jnp.dot(left, right, preferred_element_type=jnp.float32)
+
+    places = [(row, lane) for lane in range(0, owned, wide) for row in range(0, cells, tile)]
+    following = squares(*places[0])
+    for at, (row, lane) in enumerate(places):
+        squared = jnp.maximum(following, 1e-30)
+        if at + 1 < len(places):
+            following = squares(*places[at + 1])
+        near = jnp.maximum(1.0 - squared * lax.rsqrt(squared), 0.0)
+        power = near * near
+        kernel = power * power * (1.25 - near)
+        first = kernel.astype(jnp.bfloat16)
+        rest = (kernel - first.astype(jnp.float32)).astype(jnp.bfloat16)
+        here = slice(lane, lane + wide)
+        kernel_ref[row : row + tile, here] = first
+        kernel_ref[cells + row : cells + row + tile, here] = rest
 
 
 def far_wendland_kernel(
@@ -396,7 +403,7 @@
     near = [cores >> 1 >> i for i in range(cores.bit_length() - 1)]
     node_bits = [cores << i for i in range(nodes.bit_length() - 1)]
     line_bits = [cores * nodes << i for i in range(lines.bit_length() - 1)]
-    bits = near + line_bits[:1] + node_bits[:1] + line_bits[1:] + node_bits[1:]
+    bits = near + line_bits[:2] + node_bits[:1] + line_bits[2:] + node_bits[1:]
     rounds = []
     for first in range(0, len(bits), 2):
         masks = bits[first : first + 2]
@@ -431,6 +438,7 @@
     blocks = cells // LANES
     per = blocks * nodes
     slots = ffd_index.shape[1]
+    far_slots = max(1, slots * 3 // 8)
     owned = base_points.shape[1] // lax.axis_size("nodes")
     peers = lax.axis_size(CELL_AXES)
     cores = lax.axis_size("sub")
@@ -474,7 +482,7 @@
             shape((faces * per, LANES), i32),
             shape((slots * 16, owned)),
             shape((slots, owned)),
-            shape((slots // 2 * owned, LANES), bf16),
+            shape(((slots - far_slots) * owned, LANES), bf16),
             shape((5 * per, LANES)),
             shape((cells, FACTOR_ROWS), bf16),
             shape((FACTOR_ROWS, owned), bf16),
@@ -558,7 +566,7 @@
     for shift in range(1, node_peers):
         ring = [(i, (i + shift) % node_peers) for i in range(node_peers)]
         all_sens.append(lax.ppermute(part_sens, "nodes", ring))
-    hot_shape = shape(((slots - slots // 2) * owned, LANES), bf16)
+    hot_shape = shape((far_slots * owned, LANES), bf16)
     far_kernel, far_hot, adjoint = pl.pallas_call(
         functools.partial(far_wendland_kernel, half),
         out_shape=(far_shape, hot_shape, shape((5 * per, LANES))),

time: 31.1 us -> 30.5 us (0.981)
  waiting for transfers between devices: 5.9 us -> 5.3 us
    ppermute x6, waiting for transfers between devices: 5.51 us -> 4.92 us  [exchanged(): lax.ppermute(value, SUM_AXES, [(i, i ^ mask) for i in range(peers)])]
  transfers between devices with their start and end apart: 11 -> 11, of which waited for: 6 -> 5; matrix products, arithmetic and copies ran while one was open for 0% -> 0% of each run, Pallas kernels for 23% -> 23%
where the time goes in v13:
time: 30.5 us; the launch traced here: 30.4 us
  starting transfers between devices  12.2 us (40%)
  Pallas kernels  12.2 us (40%)
  waiting for transfers between devices  5.3 us (17%)
  between operations  0.72 us (2%)
    ppermute x6, starting transfers between devices, exchanged(): lax.ppermute(value, SUM_AXES, [(i, i ^ mask) for i in range(peers)])  5.73 us
    ppermute x6, waiting for transfers between devices, exchanged(): lax.ppermute(value, SUM_AXES, [(i, i ^ mask) for i in range(peers)])  4.92 us
    ppermute x2, starting transfers between devices, swaps(): return (lax.ppermute(array, SUM_AXES, pairs), close)  4.34 us
    pallas_call x1, Pallas kernels, body(): pl.pallas_call(functools.partial(wendland_kernel, 0), out_shape=near_shap...  2.72 us
    pallas_call x1, Pallas kernels, body(): pl.pallas_call(functools.partial(prepare_kernel, nodes), out_shape=(shape...  2.32 us
    pallas_call x1, Pallas kernels, body(): pl.pallas_call(functools.partial(far_wendland_kernel, half), out_shape=(f...  2.08 us
    pallas_call x1, Pallas kernels, body(): pl.pallas_call(functools.partial(control_kernel, scale), out_shape=shape(...  1.85 us
    pallas_call x1, Pallas kernels, body(): pl.pallas_call(functools.partial(last_sweep_kernel, blocks), out_shape=(s...  1.32 us
  transfers between devices with their start and end apart: 11, of which 5 were waited for; matrix products, arithmetic and copies ran while one was open for 0% of the time, Pallas kernels for 23%

profile of v13, /device:TPU:0, one launch (start us, length us, event | category | flops | bytes accessed | tf_op | source)
XLA Modules:
  0.0 30.4 jit_solution(9304105669113168396)
XLA Ops:
  0.6 0.5 %collective-permute-start = (f32[80,128]{1,0:T(8,128)}, f32[80,128]{1,0:T(8,128)S(1)}, u32[]{:S(2)}, u32[]{:S(2)}) collective-permute-start(f32[80,128]{1,0:T(8,128)} %bitcast.38), channel_id=1, source_target_pairs={{0,1},{1,0},{4,5},{5,4},{8,9},{9,8},{12,13},{13,12},{2,3},{3,2},{6... | collective-permute-start | bytes 122888 | tf_op jit(solution)/shard_map/ppermute | solution.py:455
  1.2 2.6 %collective-permute-start.1 = (f32[80,128]{1,0:T(8,128)}, f32[80,128]{1,0:T(8,128)S(1)}, u32[]{:S(2)}, u32[]{:S(2)}) collective-permute-start(f32[80,128]{1,0:T(8,128)} %bitcast.39), channel_id=1, source_target_pairs={{0,2},{2,0},{1,4},{3,6},{4,1},{6,3},{5,8},{7,10},{8,5},{10,7},{9,1... | collective-permute-start | bytes 122888 | tf_op jit(solution)/shard_map/ppermute | solution.py:470
  3.7 2.3 %prepare.1 = (f32[2400,128]{1,0:T(8,128)S(1)}, f32[400,128]{1,0:T(8,128)S(1)}, f32[80,128]{1,0:T(8,128)S(1)}, f32[240,128]{1,0:T(8,128)S(1)}, s32[96,128]{1,0:T(...) custom-call(bf16[2400,128]{1,0:T(8,128)(2,1)} %bitcast.32, ...), custom_call_target="tpu_custom_call" | custom-call | flops 1000000000 | bytes 10000000 | tf_op jit(solution)/shard_map/prepare/pallas_call | solution.py:474
  6.0 0.0 collective-permute-done.refs_0_
  6.0 0.0 collective-permute-done.1.refs_1_
  6.1 1.3 %sweep.1._.refs_2_ = f32[80,128]{1,0:T(8,128)S(1)} custom-call(f32[80,128]{1,0:T(8,128)S(1)} %collective-permute-done.refs_0_, f32[80,128]{1,0:T(8,128)S(1)} %collective-permute-done.1.refs_1_, f32[80,128]{1,0:T(8,128)S(1)} %get-tuple-element.21.refs_2_, f32[80,128]{1,0:T(8,128)S(1)} %get-tuple-element.22.refs_3_, ...), custom_call_target="tpu_custom_call" | custom-call | flops 716800 | bytes 1228800 | tf_op jit(solution)/shard_map/sweep/pallas_call | solution.py:529
  7.4 0.3 collective-permute-start.2
  7.6 1.8 %collective-permute-start.3 = (f32[80,128]{1,0:T(8,128)S(1)}, f32[80,128]{1,0:T(8,128)S(1)}, u32[]{:S(2)}, u32[]{:S(2)}) collective-permute-start(f32[80,128]{1,0:T(8,128)S(1)} %sweep.1._.refs_2_), channel_id=1, source_target_pairs={{0,2},{2,0},{1,4},{3,6},{4,1},{6,3},{5,8},{7,10},{8,5},{10,7},{9,1... | collective-permute-start | bytes 122888 | tf_op jit(solution)/shard_map/ppermute | solution.py:470
  9.4 2.7 %near_wendland.1.refs_9_.refs_2_ = bf16[1280,2048]{1,0:T(8,128)(2,1)S(1)} custom-call(bf16[1024,64]{1,0:T(8,128)(2,1)S(1)} %get-tuple-element.19.left_ref, bf16[64,2048]{1,0:T(8,128)(2,1)S(1)} %get-tuple-element.20.right_ref, f32[80,128]{1,0:T(8,128)S(1)} %sweep.1._.refs_2_), custom_call_target="tpu_custom_call" | custom-call | flops 1000000000 | bytes 10000000 | tf_op jit(solution)/shard_map/near_wendland/pallas_call | solution.py:545
  12.1 0.0 collective-permute-done.2.refs_0_
  12.1 0.0 collective-permute-done.3.refs_1_
  12.2 1.3 %last_sweep.1 = (f32[80,128]{1,0:T(8,128)S(1)}, f32[24,128]{1,0:T(8,128)S(1)}) custom-call(f32[80,128]{1,0:T(8,128)S(1)} %collective-permute-done.2.refs_0_, f32[80,128]{1,0:T(8,128)S(1)} %collective-permute-done.3.refs_1_, f32[80,128]{1,0:T(8,128)S(1)} %sweep.1._.refs_2_, f32[80,128]{1,0:T(8,128)S(1)} %get-tuple-element.22.refs_3_, ...), custom_call_target="tpu_custom_call" | custom-call | flops 716800 | bytes 1228800 | tf_op jit(solution)/shard_map/last_sweep/pallas_call | solution.py:554
  13.5 1.3 %collective-permute-start.4 = (f32[24,128]{1,0:T(8,128)S(1)}, f32[24,128]{1,0:T(8,128)S(1)}, u32[]{:S(2)}, u32[]{:S(2)}) collective-permute-start(f32[24,128]{1,0:T(8,128)S(1)} %get-tuple-element.28.after.refs_0_), channel_id=1, source_target_pairs={{0,2},{2,0},{1,3},{3,1},{4,6},{6,4},{5,7},{7,5},{8,10},{10,8},{9,1... | collective-permute-start | bytes 36872 | tf_op jit(solution)/shard_map/ppermute | solution.py:568
  14.8 2.1 %far_wendland.1 = (bf16[768,2048]{1,0:T(8,128)(2,1)S(1)}, bf16[6144,128]{1,0:T(8,128)(2,1)S(1)}, f32[80,128]{1,0:T(8,128)}) custom-call(bf16[1024,64]{1,0:T(8,128)(2,1)S(1)} %get-tuple-element.19.left_ref, bf16[64,2048]{1,0:T(8,128)(2,1)S(1)} %get-tuple-element.20.right_ref, f32[24,128]{1,0:T(8,128)S(1)} %get-tuple-element.28.after.refs_0_, ...), custom_call_target="tpu_custom_call" | custom-call | flops 1000000000 | bytes 10000000 | tf_op jit(solution)/shard_map/far_wendland/pallas_call | solution.py:570
  16.9 0.4 %collective-permute-done.4.refs_1_ = f32[24,128]{1,0:T(8,128)S(1)} collective-permute-done((f32[24,128]{1,0:T(8,128)S(1)}, f32[24,128]{1,0:T(8,128)S(1)}, u32[]{:S(2)}, u32[]{:S(2)}) %collective-permute-start.4) | collective-permute-done | bytes 12320 | tf_op jit(solution)/shard_map/ppermute | solution.py:568
  17.2 1.8 %control.1.refs_0_ = f32[12,128]{1,0:T(8,128)S(1)} custom-call(f32[24,128]{1,0:T(8,128)S(1)} %get-tuple-element.28.after.refs_0_, f32[24,128]{1,0:T(8,128)S(1)} %collective-permute-done.4.refs_1_, bf16[1280,2048]{1,0:T(8,128)(2,1)S(1)} %near_wendland.1.refs_9_.refs_2_, bf16[768,2048]{1,0:T(8,128)(2,1)S(1)} %get-tuple-element.32.refs_3_, ...), custom_call_target="tpu_custom_call" | custom-call | tf_op jit(solution)/shard_map/control/pallas_call | solution.py:582
  19.1 0.1 collective-permute-start.5
  19.2 1.1 %collective-permute-start.6 = (f32[12,128]{1,0:T(8,128)S(1)}, f32[12,128]{1,0:T(8,128)S(1)}, u32[]{:S(2)}, u32[]{:S(2)}) collective-permute-start(f32[12,128]{1,0:T(8,128)S(1)} %control.1.refs_0_), channel_id=1, source_target_pairs={{0,4},{1,5},{2,6},{3,7},{4,0},{5,1},{6,2},{7,3},{8,12},{9,13},{10,... | collective-permute-start | bytes 18440 | tf_op jit(solution)/shard_map/ppermute | solution.py:419
  20.3 0.7 %collective-permute-start.7 = (f32[12,128]{1,0:T(8,128)S(1)}, f32[12,128]{1,0:T(8,128)S(1)}, u32[]{:S(2)}, u32[]{:S(2)}) collective-permute-start(f32[12,128]{1,0:T(8,128)S(1)} %control.1.refs_0_), channel_id=1, source_target_pairs={{0,5},{1,4},{2,7},{3,6},{4,1},{5,0},{6,3},{7,2},{8,13},{9,12},{10,... | collective-permute-start | bytes 18440 | tf_op jit(solution)/shard_map/ppermute | solution.py:419
  21.0 0.0 collective-permute-done.5.refs_1_
  21.0 1.9 %collective-permute-done.6.refs_2_ = f32[12,128]{1,0:T(8,128)S(1)} collective-permute-done((f32[12,128]{1,0:T(8,128)S(1)}, f32[12,128]{1,0:T(8,128)S(1)}, u32[]{:S(2)}, u32[]{:S(2)}) %collective-permute-start.6) | collective-permute-done | bytes 6176 | tf_op jit(solution)/shard_map/ppermute | solution.py:419
  22.9 0.6 %collective-permute-done.7.refs_3_ = f32[12,128]{1,0:T(8,128)S(1)} collective-permute-done((f32[12,128]{1,0:T(8,128)S(1)}, f32[12,128]{1,0:T(8,128)S(1)}, u32[]{:S(2)}, u32[]{:S(2)}) %collective-permute-start.7) | collective-permute-done | bytes 6176 | tf_op jit(solution)/shard_map/ppermute | solution.py:419
  23.5 2.3 %collective-permute-start.10 = (f32[12,128]{1,0:T(8,128)S(1)}, f32[12,128]{1,0:T(8,128)S(1)}, u32[]{:S(2)}, u32[]{:S(2)}) collective-permute-start(f32[12,128]{1,0:T(8,128)S(1)} %add.1.refs_0_), channel_id=1, source_target_pairs={{0,11},{1,10},{2,9},{3,8},{4,15},{5,14},{6,13},{7,12},{8,3},{9,2},... | collective-permute-start | bytes 18440 | tf_op jit(solution)/shard_map/ppermute | solution.py:419
  25.8 0.8 %collective-permute-start.8 = (f32[12,128]{1,0:T(8,128)S(1)}, f32[12,128]{1,0:T(8,128)S(1)}, u32[]{:S(2)}, u32[]{:S(2)}) collective-permute-start(f32[12,128]{1,0:T(8,128)S(1)} %add.1.refs_0_), channel_id=1, source_target_pairs={{0,9},{1,8},{2,11},{3,10},{4,13},{5,12},{6,15},{7,14},{8,1},{9,0},... | collective-permute-start | bytes 18440 | tf_op jit(solution)/shard_map/ppermute | solution.py:419
  26.6 0.6 %collective-permute-start.9 = (f32[12,128]{1,0:T(8,128)S(1)}, f32[12,128]{1,0:T(8,128)S(1)}, u32[]{:S(2)}, u32[]{:S(2)}) collective-permute-start(f32[12,128]{1,0:T(8,128)S(1)} %add.1.refs_0_), channel_id=1, source_target_pairs={{0,3},{1,2},{2,1},{3,0},{4,7},{5,6},{6,5},{7,4},{8,11},{9,10},{10,... | collective-permute-start | bytes 18440 | tf_op jit(solution)/shard_map/ppermute | solution.py:419
  27.3 1.1 %collective-permute-done.10.refs_3_ = f32[12,128]{1,0:T(8,128)S(1)} collective-permute-done((f32[12,128]{1,0:T(8,128)S(1)}, f32[12,128]{1,0:T(8,128)S(1)}, u32[]{:S(2)}, u32[]{:S(2)}) %collective-permute-start.10) | collective-permute-done | bytes 6176 | tf_op jit(solution)/shard_map/ppermute | solution.py:419
  28.3 1.4 %collective-permute-done.8.refs_1_ = f32[12,128]{1,0:T(8,128)S(1)} collective-permute-done((f32[12,128]{1,0:T(8,128)S(1)}, f32[12,128]{1,0:T(8,128)S(1)}, u32[]{:S(2)}, u32[]{:S(2)}) %collective-permute-start.8) | collective-permute-done | bytes 6176 | tf_op jit(solution)/shard_map/ppermute | solution.py:419
  29.8 0.0 collective-permute-done.9.refs_2_
  29.8 0.6 %finish.1 = f32[3,512]{1,0:T(4,128)} custom-call(f32[12,128]{1,0:T(8,128)S(1)} %add.1.refs_0_, f32[12,128]{1,0:T(8,128)S(1)} %collective-permute-done.8.refs_1_, f32[12,128]{1,0:T(8,128)S(1)} %collective-permute-done.9.refs_2_, f32[12,128]{1,0:T(8,128)S(1)} %collective-permute-done.10.refs_3_), custom_call_target="tpu_custom_call" | custom-call | tf_op jit(solution)/shard_map/finish/pallas_call | solution.py:598
  (1 shorter events, 0.0 us)
Async XLA Ops:
  0.6 5.4 %collective-permute-start = (f32[80,128]{1,0:T(8,128)}, f32[80,128]{1,0:T(8,128)S(1)}, u32[]{:S(2)}, u32[]{:S(2)}) collective-permute-start(f32[80,128]{1,0:T(8,128)} %bitcast.38), channel_id=1, source_target_pairs={{0,1},{1,0},{4,5},{5,4},{8,9},{9,8},{12,13},{13,12},{2,3},{3,2},{6... | collective-permute-start | bytes 122888 | tf_op jit(solution)/shard_map/ppermute | solution.py:455
  1.2 4.9 %collective-permute-start.1 = (f32[80,128]{1,0:T(8,128)}, f32[80,128]{1,0:T(8,128)S(1)}, u32[]{:S(2)}, u32[]{:S(2)}) collective-permute-start(f32[80,128]{1,0:T(8,128)} %bitcast.39), channel_id=1, source_target_pairs={{0,2},{2,0},{1,4},{3,6},{4,1},{6,3},{5,8},{7,10},{8,5},{10,7},{9,1... | collective-permute-start | bytes 122888 | tf_op jit(solution)/shard_map/ppermute | solution.py:470
  7.4 4.8 %collective-permute-start.2 = (f32[80,128]{1,0:T(8,128)S(1)}, f32[80,128]{1,0:T(8,128)S(1)}, u32[]{:S(2)}, u32[]{:S(2)}) collective-permute-start(f32[80,128]{1,0:T(8,128)S(1)} %sweep.1._.refs_2_), channel_id=1, source_target_pairs={{0,1},{1,0},{4,5},{5,4},{8,9},{9,8},{12,13},{13,12},{2,3},{3,2},{6... | collective-permute-start | bytes 122888 | tf_op jit(solution)/shard_map/ppermute | solution.py:455
  7.6 4.5 %collective-permute-start.3 = (f32[80,128]{1,0:T(8,128)S(1)}, f32[80,128]{1,0:T(8,128)S(1)}, u32[]{:S(2)}, u32[]{:S(2)}) collective-permute-start(f32[80,128]{1,0:T(8,128)S(1)} %sweep.1._.refs_2_), channel_id=1, source_target_pairs={{0,2},{2,0},{1,4},{3,6},{4,1},{6,3},{5,8},{7,10},{8,5},{10,7},{9,1... | collective-permute-start | bytes 122888 | tf_op jit(solution)/shard_map/ppermute | solution.py:470
  13.5 3.8 %collective-permute-start.4 = (f32[24,128]{1,0:T(8,128)S(1)}, f32[24,128]{1,0:T(8,128)S(1)}, u32[]{:S(2)}, u32[]{:S(2)}) collective-permute-start(f32[24,128]{1,0:T(8,128)S(1)} %get-tuple-element.28.after.refs_0_), channel_id=1, source_target_pairs={{0,2},{2,0},{1,3},{3,1},{4,6},{6,4},{5,7},{7,5},{8,10},{10,8},{9,1... | collective-permute-start | bytes 36872 | tf_op jit(solution)/shard_map/ppermute | solution.py:568
  19.1 1.9 %collective-permute-start.5 = (f32[12,128]{1,0:T(8,128)S(1)}, f32[12,128]{1,0:T(8,128)S(1)}, u32[]{:S(2)}, u32[]{:S(2)}) collective-permute-start(f32[12,128]{1,0:T(8,128)S(1)} %control.1.refs_0_), channel_id=1, source_target_pairs={{0,1},{1,0},{2,3},{3,2},{4,5},{5,4},{6,7},{7,6},{8,9},{9,8},{10,11... | collective-permute-start | bytes 18440 | tf_op jit(solution)/shard_map/ppermute | solution.py:419
  19.2 3.7 %collective-permute-start.6 = (f32[12,128]{1,0:T(8,128)S(1)}, f32[12,128]{1,0:T(8,128)S(1)}, u32[]{:S(2)}, u32[]{:S(2)}) collective-permute-start(f32[12,128]{1,0:T(8,128)S(1)} %control.1.refs_0_), channel_id=1, source_target_pairs={{0,4},{1,5},{2,6},{3,7},{4,0},{5,1},{6,2},{7,3},{8,12},{9,13},{10,... | collective-permute-start | bytes 18440 | tf_op jit(solution)/shard_map/ppermute | solution.py:419
  20.3 3.1 %collective-permute-start.7 = (f32[12,128]{1,0:T(8,128)S(1)}, f32[12,128]{1,0:T(8,128)S(1)}, u32[]{:S(2)}, u32[]{:S(2)}) collective-permute-start(f32[12,128]{1,0:T(8,128)S(1)} %control.1.refs_0_), channel_id=1, source_target_pairs={{0,5},{1,4},{2,7},{3,6},{4,1},{5,0},{6,3},{7,2},{8,13},{9,12},{10,... | collective-permute-start | bytes 18440 | tf_op jit(solution)/shard_map/ppermute | solution.py:419
  23.5 4.9 %collective-permute-start.10 = (f32[12,128]{1,0:T(8,128)S(1)}, f32[12,128]{1,0:T(8,128)S(1)}, u32[]{:S(2)}, u32[]{:S(2)}) collective-permute-start(f32[12,128]{1,0:T(8,128)S(1)} %add.1.refs_0_), channel_id=1, source_target_pairs={{0,11},{1,10},{2,9},{3,8},{4,15},{5,14},{6,13},{7,12},{8,3},{9,2},... | collective-permute-start | bytes 18440 | tf_op jit(solution)/shard_map/ppermute | solution.py:419
  25.8 4.0 %collective-permute-start.8 = (f32[12,128]{1,0:T(8,128)S(1)}, f32[12,128]{1,0:T(8,128)S(1)}, u32[]{:S(2)}, u32[]{:S(2)}) collective-permute-start(f32[12,128]{1,0:T(8,128)S(1)} %add.1.refs_0_), channel_id=1, source_target_pairs={{0,9},{1,8},{2,11},{3,10},{4,13},{5,12},{6,15},{7,14},{8,1},{9,0},... | collective-permute-start | bytes 18440 | tf_op jit(solution)/shard_map/ppermute | solution.py:419
  26.6 3.1 %collective-permute-start.9 = (f32[12,128]{1,0:T(8,128)S(1)}, f32[12,128]{1,0:T(8,128)S(1)}, u32[]{:S(2)}, u32[]{:S(2)}) collective-permute-start(f32[12,128]{1,0:T(8,128)S(1)} %add.1.refs_0_), channel_id=1, source_target_pairs={{0,3},{1,2},{2,1},{3,0},{4,7},{5,6},{6,5},{7,4},{8,11},{9,10},{10,... | collective-permute-start | bytes 18440 | tf_op jit(solution)/shard_map/ppermute | solution.py:419

commit v14 on v13

--- a/solution.py
+++ b/solution.py
@@ -178,7 +178,7 @@
 
 
 def sweep_into(
-    blocks, first_ref, second_ref, own_ref, rhs_ref, off_ref, inverse_ref, lane_ref, step_ref,
+    blocks, far_ref, close_ref, own_ref, rhs_ref, off_ref, inverse_ref, lane_ref, step_ref,
     out_ref, window_ref, table_ref,
 ):
     per = rhs_ref.shape[0] // 5
@@ -191,9 +191,9 @@
     for b in range(5):
         rows = slice(b * per, (b + 1) * per)
         base = b * width
-        window_ref[pl.ds(base + place, per), :] = first_ref[rows, :]
+        window_ref[pl.ds(base + place, per), :] = close_ref[rows, :]
         window_ref[base + per : base + 2 * per, :] = own_ref[rows, :]
-        window_ref[pl.ds(base + other, per), :] = second_ref[rows, :]
+        window_ref[pl.ds(base + other, per), :] = far_ref[rows, :]
     for shift in range(1, 8 // nodes):
         for b in range(5):
             for tile in range(0, width - 8, 8):
@@ -408,7 +408,8 @@
     for first in range(0, len(bits), 2):
         masks = bits[first : first + 2]
         if len(masks) == 2:
-            masks = masks + [masks[0] | masks[1]]
+            both = masks[0] | masks[1]
+            masks = masks + [both] if first else [masks[1], both, masks[0]]
         rounds.append([mask | (cores - 1) for mask in masks] if first else masks)
     return rounds
 
@@ -535,7 +536,7 @@
             compiler_params=PARAMS,
             cost_estimate=sweep_cost,
             name="sweep",
-        )(close, far, adjoint, rhs, off, inverse, lane, step)
+        )(far, close, adjoint, rhs, off, inverse, lane, step)
         far, close = swaps(adjoint)
 
     half = cells * 5 // 8 // LANES * LANES
@@ -560,7 +561,7 @@
         compiler_params=PARAMS,
         cost_estimate=sweep_cost,
         name="last_sweep",
-    )(close, far, adjoint, rhs, off, inverse, lane, step, sens, near_kernel)
+    )(far, close, adjoint, rhs, off, inverse, lane, step, sens, near_kernel)
 
     all_sens = [part_sens]
     for shift in range(1, node_peers):

time: 30.5 us -> 31.1 us (1.020)
  waiting for transfers between devices: 5.3 us -> 5.7 us
    ppermute x6, waiting for transfers between devices: 4.92 us -> 5.6 us  [exchanged(): lax.ppermute(value, SUM_AXES, [(i, i ^ mask) for i in range(peers)])]
    ppermute x2, starting transfers between devices: 0.78 us -> 0.23 us  [swaps(): close = lax.ppermute(array, CELL_AXES, [(i, i ^ 1) for i in range(peers)])]
    ppermute x2, starting transfers between devices: 4.34 us -> 4.73 us  [swaps(): return (lax.ppermute(array, SUM_AXES, pairs), close)]
  transfers between devices with their start and end apart: 11 -> 11, of which waited for: 5 -> 6; matrix products, arithmetic and copies ran while one was open for 0% -> 0% of each run, Pallas kernels for 23% -> 23%
where the time goes in v14:
time: 31.1 us; the launch traced here: 31 us
  starting transfers between devices  12.4 us (40%)
  Pallas kernels  12.2 us (39%)
  waiting for transfers between devices  5.7 us (18%)
  between operations  0.72 us (2%)
    ppermute x6, starting transfers between devices, exchanged(): lax.ppermute(value, SUM_AXES, [(i, i ^ mask) for i in range(peers)])  5.84 us
    ppermute x6, waiting for transfers between devices, exchanged(): lax.ppermute(value, SUM_AXES, [(i, i ^ mask) for i in range(peers)])  5.6 us
    ppermute x2, starting transfers between devices, swaps(): return (lax.ppermute(array, SUM_AXES, pairs), close)  4.73 us
    pallas_call x1, Pallas kernels, body(): pl.pallas_call(functools.partial(wendland_kernel, 0), out_shape=near_shap...  2.7 us
    pallas_call x1, Pallas kernels, body(): pl.pallas_call(functools.partial(prepare_kernel, nodes), out_shape=(shape...  2.32 us
    pallas_call x1, Pallas kernels, body(): pl.pallas_call(functools.partial(far_wendland_kernel, half), out_shape=(f...  2.08 us
    pallas_call x1, Pallas kernels, body(): pl.pallas_call(functools.partial(control_kernel, scale), out_shape=shape(...  1.85 us
    ppermute x1, starting transfers between devices, body(): all_sens.append(lax.ppermute(part_sens, 'nodes', ring))  1.58 us
  transfers between devices with their start and end apart: 11, of which 6 were waited for; matrix products, arithmetic and copies ran while one was open for 0% of the time, Pallas kernels for 23%

profile of v14, /device:TPU:0, one launch (start us, length us, event | category | flops | bytes accessed | tf_op | source)
XLA Modules:
  0.0 31.0 jit_solution(2658100493478793460)
XLA Ops:
  0.6 3.0 %collective-permute-start = (f32[80,128]{1,0:T(8,128)}, f32[80,128]{1,0:T(8,128)S(1)}, u32[]{:S(2)}, u32[]{:S(2)}) collective-permute-start(f32[80,128]{1,0:T(8,128)} %bitcast.38), channel_id=1, source_target_pairs={{0,2},{2,0},{1,4},{3,6},{4,1},{6,3},{5,8},{7,10},{8,5},{10,7},{9,1... | collective-permute-start | bytes 122888 | tf_op jit(solution)/shard_map/ppermute | solution.py:471
  3.6 0.2 collective-permute-start.1
  3.8 2.3 %prepare.1 = (f32[2400,128]{1,0:T(8,128)S(1)}, f32[400,128]{1,0:T(8,128)S(1)}, f32[80,128]{1,0:T(8,128)S(1)}, f32[240,128]{1,0:T(8,128)S(1)}, s32[96,128]{1,0:T(...) custom-call(bf16[2400,128]{1,0:T(8,128)(2,1)} %bitcast.32, ...), custom_call_target="tpu_custom_call" | custom-call | flops 1000000000 | bytes 10000000 | tf_op jit(solution)/shard_map/prepare/pallas_call | solution.py:475
  6.2 0.0 collective-permute-done.refs_0_
  6.2 0.0 collective-permute-done.1.refs_1_
  6.2 1.3 %sweep.1._.refs_2_ = f32[80,128]{1,0:T(8,128)S(1)} custom-call(f32[80,128]{1,0:T(8,128)S(1)} %collective-permute-done.refs_0_, f32[80,128]{1,0:T(8,128)S(1)} %collective-permute-done.1.refs_1_, f32[80,128]{1,0:T(8,128)S(1)} %get-tuple-element.21.refs_2_, f32[80,128]{1,0:T(8,128)S(1)} %get-tuple-element.22.refs_3_, ...), custom_call_target="tpu_custom_call" | custom-call | flops 716800 | bytes 1228800 | tf_op jit(solution)/shard_map/sweep/pallas_call | solution.py:530
  7.5 1.7 %collective-permute-start.2 = (f32[80,128]{1,0:T(8,128)S(1)}, f32[80,128]{1,0:T(8,128)S(1)}, u32[]{:S(2)}, u32[]{:S(2)}) collective-permute-start(f32[80,128]{1,0:T(8,128)S(1)} %sweep.1._.refs_2_), channel_id=1, source_target_pairs={{0,2},{2,0},{1,4},{3,6},{4,1},{6,3},{5,8},{7,10},{8,5},{10,7},{9,1... | collective-permute-start | bytes 122888 | tf_op jit(solution)/shard_map/ppermute | solution.py:471
  9.2 0.0 collective-permute-start.3
  9.2 2.7 %near_wendland.1.refs_9_.refs_2_ = bf16[1280,2048]{1,0:T(8,128)(2,1)S(1)} custom-call(bf16[1024,64]{1,0:T(8,128)(2,1)S(1)} %get-tuple-element.19.left_ref, bf16[64,2048]{1,0:T(8,128)(2,1)S(1)} %get-tuple-element.20.right_ref, f32[80,128]{1,0:T(8,128)S(1)} %sweep.1._.refs_2_), custom_call_target="tpu_custom_call" | custom-call | flops 1000000000 | bytes 10000000 | tf_op jit(solution)/shard_map/near_wendland/pallas_call | solution.py:546
  12.0 0.0 collective-permute-done.2.refs_0_
  12.0 0.0 collective-permute-done.3.refs_1_
  12.0 1.3 %last_sweep.1 = (f32[80,128]{1,0:T(8,128)S(1)}, f32[24,128]{1,0:T(8,128)S(1)}) custom-call(f32[80,128]{1,0:T(8,128)S(1)} %collective-permute-done.2.refs_0_, f32[80,128]{1,0:T(8,128)S(1)} %collective-permute-done.3.refs_1_, f32[80,128]{1,0:T(8,128)S(1)} %sweep.1._.refs_2_, f32[80,128]{1,0:T(8,128)S(1)} %get-tuple-element.22.refs_3_, ...), custom_call_target="tpu_custom_call" | custom-call | flops 716800 | bytes 1228800 | tf_op jit(solution)/shard_map/last_sweep/pallas_call | solution.py:555
  13.3 1.6 %collective-permute-start.4 = (f32[24,128]{1,0:T(8,128)S(1)}, f32[24,128]{1,0:T(8,128)S(1)}, u32[]{:S(2)}, u32[]{:S(2)}) collective-permute-start(f32[24,128]{1,0:T(8,128)S(1)} %get-tuple-element.28.after.refs_0_), channel_id=1, source_target_pairs={{0,2},{2,0},{1,3},{3,1},{4,6},{6,4},{5,7},{7,5},{8,10},{10,8},{9,1... | collective-permute-start | bytes 36872 | tf_op jit(solution)/shard_map/ppermute | solution.py:569
  14.9 2.1 %far_wendland.1 = (bf16[768,2048]{1,0:T(8,128)(2,1)S(1)}, bf16[6144,128]{1,0:T(8,128)(2,1)S(1)}, f32[80,128]{1,0:T(8,128)}) custom-call(bf16[1024,64]{1,0:T(8,128)(2,1)S(1)} %get-tuple-element.19.left_ref, bf16[64,2048]{1,0:T(8,128)(2,1)S(1)} %get-tuple-element.20.right_ref, f32[24,128]{1,0:T(8,128)S(1)} %get-tuple-element.28.after.refs_0_, ...), custom_call_target="tpu_custom_call" | custom-call | flops 1000000000 | bytes 10000000 | tf_op jit(solution)/shard_map/far_wendland/pallas_call | solution.py:571
  17.0 0.1 collective-permute-done.4.refs_1_
  17.1 1.8 %control.1.refs_0_ = f32[12,128]{1,0:T(8,128)S(1)} custom-call(f32[24,128]{1,0:T(8,128)S(1)} %get-tuple-element.28.after.refs_0_, f32[24,128]{1,0:T(8,128)S(1)} %collective-permute-done.4.refs_1_, bf16[1280,2048]{1,0:T(8,128)(2,1)S(1)} %near_wendland.1.refs_9_.refs_2_, bf16[768,2048]{1,0:T(8,128)(2,1)S(1)} %get-tuple-element.32.refs_3_, ...), custom_call_target="tpu_custom_call" | custom-call | tf_op jit(solution)/shard_map/control/pallas_call | solution.py:583
  18.9 1.7 %collective-permute-start.5 = (f32[12,128]{1,0:T(8,128)S(1)}, f32[12,128]{1,0:T(8,128)S(1)}, u32[]{:S(2)}, u32[]{:S(2)}) collective-permute-start(f32[12,128]{1,0:T(8,128)S(1)} %control.1.refs_0_), channel_id=1, source_target_pairs={{0,4},{1,5},{2,6},{3,7},{4,0},{5,1},{6,2},{7,3},{8,12},{9,13},{10,... | collective-permute-start | bytes 18440 | tf_op jit(solution)/shard_map/ppermute | solution.py:420
  20.6 0.0 collective-permute-start.6
  20.6 0.5 %collective-permute-start.7 = (f32[12,128]{1,0:T(8,128)S(1)}, f32[12,128]{1,0:T(8,128)S(1)}, u32[]{:S(2)}, u32[]{:S(2)}) collective-permute-start(f32[12,128]{1,0:T(8,128)S(1)} %control.1.refs_0_), channel_id=1, source_target_pairs={{0,1},{1,0},{2,3},{3,2},{4,5},{5,4},{6,7},{7,6},{8,9},{9,8},{10,11... | collective-permute-start | bytes 18440 | tf_op jit(solution)/shard_map/ppermute | solution.py:420
  21.1 1.5 %collective-permute-done.5.refs_1_ = f32[12,128]{1,0:T(8,128)S(1)} collective-permute-done((f32[12,128]{1,0:T(8,128)S(1)}, f32[12,128]{1,0:T(8,128)S(1)}, u32[]{:S(2)}, u32[]{:S(2)}) %collective-permute-start.5) | collective-permute-done | bytes 6176 | tf_op jit(solution)/shard_map/ppermute | solution.py:420
  22.6 1.0 %collective-permute-done.6.refs_2_ = f32[12,128]{1,0:T(8,128)S(1)} collective-permute-done((f32[12,128]{1,0:T(8,128)S(1)}, f32[12,128]{1,0:T(8,128)S(1)}, u32[]{:S(2)}, u32[]{:S(2)}) %collective-permute-start.6) | collective-permute-done | bytes 6176 | tf_op jit(solution)/shard_map/ppermute | solution.py:420
  23.7 0.0 collective-permute-done.7.refs_3_
  23.7 2.0 %collective-permute-start.10 = (f32[12,128]{1,0:T(8,128)S(1)}, f32[12,128]{1,0:T(8,128)S(1)}, u32[]{:S(2)}, u32[]{:S(2)}) collective-permute-start(f32[12,128]{1,0:T(8,128)S(1)} %add.1.refs_0_), channel_id=1, source_target_pairs={{0,11},{1,10},{2,9},{3,8},{4,15},{5,14},{6,13},{7,12},{8,3},{9,2},... | collective-permute-start | bytes 18440 | tf_op jit(solution)/shard_map/ppermute | solution.py:420
  25.6 1.7 %collective-permute-start.8 = (f32[12,128]{1,0:T(8,128)S(1)}, f32[12,128]{1,0:T(8,128)S(1)}, u32[]{:S(2)}, u32[]{:S(2)}) collective-permute-start(f32[12,128]{1,0:T(8,128)S(1)} %add.1.refs_0_), channel_id=1, source_target_pairs={{0,9},{1,8},{2,11},{3,10},{4,13},{5,12},{6,15},{7,14},{8,1},{9,0},... | collective-permute-start | bytes 18440 | tf_op jit(solution)/shard_map/ppermute | solution.py:420
  27.3 0.0 collective-permute-start.9
  27.3 1.3 %collective-permute-done.10.refs_3_ = f32[12,128]{1,0:T(8,128)S(1)} collective-permute-done((f32[12,128]{1,0:T(8,128)S(1)}, f32[12,128]{1,0:T(8,128)S(1)}, u32[]{:S(2)}, u32[]{:S(2)}) %collective-permute-start.10) | collective-permute-done | bytes 6176 | tf_op jit(solution)/shard_map/ppermute | solution.py:420
  28.6 1.0 %collective-permute-done.8.refs_1_ = f32[12,128]{1,0:T(8,128)S(1)} collective-permute-done((f32[12,128]{1,0:T(8,128)S(1)}, f32[12,128]{1,0:T(8,128)S(1)}, u32[]{:S(2)}, u32[]{:S(2)}) %collective-permute-start.8) | collective-permute-done | bytes 6176 | tf_op jit(solution)/shard_map/ppermute | solution.py:420
  29.6 0.8 %collective-permute-done.9.refs_2_ = f32[12,128]{1,0:T(8,128)S(1)} collective-permute-done((f32[12,128]{1,0:T(8,128)S(1)}, f32[12,128]{1,0:T(8,128)S(1)}, u32[]{:S(2)}, u32[]{:S(2)}) %collective-permute-start.9) | collective-permute-done | bytes 6176 | tf_op jit(solution)/shard_map/ppermute | solution.py:420
  30.4 0.6 %finish.1 = f32[3,512]{1,0:T(4,128)} custom-call(f32[12,128]{1,0:T(8,128)S(1)} %add.1.refs_0_, f32[12,128]{1,0:T(8,128)S(1)} %collective-permute-done.8.refs_1_, f32[12,128]{1,0:T(8,128)S(1)} %collective-permute-done.9.refs_2_, f32[12,128]{1,0:T(8,128)S(1)} %collective-permute-done.10.refs_3_), custom_call_target="tpu_custom_call" | custom-call | tf_op jit(solution)/shard_map/finish/pallas_call | solution.py:599
  (1 shorter events, 0.0 us)
Async XLA Ops:
  0.6 5.5 %collective-permute-start = (f32[80,128]{1,0:T(8,128)}, f32[80,128]{1,0:T(8,128)S(1)}, u32[]{:S(2)}, u32[]{:S(2)}) collective-permute-start(f32[80,128]{1,0:T(8,128)} %bitcast.38), channel_id=1, source_target_pairs={{0,2},{2,0},{1,4},{3,6},{4,1},{6,3},{5,8},{7,10},{8,5},{10,7},{9,1... | collective-permute-start | bytes 122888 | tf_op jit(solution)/shard_map/ppermute | solution.py:471
  3.6 2.5 %collective-permute-start.1 = (f32[80,128]{1,0:T(8,128)}, f32[80,128]{1,0:T(8,128)S(1)}, u32[]{:S(2)}, u32[]{:S(2)}) collective-permute-start(f32[80,128]{1,0:T(8,128)} %bitcast.39), channel_id=1, source_target_pairs={{0,1},{1,0},{4,5},{5,4},{8,9},{9,8},{12,13},{13,12},{2,3},{3,2},{6... | collective-permute-start | bytes 122888 | tf_op jit(solution)/shard_map/ppermute | solution.py:456
  7.5 4.5 %collective-permute-start.2 = (f32[80,128]{1,0:T(8,128)S(1)}, f32[80,128]{1,0:T(8,128)S(1)}, u32[]{:S(2)}, u32[]{:S(2)}) collective-permute-start(f32[80,128]{1,0:T(8,128)S(1)} %sweep.1._.refs_2_), channel_id=1, source_target_pairs={{0,2},{2,0},{1,4},{3,6},{4,1},{6,3},{5,8},{7,10},{8,5},{10,7},{9,1... | collective-permute-start | bytes 122888 | tf_op jit(solution)/shard_map/ppermute | solution.py:471
  9.2 2.8 %collective-permute-start.3 = (f32[80,128]{1,0:T(8,128)S(1)}, f32[80,128]{1,0:T(8,128)S(1)}, u32[]{:S(2)}, u32[]{:S(2)}) collective-permute-start(f32[80,128]{1,0:T(8,128)S(1)} %sweep.1._.refs_2_), channel_id=1, source_target_pairs={{0,1},{1,0},{4,5},{5,4},{8,9},{9,8},{12,13},{13,12},{2,3},{3,2},{6... | collective-permute-start | bytes 122888 | tf_op jit(solution)/shard_map/ppermute | solution.py:456
  13.3 3.8 %collective-permute-start.4 = (f32[24,128]{1,0:T(8,128)S(1)}, f32[24,128]{1,0:T(8,128)S(1)}, u32[]{:S(2)}, u32[]{:S(2)}) collective-permute-start(f32[24,128]{1,0:T(8,128)S(1)} %get-tuple-element.28.after.refs_0_), channel_id=1, source_target_pairs={{0,2},{2,0},{1,3},{3,1},{4,6},{6,4},{5,7},{7,5},{8,10},{10,8},{9,1... | collective-permute-start | bytes 36872 | tf_op jit(solution)/shard_map/ppermute | solution.py:569
  18.9 3.7 %collective-permute-start.5 = (f32[12,128]{1,0:T(8,128)S(1)}, f32[12,128]{1,0:T(8,128)S(1)}, u32[]{:S(2)}, u32[]{:S(2)}) collective-permute-start(f32[12,128]{1,0:T(8,128)S(1)} %control.1.refs_0_), channel_id=1, source_target_pairs={{0,4},{1,5},{2,6},{3,7},{4,0},{5,1},{6,2},{7,3},{8,12},{9,13},{10,... | collective-permute-start | bytes 18440 | tf_op jit(solution)/shard_map/ppermute | solution.py:420
  20.6 3.1 %collective-permute-start.6 = (f32[12,128]{1,0:T(8,128)S(1)}, f32[12,128]{1,0:T(8,128)S(1)}, u32[]{:S(2)}, u32[]{:S(2)}) collective-permute-start(f32[12,128]{1,0:T(8,128)S(1)} %control.1.refs_0_), channel_id=1, source_target_pairs={{0,5},{1,4},{2,7},{3,6},{4,1},{5,0},{6,3},{7,2},{8,13},{9,12},{10,... | collective-permute-start | bytes 18440 | tf_op jit(solution)/shard_map/ppermute | solution.py:420
  20.6 3.1 %collective-permute-start.7 = (f32[12,128]{1,0:T(8,128)S(1)}, f32[12,128]{1,0:T(8,128)S(1)}, u32[]{:S(2)}, u32[]{:S(2)}) collective-permute-start(f32[12,128]{1,0:T(8,128)S(1)} %control.1.refs_0_), channel_id=1, source_target_pairs={{0,1},{1,0},{2,3},{3,2},{4,5},{5,4},{6,7},{7,6},{8,9},{9,8},{10,11... | collective-permute-start | bytes 18440 | tf_op jit(solution)/shard_map/ppermute | solution.py:420
  23.7 5.0 %collective-permute-start.10 = (f32[12,128]{1,0:T(8,128)S(1)}, f32[12,128]{1,0:T(8,128)S(1)}, u32[]{:S(2)}, u32[]{:S(2)}) collective-permute-start(f32[12,128]{1,0:T(8,128)S(1)} %add.1.refs_0_), channel_id=1, source_target_pairs={{0,11},{1,10},{2,9},{3,8},{4,15},{5,14},{6,13},{7,12},{8,3},{9,2},... | collective-permute-start | bytes 18440 | tf_op jit(solution)/shard_map/ppermute | solution.py:420
  25.6 4.0 %collective-permute-start.8 = (f32[12,128]{1,0:T(8,128)S(1)}, f32[12,128]{1,0:T(8,128)S(1)}, u32[]{:S(2)}, u32[]{:S(2)}) collective-permute-start(f32[12,128]{1,0:T(8,128)S(1)} %add.1.refs_0_), channel_id=1, source_target_pairs={{0,9},{1,8},{2,11},{3,10},{4,13},{5,12},{6,15},{7,14},{8,1},{9,0},... | collective-permute-start | bytes 18440 | tf_op jit(solution)/shard_map/ppermute | solution.py:420
  27.3 3.1 %collective-permute-start.9 = (f32[12,128]{1,0:T(8,128)S(1)}, f32[12,128]{1,0:T(8,128)S(1)}, u32[]{:S(2)}, u32[]{:S(2)}) collective-permute-start(f32[12,128]{1,0:T(8,128)S(1)} %add.1.refs_0_), channel_id=1, source_target_pairs={{0,3},{1,2},{2,1},{3,0},{4,7},{5,6},{6,5},{7,4},{8,11},{9,10},{10,... | collective-permute-start | bytes 18440 | tf_op jit(solution)/shard_map/ppermute | solution.py:420

commit v15 on v14

--- a/solution.py
+++ b/solution.py
@@ -287,8 +287,8 @@
     return jnp.concatenate(blocks, axis=0)
 
 
-def wendland_kernel(first_cell, left_ref, right_ref, _, kernel_ref):
-    cells, owned = kernel_ref.shape[0] // 2, kernel_ref.shape[1]
+def wendland_blocks(first_cell, left_ref, right_ref, cells, store):
+    owned = right_ref.shape[1]
     tile, wide = min(128, cells), min(256, owned)
 
     def squares(row, lane):
@@ -304,31 +304,43 @@
             following = squares(*places[at + 1])
         near = jnp.maximum(1.0 - squared * lax.rsqrt(squared), 0.0)
         power = near * near
-        kernel = power * power * (1.25 - near)
+        store(slice(row, row + tile), slice(lane, lane + wide), power * power * (1.25 - near))
+
+
+def near_wendland_kernel(left_ref, right_ref, _, kernel_ref):
+    cells = kernel_ref.shape[0] // 2
+
+    def store(rows, lanes, kernel):
         first = kernel.astype(jnp.bfloat16)
         rest = (kernel - first.astype(jnp.float32)).astype(jnp.bfloat16)
-        here = slice(lane, lane + wide)
-        kernel_ref[row : row + tile, here] = first
-        kernel_ref[cells + row : cells + row + tile, here] = rest
+        kernel_ref[rows, lanes] = first
+        kernel_ref[cells + rows.start : cells + rows.stop, lanes] = rest
+
+    wendland_blocks(0, left_ref, right_ref, cells, store)
 
 
 def far_wendland_kernel(
-    first_cell, left_ref, right_ref, after, adjoint_ref, low_ref, *rest
+    left_ref, right_ref, _, adjoint_ref, low_ref, kernel_ref, one_hot_ref, result_ref, sem
 ):
-    kernel_ref, one_hot_ref, result_ref, sem = rest
     copy = pltpu.make_async_copy(adjoint_ref, result_ref, sem)
     copy.start()
     owned = low_ref.shape[1]
     write_one_hot(low_ref, one_hot_ref, low_ref.shape[0] - one_hot_ref.shape[0] // owned)
-    wendland_kernel(first_cell, left_ref, right_ref, after, kernel_ref)
+    cells = kernel_ref.shape[0]
+
+    def store(rows, lanes, kernel):
+        kernel_ref[rows, lanes] = kernel
+
+    wendland_blocks(left_ref.shape[0] - cells, left_ref, right_ref, cells, store)
     copy.wait()
 
 
 def control_kernel(scale, *refs):
-    *sens_refs, near_ref, far_ref = refs[:-4]
-    spread_ref, near_hot, far_hot, out_ref = refs[-4:]
+    *sens_refs, near_ref, far_ref = refs[:-5]
+    spread_ref, near_hot, far_hot, out_ref, column_ref = refs[-5:]
     blocks = sens_refs[0].shape[0] // 3
     half = near_ref.shape[0] // 2
+    far, owned = far_ref.shape
     groups = FFD // LANES
     total = sens_refs[0][...]
     for ref in sens_refs[1:]:
@@ -340,28 +352,44 @@
         rest = (value - first.astype(jnp.float32)).astype(jnp.bfloat16)
         return first, rest
 
+    columns = total.T
+    for k in range(3):
+        for block in range(half // LANES, blocks):
+            to = k * far + block * LANES - half
+            column = columns[:, k * blocks + block : k * blocks + block + 1]
+            column_ref[to : to + LANES, :] = jnp.broadcast_to(column, (LANES, LANES))
+
     row = lax.broadcasted_iota(jnp.int32, (8, LANES), 0)
     wide = []
-    for block in range(blocks):
+    for block in range(half // LANES):
         sens = jnp.zeros((8, LANES), jnp.float32)
         for k in range(3):
             sens = jnp.where(row == k, total[k * blocks + block : k * blocks + block + 1], sens)
         first = sens.astype(jnp.bfloat16).astype(jnp.float32)
         wide.append(jnp.concatenate([first, sens - first], axis=0))
     sens = jnp.concatenate(wide, axis=1).astype(jnp.bfloat16)
-    grad = None
-    for part, ref in ((sens[:, :half], near_ref), (sens[:, half:], far_ref)):
-        both = jnp.concatenate([part, part], axis=1)
-        term = jnp.dot(both, ref[...], preferred_element_type=jnp.float32)
-        grad = term if grad is None else grad + term
+    both = jnp.concatenate([sens, sens], axis=1)
+    grad = jnp.dot(both, near_ref[...], preferred_element_type=jnp.float32)
+
+    span = min(4 * LANES, owned)
+    parts = []
+    for first in range(0, owned, span):
+        sums = [None] * 3
+        for at in range(0, far, 8):
+            kernel = far_ref[at : at + 8, first : first + span]
+            for k in range(3):
+                column = column_ref[k * far + at : k * far + at + 8, :]
+                term = kernel * jnp.concatenate([column] * (span // LANES), axis=1)
+                sums[k] = term if sums[k] is None else sums[k] + term
+        parts.append([jnp.sum(value, axis=0, keepdims=True) for value in sums])
     grad = grad[:8] + grad[8:]
-    row = lax.broadcasted_iota(jnp.int32, (16, grad.shape[1]), 0)
+    row = lax.broadcasted_iota(jnp.int32, (16, owned), 0)
     wide = jnp.zeros(row.shape, jnp.float32)
     for k in range(3):
         mine = jnp.logical_and(row >= k * groups, row < (k + 1) * groups)
-        wide = jnp.where(mine, grad[k : k + 1], wide)
+        part = jnp.concatenate([sums[k] for sums in parts], axis=1)
+        wide = jnp.where(mine, grad[k : k + 1] + part, wide)
     grad = wide
-    owned = grad.shape[1]
     result = None
     places = [
         (ref, first) for ref in (near_hot, far_hot) for first in range(0, ref.shape[0], owned)
@@ -408,8 +436,7 @@
     for first in range(0, len(bits), 2):
         masks = bits[first : first + 2]
         if len(masks) == 2:
-            both = masks[0] | masks[1]
-            masks = masks + [both] if first else [masks[1], both, masks[0]]
+            masks = masks + [masks[0] | masks[1]]
         rounds.append([mask | (cores - 1) for mask in masks] if first else masks)
     return rounds
 
@@ -439,7 +466,7 @@
     blocks = cells // LANES
     per = blocks * nodes
     slots = ffd_index.shape[1]
-    far_slots = max(1, slots * 3 // 8)
+    far_slots = slots // 2
     owned = base_points.shape[1] // lax.axis_size("nodes")
     peers = lax.axis_size(CELL_AXES)
     cores = lax.axis_size("sub")
@@ -539,12 +566,12 @@
         )(far, close, adjoint, rhs, off, inverse, lane, step)
         far, close = swaps(adjoint)
 
-    half = cells * 5 // 8 // LANES * LANES
+    half = cells // 2 // LANES * LANES
     wendland_cost = cost(10**9, 10**7)
     near_shape = shape((2 * half, owned), bf16)
-    far_shape = shape((2 * (cells - half), owned), bf16)
+    far_shape = shape((cells - half, owned))
     near_kernel = pl.pallas_call(
-        functools.partial(wendland_kernel, 0),
+        near_wendland_kernel,
         out_shape=near_shape,
         in_specs=[VMEM] * 3,
         out_specs=VMEM,
@@ -569,7 +596,7 @@
         all_sens.append(lax.ppermute(part_sens, "nodes", ring))
     hot_shape = shape((far_slots * owned, LANES), bf16)
     far_kernel, far_hot, adjoint = pl.pallas_call(
-        functools.partial(far_wendland_kernel, half),
+        far_wendland_kernel,
         out_shape=(far_shape, hot_shape, shape((5 * per, LANES))),
         in_specs=[VMEM] * 5,
         out_specs=(VMEM, VMEM, HBM),
@@ -585,6 +612,7 @@
         out_shape=shape((rows, LANES)),
         in_specs=[VMEM] * (len(all_sens) + 5),
         out_specs=VMEM,
+        scratch_shapes=[pltpu.VMEM((3 * (cells - half), LANES), f32)],
         compiler_params=PARAMS,
         name="control",
     )(*all_sens, near_kernel, far_kernel, spread, near_hot, far_hot)

time: 31.1 us -> 30.9 us (level)
  waiting for transfers between devices: 5.7 us -> 5.08 us
    ppermute x6, waiting for transfers between devices: 5.6 us -> 5.05 us  [exchanged(): lax.ppermute(value, SUM_AXES, [(i, i ^ mask) for i in range(peers)])]
    pallas_call x1, Pallas kernels: 1.85 us -> 2.25 us  [body(): pl.pallas_call(functools.partial(control_kernel, scale), out_shape=shape(...]
  transfers between devices with their start and end apart: 11 -> 11, of which waited for: 6 -> 5; matrix products, arithmetic and copies ran while one was open for 0% -> 0% of each run, Pallas kernels for 23% -> 22%
where the time goes in v15:
time: 30.9 us; the launch traced here: 30.7 us
  starting transfers between devices  12.7 us (41%)
  Pallas kernels  12.2 us (39%)
  waiting for transfers between devices  5.08 us (16%)
  between operations  0.71 us (2%)
    ppermute x6, starting transfers between devices, exchanged(): lax.ppermute(value, SUM_AXES, [(i, i ^ mask) for i in range(peers)])  5.81 us
    ppermute x6, waiting for transfers between devices, exchanged(): lax.ppermute(value, SUM_AXES, [(i, i ^ mask) for i in range(peers)])  5.05 us
    ppermute x2, starting transfers between devices, swaps(): return (lax.ppermute(array, SUM_AXES, pairs), close)  4.87 us
    pallas_call x1, Pallas kernels, body(): pl.pallas_call(far_wendland_kernel, out_shape=(far_shape, hot_shape, shap...  2.35 us
    pallas_call x1, Pallas kernels, body(): pl.pallas_call(functools.partial(control_kernel, scale), out_shape=shape(...  2.25 us
    pallas_call x1, Pallas kernels, body(): pl.pallas_call(functools.partial(prepare_kernel, nodes), out_shape=(shape...  2.18 us
    pallas_call x1, Pallas kernels, body(): pl.pallas_call(near_wendland_kernel, out_shape=near_shape, in_specs=[VMEM...  2.17 us
    ppermute x1, starting transfers between devices, body(): all_sens.append(lax.ppermute(part_sens, 'nodes', ring))  1.86 us
  transfers between devices with their start and end apart: 11, of which 5 were waited for; matrix products, arithmetic and copies ran while one was open for 0% of the time, Pallas kernels for 22%

profile of v15, /device:TPU:0, one launch (start us, length us, event | category | flops | bytes accessed | tf_op | source)
XLA Modules:
  0.0 30.7 jit_solution(7182270078561760109)
XLA Ops:
  0.6 3.0 %collective-permute-start = (f32[80,128]{1,0:T(8,128)}, f32[80,128]{1,0:T(8,128)S(1)}, u32[]{:S(2)}, u32[]{:S(2)}) collective-permute-start(f32[80,128]{1,0:T(8,128)} %bitcast.38), channel_id=1, source_target_pairs={{0,2},{2,0},{1,4},{3,6},{4,1},{6,3},{5,8},{7,10},{8,5},{10,7},{9,1... | collective-permute-start | bytes 122888 | tf_op jit(solution)/shard_map/ppermute | solution.py:498
  3.6 0.2 collective-permute-start.1
  3.8 2.2 %prepare.1 = (f32[2400,128]{1,0:T(8,128)S(1)}, f32[400,128]{1,0:T(8,128)S(1)}, f32[80,128]{1,0:T(8,128)S(1)}, f32[240,128]{1,0:T(8,128)S(1)}, s32[96,128]{1,0:T(...) custom-call(bf16[2400,128]{1,0:T(8,128)(2,1)} %bitcast.32, ...), custom_call_target="tpu_custom_call" | custom-call | flops 1000000000 | bytes 10000000 | tf_op jit(solution)/shard_map/prepare/pallas_call | solution.py:502
  6.0 0.0 collective-permute-done.refs_0_
  6.0 0.0 collective-permute-done.1.refs_1_
  6.0 1.3 %sweep.1._.refs_2_ = f32[80,128]{1,0:T(8,128)S(1)} custom-call(f32[80,128]{1,0:T(8,128)S(1)} %collective-permute-done.refs_0_, f32[80,128]{1,0:T(8,128)S(1)} %collective-permute-done.1.refs_1_, f32[80,128]{1,0:T(8,128)S(1)} %get-tuple-element.21.refs_2_, f32[80,128]{1,0:T(8,128)S(1)} %get-tuple-element.22.refs_3_, ...), custom_call_target="tpu_custom_call" | custom-call | flops 716800 | bytes 1228800 | tf_op jit(solution)/shard_map/sweep/pallas_call | solution.py:557
  7.3 1.9 %collective-permute-start.2 = (f32[80,128]{1,0:T(8,128)S(1)}, f32[80,128]{1,0:T(8,128)S(1)}, u32[]{:S(2)}, u32[]{:S(2)}) collective-permute-start(f32[80,128]{1,0:T(8,128)S(1)} %sweep.1._.refs_2_), channel_id=1, source_target_pairs={{0,2},{2,0},{1,4},{3,6},{4,1},{6,3},{5,8},{7,10},{8,5},{10,7},{9,1... | collective-permute-start | bytes 122888 | tf_op jit(solution)/shard_map/ppermute | solution.py:498
  9.2 0.0 collective-permute-start.3
  9.2 2.2 %near_wendland.1.refs_9_.refs_2_ = bf16[1024,2048]{1,0:T(8,128)(2,1)S(1)} custom-call(bf16[1024,64]{1,0:T(8,128)(2,1)S(1)} %get-tuple-element.19.left_ref, bf16[64,2048]{1,0:T(8,128)(2,1)S(1)} %get-tuple-element.20.right_ref, f32[80,128]{1,0:T(8,128)S(1)} %sweep.1._.refs_2_), custom_call_target="tpu_custom_call" | custom-call | flops 1000000000 | bytes 10000000 | tf_op jit(solution)/shard_map/near_wendland/pallas_call | solution.py:573
  11.4 0.0 collective-permute-done.2.refs_0_
  11.4 0.0 collective-permute-done.3.refs_1_
  11.4 1.3 %last_sweep.1 = (f32[80,128]{1,0:T(8,128)S(1)}, f32[24,128]{1,0:T(8,128)S(1)}) custom-call(f32[80,128]{1,0:T(8,128)S(1)} %collective-permute-done.2.refs_0_, f32[80,128]{1,0:T(8,128)S(1)} %collective-permute-done.3.refs_1_, f32[80,128]{1,0:T(8,128)S(1)} %sweep.1._.refs_2_, f32[80,128]{1,0:T(8,128)S(1)} %get-tuple-element.22.refs_3_, ...), custom_call_target="tpu_custom_call" | custom-call | flops 716800 | bytes 1228800 | tf_op jit(solution)/shard_map/last_sweep/pallas_call | solution.py:582
  12.7 1.9 %collective-permute-start.4 = (f32[24,128]{1,0:T(8,128)S(1)}, f32[24,128]{1,0:T(8,128)S(1)}, u32[]{:S(2)}, u32[]{:S(2)}) collective-permute-start(f32[24,128]{1,0:T(8,128)S(1)} %get-tuple-element.28._.refs_0_), channel_id=1, source_target_pairs={{0,2},{2,0},{1,3},{3,1},{4,6},{6,4},{5,7},{7,5},{8,10},{10,8},{9,1... | collective-permute-start | bytes 36872 | tf_op jit(solution)/shard_map/ppermute | solution.py:596
  14.6 2.3 %far_wendland.1 = (f32[512,2048]{1,0:T(8,128)S(1)}, bf16[8192,128]{1,0:T(8,128)(2,1)S(1)}, f32[80,128]{1,0:T(8,128)}) custom-call(bf16[1024,64]{1,0:T(8,128)(2,1)S(1)} %get-tuple-element.19.left_ref, bf16[64,2048]{1,0:T(8,128)(2,1)S(1)} %get-tuple-element.20.right_ref, f32[24,128]{1,0:T(8,128)S(1)} %get-tuple-element.28._.refs_0_, ...), custom_call_target="tpu_custom_call" | custom-call | flops 1000000000 | bytes 10000000 | tf_op jit(solution)/shard_map/far_wendland/pallas_call | solution.py:598
  17.0 0.0 collective-permute-done.4.refs_1_
  17.0 2.3 %control.1.refs_0_ = f32[12,128]{1,0:T(8,128)S(1)} custom-call(f32[24,128]{1,0:T(8,128)S(1)} %get-tuple-element.28._.refs_0_, f32[24,128]{1,0:T(8,128)S(1)} %collective-permute-done.4.refs_1_, bf16[1024,2048]{1,0:T(8,128)(2,1)S(1)} %near_wendland.1.refs_9_.refs_2_, f32[512,2048]{1,0:T(8,128)S(1)} %get-tuple-element.32.refs_3_, ...), custom_call_target="tpu_custom_call" | custom-call | tf_op jit(solution)/shard_map/control/pallas_call | solution.py:610
  19.2 0.1 collective-permute-start.5
  19.3 1.2 %collective-permute-start.6 = (f32[12,128]{1,0:T(8,128)S(1)}, f32[12,128]{1,0:T(8,128)S(1)}, u32[]{:S(2)}, u32[]{:S(2)}) collective-permute-start(f32[12,128]{1,0:T(8,128)S(1)} %control.1.refs_0_), channel_id=1, source_target_pairs={{0,4},{1,5},{2,6},{3,7},{4,0},{5,1},{6,2},{7,3},{8,12},{9,13},{10,... | collective-permute-start | bytes 18440 | tf_op jit(solution)/shard_map/ppermute | solution.py:447
  20.5 0.6 %collective-permute-start.7 = (f32[12,128]{1,0:T(8,128)S(1)}, f32[12,128]{1,0:T(8,128)S(1)}, u32[]{:S(2)}, u32[]{:S(2)}) collective-permute-start(f32[12,128]{1,0:T(8,128)S(1)} %control.1.refs_0_), channel_id=1, source_target_pairs={{0,5},{1,4},{2,7},{3,6},{4,1},{5,0},{6,3},{7,2},{8,13},{9,12},{10,... | collective-permute-start | bytes 18440 | tf_op jit(solution)/shard_map/ppermute | solution.py:447
  21.2 0.0 collective-permute-done.5.refs_1_
  21.2 1.9 %collective-permute-done.6.refs_2_ = f32[12,128]{1,0:T(8,128)S(1)} collective-permute-done((f32[12,128]{1,0:T(8,128)S(1)}, f32[12,128]{1,0:T(8,128)S(1)}, u32[]{:S(2)}, u32[]{:S(2)}) %collective-permute-start.6) | collective-permute-done | bytes 6176 | tf_op jit(solution)/shard_map/ppermute | solution.py:447
  23.0 0.6 %collective-permute-done.7.refs_3_ = f32[12,128]{1,0:T(8,128)S(1)} collective-permute-done((f32[12,128]{1,0:T(8,128)S(1)}, f32[12,128]{1,0:T(8,128)S(1)}, u32[]{:S(2)}, u32[]{:S(2)}) %collective-permute-start.7) | collective-permute-done | bytes 6176 | tf_op jit(solution)/shard_map/ppermute | solution.py:447
  23.6 2.4 %collective-permute-start.10 = (f32[12,128]{1,0:T(8,128)S(1)}, f32[12,128]{1,0:T(8,128)S(1)}, u32[]{:S(2)}, u32[]{:S(2)}) collective-permute-start(f32[12,128]{1,0:T(8,128)S(1)} %add.1.refs_0_), channel_id=1, source_target_pairs={{0,11},{1,10},{2,9},{3,8},{4,15},{5,14},{6,13},{7,12},{8,3},{9,2},... | collective-permute-start | bytes 18440 | tf_op jit(solution)/shard_map/ppermute | solution.py:447
  26.0 1.0 %collective-permute-start.8 = (f32[12,128]{1,0:T(8,128)S(1)}, f32[12,128]{1,0:T(8,128)S(1)}, u32[]{:S(2)}, u32[]{:S(2)}) collective-permute-start(f32[12,128]{1,0:T(8,128)S(1)} %add.1.refs_0_), channel_id=1, source_target_pairs={{0,9},{1,8},{2,11},{3,10},{4,13},{5,12},{6,15},{7,14},{8,1},{9,0},... | collective-permute-start | bytes 18440 | tf_op jit(solution)/shard_map/ppermute | solution.py:447
  27.0 0.5 %collective-permute-start.9 = (f32[12,128]{1,0:T(8,128)S(1)}, f32[12,128]{1,0:T(8,128)S(1)}, u32[]{:S(2)}, u32[]{:S(2)}) collective-permute-start(f32[12,128]{1,0:T(8,128)S(1)} %add.1.refs_0_), channel_id=1, source_target_pairs={{0,3},{1,2},{2,1},{3,0},{4,7},{5,6},{6,5},{7,4},{8,11},{9,10},{10,... | collective-permute-start | bytes 18440 | tf_op jit(solution)/shard_map/ppermute | solution.py:447
  27.5 1.0 %collective-permute-done.10.refs_3_ = f32[12,128]{1,0:T(8,128)S(1)} collective-permute-done((f32[12,128]{1,0:T(8,128)S(1)}, f32[12,128]{1,0:T(8,128)S(1)}, u32[]{:S(2)}, u32[]{:S(2)}) %collective-permute-start.10) | collective-permute-done | bytes 6176 | tf_op jit(solution)/shard_map/ppermute | solution.py:447
  28.5 1.5 %collective-permute-done.8.refs_1_ = f32[12,128]{1,0:T(8,128)S(1)} collective-permute-done((f32[12,128]{1,0:T(8,128)S(1)}, f32[12,128]{1,0:T(8,128)S(1)}, u32[]{:S(2)}, u32[]{:S(2)}) %collective-permute-start.8) | collective-permute-done | bytes 6176 | tf_op jit(solution)/shard_map/ppermute | solution.py:447
  30.0 0.1 collective-permute-done.9.refs_2_
  30.1 0.6 %finish.1 = f32[3,512]{1,0:T(4,128)} custom-call(f32[12,128]{1,0:T(8,128)S(1)} %add.1.refs_0_, f32[12,128]{1,0:T(8,128)S(1)} %collective-permute-done.8.refs_1_, f32[12,128]{1,0:T(8,128)S(1)} %collective-permute-done.9.refs_2_, f32[12,128]{1,0:T(8,128)S(1)} %collective-permute-done.10.refs_3_), custom_call_target="tpu_custom_call" | custom-call | tf_op jit(solution)/shard_map/finish/pallas_call | solution.py:627
  (1 shorter events, 0.0 us)
Async XLA Ops:
  0.6 5.4 %collective-permute-start = (f32[80,128]{1,0:T(8,128)}, f32[80,128]{1,0:T(8,128)S(1)}, u32[]{:S(2)}, u32[]{:S(2)}) collective-permute-start(f32[80,128]{1,0:T(8,128)} %bitcast.38), channel_id=1, source_target_pairs={{0,2},{2,0},{1,4},{3,6},{4,1},{6,3},{5,8},{7,10},{8,5},{10,7},{9,1... | collective-permute-start | bytes 122888 | tf_op jit(solution)/shard_map/ppermute | solution.py:498
  3.6 2.4 %collective-permute-start.1 = (f32[80,128]{1,0:T(8,128)}, f32[80,128]{1,0:T(8,128)S(1)}, u32[]{:S(2)}, u32[]{:S(2)}) collective-permute-start(f32[80,128]{1,0:T(8,128)} %bitcast.39), channel_id=1, source_target_pairs={{0,1},{1,0},{4,5},{5,4},{8,9},{9,8},{12,13},{13,12},{2,3},{3,2},{6... | collective-permute-start | bytes 122888 | tf_op jit(solution)/shard_map/ppermute | solution.py:483
  7.3 4.1 %collective-permute-start.2 = (f32[80,128]{1,0:T(8,128)S(1)}, f32[80,128]{1,0:T(8,128)S(1)}, u32[]{:S(2)}, u32[]{:S(2)}) collective-permute-start(f32[80,128]{1,0:T(8,128)S(1)} %sweep.1._.refs_2_), channel_id=1, source_target_pairs={{0,2},{2,0},{1,4},{3,6},{4,1},{6,3},{5,8},{7,10},{8,5},{10,7},{9,1... | collective-permute-start | bytes 122888 | tf_op jit(solution)/shard_map/ppermute | solution.py:498
  9.2 2.2 %collective-permute-start.3 = (f32[80,128]{1,0:T(8,128)S(1)}, f32[80,128]{1,0:T(8,128)S(1)}, u32[]{:S(2)}, u32[]{:S(2)}) collective-permute-start(f32[80,128]{1,0:T(8,128)S(1)} %sweep.1._.refs_2_), channel_id=1, source_target_pairs={{0,1},{1,0},{4,5},{5,4},{8,9},{9,8},{12,13},{13,12},{2,3},{3,2},{6... | collective-permute-start | bytes 122888 | tf_op jit(solution)/shard_map/ppermute | solution.py:483
  12.7 4.2 %collective-permute-start.4 = (f32[24,128]{1,0:T(8,128)S(1)}, f32[24,128]{1,0:T(8,128)S(1)}, u32[]{:S(2)}, u32[]{:S(2)}) collective-permute-start(f32[24,128]{1,0:T(8,128)S(1)} %get-tuple-element.28._.refs_0_), channel_id=1, source_target_pairs={{0,2},{2,0},{1,3},{3,1},{4,6},{6,4},{5,7},{7,5},{8,10},{10,8},{9,1... | collective-permute-start | bytes 36872 | tf_op jit(solution)/shard_map/ppermute | solution.py:596
  19.2 1.9 %collective-permute-start.5 = (f32[12,128]{1,0:T(8,128)S(1)}, f32[12,128]{1,0:T(8,128)S(1)}, u32[]{:S(2)}, u32[]{:S(2)}) collective-permute-start(f32[12,128]{1,0:T(8,128)S(1)} %control.1.refs_0_), channel_id=1, source_target_pairs={{0,1},{1,0},{2,3},{3,2},{4,5},{5,4},{6,7},{7,6},{8,9},{9,8},{10,11... | collective-permute-start | bytes 18440 | tf_op jit(solution)/shard_map/ppermute | solution.py:447
  19.3 3.7 %collective-permute-start.6 = (f32[12,128]{1,0:T(8,128)S(1)}, f32[12,128]{1,0:T(8,128)S(1)}, u32[]{:S(2)}, u32[]{:S(2)}) collective-permute-start(f32[12,128]{1,0:T(8,128)S(1)} %control.1.refs_0_), channel_id=1, source_target_pairs={{0,4},{1,5},{2,6},{3,7},{4,0},{5,1},{6,2},{7,3},{8,12},{9,13},{10,... | collective-permute-start | bytes 18440 | tf_op jit(solution)/shard_map/ppermute | solution.py:447
  20.5 3.1 %collective-permute-start.7 = (f32[12,128]{1,0:T(8,128)S(1)}, f32[12,128]{1,0:T(8,128)S(1)}, u32[]{:S(2)}, u32[]{:S(2)}) collective-permute-start(f32[12,128]{1,0:T(8,128)S(1)} %control.1.refs_0_), channel_id=1, source_target_pairs={{0,5},{1,4},{2,7},{3,6},{4,1},{5,0},{6,3},{7,2},{8,13},{9,12},{10,... | collective-permute-start | bytes 18440 | tf_op jit(solution)/shard_map/ppermute | solution.py:447
  23.6 4.9 %collective-permute-start.10 = (f32[12,128]{1,0:T(8,128)S(1)}, f32[12,128]{1,0:T(8,128)S(1)}, u32[]{:S(2)}, u32[]{:S(2)}) collective-permute-start(f32[12,128]{1,0:T(8,128)S(1)} %add.1.refs_0_), channel_id=1, source_target_pairs={{0,11},{1,10},{2,9},{3,8},{4,15},{5,14},{6,13},{7,12},{8,3},{9,2},... | collective-permute-start | bytes 18440 | tf_op jit(solution)/shard_map/ppermute | solution.py:447
  26.0 4.0 %collective-permute-start.8 = (f32[12,128]{1,0:T(8,128)S(1)}, f32[12,128]{1,0:T(8,128)S(1)}, u32[]{:S(2)}, u32[]{:S(2)}) collective-permute-start(f32[12,128]{1,0:T(8,128)S(1)} %add.1.refs_0_), channel_id=1, source_target_pairs={{0,9},{1,8},{2,11},{3,10},{4,13},{5,12},{6,15},{7,14},{8,1},{9,0},... | collective-permute-start | bytes 18440 | tf_op jit(solution)/shard_map/ppermute | solution.py:447
  27.0 3.1 %collective-permute-start.9 = (f32[12,128]{1,0:T(8,128)S(1)}, f32[12,128]{1,0:T(8,128)S(1)}, u32[]{:S(2)}, u32[]{:S(2)}) collective-permute-start(f32[12,128]{1,0:T(8,128)S(1)} %add.1.refs_0_), channel_id=1, source_target_pairs={{0,3},{1,2},{2,1},{3,0},{4,7},{5,6},{6,5},{7,4},{8,11},{9,10},{10,... | collective-permute-start | bytes 18440 | tf_op jit(solution)/shard_map/ppermute | solution.py:447

commit v16 on v14

--- a/solution.py
+++ b/solution.py
@@ -37,19 +37,25 @@
     return [pltpu.with_memory_space_constraint(array, pltpu.HBM) for array in arrays]
 
 
-def write_one_hot(low_ref, one_hot_ref, first_slot):
+def one_hot_steps(low_ref, one_hot_ref, first_slot):
     owned = low_ref.shape[1]
     piece = min(512, owned)
-    lane = lax.broadcasted_iota(jnp.int32, (piece, LANES), 1).astype(jnp.float32)
-    lane = lane.astype(jnp.bfloat16)
-    for first in range(0, owned, piece):
+
+    def step(first, j):
+        lane = lax.broadcasted_iota(jnp.int32, (piece, LANES), 1).astype(jnp.float32)
+        lane = lane.astype(jnp.bfloat16)
         low = low_ref[:, first : first + piece].T.astype(jnp.bfloat16)
-        for j in range(one_hot_ref.shape[0] // owned):
-            column = low[:, first_slot + j : first_slot + j + 1]
-            hit = jnp.broadcast_to(column, (piece, LANES)) == lane
-            one_hot_ref[j * owned + first : j * owned + first + piece, :] = jnp.where(
-                hit, jnp.bfloat16(1.0), jnp.bfloat16(0.0)
-            )
+        column = low[:, first_slot + j : first_slot + j + 1]
+        hit = jnp.broadcast_to(column, (piece, LANES)) == lane
+        one_hot_ref[j * owned + first : j * owned + first + piece, :] = jnp.where(
+            hit, jnp.bfloat16(1.0), jnp.bfloat16(0.0)
+        )
+
+    return [
+        functools.partial(step, first, j)
+        for first in range(0, owned, piece)
+        for j in range(one_hot_ref.shape[0] // owned)
+    ]
 
 
 def prepare_kernel(
@@ -73,10 +79,10 @@
     step_ref,
     spread_ref,
     low_ref,
-    one_hot_ref,
     start_ref,
     left_ref,
     right_ref,
+    kernel_ref,
     off_buf,
     sens_buf,
     neigh_buf,
@@ -138,12 +144,12 @@
             )
 
     low_ref[...] = jnp.bitwise_and(index_buf[...], LANES - 1).astype(jnp.float32)
-    write_one_hot(low_ref, one_hot_ref, 0)
 
     copies[3].wait()
     left_ref[...] = distance_factors(cell_buf[...], True).T.astype(jnp.bfloat16)
     copies[4].wait()
     right_ref[...] = distance_factors(base_buf[...], False).astype(jnp.bfloat16)
+    wendland_blocks(0, left_ref, right_ref, kernel_ref)
 
     copies[5].wait()
     off_ref[...] = off_buf[...].astype(jnp.float32)
@@ -287,7 +293,7 @@
     return jnp.concatenate(blocks, axis=0)
 
 
-def wendland_kernel(first_cell, left_ref, right_ref, _, kernel_ref):
+def wendland_blocks(first_cell, left_ref, right_ref, kernel_ref, steps=()):
     cells, owned = kernel_ref.shape[0] // 2, kernel_ref.shape[1]
     tile, wide = min(128, cells), min(256, owned)
 
@@ -298,10 +304,14 @@
 
     places = [(row, lane) for lane in range(0, owned, wide) for row in range(0, cells, tile)]
     following = squares(*places[0])
+    done = 0
     for at, (row, lane) in enumerate(places):
         squared = jnp.maximum(following, 1e-30)
         if at + 1 < len(places):
             following = squares(*places[at + 1])
+        while done * len(places) < len(steps) * (at + 1):
+            steps[done]()
+            done += 1
         near = jnp.maximum(1.0 - squared * lax.rsqrt(squared), 0.0)
         power = near * near
         kernel = power * power * (1.25 - near)
@@ -312,23 +322,25 @@
         kernel_ref[cells + row : cells + row + tile, here] = rest
 
 
-def far_wendland_kernel(
-    first_cell, left_ref, right_ref, after, adjoint_ref, low_ref, *rest
-):
+def near_wendland_kernel(first_cell, left_ref, right_ref, low_ref, _, kernel_ref, one_hot_ref):
+    steps = one_hot_steps(low_ref, one_hot_ref, 0)
+    wendland_blocks(first_cell, left_ref, right_ref, kernel_ref, steps)
+
+
+def far_wendland_kernel(first_cell, left_ref, right_ref, low_ref, _, adjoint_ref, *rest):
     kernel_ref, one_hot_ref, result_ref, sem = rest
     copy = pltpu.make_async_copy(adjoint_ref, result_ref, sem)
     copy.start()
-    owned = low_ref.shape[1]
-    write_one_hot(low_ref, one_hot_ref, low_ref.shape[0] - one_hot_ref.shape[0] // owned)
-    wendland_kernel(first_cell, left_ref, right_ref, after, kernel_ref)
+    first_slot = low_ref.shape[0] - one_hot_ref.shape[0] // low_ref.shape[1]
+    steps = one_hot_steps(low_ref, one_hot_ref, first_slot)
+    wendland_blocks(first_cell, left_ref, right_ref, kernel_ref, steps)
     copy.wait()
 
 
 def control_kernel(scale, *refs):
-    *sens_refs, near_ref, far_ref = refs[:-4]
+    *sens_refs, first_ref, near_ref, far_ref = refs[:-4]
     spread_ref, near_hot, far_hot, out_ref = refs[-4:]
     blocks = sens_refs[0].shape[0] // 3
-    half = near_ref.shape[0] // 2
     groups = FFD // LANES
     total = sens_refs[0][...]
     for ref in sens_refs[1:]:
@@ -350,7 +362,10 @@
         wide.append(jnp.concatenate([first, sens - first], axis=0))
     sens = jnp.concatenate(wide, axis=1).astype(jnp.bfloat16)
     grad = None
-    for part, ref in ((sens[:, :half], near_ref), (sens[:, half:], far_ref)):
+    cell = 0
+    for ref in (first_ref, near_ref, far_ref):
+        part = sens[:, cell : cell + ref.shape[0] // 2]
+        cell += ref.shape[0] // 2
         both = jnp.concatenate([part, part], axis=1)
         term = jnp.dot(both, ref[...], preferred_element_type=jnp.float32)
         grad = term if grad is None else grad + term
@@ -408,8 +423,7 @@
     for first in range(0, len(bits), 2):
         masks = bits[first : first + 2]
         if len(masks) == 2:
-            both = masks[0] | masks[1]
-            masks = masks + [both] if first else [masks[1], both, masks[0]]
+            masks = masks + [masks[0] | masks[1]]
         rounds.append([mask | (cores - 1) for mask in masks] if first else masks)
     return rounds
 
@@ -439,7 +453,9 @@
     blocks = cells // LANES
     per = blocks * nodes
     slots = ffd_index.shape[1]
-    far_slots = max(1, slots * 3 // 8)
+    far_slots = slots // 2
+    parts = [cells // 8, cells // 2]
+    parts.append(cells - sum(parts))
     owned = base_points.shape[1] // lax.axis_size("nodes")
     peers = lax.axis_size(CELL_AXES)
     cores = lax.axis_size("sub")
@@ -483,10 +499,10 @@
             shape((faces * per, LANES), i32),
             shape((slots * 16, owned)),
             shape((slots, owned)),
-            shape(((slots - far_slots) * owned, LANES), bf16),
             shape((5 * per, LANES)),
             shape((cells, FACTOR_ROWS), bf16),
             shape((FACTOR_ROWS, owned), bf16),
+            shape((2 * parts[0], owned), bf16),
         ),
         in_specs=[HBM] * 11,
         out_specs=(VMEM,) * 12,
@@ -519,7 +535,7 @@
             base_points,
         )
     )
-    off, inverse, rhs, sens, lane, step, spread, low, near_hot, adjoint, left, right = prepared
+    off, inverse, rhs, sens, lane, step, spread, low, adjoint, left, right, first_kernel = prepared
     scratch = [
         pltpu.VMEM((3 * 5 * per, LANES), f32),
         pltpu.VMEM((max(8 // nodes - 1, 1) * 3 * 5 * per, LANES), f32),
@@ -539,19 +555,19 @@
         )(far, close, adjoint, rhs, off, inverse, lane, step)
         far, close = swaps(adjoint)
 
-    half = cells * 5 // 8 // LANES * LANES
     wendland_cost = cost(10**9, 10**7)
-    near_shape = shape((2 * half, owned), bf16)
-    far_shape = shape((2 * (cells - half), owned), bf16)
-    near_kernel = pl.pallas_call(
-        functools.partial(wendland_kernel, 0),
-        out_shape=near_shape,
-        in_specs=[VMEM] * 3,
-        out_specs=VMEM,
+    near_kernel, near_hot = pl.pallas_call(
+        functools.partial(near_wendland_kernel, parts[0]),
+        out_shape=(
+            shape((2 * parts[1], owned), bf16),
+            shape(((slots - far_slots) * owned, LANES), bf16),
+        ),
+        in_specs=[VMEM] * 4,
+        out_specs=(VMEM, VMEM),
         compiler_params=PARAMS,
         cost_estimate=wendland_cost,
         name="near_wendland",
-    )(left, right, adjoint)
+    )(left, right, low, adjoint)
     adjoint, part_sens = pl.pallas_call(
         functools.partial(last_sweep_kernel, blocks),
         out_shape=(shape((5 * per, LANES)), shape((3 * blocks, LANES))),
@@ -567,27 +583,30 @@
     for shift in range(1, node_peers):
         ring = [(i, (i + shift) % node_peers) for i in range(node_peers)]
         all_sens.append(lax.ppermute(part_sens, "nodes", ring))
-    hot_shape = shape((far_slots * owned, LANES), bf16)
     far_kernel, far_hot, adjoint = pl.pallas_call(
-        functools.partial(far_wendland_kernel, half),
-        out_shape=(far_shape, hot_shape, shape((5 * per, LANES))),
+        functools.partial(far_wendland_kernel, parts[0] + parts[1]),
+        out_shape=(
+            shape((2 * parts[2], owned), bf16),
+            shape((far_slots * owned, LANES), bf16),
+            shape((5 * per, LANES)),
+        ),
         in_specs=[VMEM] * 5,
         out_specs=(VMEM, VMEM, HBM),
         scratch_shapes=[pltpu.SemaphoreType.DMA],
         compiler_params=PARAMS,
         cost_estimate=wendland_cost,
         name="far_wendland",
-    )(left, right, part_sens, adjoint, low)
+    )(left, right, low, part_sens, adjoint)
     scale = 4.0 / math.sqrt(cells * peers)
     rows = 3 * FFD // LANES
     partial = pl.pallas_call(
         functools.partial(control_kernel, scale),
         out_shape=shape((rows, LANES)),
-        in_specs=[VMEM] * (len(all_sens) + 5),
+        in_specs=[VMEM] * (len(all_sens) + 6),
         out_specs=VMEM,
         compiler_params=PARAMS,
         name="control",
-    )(*all_sens, near_kernel, far_kernel, spread, near_hot, far_hot)
+    )(*all_sens, first_kernel, near_kernel, far_kernel, spread, near_hot, far_hot)
     rounds = sum_rounds()
     terms = [partial] if rounds else [lax.psum(partial, SUM_AXES)]
     for masks in rounds or ():

time: 31.1 us -> 31.1 us (level)
  waiting for transfers between devices: 5.7 us -> 5.29 us
  Pallas kernels: 12.2 us -> 12.6 us
    pallas_call x2, Pallas kernels: 4.78 us -> 5.52 us  [the longest x1 3 us: body(): pl.pallas_call(functools.partial(near_wendland_kernel, parts[0]), out_sha...]
    pallas_call x1, Pallas kernels: 2.32 us -> 1.98 us  [body(): pl.pallas_call(functools.partial(prepare_kernel, nodes), out_shape=(shape...]
    ppermute x2, starting transfers between devices: 4.73 us -> 5.07 us  [swaps(): return (lax.ppermute(array, SUM_AXES, pairs), close)]
    ppermute x1, starting transfers between devices: 1.58 us -> 1.25 us  [body(): all_sens.append(lax.ppermute(part_sens, 'nodes', ring))]
    ppermute x6, waiting for transfers between devices: 5.6 us -> 5.28 us  [exchanged(): lax.ppermute(value, SUM_AXES, [(i, i ^ mask) for i in range(peers)])]
  transfers between devices with their start and end apart: 11 -> 11, of which waited for: 6 -> 5; matrix products, arithmetic and copies ran while one was open for 0% -> 0% of each run, Pallas kernels for 23% -> 24%
where the time goes in v16:
time: 31.1 us; the launch traced here: 31 us
  Pallas kernels  12.6 us (41%)
  starting transfers between devices  12.3 us (40%)
  waiting for transfers between devices  5.29 us (17%)
  between operations  0.73 us (2%)
    ppermute x6, starting transfers between devices, exchanged(): lax.ppermute(value, SUM_AXES, [(i, i ^ mask) for i in range(peers)])  5.81 us
    ppermute x6, waiting for transfers between devices, exchanged(): lax.ppermute(value, SUM_AXES, [(i, i ^ mask) for i in range(peers)])  5.28 us
    ppermute x2, starting transfers between devices, swaps(): return (lax.ppermute(array, SUM_AXES, pairs), close)  5.07 us
    pallas_call x1, Pallas kernels, body(): pl.pallas_call(functools.partial(near_wendland_kernel, parts[0]), out_sha...  3 us
    pallas_call x1, Pallas kernels, body(): pl.pallas_call(functools.partial(far_wendland_kernel, parts[0] + parts[1]...  2.52 us
    pallas_call x1, Pallas kernels, body(): pl.pallas_call(functools.partial(prepare_kernel, nodes), out_shape=(shape...  1.98 us
    pallas_call x1, Pallas kernels, body(): pl.pallas_call(functools.partial(control_kernel, scale), out_shape=shape(...  1.85 us
    pallas_call x1, Pallas kernels, body(): pl.pallas_call(functools.partial(last_sweep_kernel, blocks), out_shape=(s...  1.33 us
  transfers between devices with their start and end apart: 11, of which 5 were waited for; matrix products, arithmetic and copies ran while one was open for 0% of the time, Pallas kernels for 24%

profile of v16, /device:TPU:0, one launch (start us, length us, event | category | flops | bytes accessed | tf_op | source)
XLA Modules:
  0.0 31.0 jit_solution(15906073342925492525)
XLA Ops:
  0.6 3.0 %collective-permute-start = (f32[80,128]{1,0:T(8,128)}, f32[80,128]{1,0:T(8,128)S(1)}, u32[]{:S(2)}, u32[]{:S(2)}) collective-permute-start(f32[80,128]{1,0:T(8,128)} %bitcast.38), channel_id=1, source_target_pairs={{0,2},{2,0},{1,4},{3,6},{4,1},{6,3},{5,8},{7,10},{8,5},{10,7},{9,1... | collective-permute-start | bytes 122888 | tf_op jit(solution)/shard_map/ppermute | solution.py:487
  3.6 0.2 collective-permute-start.1
  3.8 2.0 %prepare.1 = (f32[2400,128]{1,0:T(8,128)S(1)}, f32[400,128]{1,0:T(8,128)S(1)}, f32[80,128]{1,0:T(8,128)S(1)}, f32[240,128]{1,0:T(8,128)S(1)}, s32[96,128]{1,0:T(...) custom-call(bf16[2400,128]{1,0:T(8,128)(2,1)} %bitcast.32, ...), custom_call_target="tpu_custom_call" | custom-call | flops 1000000000 | bytes 10000000 | tf_op jit(solution)/shard_map/prepare/pallas_call | solution.py:491
  5.8 0.0 collective-permute-done.refs_0_
  5.8 0.0 collective-permute-done.1.refs_1_
  5.8 1.3 %sweep.1._.refs_2_ = f32[80,128]{1,0:T(8,128)S(1)} custom-call(f32[80,128]{1,0:T(8,128)S(1)} %collective-permute-done.refs_0_, f32[80,128]{1,0:T(8,128)S(1)} %collective-permute-done.1.refs_1_, f32[80,128]{1,0:T(8,128)S(1)} %get-tuple-element.24.refs_2_, f32[80,128]{1,0:T(8,128)S(1)} %get-tuple-element.25.refs_3_, ...), custom_call_target="tpu_custom_call" | custom-call | flops 716800 | bytes 1228800 | tf_op jit(solution)/shard_map/sweep/pallas_call | solution.py:546
  7.2 2.1 %collective-permute-start.2 = (f32[80,128]{1,0:T(8,128)S(1)}, f32[80,128]{1,0:T(8,128)S(1)}, u32[]{:S(2)}, u32[]{:S(2)}) collective-permute-start(f32[80,128]{1,0:T(8,128)S(1)} %sweep.1._.refs_2_), channel_id=1, source_target_pairs={{0,2},{2,0},{1,4},{3,6},{4,1},{6,3},{5,8},{7,10},{8,5},{10,7},{9,1... | collective-permute-start | bytes 122888 | tf_op jit(solution)/shard_map/ppermute | solution.py:487
  9.2 0.0 collective-permute-start.3
  9.2 3.0 %near_wendland.1 = (bf16[1024,2048]{1,0:T(8,128)(2,1)S(1)}, bf16[8192,128]{1,0:T(8,128)(2,1)S(1)}) custom-call(bf16[1024,64]{1,0:T(8,128)(2,1)S(1)} %get-tuple-element.21.left_ref, bf16[64,2048]{1,0:T(8,128)(2,1)S(1)} %get-tuple-element.22.right_ref, f32[8,2048]{1,0:T(8,128)S(1)} %get-tuple-element.23.low_ref, f32[80,128]{1,0:T(8,128)S(1)} %sweep.1._.refs_2_), custom_call_target="tpu_custom_call" | custom-call | flops 1000000000 | bytes 10000000 | tf_op jit(solution)/shard_map/near_wendland/pallas_call | solution.py:559
  12.2 0.0 collective-permute-done.2.refs_0_
  12.2 0.0 collective-permute-done.3.refs_1_
  12.3 1.3 %last_sweep.1 = (f32[80,128]{1,0:T(8,128)S(1)}, f32[24,128]{1,0:T(8,128)S(1)}) custom-call(f32[80,128]{1,0:T(8,128)S(1)} %collective-permute-done.2.refs_0_, f32[80,128]{1,0:T(8,128)S(1)} %collective-permute-done.3.refs_1_, f32[80,128]{1,0:T(8,128)S(1)} %sweep.1._.refs_2_, f32[80,128]{1,0:T(8,128)S(1)} %get-tuple-element.25.refs_3_, ...), custom_call_target="tpu_custom_call" | custom-call | flops 716800 | bytes 1228800 | tf_op jit(solution)/shard_map/last_sweep/pallas_call | solution.py:571
  13.6 1.2 %collective-permute-start.4 = (f32[24,128]{1,0:T(8,128)S(1)}, f32[24,128]{1,0:T(8,128)S(1)}, u32[]{:S(2)}, u32[]{:S(2)}) collective-permute-start(f32[24,128]{1,0:T(8,128)S(1)} %get-tuple-element.32._.refs_0_), channel_id=1, source_target_pairs={{0,2},{2,0},{1,3},{3,1},{4,6},{6,4},{5,7},{7,5},{8,10},{10,8},{9,1... | collective-permute-start | bytes 36872 | tf_op jit(solution)/shard_map/ppermute | solution.py:585
  14.8 2.5 %far_wendland.1 = (bf16[768,2048]{1,0:T(8,128)(2,1)S(1)}, bf16[8192,128]{1,0:T(8,128)(2,1)S(1)}, f32[80,128]{1,0:T(8,128)}) custom-call(bf16[1024,64]{1,0:T(8,128)(2,1)S(1)} %get-tuple-element.21.left_ref, bf16[64,2048]{1,0:T(8,128)(2,1)S(1)} %get-tuple-element.22.right_ref, f32[8,2048]{1,0:T(8,128)S(1)} %get-tuple-element.23.low_ref, ...), custom_call_target="tpu_custom_call" | custom-call | flops 1000000000 | bytes 10000000 | tf_op jit(solution)/shard_map/far_wendland/pallas_call | solution.py:586
  17.4 0.0 collective-permute-done.4.refs_1_
  17.4 1.8 %control.1.refs_0_ = f32[12,128]{1,0:T(8,128)S(1)} custom-call(f32[24,128]{1,0:T(8,128)S(1)} %get-tuple-element.32._.refs_0_, f32[24,128]{1,0:T(8,128)S(1)} %collective-permute-done.4.refs_1_, bf16[256,2048]{1,0:T(8,128)(2,1)S(1)} %get-tuple-element.35.refs_2_, bf16[1024,2048]{1,0:T(8,128)(2,1)S(1)} %get-tuple-element.31.refs_9_.refs_3_, ...), custom_call_target="tpu_custom_call" | custom-call | tf_op jit(solution)/shard_map/control/pallas_call | solution.py:602
  19.2 0.1 collective-permute-start.5
  19.3 1.6 %collective-permute-start.6 = (f32[12,128]{1,0:T(8,128)S(1)}, f32[12,128]{1,0:T(8,128)S(1)}, u32[]{:S(2)}, u32[]{:S(2)}) collective-permute-start(f32[12,128]{1,0:T(8,128)S(1)} %control.1.refs_0_), channel_id=1, source_target_pairs={{0,4},{1,5},{2,6},{3,7},{4,0},{5,1},{6,2},{7,3},{8,12},{9,13},{10,... | collective-permute-start | bytes 18440 | tf_op jit(solution)/shard_map/ppermute | solution.py:434
  21.0 0.2 collective-permute-start.7
  21.2 0.0 collective-permute-done.5.refs_1_
  21.2 1.9 %collective-permute-done.6.refs_2_ = f32[12,128]{1,0:T(8,128)S(1)} collective-permute-done((f32[12,128]{1,0:T(8,128)S(1)}, f32[12,128]{1,0:T(8,128)S(1)}, u32[]{:S(2)}, u32[]{:S(2)}) %collective-permute-start.6) | collective-permute-done | bytes 6176 | tf_op jit(solution)/shard_map/ppermute | solution.py:434
  23.0 1.0 %collective-permute-done.7.refs_3_ = f32[12,128]{1,0:T(8,128)S(1)} collective-permute-done((f32[12,128]{1,0:T(8,128)S(1)}, f32[12,128]{1,0:T(8,128)S(1)}, u32[]{:S(2)}, u32[]{:S(2)}) %collective-permute-start.7) | collective-permute-done | bytes 6176 | tf_op jit(solution)/shard_map/ppermute | solution.py:434
  24.0 1.8 %collective-permute-start.10 = (f32[12,128]{1,0:T(8,128)S(1)}, f32[12,128]{1,0:T(8,128)S(1)}, u32[]{:S(2)}, u32[]{:S(2)}) collective-permute-start(f32[12,128]{1,0:T(8,128)S(1)} %add.1.refs_0_), channel_id=1, source_target_pairs={{0,11},{1,10},{2,9},{3,8},{4,15},{5,14},{6,13},{7,12},{8,3},{9,2},... | collective-permute-start | bytes 18440 | tf_op jit(solution)/shard_map/ppermute | solution.py:434
  25.9 1.4 %collective-permute-start.8 = (f32[12,128]{1,0:T(8,128)S(1)}, f32[12,128]{1,0:T(8,128)S(1)}, u32[]{:S(2)}, u32[]{:S(2)}) collective-permute-start(f32[12,128]{1,0:T(8,128)S(1)} %add.1.refs_0_), channel_id=1, source_target_pairs={{0,9},{1,8},{2,11},{3,10},{4,13},{5,12},{6,15},{7,14},{8,1},{9,0},... | collective-permute-start | bytes 18440 | tf_op jit(solution)/shard_map/ppermute | solution.py:434
  27.3 0.6 %collective-permute-start.9 = (f32[12,128]{1,0:T(8,128)S(1)}, f32[12,128]{1,0:T(8,128)S(1)}, u32[]{:S(2)}, u32[]{:S(2)}) collective-permute-start(f32[12,128]{1,0:T(8,128)S(1)} %add.1.refs_0_), channel_id=1, source_target_pairs={{0,3},{1,2},{2,1},{3,0},{4,7},{5,6},{6,5},{7,4},{8,11},{9,10},{10,... | collective-permute-start | bytes 18440 | tf_op jit(solution)/shard_map/ppermute | solution.py:434
  27.9 1.0 %collective-permute-done.10.refs_3_ = f32[12,128]{1,0:T(8,128)S(1)} collective-permute-done((f32[12,128]{1,0:T(8,128)S(1)}, f32[12,128]{1,0:T(8,128)S(1)}, u32[]{:S(2)}, u32[]{:S(2)}) %collective-permute-start.10) | collective-permute-done | bytes 6176 | tf_op jit(solution)/shard_map/ppermute | solution.py:434
  28.9 0.9 %collective-permute-done.8.refs_1_ = f32[12,128]{1,0:T(8,128)S(1)} collective-permute-done((f32[12,128]{1,0:T(8,128)S(1)}, f32[12,128]{1,0:T(8,128)S(1)}, u32[]{:S(2)}, u32[]{:S(2)}) %collective-permute-start.8) | collective-permute-done | bytes 6176 | tf_op jit(solution)/shard_map/ppermute | solution.py:434
  29.8 0.5 %collective-permute-done.9.refs_2_ = f32[12,128]{1,0:T(8,128)S(1)} collective-permute-done((f32[12,128]{1,0:T(8,128)S(1)}, f32[12,128]{1,0:T(8,128)S(1)}, u32[]{:S(2)}, u32[]{:S(2)}) %collective-permute-start.9) | collective-permute-done | bytes 6176 | tf_op jit(solution)/shard_map/ppermute | solution.py:434
  30.3 0.6 %finish.1 = f32[3,512]{1,0:T(4,128)} custom-call(f32[12,128]{1,0:T(8,128)S(1)} %add.1.refs_0_, f32[12,128]{1,0:T(8,128)S(1)} %collective-permute-done.8.refs_1_, f32[12,128]{1,0:T(8,128)S(1)} %collective-permute-done.9.refs_2_, f32[12,128]{1,0:T(8,128)S(1)} %collective-permute-done.10.refs_3_), custom_call_target="tpu_custom_call" | custom-call | tf_op jit(solution)/shard_map/finish/pallas_call | solution.py:618
  (1 shorter events, 0.0 us)
Async XLA Ops:
  0.6 5.2 %collective-permute-start = (f32[80,128]{1,0:T(8,128)}, f32[80,128]{1,0:T(8,128)S(1)}, u32[]{:S(2)}, u32[]{:S(2)}) collective-permute-start(f32[80,128]{1,0:T(8,128)} %bitcast.38), channel_id=1, source_target_pairs={{0,2},{2,0},{1,4},{3,6},{4,1},{6,3},{5,8},{7,10},{8,5},{10,7},{9,1... | collective-permute-start | bytes 122888 | tf_op jit(solution)/shard_map/ppermute | solution.py:487
  3.6 2.2 %collective-permute-start.1 = (f32[80,128]{1,0:T(8,128)}, f32[80,128]{1,0:T(8,128)S(1)}, u32[]{:S(2)}, u32[]{:S(2)}) collective-permute-start(f32[80,128]{1,0:T(8,128)} %bitcast.39), channel_id=1, source_target_pairs={{0,1},{1,0},{4,5},{5,4},{8,9},{9,8},{12,13},{13,12},{2,3},{3,2},{6... | collective-permute-start | bytes 122888 | tf_op jit(solution)/shard_map/ppermute | solution.py:472
  7.2 5.1 %collective-permute-start.2 = (f32[80,128]{1,0:T(8,128)S(1)}, f32[80,128]{1,0:T(8,128)S(1)}, u32[]{:S(2)}, u32[]{:S(2)}) collective-permute-start(f32[80,128]{1,0:T(8,128)S(1)} %sweep.1._.refs_2_), channel_id=1, source_target_pairs={{0,2},{2,0},{1,4},{3,6},{4,1},{6,3},{5,8},{7,10},{8,5},{10,7},{9,1... | collective-permute-start | bytes 122888 | tf_op jit(solution)/shard_map/ppermute | solution.py:487
  9.2 3.0 %collective-permute-start.3 = (f32[80,128]{1,0:T(8,128)S(1)}, f32[80,128]{1,0:T(8,128)S(1)}, u32[]{:S(2)}, u32[]{:S(2)}) collective-permute-start(f32[80,128]{1,0:T(8,128)S(1)} %sweep.1._.refs_2_), channel_id=1, source_target_pairs={{0,1},{1,0},{4,5},{5,4},{8,9},{9,8},{12,13},{13,12},{2,3},{3,2},{6... | collective-permute-start | bytes 122888 | tf_op jit(solution)/shard_map/ppermute | solution.py:472
  13.6 3.8 %collective-permute-start.4 = (f32[24,128]{1,0:T(8,128)S(1)}, f32[24,128]{1,0:T(8,128)S(1)}, u32[]{:S(2)}, u32[]{:S(2)}) collective-permute-start(f32[24,128]{1,0:T(8,128)S(1)} %get-tuple-element.32._.refs_0_), channel_id=1, source_target_pairs={{0,2},{2,0},{1,3},{3,1},{4,6},{6,4},{5,7},{7,5},{8,10},{10,8},{9,1... | collective-permute-start | bytes 36872 | tf_op jit(solution)/shard_map/ppermute | solution.py:585
  19.2 1.9 %collective-permute-start.5 = (f32[12,128]{1,0:T(8,128)S(1)}, f32[12,128]{1,0:T(8,128)S(1)}, u32[]{:S(2)}, u32[]{:S(2)}) collective-permute-start(f32[12,128]{1,0:T(8,128)S(1)} %control.1.refs_0_), channel_id=1, source_target_pairs={{0,1},{1,0},{2,3},{3,2},{4,5},{5,4},{6,7},{7,6},{8,9},{9,8},{10,11... | collective-permute-start | bytes 18440 | tf_op jit(solution)/shard_map/ppermute | solution.py:434
  19.3 3.7 %collective-permute-start.6 = (f32[12,128]{1,0:T(8,128)S(1)}, f32[12,128]{1,0:T(8,128)S(1)}, u32[]{:S(2)}, u32[]{:S(2)}) collective-permute-start(f32[12,128]{1,0:T(8,128)S(1)} %control.1.refs_0_), channel_id=1, source_target_pairs={{0,4},{1,5},{2,6},{3,7},{4,0},{5,1},{6,2},{7,3},{8,12},{9,13},{10,... | collective-permute-start | bytes 18440 | tf_op jit(solution)/shard_map/ppermute | solution.py:434
  21.0 3.1 %collective-permute-start.7 = (f32[12,128]{1,0:T(8,128)S(1)}, f32[12,128]{1,0:T(8,128)S(1)}, u32[]{:S(2)}, u32[]{:S(2)}) collective-permute-start(f32[12,128]{1,0:T(8,128)S(1)} %control.1.refs_0_), channel_id=1, source_target_pairs={{0,5},{1,4},{2,7},{3,6},{4,1},{5,0},{6,3},{7,2},{8,13},{9,12},{10,... | collective-permute-start | bytes 18440 | tf_op jit(solution)/shard_map/ppermute | solution.py:434
  24.0 4.9 %collective-permute-start.10 = (f32[12,128]{1,0:T(8,128)S(1)}, f32[12,128]{1,0:T(8,128)S(1)}, u32[]{:S(2)}, u32[]{:S(2)}) collective-permute-start(f32[12,128]{1,0:T(8,128)S(1)} %add.1.refs_0_), channel_id=1, source_target_pairs={{0,11},{1,10},{2,9},{3,8},{4,15},{5,14},{6,13},{7,12},{8,3},{9,2},... | collective-permute-start | bytes 18440 | tf_op jit(solution)/shard_map/ppermute | solution.py:434
  25.9 4.0 %collective-permute-start.8 = (f32[12,128]{1,0:T(8,128)S(1)}, f32[12,128]{1,0:T(8,128)S(1)}, u32[]{:S(2)}, u32[]{:S(2)}) collective-permute-start(f32[12,128]{1,0:T(8,128)S(1)} %add.1.refs_0_), channel_id=1, source_target_pairs={{0,9},{1,8},{2,11},{3,10},{4,13},{5,12},{6,15},{7,14},{8,1},{9,0},... | collective-permute-start | bytes 18440 | tf_op jit(solution)/shard_map/ppermute | solution.py:434
  27.3 3.1 %collective-permute-start.9 = (f32[12,128]{1,0:T(8,128)S(1)}, f32[12,128]{1,0:T(8,128)S(1)}, u32[]{:S(2)}, u32[]{:S(2)}) collective-permute-start(f32[12,128]{1,0:T(8,128)S(1)} %add.1.refs_0_), channel_id=1, source_target_pairs={{0,3},{1,2},{2,1},{3,0},{4,7},{5,6},{6,5},{7,4},{8,11},{9,10},{10,... | collective-permute-start | bytes 18440 | tf_op jit(solution)/shard_map/ppermute | solution.py:434

commit v17 on v13

--- a/solution.py
+++ b/solution.py
@@ -302,7 +302,7 @@
         squared = jnp.maximum(following, 1e-30)
         if at + 1 < len(places):
             following = squares(*places[at + 1])
-        near = jnp.maximum(1.0 - squared * lax.rsqrt(squared), 0.0)
+        near = jnp.maximum(1.0 - jnp.exp(0.5 * jnp.log(squared)), 0.0)
         power = near * near
         kernel = power * power * (1.25 - near)
         first = kernel.astype(jnp.bfloat16)

time: 30.5 us -> 30.9 us (1.013)
  Pallas kernels: 12.2 us -> 12.8 us
  starting transfers between devices: 12.2 us -> 11.7 us
    ppermute x1, starting transfers between devices: 1.31 us -> 0.89 us  [body(): all_sens.append(lax.ppermute(part_sens, 'nodes', ring))]
    pallas_call x1, Pallas kernels: 2.72 us -> 3.14 us  [body(): pl.pallas_call(functools.partial(wendland_kernel, 0), out_shape=near_shap...]
  transfers between devices with their start and end apart: 11 -> 11, of which waited for: 5 -> 6; matrix products, arithmetic and copies ran while one was open for 0% -> 0% of each run, Pallas kernels for 23% -> 25%
where the time goes in v17:
time: 30.9 us; the launch traced here: 30.8 us
  Pallas kernels  12.8 us (41%)
  starting transfers between devices  11.7 us (38%)
  waiting for transfers between devices  5.53 us (18%)
  between operations  0.72 us (2%)
    ppermute x6, starting transfers between devices, exchanged(): lax.ppermute(value, SUM_AXES, [(i, i ^ mask) for i in range(peers)])  5.73 us
    ppermute x6, waiting for transfers between devices, exchanged(): lax.ppermute(value, SUM_AXES, [(i, i ^ mask) for i in range(peers)])  4.89 us
    ppermute x2, starting transfers between devices, swaps(): return (lax.ppermute(array, SUM_AXES, pairs), close)  4.34 us
    pallas_call x1, Pallas kernels, body(): pl.pallas_call(functools.partial(wendland_kernel, 0), out_shape=near_shap...  3.14 us
    pallas_call x1, Pallas kernels, body(): pl.pallas_call(functools.partial(prepare_kernel, nodes), out_shape=(shape...  2.32 us
    pallas_call x1, Pallas kernels, body(): pl.pallas_call(functools.partial(far_wendland_kernel, half), out_shape=(f...  2.23 us
    pallas_call x1, Pallas kernels, body(): pl.pallas_call(functools.partial(control_kernel, scale), out_shape=shape(...  1.85 us
    pallas_call x1, Pallas kernels, body(): pl.pallas_call(functools.partial(last_sweep_kernel, blocks), out_shape=(s...  1.32 us
  transfers between devices with their start and end apart: 11, of which 6 were waited for; matrix products, arithmetic and copies ran while one was open for 0% of the time, Pallas kernels for 25%

profile of v17, /device:TPU:0, one launch (start us, length us, event | category | flops | bytes accessed | tf_op | source)
XLA Modules:
  0.0 30.8 jit_solution(2000436201820215712)
XLA Ops:
  0.6 0.5 %collective-permute-start = (f32[80,128]{1,0:T(8,128)}, f32[80,128]{1,0:T(8,128)S(1)}, u32[]{:S(2)}, u32[]{:S(2)}) collective-permute-start(f32[80,128]{1,0:T(8,128)} %bitcast.38), channel_id=1, source_target_pairs={{0,1},{1,0},{4,5},{5,4},{8,9},{9,8},{12,13},{13,12},{2,3},{3,2},{6... | collective-permute-start | bytes 122888 | tf_op jit(solution)/shard_map/ppermute | solution.py:455
  1.2 2.6 %collective-permute-start.1 = (f32[80,128]{1,0:T(8,128)}, f32[80,128]{1,0:T(8,128)S(1)}, u32[]{:S(2)}, u32[]{:S(2)}) collective-permute-start(f32[80,128]{1,0:T(8,128)} %bitcast.39), channel_id=1, source_target_pairs={{0,2},{2,0},{1,4},{3,6},{4,1},{6,3},{5,8},{7,10},{8,5},{10,7},{9,1... | collective-permute-start | bytes 122888 | tf_op jit(solution)/shard_map/ppermute | solution.py:470
  3.7 2.3 %prepare.1 = (f32[2400,128]{1,0:T(8,128)S(1)}, f32[400,128]{1,0:T(8,128)S(1)}, f32[80,128]{1,0:T(8,128)S(1)}, f32[240,128]{1,0:T(8,128)S(1)}, s32[96,128]{1,0:T(...) custom-call(bf16[2400,128]{1,0:T(8,128)(2,1)} %bitcast.32, ...), custom_call_target="tpu_custom_call" | custom-call | flops 1000000000 | bytes 10000000 | tf_op jit(solution)/shard_map/prepare/pallas_call | solution.py:474
  6.0 0.0 collective-permute-done.refs_0_
  6.0 0.0 collective-permute-done.1.refs_1_
  6.1 1.3 %sweep.1._.refs_2_ = f32[80,128]{1,0:T(8,128)S(1)} custom-call(f32[80,128]{1,0:T(8,128)S(1)} %collective-permute-done.refs_0_, f32[80,128]{1,0:T(8,128)S(1)} %collective-permute-done.1.refs_1_, f32[80,128]{1,0:T(8,128)S(1)} %get-tuple-element.21.refs_2_, f32[80,128]{1,0:T(8,128)S(1)} %get-tuple-element.22.refs_3_, ...), custom_call_target="tpu_custom_call" | custom-call | flops 716800 | bytes 1228800 | tf_op jit(solution)/shard_map/sweep/pallas_call | solution.py:529
  7.4 0.3 collective-permute-start.2
  7.6 1.8 %collective-permute-start.3 = (f32[80,128]{1,0:T(8,128)S(1)}, f32[80,128]{1,0:T(8,128)S(1)}, u32[]{:S(2)}, u32[]{:S(2)}) collective-permute-start(f32[80,128]{1,0:T(8,128)S(1)} %sweep.1._.refs_2_), channel_id=1, source_target_pairs={{0,2},{2,0},{1,4},{3,6},{4,1},{6,3},{5,8},{7,10},{8,5},{10,7},{9,1... | collective-permute-start | bytes 122888 | tf_op jit(solution)/shard_map/ppermute | solution.py:470
  9.4 3.1 %near_wendland.1.refs_9_.refs_2_ = bf16[1280,2048]{1,0:T(8,128)(2,1)S(1)} custom-call(bf16[1024,64]{1,0:T(8,128)(2,1)S(1)} %get-tuple-element.19.left_ref, bf16[64,2048]{1,0:T(8,128)(2,1)S(1)} %get-tuple-element.20.right_ref, f32[80,128]{1,0:T(8,128)S(1)} %sweep.1._.refs_2_), custom_call_target="tpu_custom_call" | custom-call | flops 1000000000 | bytes 10000000 | tf_op jit(solution)/shard_map/near_wendland/pallas_call | solution.py:545
  12.6 0.0 collective-permute-done.2.refs_0_
  12.6 0.0 collective-permute-done.3.refs_1_
  12.6 1.3 %last_sweep.1 = (f32[80,128]{1,0:T(8,128)S(1)}, f32[24,128]{1,0:T(8,128)S(1)}) custom-call(f32[80,128]{1,0:T(8,128)S(1)} %collective-permute-done.2.refs_0_, f32[80,128]{1,0:T(8,128)S(1)} %collective-permute-done.3.refs_1_, f32[80,128]{1,0:T(8,128)S(1)} %sweep.1._.refs_2_, f32[80,128]{1,0:T(8,128)S(1)} %get-tuple-element.22.refs_3_, ...), custom_call_target="tpu_custom_call" | custom-call | flops 716800 | bytes 1228800 | tf_op jit(solution)/shard_map/last_sweep/pallas_call | solution.py:554
  13.9 0.9 %collective-permute-start.4 = (f32[24,128]{1,0:T(8,128)S(1)}, f32[24,128]{1,0:T(8,128)S(1)}, u32[]{:S(2)}, u32[]{:S(2)}) collective-permute-start(f32[24,128]{1,0:T(8,128)S(1)} %get-tuple-element.28.after.refs_0_), channel_id=1, source_target_pairs={{0,2},{2,0},{1,3},{3,1},{4,6},{6,4},{5,7},{7,5},{8,10},{10,8},{9,1... | collective-permute-start | bytes 36872 | tf_op jit(solution)/shard_map/ppermute | solution.py:568
  14.8 2.2 %far_wendland.1 = (bf16[768,2048]{1,0:T(8,128)(2,1)S(1)}, bf16[6144,128]{1,0:T(8,128)(2,1)S(1)}, f32[80,128]{1,0:T(8,128)}) custom-call(bf16[1024,64]{1,0:T(8,128)(2,1)S(1)} %get-tuple-element.19.left_ref, bf16[64,2048]{1,0:T(8,128)(2,1)S(1)} %get-tuple-element.20.right_ref, f32[24,128]{1,0:T(8,128)S(1)} %get-tuple-element.28.after.refs_0_, ...), custom_call_target="tpu_custom_call" | custom-call | flops 1000000000 | bytes 10000000 | tf_op jit(solution)/shard_map/far_wendland/pallas_call | solution.py:570
  17.0 0.6 %collective-permute-done.4.refs_1_ = f32[24,128]{1,0:T(8,128)S(1)} collective-permute-done((f32[24,128]{1,0:T(8,128)S(1)}, f32[24,128]{1,0:T(8,128)S(1)}, u32[]{:S(2)}, u32[]{:S(2)}) %collective-permute-start.4) | collective-permute-done | bytes 12320 | tf_op jit(solution)/shard_map/ppermute | solution.py:568
  17.7 1.8 %control.1.refs_0_ = f32[12,128]{1,0:T(8,128)S(1)} custom-call(f32[24,128]{1,0:T(8,128)S(1)} %get-tuple-element.28.after.refs_0_, f32[24,128]{1,0:T(8,128)S(1)} %collective-permute-done.4.refs_1_, bf16[1280,2048]{1,0:T(8,128)(2,1)S(1)} %near_wendland.1.refs_9_.refs_2_, bf16[768,2048]{1,0:T(8,128)(2,1)S(1)} %get-tuple-element.32.refs_3_, ...), custom_call_target="tpu_custom_call" | custom-call | tf_op jit(solution)/shard_map/control/pallas_call | solution.py:582
  19.5 0.1 collective-permute-start.5
  19.6 1.3 %collective-permute-start.6 = (f32[12,128]{1,0:T(8,128)S(1)}, f32[12,128]{1,0:T(8,128)S(1)}, u32[]{:S(2)}, u32[]{:S(2)}) collective-permute-start(f32[12,128]{1,0:T(8,128)S(1)} %control.1.refs_0_), channel_id=1, source_target_pairs={{0,4},{1,5},{2,6},{3,7},{4,0},{5,1},{6,2},{7,3},{8,12},{9,13},{10,... | collective-permute-start | bytes 18440 | tf_op jit(solution)/shard_map/ppermute | solution.py:419
  20.9 0.6 %collective-permute-start.7 = (f32[12,128]{1,0:T(8,128)S(1)}, f32[12,128]{1,0:T(8,128)S(1)}, u32[]{:S(2)}, u32[]{:S(2)}) collective-permute-start(f32[12,128]{1,0:T(8,128)S(1)} %control.1.refs_0_), channel_id=1, source_target_pairs={{0,5},{1,4},{2,7},{3,6},{4,1},{5,0},{6,3},{7,2},{8,13},{9,12},{10,... | collective-permute-start | bytes 18440 | tf_op jit(solution)/shard_map/ppermute | solution.py:419
  21.5 0.0 collective-permute-done.5.refs_1_
  21.5 1.9 %collective-permute-done.6.refs_2_ = f32[12,128]{1,0:T(8,128)S(1)} collective-permute-done((f32[12,128]{1,0:T(8,128)S(1)}, f32[12,128]{1,0:T(8,128)S(1)}, u32[]{:S(2)}, u32[]{:S(2)}) %collective-permute-start.6) | collective-permute-done | bytes 6176 | tf_op jit(solution)/shard_map/ppermute | solution.py:419
  23.3 0.7 %collective-permute-done.7.refs_3_ = f32[12,128]{1,0:T(8,128)S(1)} collective-permute-done((f32[12,128]{1,0:T(8,128)S(1)}, f32[12,128]{1,0:T(8,128)S(1)}, u32[]{:S(2)}, u32[]{:S(2)}) %collective-permute-start.7) | collective-permute-done | bytes 6176 | tf_op jit(solution)/shard_map/ppermute | solution.py:419
  24.0 2.0 %collective-permute-start.10 = (f32[12,128]{1,0:T(8,128)S(1)}, f32[12,128]{1,0:T(8,128)S(1)}, u32[]{:S(2)}, u32[]{:S(2)}) collective-permute-start(f32[12,128]{1,0:T(8,128)S(1)} %add.1.refs_0_), channel_id=1, source_target_pairs={{0,11},{1,10},{2,9},{3,8},{4,15},{5,14},{6,13},{7,12},{8,3},{9,2},... | collective-permute-start | bytes 18440 | tf_op jit(solution)/shard_map/ppermute | solution.py:419
  26.0 1.1 %collective-permute-start.8 = (f32[12,128]{1,0:T(8,128)S(1)}, f32[12,128]{1,0:T(8,128)S(1)}, u32[]{:S(2)}, u32[]{:S(2)}) collective-permute-start(f32[12,128]{1,0:T(8,128)S(1)} %add.1.refs_0_), channel_id=1, source_target_pairs={{0,9},{1,8},{2,11},{3,10},{4,13},{5,12},{6,15},{7,14},{8,1},{9,0},... | collective-permute-start | bytes 18440 | tf_op jit(solution)/shard_map/ppermute | solution.py:419
  27.1 0.7 %collective-permute-start.9 = (f32[12,128]{1,0:T(8,128)S(1)}, f32[12,128]{1,0:T(8,128)S(1)}, u32[]{:S(2)}, u32[]{:S(2)}) collective-permute-start(f32[12,128]{1,0:T(8,128)S(1)} %add.1.refs_0_), channel_id=1, source_target_pairs={{0,3},{1,2},{2,1},{3,0},{4,7},{5,6},{6,5},{7,4},{8,11},{9,10},{10,... | collective-permute-start | bytes 18440 | tf_op jit(solution)/shard_map/ppermute | solution.py:419
  27.8 1.1 %collective-permute-done.10.refs_3_ = f32[12,128]{1,0:T(8,128)S(1)} collective-permute-done((f32[12,128]{1,0:T(8,128)S(1)}, f32[12,128]{1,0:T(8,128)S(1)}, u32[]{:S(2)}, u32[]{:S(2)}) %collective-permute-start.10) | collective-permute-done | bytes 6176 | tf_op jit(solution)/shard_map/ppermute | solution.py:419
  28.9 1.1 %collective-permute-done.8.refs_1_ = f32[12,128]{1,0:T(8,128)S(1)} collective-permute-done((f32[12,128]{1,0:T(8,128)S(1)}, f32[12,128]{1,0:T(8,128)S(1)}, u32[]{:S(2)}, u32[]{:S(2)}) %collective-permute-start.8) | collective-permute-done | bytes 6176 | tf_op jit(solution)/shard_map/ppermute | solution.py:419
  30.0 0.2 collective-permute-done.9.refs_2_
  30.2 0.6 %finish.1 = f32[3,512]{1,0:T(4,128)} custom-call(f32[12,128]{1,0:T(8,128)S(1)} %add.1.refs_0_, f32[12,128]{1,0:T(8,128)S(1)} %collective-permute-done.8.refs_1_, f32[12,128]{1,0:T(8,128)S(1)} %collective-permute-done.9.refs_2_, f32[12,128]{1,0:T(8,128)S(1)} %collective-permute-done.10.refs_3_), custom_call_target="tpu_custom_call" | custom-call | tf_op jit(solution)/shard_map/finish/pallas_call | solution.py:598
  (1 shorter events, 0.0 us)
Async XLA Ops:
  0.6 5.4 %collective-permute-start = (f32[80,128]{1,0:T(8,128)}, f32[80,128]{1,0:T(8,128)S(1)}, u32[]{:S(2)}, u32[]{:S(2)}) collective-permute-start(f32[80,128]{1,0:T(8,128)} %bitcast.38), channel_id=1, source_target_pairs={{0,1},{1,0},{4,5},{5,4},{8,9},{9,8},{12,13},{13,12},{2,3},{3,2},{6... | collective-permute-start | bytes 122888 | tf_op jit(solution)/shard_map/ppermute | solution.py:455
  1.2 4.9 %collective-permute-start.1 = (f32[80,128]{1,0:T(8,128)}, f32[80,128]{1,0:T(8,128)S(1)}, u32[]{:S(2)}, u32[]{:S(2)}) collective-permute-start(f32[80,128]{1,0:T(8,128)} %bitcast.39), channel_id=1, source_target_pairs={{0,2},{2,0},{1,4},{3,6},{4,1},{6,3},{5,8},{7,10},{8,5},{10,7},{9,1... | collective-permute-start | bytes 122888 | tf_op jit(solution)/shard_map/ppermute | solution.py:470
  7.4 5.2 %collective-permute-start.2 = (f32[80,128]{1,0:T(8,128)S(1)}, f32[80,128]{1,0:T(8,128)S(1)}, u32[]{:S(2)}, u32[]{:S(2)}) collective-permute-start(f32[80,128]{1,0:T(8,128)S(1)} %sweep.1._.refs_2_), channel_id=1, source_target_pairs={{0,1},{1,0},{4,5},{5,4},{8,9},{9,8},{12,13},{13,12},{2,3},{3,2},{6... | collective-permute-start | bytes 122888 | tf_op jit(solution)/shard_map/ppermute | solution.py:455
  7.6 4.9 %collective-permute-start.3 = (f32[80,128]{1,0:T(8,128)S(1)}, f32[80,128]{1,0:T(8,128)S(1)}, u32[]{:S(2)}, u32[]{:S(2)}) collective-permute-start(f32[80,128]{1,0:T(8,128)S(1)} %sweep.1._.refs_2_), channel_id=1, source_target_pairs={{0,2},{2,0},{1,4},{3,6},{4,1},{6,3},{5,8},{7,10},{8,5},{10,7},{9,1... | collective-permute-start | bytes 122888 | tf_op jit(solution)/shard_map/ppermute | solution.py:470
  13.9 3.8 %collective-permute-start.4 = (f32[24,128]{1,0:T(8,128)S(1)}, f32[24,128]{1,0:T(8,128)S(1)}, u32[]{:S(2)}, u32[]{:S(2)}) collective-permute-start(f32[24,128]{1,0:T(8,128)S(1)} %get-tuple-element.28.after.refs_0_), channel_id=1, source_target_pairs={{0,2},{2,0},{1,3},{3,1},{4,6},{6,4},{5,7},{7,5},{8,10},{10,8},{9,1... | collective-permute-start | bytes 36872 | tf_op jit(solution)/shard_map/ppermute | solution.py:568
  19.5 1.9 %collective-permute-start.5 = (f32[12,128]{1,0:T(8,128)S(1)}, f32[12,128]{1,0:T(8,128)S(1)}, u32[]{:S(2)}, u32[]{:S(2)}) collective-permute-start(f32[12,128]{1,0:T(8,128)S(1)} %control.1.refs_0_), channel_id=1, source_target_pairs={{0,1},{1,0},{2,3},{3,2},{4,5},{5,4},{6,7},{7,6},{8,9},{9,8},{10,11... | collective-permute-start | bytes 18440 | tf_op jit(solution)/shard_map/ppermute | solution.py:419
  19.6 3.7 %collective-permute-start.6 = (f32[12,128]{1,0:T(8,128)S(1)}, f32[12,128]{1,0:T(8,128)S(1)}, u32[]{:S(2)}, u32[]{:S(2)}) collective-permute-start(f32[12,128]{1,0:T(8,128)S(1)} %control.1.refs_0_), channel_id=1, source_target_pairs={{0,4},{1,5},{2,6},{3,7},{4,0},{5,1},{6,2},{7,3},{8,12},{9,13},{10,... | collective-permute-start | bytes 18440 | tf_op jit(solution)/shard_map/ppermute | solution.py:419
  20.9 3.1 %collective-permute-start.7 = (f32[12,128]{1,0:T(8,128)S(1)}, f32[12,128]{1,0:T(8,128)S(1)}, u32[]{:S(2)}, u32[]{:S(2)}) collective-permute-start(f32[12,128]{1,0:T(8,128)S(1)} %control.1.refs_0_), channel_id=1, source_target_pairs={{0,5},{1,4},{2,7},{3,6},{4,1},{5,0},{6,3},{7,2},{8,13},{9,12},{10,... | collective-permute-start | bytes 18440 | tf_op jit(solution)/shard_map/ppermute | solution.py:419
  24.0 4.9 %collective-permute-start.10 = (f32[12,128]{1,0:T(8,128)S(1)}, f32[12,128]{1,0:T(8,128)S(1)}, u32[]{:S(2)}, u32[]{:S(2)}) collective-permute-start(f32[12,128]{1,0:T(8,128)S(1)} %add.1.refs_0_), channel_id=1, source_target_pairs={{0,11},{1,10},{2,9},{3,8},{4,15},{5,14},{6,13},{7,12},{8,3},{9,2},... | collective-permute-start | bytes 18440 | tf_op jit(solution)/shard_map/ppermute | solution.py:419
  26.0 4.0 %collective-permute-start.8 = (f32[12,128]{1,0:T(8,128)S(1)}, f32[12,128]{1,0:T(8,128)S(1)}, u32[]{:S(2)}, u32[]{:S(2)}) collective-permute-start(f32[12,128]{1,0:T(8,128)S(1)} %add.1.refs_0_), channel_id=1, source_target_pairs={{0,9},{1,8},{2,11},{3,10},{4,13},{5,12},{6,15},{7,14},{8,1},{9,0},... | collective-permute-start | bytes 18440 | tf_op jit(solution)/shard_map/ppermute | solution.py:419
  27.1 3.1 %collective-permute-start.9 = (f32[12,128]{1,0:T(8,128)S(1)}, f32[12,128]{1,0:T(8,128)S(1)}, u32[]{:S(2)}, u32[]{:S(2)}) collective-permute-start(f32[12,128]{1,0:T(8,128)S(1)} %add.1.refs_0_), channel_id=1, source_target_pairs={{0,3},{1,2},{2,1},{3,0},{4,7},{5,6},{6,5},{7,4},{8,11},{9,10},{10,... | collective-permute-start | bytes 18440 | tf_op jit(solution)/shard_map/ppermute | solution.py:419

commit v18 on v17

--- a/solution.py
+++ b/solution.py
@@ -8,7 +8,6 @@
 from jax.experimental.pallas import tpu as pltpu
 from jax.sharding import PartitionSpec as P
 
-SWEEPS = 2
 FFD = 512
 SUPPORT_RADIUS = 0.3
 LANES = 128
@@ -179,8 +178,9 @@
 
 def sweep_into(
     blocks, first_ref, second_ref, own_ref, rhs_ref, off_ref, inverse_ref, lane_ref, step_ref,
-    out_ref, window_ref, table_ref,
+    first_cell, left_ref, right_ref, out_ref, kernel_ref, window_ref, table_ref,
 ):
+    places, squares = wendland_places(first_cell, left_ref, right_ref, kernel_ref)
     per = rhs_ref.shape[0] // 5
     nodes = per // blocks
     faces = lane_ref.shape[0] // per
@@ -207,6 +207,10 @@
             lanes = lane_ref[f * per + half : f * per + half + 8, :]
             dist = step_ref[f * per + half : f * per + half + 8, :]
             beside = [jnp.zeros((8, LANES), jnp.float32)] * 5
+            squared = None
+            if places:
+                row, lane = places.pop(0)
+                squared = squares(row, lane)
             for d in range(2 * blocks + 1):
                 here = dist == d
                 first = half + d * nodes
@@ -218,10 +222,13 @@
                     else:
                         table = window_ref[at : at + 8, :]
                     beside[b] = jnp.where(here, take_lanes(table, lanes), beside[b])
+                if squared is not None and d % 2 and d // 2 * 16 < squared.shape[0]:
+                    at = d // 2 * 16
+                    wendland_store(squared[at : at + 16], kernel_ref, row + at, lane)
             for a in range(5):
                 for b in range(5):
-                    row = (f * 25 + 5 * a + b) * per + half
-                    remaining[a] = remaining[a] - off_ref[row : row + 8, :] * beside[b]
+                    at = (f * 25 + 5 * a + b) * per + half
+                    remaining[a] = remaining[a] - off_ref[at : at + 8, :] * beside[b]
         for a in range(5):
             total = None
             for b in range(5):
@@ -229,16 +236,21 @@
                 term = inverse_ref[row : row + 8, :] * remaining[b]
                 total = term if total is None else total + term
             out_ref[a * per + half : a * per + half + 8, :] = total
-
-
-def sweep_kernel(blocks, *refs):
-    sweep_into(blocks, *refs)
-
-
-def last_sweep_kernel(blocks, *refs):
-    ins, rest = refs[:8], refs[8:]
-    sens_ref, _, out_ref, sens_out_ref, window_ref, table_ref, part_ref = rest
-    sweep_into(blocks, *ins, out_ref, window_ref, table_ref)
+    while places:
+        row, lane = places.pop(0)
+        wendland_store(squares(row, lane), kernel_ref, row, lane)
+
+
+def sweep_kernel(blocks, first_cell, *refs):
+    sweep_into(blocks, *refs[:8], first_cell, *refs[8:])
+
+
+def last_sweep_kernel(blocks, first_cell, *refs):
+    ins, (left_ref, right_ref, sens_ref, _, *outs) = refs[:8], refs[8:]
+    out_ref, kernel_ref, sens_out_ref, window_ref, table_ref, part_ref = outs
+    sweep_into(
+        blocks, *ins, first_cell, left_ref, right_ref, out_ref, kernel_ref, window_ref, table_ref
+    )
     per = out_ref.shape[0] // 5
     nodes = per // blocks
     for k in range(3):
@@ -287,7 +299,20 @@
     return jnp.concatenate(blocks, axis=0)
 
 
-def wendland_kernel(first_cell, left_ref, right_ref, _, kernel_ref):
+def wendland_store(squared, kernel_ref, row, lane):
+    squared = jnp.maximum(squared, 1e-30)
+    near = jnp.maximum(1.0 - squared * lax.rsqrt(squared), 0.0)
+    power = near * near
+    kernel = power * power * (1.25 - near)
+    first = kernel.astype(jnp.bfloat16)
+    rest = (kernel - first.astype(jnp.float32)).astype(jnp.bfloat16)
+    cells = kernel_ref.shape[0] // 2
+    here = slice(lane, lane + squared.shape[1])
+    kernel_ref[row : row + squared.shape[0], here] = first
+    kernel_ref[cells + row : cells + row + squared.shape[0], here] = rest
+
+
+def wendland_places(first_cell, left_ref, right_ref, kernel_ref):
     cells, owned = kernel_ref.shape[0] // 2, kernel_ref.shape[1]
     tile, wide = min(128, cells), min(256, owned)
 
@@ -297,19 +322,17 @@
         return jnp.dot(left, right, preferred_element_type=jnp.float32)
 
     places = [(row, lane) for lane in range(0, owned, wide) for row in range(0, cells, tile)]
+    return places, squares
+
+
+def wendland_kernel(first_cell, left_ref, right_ref, _, kernel_ref):
+    places, squares = wendland_places(first_cell, left_ref, right_ref, kernel_ref)
     following = squares(*places[0])
     for at, (row, lane) in enumerate(places):
-        squared = jnp.maximum(following, 1e-30)
+        squared = following
         if at + 1 < len(places):
             following = squares(*places[at + 1])
-        near = jnp.maximum(1.0 - jnp.exp(0.5 * jnp.log(squared)), 0.0)
-        power = near * near
-        kernel = power * power * (1.25 - near)
-        first = kernel.astype(jnp.bfloat16)
-        rest = (kernel - first.astype(jnp.float32)).astype(jnp.bfloat16)
-        here = slice(lane, lane + wide)
-        kernel_ref[row : row + tile, here] = first
-        kernel_ref[cells + row : cells + row + tile, here] = rest
+        wendland_store(squared, kernel_ref, row, lane)
 
 
 def far_wendland_kernel(
@@ -325,10 +348,9 @@
 
 
 def control_kernel(scale, *refs):
-    *sens_refs, near_ref, far_ref = refs[:-4]
+    *sens_refs, first_ref, near_ref, third_ref, far_ref = refs[:-4]
     spread_ref, near_hot, far_hot, out_ref = refs[-4:]
     blocks = sens_refs[0].shape[0] // 3
-    half = near_ref.shape[0] // 2
     groups = FFD // LANES
     total = sens_refs[0][...]
     for ref in sens_refs[1:]:
@@ -350,7 +372,10 @@
         wide.append(jnp.concatenate([first, sens - first], axis=0))
     sens = jnp.concatenate(wide, axis=1).astype(jnp.bfloat16)
     grad = None
-    for part, ref in ((sens[:, :half], near_ref), (sens[:, half:], far_ref)):
+    cell = 0
+    for ref in (first_ref, near_ref, third_ref, far_ref):
+        part = sens[:, cell : cell + ref.shape[0] // 2]
+        cell += ref.shape[0] // 2
         both = jnp.concatenate([part, part], axis=1)
         term = jnp.dot(both, ref[...], preferred_element_type=jnp.float32)
         grad = term if grad is None else grad + term
@@ -438,7 +463,10 @@
     blocks = cells // LANES
     per = blocks * nodes
     slots = ffd_index.shape[1]
-    far_slots = max(1, slots * 3 // 8)
+    far_slots = slots // 2
+    parts = [cells // 8, cells // 2, cells // 8]
+    parts.append(cells - sum(parts))
+    firsts = [sum(parts[:i]) for i in range(4)]
     owned = base_points.shape[1] // lax.axis_size("nodes")
     peers = lax.axis_size(CELL_AXES)
     cores = lax.axis_size("sub")
@@ -525,42 +553,39 @@
     ]
     sweep_cost = cost(2 * 10 * 35 * cells, 4 * faces * 25 * per * LANES)
 
-    for _ in range(SWEEPS - 1):
-        adjoint = pl.pallas_call(
-            functools.partial(sweep_kernel, blocks),
-            out_shape=shape((5 * per, LANES)),
-            in_specs=[VMEM] * 8,
-            out_specs=VMEM,
-            scratch_shapes=scratch,
-            compiler_params=PARAMS,
-            cost_estimate=sweep_cost,
-            name="sweep",
-        )(close, far, adjoint, rhs, off, inverse, lane, step)
-        far, close = swaps(adjoint)
-
-    half = cells * 5 // 8 // LANES * LANES
+    kernel_shapes = [shape((2 * count, owned), bf16) for count in parts]
+    adjoint, first_kernel = pl.pallas_call(
+        functools.partial(sweep_kernel, blocks, firsts[0]),
+        out_shape=(shape((5 * per, LANES)), kernel_shapes[0]),
+        in_specs=[VMEM] * 10,
+        out_specs=(VMEM, VMEM),
+        scratch_shapes=scratch,
+        compiler_params=PARAMS,
+        cost_estimate=sweep_cost,
+        name="sweep",
+    )(close, far, adjoint, rhs, off, inverse, lane, step, left, right)
+    far, close = swaps(adjoint)
+
     wendland_cost = cost(10**9, 10**7)
-    near_shape = shape((2 * half, owned), bf16)
-    far_shape = shape((2 * (cells - half), owned), bf16)
     near_kernel = pl.pallas_call(
-        functools.partial(wendland_kernel, 0),
-        out_shape=near_shape,
+        functools.partial(wendland_kernel, firsts[1]),
+        out_shape=kernel_shapes[1],
         in_specs=[VMEM] * 3,
         out_specs=VMEM,
         compiler_params=PARAMS,
         cost_estimate=wendland_cost,
         name="near_wendland",
     )(left, right, adjoint)
-    adjoint, part_sens = pl.pallas_call(
-        functools.partial(last_sweep_kernel, blocks),
-        out_shape=(shape((5 * per, LANES)), shape((3 * blocks, LANES))),
-        in_specs=[VMEM] * 9 + [pl.BlockSpec(memory_space=pl.ANY)],
-        out_specs=(VMEM, VMEM),
+    adjoint, third_kernel, part_sens = pl.pallas_call(
+        functools.partial(last_sweep_kernel, blocks, firsts[2]),
+        out_shape=(shape((5 * per, LANES)), kernel_shapes[2], shape((3 * blocks, LANES))),
+        in_specs=[VMEM] * 11 + [pl.BlockSpec(memory_space=pl.ANY)],
+        out_specs=(VMEM, VMEM, VMEM),
         scratch_shapes=scratch + [pltpu.VMEM((3 * per, LANES), f32)],
         compiler_params=PARAMS,
         cost_estimate=sweep_cost,
         name="last_sweep",
-    )(close, far, adjoint, rhs, off, inverse, lane, step, sens, near_kernel)
+    )(close, far, adjoint, rhs, off, inverse, lane, step, left, right, sens, near_kernel)
 
     all_sens = [part_sens]
     for shift in range(1, node_peers):
@@ -568,8 +593,8 @@
         all_sens.append(lax.ppermute(part_sens, "nodes", ring))
     hot_shape = shape((far_slots * owned, LANES), bf16)
     far_kernel, far_hot, adjoint = pl.pallas_call(
-        functools.partial(far_wendland_kernel, half),
-        out_shape=(far_shape, hot_shape, shape((5 * per, LANES))),
+        functools.partial(far_wendland_kernel, firsts[3]),
+        out_shape=(kernel_shapes[3], hot_shape, shape((5 * per, LANES))),
         in_specs=[VMEM] * 5,
         out_specs=(VMEM, VMEM, HBM),
         scratch_shapes=[pltpu.SemaphoreType.DMA],
@@ -582,11 +607,11 @@
     partial = pl.pallas_call(
         functools.partial(control_kernel, scale),
         out_shape=shape((rows, LANES)),
-        in_specs=[VMEM] * (len(all_sens) + 5),
+        in_specs=[VMEM] * (len(all_sens) + 7),
         out_specs=VMEM,
         compiler_params=PARAMS,
         name="control",
-    )(*all_sens, near_kernel, far_kernel, spread, near_hot, far_hot)
+    )(*all_sens, first_kernel, near_kernel, third_kernel, far_kernel, spread, near_hot, far_hot)
     rounds = sum_rounds()
     terms = [partial] if rounds else [lax.psum(partial, SUM_AXES)]
     for masks in rounds or ():

time: 30.9 us -> 31.2 us (level)
  starting transfers between devices: 11.7 us -> 12.9 us
  Pallas kernels: 12.8 us -> 11.7 us
    ppermute x1, starting transfers between devices: 0.89 us -> 1.87 us  [body(): all_sens.append(lax.ppermute(part_sens, 'nodes', ring))]
    pallas_call x4, Pallas kernels: 7.99 us -> 7.09 us  [the longest x1 2.16 us: body(): pl.pallas_call(functools.partial(wendland_kernel, firsts[1]), out_shape=k...]
    ppermute x6, waiting for transfers between devices: 4.89 us -> 5.4 us  [exchanged(): lax.ppermute(value, SUM_AXES, [(i, i ^ mask) for i in range(peers)])]
    ppermute x1, waiting for transfers between devices: 0.64 us -> 0.21 us  [body(): all_sens.append(lax.ppermute(part_sens, 'nodes', ring))]
  transfers between devices with their start and end apart: 11 -> 11, of which waited for: 6 -> 5; matrix products, arithmetic and copies ran while one was open for 0% -> 0% of each run, Pallas kernels for 25% -> 19%
where the time goes in v18:
time: 31.2 us; the launch traced here: 31 us
  starting transfers between devices  12.9 us (41%)
  Pallas kernels  11.7 us (38%)
  waiting for transfers between devices  5.62 us (18%)
  between operations  0.72 us (2%)
    ppermute x6, starting transfers between devices, exchanged(): lax.ppermute(value, SUM_AXES, [(i, i ^ mask) for i in range(peers)])  5.81 us
    ppermute x6, waiting for transfers between devices, exchanged(): lax.ppermute(value, SUM_AXES, [(i, i ^ mask) for i in range(peers)])  5.4 us
    ppermute x2, starting transfers between devices, swaps(): return (lax.ppermute(array, SUM_AXES, pairs), close)  4.47 us
    pallas_call x1, Pallas kernels, body(): pl.pallas_call(functools.partial(prepare_kernel, nodes), out_shape=(shape...  2.18 us
    pallas_call x1, Pallas kernels, body(): pl.pallas_call(functools.partial(wendland_kernel, firsts[1]), out_shape=k...  2.16 us
    ppermute x1, starting transfers between devices, body(): all_sens.append(lax.ppermute(part_sens, 'nodes', ring))  1.87 us
    pallas_call x1, Pallas kernels, body(): pl.pallas_call(functools.partial(control_kernel, scale), out_shape=shape(...  1.85 us
    pallas_call x1, Pallas kernels, body(): pl.pallas_call(functools.partial(far_wendland_kernel, firsts[3]), out_sha...  1.67 us
  transfers between devices with their start and end apart: 11, of which 5 were waited for; matrix products, arithmetic and copies ran while one was open for 0% of the time, Pallas kernels for 19%

profile of v18, /device:TPU:0, one launch (start us, length us, event | category | flops | bytes accessed | tf_op | source)
XLA Modules:
  0.0 31.0 jit_solution(8998759940434854295)
XLA Ops:
  0.6 0.5 %collective-permute-start = (f32[80,128]{1,0:T(8,128)}, f32[80,128]{1,0:T(8,128)S(1)}, u32[]{:S(2)}, u32[]{:S(2)}) collective-permute-start(f32[80,128]{1,0:T(8,128)} %bitcast.38), channel_id=1, source_target_pairs={{0,1},{1,0},{4,5},{5,4},{8,9},{9,8},{12,13},{13,12},{2,3},{3,2},{6... | collective-permute-start | bytes 122888 | tf_op jit(solution)/shard_map/ppermute | solution.py:483
  1.2 2.6 %collective-permute-start.1 = (f32[80,128]{1,0:T(8,128)}, f32[80,128]{1,0:T(8,128)S(1)}, u32[]{:S(2)}, u32[]{:S(2)}) collective-permute-start(f32[80,128]{1,0:T(8,128)} %bitcast.39), channel_id=1, source_target_pairs={{0,2},{2,0},{1,4},{3,6},{4,1},{6,3},{5,8},{7,10},{8,5},{10,7},{9,1... | collective-permute-start | bytes 122888 | tf_op jit(solution)/shard_map/ppermute | solution.py:498
  3.7 2.2 %prepare.1 = (f32[2400,128]{1,0:T(8,128)S(1)}, f32[400,128]{1,0:T(8,128)S(1)}, f32[80,128]{1,0:T(8,128)S(1)}, f32[240,128]{1,0:T(8,128)S(1)}, s32[96,128]{1,0:T(...) custom-call(bf16[2400,128]{1,0:T(8,128)(2,1)} %bitcast.32, ...), custom_call_target="tpu_custom_call" | custom-call | flops 1000000000 | bytes 10000000 | tf_op jit(solution)/shard_map/prepare/pallas_call | solution.py:502
  5.9 0.0 collective-permute-done.refs_0_
  5.9 0.0 collective-permute-done.1.refs_1_
  5.9 1.6 %sweep.1 = (f32[80,128]{1,0:T(8,128)S(1)}, bf16[256,2048]{1,0:T(8,128)(2,1)S(1)}) custom-call(f32[80,128]{1,0:T(8,128)S(1)} %collective-permute-done.refs_0_, f32[80,128]{1,0:T(8,128)S(1)} %collective-permute-done.1.refs_1_, f32[80,128]{1,0:T(8,128)S(1)} %get-tuple-element.24.refs_2_, f32[80,128]{1,0:T(8,128)S(1)} %get-tuple-element.25.refs_3_, ...), custom_call_target="tpu_custom_call" | custom-call | flops 716800 | bytes 1228800 | tf_op jit(solution)/shard_map/sweep/pallas_call | solution.py:557
  7.5 0.3 collective-permute-start.2
  7.8 1.9 %collective-permute-start.3 = (f32[80,128]{1,0:T(8,128)S(1)}, f32[80,128]{1,0:T(8,128)S(1)}, u32[]{:S(2)}, u32[]{:S(2)}) collective-permute-start(f32[80,128]{1,0:T(8,128)S(1)} %get-tuple-element.30._.refs_2_), channel_id=1, source_target_pairs={{0,2},{2,0},{1,4},{3,6},{4,1},{6,3},{5,8},{7,10},{8,5},{10,7},{9,1... | collective-permute-start | bytes 122888 | tf_op jit(solution)/shard_map/ppermute | solution.py:498
  9.7 2.2 %near_wendland.1.refs_11_.refs_3_ = bf16[1024,2048]{1,0:T(8,128)(2,1)S(1)} custom-call(bf16[1024,64]{1,0:T(8,128)(2,1)S(1)} %get-tuple-element.22.refs_8_.left_ref, bf16[64,2048]{1,0:T(8,128)(2,1)S(1)} %get-tuple-element.23.refs_9_.right_ref, f32[80,128]{1,0:T(8,128)S(1)} %get-tuple-element.30._.refs_2_), custom_call_target="tpu_custom_call" | custom-call | flops 1000000000 | bytes 10000000 | tf_op jit(solution)/shard_map/near_wendland/pallas_call | solution.py:570
  11.9 0.0 collective-permute-done.2.refs_0_
  11.9 0.0 collective-permute-done.3.refs_1_
  11.9 1.6 %last_sweep.1 = (f32[80,128]{1,0:T(8,128)S(1)}, bf16[256,2048]{1,0:T(8,128)(2,1)S(1)}, f32[24,128]{1,0:T(8,128)S(1)}) custom-call(f32[80,128]{1,0:T(8,128)S(1)} %collective-permute-done.2.refs_0_, f32[80,128]{1,0:T(8,128)S(1)} %collective-permute-done.3.refs_1_, f32[80,128]{1,0:T(8,128)S(1)} %get-tuple-element.30._.refs_2_, ...), custom_call_target="tpu_custom_call" | custom-call | flops 716800 | bytes 1228800 | tf_op jit(solution)/shard_map/last_sweep/pallas_call | solution.py:579
  13.6 1.9 %collective-permute-start.4 = (f32[24,128]{1,0:T(8,128)S(1)}, f32[24,128]{1,0:T(8,128)S(1)}, u32[]{:S(2)}, u32[]{:S(2)}) collective-permute-start(f32[24,128]{1,0:T(8,128)S(1)} %get-tuple-element.32.after.refs_0_), channel_id=1, source_target_pairs={{0,2},{2,0},{1,3},{3,1},{4,6},{6,4},{5,7},{7,5},{8,10},{10,8},{9,1... | collective-permute-start | bytes 36872 | tf_op jit(solution)/shard_map/ppermute | solution.py:593
  15.4 1.7 %far_wendland.1 = (bf16[512,2048]{1,0:T(8,128)(2,1)S(1)}, bf16[8192,128]{1,0:T(8,128)(2,1)S(1)}, f32[80,128]{1,0:T(8,128)}) custom-call(bf16[1024,64]{1,0:T(8,128)(2,1)S(1)} %get-tuple-element.22.refs_8_.left_ref, bf16[64,2048]{1,0:T(8,128)(2,1)S(1)} %get-tuple-element.23.refs_9_.right_ref, f32[24,128]{1,0:T(8,128)S(1)} %get-tuple-element.32.after.refs_0_, ...), custom_call_target="tpu_custom_call" | custom-call | flops 1000000000 | bytes 10000000 | tf_op jit(solution)/shard_map/far_wendland/pallas_call | solution.py:595
  17.1 0.2 collective-permute-done.4.refs_1_
  17.3 1.9 %control.1.refs_0_ = f32[12,128]{1,0:T(8,128)S(1)} custom-call(f32[24,128]{1,0:T(8,128)S(1)} %get-tuple-element.32.after.refs_0_, f32[24,128]{1,0:T(8,128)S(1)} %collective-permute-done.4.refs_1_, bf16[256,2048]{1,0:T(8,128)(2,1)S(1)} %get-tuple-element.36.refs_2_, bf16[1024,2048]{1,0:T(8,128)(2,1)S(1)} %near_wendland.1.refs_11_.refs_3_, ...), custom_call_target="tpu_custom_call" | custom-call | tf_op jit(solution)/shard_map/control/pallas_call | solution.py:607
  19.2 0.1 collective-permute-start.5
  19.3 1.1 %collective-permute-start.6 = (f32[12,128]{1,0:T(8,128)S(1)}, f32[12,128]{1,0:T(8,128)S(1)}, u32[]{:S(2)}, u32[]{:S(2)}) collective-permute-start(f32[12,128]{1,0:T(8,128)S(1)} %control.1.refs_0_), channel_id=1, source_target_pairs={{0,4},{1,5},{2,6},{3,7},{4,0},{5,1},{6,2},{7,3},{8,12},{9,13},{10,... | collective-permute-start | bytes 18440 | tf_op jit(solution)/shard_map/ppermute | solution.py:444
  20.4 0.7 %collective-permute-start.7 = (f32[12,128]{1,0:T(8,128)S(1)}, f32[12,128]{1,0:T(8,128)S(1)}, u32[]{:S(2)}, u32[]{:S(2)}) collective-permute-start(f32[12,128]{1,0:T(8,128)S(1)} %control.1.refs_0_), channel_id=1, source_target_pairs={{0,5},{1,4},{2,7},{3,6},{4,1},{5,0},{6,3},{7,2},{8,13},{9,12},{10,... | collective-permute-start | bytes 18440 | tf_op jit(solution)/shard_map/ppermute | solution.py:444
  21.1 0.0 collective-permute-done.5.refs_1_
  21.1 1.9 %collective-permute-done.6.refs_2_ = f32[12,128]{1,0:T(8,128)S(1)} collective-permute-done((f32[12,128]{1,0:T(8,128)S(1)}, f32[12,128]{1,0:T(8,128)S(1)}, u32[]{:S(2)}, u32[]{:S(2)}) %collective-permute-start.6) | collective-permute-done | bytes 6176 | tf_op jit(solution)/shard_map/ppermute | solution.py:444
  23.0 0.5 %collective-permute-done.7.refs_3_ = f32[12,128]{1,0:T(8,128)S(1)} collective-permute-done((f32[12,128]{1,0:T(8,128)S(1)}, f32[12,128]{1,0:T(8,128)S(1)}, u32[]{:S(2)}, u32[]{:S(2)}) %collective-permute-start.7) | collective-permute-done | bytes 6176 | tf_op jit(solution)/shard_map/ppermute | solution.py:444
  23.5 3.0 %collective-permute-start.10 = (f32[12,128]{1,0:T(8,128)S(1)}, f32[12,128]{1,0:T(8,128)S(1)}, u32[]{:S(2)}, u32[]{:S(2)}) collective-permute-start(f32[12,128]{1,0:T(8,128)S(1)} %add.1.refs_0_), channel_id=1, source_target_pairs={{0,11},{1,10},{2,9},{3,8},{4,15},{5,14},{6,13},{7,12},{8,3},{9,2},... | collective-permute-start | bytes 18440 | tf_op jit(solution)/shard_map/ppermute | solution.py:444
  26.4 0.6 %collective-permute-start.8 = (f32[12,128]{1,0:T(8,128)S(1)}, f32[12,128]{1,0:T(8,128)S(1)}, u32[]{:S(2)}, u32[]{:S(2)}) collective-permute-start(f32[12,128]{1,0:T(8,128)S(1)} %add.1.refs_0_), channel_id=1, source_target_pairs={{0,9},{1,8},{2,11},{3,10},{4,13},{5,12},{6,15},{7,14},{8,1},{9,0},... | collective-permute-start | bytes 18440 | tf_op jit(solution)/shard_map/ppermute | solution.py:444
  27.0 0.3 %collective-permute-start.9 = (f32[12,128]{1,0:T(8,128)S(1)}, f32[12,128]{1,0:T(8,128)S(1)}, u32[]{:S(2)}, u32[]{:S(2)}) collective-permute-start(f32[12,128]{1,0:T(8,128)S(1)} %add.1.refs_0_), channel_id=1, source_target_pairs={{0,3},{1,2},{2,1},{3,0},{4,7},{5,6},{6,5},{7,4},{8,11},{9,10},{10,... | collective-permute-start | bytes 18440 | tf_op jit(solution)/shard_map/ppermute | solution.py:444
  27.3 1.0 %collective-permute-done.10.refs_3_ = f32[12,128]{1,0:T(8,128)S(1)} collective-permute-done((f32[12,128]{1,0:T(8,128)S(1)}, f32[12,128]{1,0:T(8,128)S(1)}, u32[]{:S(2)}, u32[]{:S(2)}) %collective-permute-start.10) | collective-permute-done | bytes 6176 | tf_op jit(solution)/shard_map/ppermute | solution.py:444
  28.3 2.1 %collective-permute-done.8.refs_1_ = f32[12,128]{1,0:T(8,128)S(1)} collective-permute-done((f32[12,128]{1,0:T(8,128)S(1)}, f32[12,128]{1,0:T(8,128)S(1)}, u32[]{:S(2)}, u32[]{:S(2)}) %collective-permute-start.8) | collective-permute-done | bytes 6176 | tf_op jit(solution)/shard_map/ppermute | solution.py:444
  30.4 0.0 collective-permute-done.9.refs_2_
  30.4 0.6 %finish.1 = f32[3,512]{1,0:T(4,128)} custom-call(f32[12,128]{1,0:T(8,128)S(1)} %add.1.refs_0_, f32[12,128]{1,0:T(8,128)S(1)} %collective-permute-done.8.refs_1_, f32[12,128]{1,0:T(8,128)S(1)} %collective-permute-done.9.refs_2_, f32[12,128]{1,0:T(8,128)S(1)} %collective-permute-done.10.refs_3_), custom_call_target="tpu_custom_call" | custom-call | tf_op jit(solution)/shard_map/finish/pallas_call | solution.py:623
  (1 shorter events, 0.0 us)
Async XLA Ops:
  0.6 5.3 %collective-permute-start = (f32[80,128]{1,0:T(8,128)}, f32[80,128]{1,0:T(8,128)S(1)}, u32[]{:S(2)}, u32[]{:S(2)}) collective-permute-start(f32[80,128]{1,0:T(8,128)} %bitcast.38), channel_id=1, source_target_pairs={{0,1},{1,0},{4,5},{5,4},{8,9},{9,8},{12,13},{13,12},{2,3},{3,2},{6... | collective-permute-start | bytes 122888 | tf_op jit(solution)/shard_map/ppermute | solution.py:483
  1.2 4.8 %collective-permute-start.1 = (f32[80,128]{1,0:T(8,128)}, f32[80,128]{1,0:T(8,128)S(1)}, u32[]{:S(2)}, u32[]{:S(2)}) collective-permute-start(f32[80,128]{1,0:T(8,128)} %bitcast.39), channel_id=1, source_target_pairs={{0,2},{2,0},{1,4},{3,6},{4,1},{6,3},{5,8},{7,10},{8,5},{10,7},{9,1... | collective-permute-start | bytes 122888 | tf_op jit(solution)/shard_map/ppermute | solution.py:498
  7.5 4.3 %collective-permute-start.2 = (f32[80,128]{1,0:T(8,128)S(1)}, f32[80,128]{1,0:T(8,128)S(1)}, u32[]{:S(2)}, u32[]{:S(2)}) collective-permute-start(f32[80,128]{1,0:T(8,128)S(1)} %get-tuple-element.30._.refs_2_), channel_id=1, source_target_pairs={{0,1},{1,0},{4,5},{5,4},{8,9},{9,8},{12,13},{13,12},{2,3},{3,2},{6... | collective-permute-start | bytes 122888 | tf_op jit(solution)/shard_map/ppermute | solution.py:483
  7.8 4.1 %collective-permute-start.3 = (f32[80,128]{1,0:T(8,128)S(1)}, f32[80,128]{1,0:T(8,128)S(1)}, u32[]{:S(2)}, u32[]{:S(2)}) collective-permute-start(f32[80,128]{1,0:T(8,128)S(1)} %get-tuple-element.30._.refs_2_), channel_id=1, source_target_pairs={{0,2},{2,0},{1,4},{3,6},{4,1},{6,3},{5,8},{7,10},{8,5},{10,7},{9,1... | collective-permute-start | bytes 122888 | tf_op jit(solution)/shard_map/ppermute | solution.py:498
  13.6 3.8 %collective-permute-start.4 = (f32[24,128]{1,0:T(8,128)S(1)}, f32[24,128]{1,0:T(8,128)S(1)}, u32[]{:S(2)}, u32[]{:S(2)}) collective-permute-start(f32[24,128]{1,0:T(8,128)S(1)} %get-tuple-element.32.after.refs_0_), channel_id=1, source_target_pairs={{0,2},{2,0},{1,3},{3,1},{4,6},{6,4},{5,7},{7,5},{8,10},{10,8},{9,1... | collective-permute-start | bytes 36872 | tf_op jit(solution)/shard_map/ppermute | solution.py:593
  19.2 1.9 %collective-permute-start.5 = (f32[12,128]{1,0:T(8,128)S(1)}, f32[12,128]{1,0:T(8,128)S(1)}, u32[]{:S(2)}, u32[]{:S(2)}) collective-permute-start(f32[12,128]{1,0:T(8,128)S(1)} %control.1.refs_0_), channel_id=1, source_target_pairs={{0,1},{1,0},{2,3},{3,2},{4,5},{5,4},{6,7},{7,6},{8,9},{9,8},{10,11... | collective-permute-start | bytes 18440 | tf_op jit(solution)/shard_map/ppermute | solution.py:444
  19.3 3.7 %collective-permute-start.6 = (f32[12,128]{1,0:T(8,128)S(1)}, f32[12,128]{1,0:T(8,128)S(1)}, u32[]{:S(2)}, u32[]{:S(2)}) collective-permute-start(f32[12,128]{1,0:T(8,128)S(1)} %control.1.refs_0_), channel_id=1, source_target_pairs={{0,4},{1,5},{2,6},{3,7},{4,0},{5,1},{6,2},{7,3},{8,12},{9,13},{10,... | collective-permute-start | bytes 18440 | tf_op jit(solution)/shard_map/ppermute | solution.py:444
  20.4 3.1 %collective-permute-start.7 = (f32[12,128]{1,0:T(8,128)S(1)}, f32[12,128]{1,0:T(8,128)S(1)}, u32[]{:S(2)}, u32[]{:S(2)}) collective-permute-start(f32[12,128]{1,0:T(8,128)S(1)} %control.1.refs_0_), channel_id=1, source_target_pairs={{0,5},{1,4},{2,7},{3,6},{4,1},{5,0},{6,3},{7,2},{8,13},{9,12},{10,... | collective-permute-start | bytes 18440 | tf_op jit(solution)/shard_map/ppermute | solution.py:444
  23.5 4.9 %collective-permute-start.10 = (f32[12,128]{1,0:T(8,128)S(1)}, f32[12,128]{1,0:T(8,128)S(1)}, u32[]{:S(2)}, u32[]{:S(2)}) collective-permute-start(f32[12,128]{1,0:T(8,128)S(1)} %add.1.refs_0_), channel_id=1, source_target_pairs={{0,11},{1,10},{2,9},{3,8},{4,15},{5,14},{6,13},{7,12},{8,3},{9,2},... | collective-permute-start | bytes 18440 | tf_op jit(solution)/shard_map/ppermute | solution.py:444
  26.4 4.0 %collective-permute-start.8 = (f32[12,128]{1,0:T(8,128)S(1)}, f32[12,128]{1,0:T(8,128)S(1)}, u32[]{:S(2)}, u32[]{:S(2)}) collective-permute-start(f32[12,128]{1,0:T(8,128)S(1)} %add.1.refs_0_), channel_id=1, source_target_pairs={{0,9},{1,8},{2,11},{3,10},{4,13},{5,12},{6,15},{7,14},{8,1},{9,0},... | collective-permute-start | bytes 18440 | tf_op jit(solution)/shard_map/ppermute | solution.py:444
  27.0 3.4 %collective-permute-start.9 = (f32[12,128]{1,0:T(8,128)S(1)}, f32[12,128]{1,0:T(8,128)S(1)}, u32[]{:S(2)}, u32[]{:S(2)}) collective-permute-start(f32[12,128]{1,0:T(8,128)S(1)} %add.1.refs_0_), channel_id=1, source_target_pairs={{0,3},{1,2},{2,1},{3,0},{4,7},{5,6},{6,5},{7,4},{8,11},{9,10},{10,... | collective-permute-start | bytes 18440 | tf_op jit(solution)/shard_map/ppermute | solution.py:444

commit v19 on v18

--- a/solution.py
+++ b/solution.py
@@ -177,7 +177,7 @@
 
 
 def sweep_into(
-    blocks, first_ref, second_ref, own_ref, rhs_ref, off_ref, inverse_ref, lane_ref, step_ref,
+    blocks, far_ref, close_ref, own_ref, rhs_ref, off_ref, inverse_ref, lane_ref, step_ref,
     first_cell, left_ref, right_ref, out_ref, kernel_ref, window_ref, table_ref,
 ):
     places, squares = wendland_places(first_cell, left_ref, right_ref, kernel_ref)
@@ -191,9 +191,9 @@
     for b in range(5):
         rows = slice(b * per, (b + 1) * per)
         base = b * width
-        window_ref[pl.ds(base + place, per), :] = first_ref[rows, :]
+        window_ref[pl.ds(base + place, per), :] = close_ref[rows, :]
         window_ref[base + per : base + 2 * per, :] = own_ref[rows, :]
-        window_ref[pl.ds(base + other, per), :] = second_ref[rows, :]
+        window_ref[pl.ds(base + other, per), :] = far_ref[rows, :]
     for shift in range(1, 8 // nodes):
         for b in range(5):
             for tile in range(0, width - 8, 8):
@@ -464,7 +464,7 @@
     per = blocks * nodes
     slots = ffd_index.shape[1]
     far_slots = slots // 2
-    parts = [cells // 8, cells // 2, cells // 8]
+    parts = [cells // 8, cells * 3 // 8, cells // 8]
     parts.append(cells - sum(parts))
     firsts = [sum(parts[:i]) for i in range(4)]
     owned = base_points.shape[1] // lax.axis_size("nodes")
@@ -563,7 +563,7 @@
         compiler_params=PARAMS,
         cost_estimate=sweep_cost,
         name="sweep",
-    )(close, far, adjoint, rhs, off, inverse, lane, step, left, right)
+    )(far, close, adjoint, rhs, off, inverse, lane, step, left, right)
     far, close = swaps(adjoint)
 
     wendland_cost = cost(10**9, 10**7)
@@ -585,7 +585,7 @@
         compiler_params=PARAMS,
         cost_estimate=sweep_cost,
         name="last_sweep",
-    )(close, far, adjoint, rhs, off, inverse, lane, step, left, right, sens, near_kernel)
+    )(far, close, adjoint, rhs, off, inverse, lane, step, left, right, sens, near_kernel)
 
     all_sens = [part_sens]
     for shift in range(1, node_peers):

time: 31.2 us -> 31 us (level)
    ppermute x2, starting transfers between devices: 0.78 us -> 0.2 us  [swaps(): close = lax.ppermute(array, CELL_AXES, [(i, i ^ 1) for i in range(peers)])]
    ppermute x2, waiting for transfers between devices: 0.01 us -> 0.55 us  [swaps(): return (lax.ppermute(array, SUM_AXES, pairs), close)]
    pallas_call x1, Pallas kernels: 2.16 us -> 1.64 us  [body(): pl.pallas_call(functools.partial(wendland_kernel, firsts[1]), out_shape=k...]
    pallas_call x1, Pallas kernels: 1.67 us -> 2.13 us  [body(): pl.pallas_call(functools.partial(far_wendland_kernel, firsts[3]), out_sha...]
    ppermute x2, starting transfers between devices: 4.47 us -> 4.87 us  [swaps(): return (lax.ppermute(array, SUM_AXES, pairs), close)]
where the time goes in v19:
time: 31 us; the launch traced here: 30.9 us
  starting transfers between devices  12.7 us (41%)
  Pallas kernels  11.7 us (38%)
  waiting for transfers between devices  5.71 us (18%)
  between operations  0.71 us (2%)
    ppermute x6, starting transfers between devices, exchanged(): lax.ppermute(value, SUM_AXES, [(i, i ^ mask) for i in range(peers)])  5.81 us
    ppermute x6, waiting for transfers between devices, exchanged(): lax.ppermute(value, SUM_AXES, [(i, i ^ mask) for i in range(peers)])  5.14 us
    ppermute x2, starting transfers between devices, swaps(): return (lax.ppermute(array, SUM_AXES, pairs), close)  4.87 us
    pallas_call x1, Pallas kernels, body(): pl.pallas_call(functools.partial(prepare_kernel, nodes), out_shape=(shape...  2.18 us
    pallas_call x1, Pallas kernels, body(): pl.pallas_call(functools.partial(far_wendland_kernel, firsts[3]), out_sha...  2.13 us
    ppermute x1, starting transfers between devices, body(): all_sens.append(lax.ppermute(part_sens, 'nodes', ring))  1.86 us
    pallas_call x1, Pallas kernels, body(): pl.pallas_call(functools.partial(control_kernel, scale), out_shape=shape(...  1.86 us
    pallas_call x1, Pallas kernels, body(): pl.pallas_call(functools.partial(last_sweep_kernel, blocks, firsts[2]), o...  1.64 us
  transfers between devices with their start and end apart: 11, of which 5 were waited for; matrix products, arithmetic and copies ran while one was open for 0% of the time, Pallas kernels for 19%

profile of v19, /device:TPU:0, one launch (start us, length us, event | category | flops | bytes accessed | tf_op | source)
XLA Modules:
  0.0 30.9 jit_solution(6690638197237179130)
XLA Ops:
  0.6 3.0 %collective-permute-start = (f32[80,128]{1,0:T(8,128)}, f32[80,128]{1,0:T(8,128)S(1)}, u32[]{:S(2)}, u32[]{:S(2)}) collective-permute-start(f32[80,128]{1,0:T(8,128)} %bitcast.38), channel_id=1, source_target_pairs={{0,2},{2,0},{1,4},{3,6},{4,1},{6,3},{5,8},{7,10},{8,5},{10,7},{9,1... | collective-permute-start | bytes 122888 | tf_op jit(solution)/shard_map/ppermute | solution.py:498
  3.6 0.2 collective-permute-start.1
  3.8 2.2 %prepare.1 = (f32[2400,128]{1,0:T(8,128)S(1)}, f32[400,128]{1,0:T(8,128)S(1)}, f32[80,128]{1,0:T(8,128)S(1)}, f32[240,128]{1,0:T(8,128)S(1)}, s32[96,128]{1,0:T(...) custom-call(bf16[2400,128]{1,0:T(8,128)(2,1)} %bitcast.32, ...), custom_call_target="tpu_custom_call" | custom-call | flops 1000000000 | bytes 10000000 | tf_op jit(solution)/shard_map/prepare/pallas_call | solution.py:502
  6.0 0.0 collective-permute-done.refs_0_
  6.0 0.0 collective-permute-done.1.refs_1_
  6.0 1.6 %sweep.1 = (f32[80,128]{1,0:T(8,128)S(1)}, bf16[256,2048]{1,0:T(8,128)(2,1)S(1)}) custom-call(f32[80,128]{1,0:T(8,128)S(1)} %collective-permute-done.refs_0_, f32[80,128]{1,0:T(8,128)S(1)} %collective-permute-done.1.refs_1_, f32[80,128]{1,0:T(8,128)S(1)} %get-tuple-element.24.refs_2_, f32[80,128]{1,0:T(8,128)S(1)} %get-tuple-element.25.refs_3_, ...), custom_call_target="tpu_custom_call" | custom-call | flops 716800 | bytes 1228800 | tf_op jit(solution)/shard_map/sweep/pallas_call | solution.py:557
  7.7 1.9 %collective-permute-start.2 = (f32[80,128]{1,0:T(8,128)S(1)}, f32[80,128]{1,0:T(8,128)S(1)}, u32[]{:S(2)}, u32[]{:S(2)}) collective-permute-start(f32[80,128]{1,0:T(8,128)S(1)} %get-tuple-element.30._.refs_2_), channel_id=1, source_target_pairs={{0,2},{2,0},{1,4},{3,6},{4,1},{6,3},{5,8},{7,10},{8,5},{10,7},{9,1... | collective-permute-start | bytes 122888 | tf_op jit(solution)/shard_map/ppermute | solution.py:498
  9.5 0.0 collective-permute-start.3
  9.5 1.6 %near_wendland.1.refs_11_.refs_3_ = bf16[768,2048]{1,0:T(8,128)(2,1)S(1)} custom-call(bf16[1024,64]{1,0:T(8,128)(2,1)S(1)} %get-tuple-element.22.refs_8_.left_ref, bf16[64,2048]{1,0:T(8,128)(2,1)S(1)} %get-tuple-element.23.refs_9_.right_ref, f32[80,128]{1,0:T(8,128)S(1)} %get-tuple-element.30._.refs_2_), custom_call_target="tpu_custom_call" | custom-call | flops 1000000000 | bytes 10000000 | tf_op jit(solution)/shard_map/near_wendland/pallas_call | solution.py:570
  11.2 0.6 %collective-permute-done.2.refs_0_ = f32[80,128]{1,0:T(8,128)S(1)} collective-permute-done((f32[80,128]{1,0:T(8,128)S(1)}, f32[80,128]{1,0:T(8,128)S(1)}, u32[]{:S(2)}, u32[]{:S(2)}) %collective-permute-start.2) | collective-permute-done | bytes 40992 | tf_op jit(solution)/shard_map/ppermute | solution.py:498
  11.7 0.0 collective-permute-done.3.refs_1_
  11.8 1.6 %last_sweep.1 = (f32[80,128]{1,0:T(8,128)S(1)}, bf16[256,2048]{1,0:T(8,128)(2,1)S(1)}, f32[24,128]{1,0:T(8,128)S(1)}) custom-call(f32[80,128]{1,0:T(8,128)S(1)} %collective-permute-done.2.refs_0_, f32[80,128]{1,0:T(8,128)S(1)} %collective-permute-done.3.refs_1_, f32[80,128]{1,0:T(8,128)S(1)} %get-tuple-element.30._.refs_2_, ...), custom_call_target="tpu_custom_call" | custom-call | flops 716800 | bytes 1228800 | tf_op jit(solution)/shard_map/last_sweep/pallas_call | solution.py:579
  13.4 1.9 %collective-permute-start.4 = (f32[24,128]{1,0:T(8,128)S(1)}, f32[24,128]{1,0:T(8,128)S(1)}, u32[]{:S(2)}, u32[]{:S(2)}) collective-permute-start(f32[24,128]{1,0:T(8,128)S(1)} %get-tuple-element.32.after.refs_0_), channel_id=1, source_target_pairs={{0,2},{2,0},{1,3},{3,1},{4,6},{6,4},{5,7},{7,5},{8,10},{10,8},{9,1... | collective-permute-start | bytes 36872 | tf_op jit(solution)/shard_map/ppermute | solution.py:593
  15.3 2.1 %far_wendland.1 = (bf16[768,2048]{1,0:T(8,128)(2,1)S(1)}, bf16[8192,128]{1,0:T(8,128)(2,1)S(1)}, f32[80,128]{1,0:T(8,128)}) custom-call(bf16[1024,64]{1,0:T(8,128)(2,1)S(1)} %get-tuple-element.22.refs_8_.left_ref, bf16[64,2048]{1,0:T(8,128)(2,1)S(1)} %get-tuple-element.23.refs_9_.right_ref, f32[24,128]{1,0:T(8,128)S(1)} %get-tuple-element.32.after.refs_0_, ...), custom_call_target="tpu_custom_call" | custom-call | flops 1000000000 | bytes 10000000 | tf_op jit(solution)/shard_map/far_wendland/pallas_call | solution.py:595
  17.4 0.0 collective-permute-done.4.refs_1_
  17.4 1.9 %control.1.refs_0_ = f32[12,128]{1,0:T(8,128)S(1)} custom-call(f32[24,128]{1,0:T(8,128)S(1)} %get-tuple-element.32.after.refs_0_, f32[24,128]{1,0:T(8,128)S(1)} %collective-permute-done.4.refs_1_, bf16[256,2048]{1,0:T(8,128)(2,1)S(1)} %get-tuple-element.36.refs_2_, bf16[768,2048]{1,0:T(8,128)(2,1)S(1)} %near_wendland.1.refs_11_.refs_3_, ...), custom_call_target="tpu_custom_call" | custom-call | tf_op jit(solution)/shard_map/control/pallas_call | solution.py:607
  19.3 0.1 collective-permute-start.5
  19.4 0.8 %collective-permute-start.6 = (f32[12,128]{1,0:T(8,128)S(1)}, f32[12,128]{1,0:T(8,128)S(1)}, u32[]{:S(2)}, u32[]{:S(2)}) collective-permute-start(f32[12,128]{1,0:T(8,128)S(1)} %control.1.refs_0_), channel_id=1, source_target_pairs={{0,4},{1,5},{2,6},{3,7},{4,0},{5,1},{6,2},{7,3},{8,12},{9,13},{10,... | collective-permute-start | bytes 18440 | tf_op jit(solution)/shard_map/ppermute | solution.py:444
  20.2 1.1 %collective-permute-start.7 = (f32[12,128]{1,0:T(8,128)S(1)}, f32[12,128]{1,0:T(8,128)S(1)}, u32[]{:S(2)}, u32[]{:S(2)}) collective-permute-start(f32[12,128]{1,0:T(8,128)S(1)} %control.1.refs_0_), channel_id=1, source_target_pairs={{0,5},{1,4},{2,7},{3,6},{4,1},{5,0},{6,3},{7,2},{8,13},{9,12},{10,... | collective-permute-start | bytes 18440 | tf_op jit(solution)/shard_map/ppermute | solution.py:444
  21.2 0.0 collective-permute-done.5.refs_1_
  21.2 1.9 %collective-permute-done.6.refs_2_ = f32[12,128]{1,0:T(8,128)S(1)} collective-permute-done((f32[12,128]{1,0:T(8,128)S(1)}, f32[12,128]{1,0:T(8,128)S(1)}, u32[]{:S(2)}, u32[]{:S(2)}) %collective-permute-start.6) | collective-permute-done | bytes 6176 | tf_op jit(solution)/shard_map/ppermute | solution.py:444
  23.1 0.2 collective-permute-done.7.refs_3_
  23.3 3.0 %collective-permute-start.10 = (f32[12,128]{1,0:T(8,128)S(1)}, f32[12,128]{1,0:T(8,128)S(1)}, u32[]{:S(2)}, u32[]{:S(2)}) collective-permute-start(f32[12,128]{1,0:T(8,128)S(1)} %add.1.refs_0_), channel_id=1, source_target_pairs={{0,11},{1,10},{2,9},{3,8},{4,15},{5,14},{6,13},{7,12},{8,3},{9,2},... | collective-permute-start | bytes 18440 | tf_op jit(solution)/shard_map/ppermute | solution.py:444
  26.3 0.6 %collective-permute-start.8 = (f32[12,128]{1,0:T(8,128)S(1)}, f32[12,128]{1,0:T(8,128)S(1)}, u32[]{:S(2)}, u32[]{:S(2)}) collective-permute-start(f32[12,128]{1,0:T(8,128)S(1)} %add.1.refs_0_), channel_id=1, source_target_pairs={{0,9},{1,8},{2,11},{3,10},{4,13},{5,12},{6,15},{7,14},{8,1},{9,0},... | collective-permute-start | bytes 18440 | tf_op jit(solution)/shard_map/ppermute | solution.py:444
  26.8 0.3 collective-permute-start.9
  27.1 1.0 %collective-permute-done.10.refs_3_ = f32[12,128]{1,0:T(8,128)S(1)} collective-permute-done((f32[12,128]{1,0:T(8,128)S(1)}, f32[12,128]{1,0:T(8,128)S(1)}, u32[]{:S(2)}, u32[]{:S(2)}) %collective-permute-start.10) | collective-permute-done | bytes 6176 | tf_op jit(solution)/shard_map/ppermute | solution.py:444
  28.1 2.1 %collective-permute-done.8.refs_1_ = f32[12,128]{1,0:T(8,128)S(1)} collective-permute-done((f32[12,128]{1,0:T(8,128)S(1)}, f32[12,128]{1,0:T(8,128)S(1)}, u32[]{:S(2)}, u32[]{:S(2)}) %collective-permute-start.8) | collective-permute-done | bytes 6176 | tf_op jit(solution)/shard_map/ppermute | solution.py:444
  30.2 0.0 collective-permute-done.9.refs_2_
  30.3 0.6 %finish.1 = f32[3,512]{1,0:T(4,128)} custom-call(f32[12,128]{1,0:T(8,128)S(1)} %add.1.refs_0_, f32[12,128]{1,0:T(8,128)S(1)} %collective-permute-done.8.refs_1_, f32[12,128]{1,0:T(8,128)S(1)} %collective-permute-done.9.refs_2_, f32[12,128]{1,0:T(8,128)S(1)} %collective-permute-done.10.refs_3_), custom_call_target="tpu_custom_call" | custom-call | tf_op jit(solution)/shard_map/finish/pallas_call | solution.py:623
  (1 shorter events, 0.0 us)
Async XLA Ops:
  0.6 5.4 %collective-permute-start = (f32[80,128]{1,0:T(8,128)}, f32[80,128]{1,0:T(8,128)S(1)}, u32[]{:S(2)}, u32[]{:S(2)}) collective-permute-start(f32[80,128]{1,0:T(8,128)} %bitcast.38), channel_id=1, source_target_pairs={{0,2},{2,0},{1,4},{3,6},{4,1},{6,3},{5,8},{7,10},{8,5},{10,7},{9,1... | collective-permute-start | bytes 122888 | tf_op jit(solution)/shard_map/ppermute | solution.py:498
  3.6 2.4 %collective-permute-start.1 = (f32[80,128]{1,0:T(8,128)}, f32[80,128]{1,0:T(8,128)S(1)}, u32[]{:S(2)}, u32[]{:S(2)}) collective-permute-start(f32[80,128]{1,0:T(8,128)} %bitcast.39), channel_id=1, source_target_pairs={{0,1},{1,0},{4,5},{5,4},{8,9},{9,8},{12,13},{13,12},{2,3},{3,2},{6... | collective-permute-start | bytes 122888 | tf_op jit(solution)/shard_map/ppermute | solution.py:483
  7.7 4.1 %collective-permute-start.2 = (f32[80,128]{1,0:T(8,128)S(1)}, f32[80,128]{1,0:T(8,128)S(1)}, u32[]{:S(2)}, u32[]{:S(2)}) collective-permute-start(f32[80,128]{1,0:T(8,128)S(1)} %get-tuple-element.30._.refs_2_), channel_id=1, source_target_pairs={{0,2},{2,0},{1,4},{3,6},{4,1},{6,3},{5,8},{7,10},{8,5},{10,7},{9,1... | collective-permute-start | bytes 122888 | tf_op jit(solution)/shard_map/ppermute | solution.py:498
  9.5 2.2 %collective-permute-start.3 = (f32[80,128]{1,0:T(8,128)S(1)}, f32[80,128]{1,0:T(8,128)S(1)}, u32[]{:S(2)}, u32[]{:S(2)}) collective-permute-start(f32[80,128]{1,0:T(8,128)S(1)} %get-tuple-element.30._.refs_2_), channel_id=1, source_target_pairs={{0,1},{1,0},{4,5},{5,4},{8,9},{9,8},{12,13},{13,12},{2,3},{3,2},{6... | collective-permute-start | bytes 122888 | tf_op jit(solution)/shard_map/ppermute | solution.py:483
  13.4 4.0 %collective-permute-start.4 = (f32[24,128]{1,0:T(8,128)S(1)}, f32[24,128]{1,0:T(8,128)S(1)}, u32[]{:S(2)}, u32[]{:S(2)}) collective-permute-start(f32[24,128]{1,0:T(8,128)S(1)} %get-tuple-element.32.after.refs_0_), channel_id=1, source_target_pairs={{0,2},{2,0},{1,3},{3,1},{4,6},{6,4},{5,7},{7,5},{8,10},{10,8},{9,1... | collective-permute-start | bytes 36872 | tf_op jit(solution)/shard_map/ppermute | solution.py:593
  19.3 1.9 %collective-permute-start.5 = (f32[12,128]{1,0:T(8,128)S(1)}, f32[12,128]{1,0:T(8,128)S(1)}, u32[]{:S(2)}, u32[]{:S(2)}) collective-permute-start(f32[12,128]{1,0:T(8,128)S(1)} %control.1.refs_0_), channel_id=1, source_target_pairs={{0,1},{1,0},{2,3},{3,2},{4,5},{5,4},{6,7},{7,6},{8,9},{9,8},{10,11... | collective-permute-start | bytes 18440 | tf_op jit(solution)/shard_map/ppermute | solution.py:444
  19.4 3.7 %collective-permute-start.6 = (f32[12,128]{1,0:T(8,128)S(1)}, f32[12,128]{1,0:T(8,128)S(1)}, u32[]{:S(2)}, u32[]{:S(2)}) collective-permute-start(f32[12,128]{1,0:T(8,128)S(1)} %control.1.refs_0_), channel_id=1, source_target_pairs={{0,4},{1,5},{2,6},{3,7},{4,0},{5,1},{6,2},{7,3},{8,12},{9,13},{10,... | collective-permute-start | bytes 18440 | tf_op jit(solution)/shard_map/ppermute | solution.py:444
  20.2 3.1 %collective-permute-start.7 = (f32[12,128]{1,0:T(8,128)S(1)}, f32[12,128]{1,0:T(8,128)S(1)}, u32[]{:S(2)}, u32[]{:S(2)}) collective-permute-start(f32[12,128]{1,0:T(8,128)S(1)} %control.1.refs_0_), channel_id=1, source_target_pairs={{0,5},{1,4},{2,7},{3,6},{4,1},{5,0},{6,3},{7,2},{8,13},{9,12},{10,... | collective-permute-start | bytes 18440 | tf_op jit(solution)/shard_map/ppermute | solution.py:444
  23.3 4.9 %collective-permute-start.10 = (f32[12,128]{1,0:T(8,128)S(1)}, f32[12,128]{1,0:T(8,128)S(1)}, u32[]{:S(2)}, u32[]{:S(2)}) collective-permute-start(f32[12,128]{1,0:T(8,128)S(1)} %add.1.refs_0_), channel_id=1, source_target_pairs={{0,11},{1,10},{2,9},{3,8},{4,15},{5,14},{6,13},{7,12},{8,3},{9,2},... | collective-permute-start | bytes 18440 | tf_op jit(solution)/shard_map/ppermute | solution.py:444
  26.3 4.0 %collective-permute-start.8 = (f32[12,128]{1,0:T(8,128)S(1)}, f32[12,128]{1,0:T(8,128)S(1)}, u32[]{:S(2)}, u32[]{:S(2)}) collective-permute-start(f32[12,128]{1,0:T(8,128)S(1)} %add.1.refs_0_), channel_id=1, source_target_pairs={{0,9},{1,8},{2,11},{3,10},{4,13},{5,12},{6,15},{7,14},{8,1},{9,0},... | collective-permute-start | bytes 18440 | tf_op jit(solution)/shard_map/ppermute | solution.py:444
  26.8 3.4 %collective-permute-start.9 = (f32[12,128]{1,0:T(8,128)S(1)}, f32[12,128]{1,0:T(8,128)S(1)}, u32[]{:S(2)}, u32[]{:S(2)}) collective-permute-start(f32[12,128]{1,0:T(8,128)S(1)} %add.1.refs_0_), channel_id=1, source_target_pairs={{0,3},{1,2},{2,1},{3,0},{4,7},{5,6},{6,5},{7,4},{8,11},{9,10},{10,... | collective-permute-start | bytes 18440 | tf_op jit(solution)/shard_map/ppermute | solution.py:444

commit v20 on v13

--- a/solution.py
+++ b/solution.py
@@ -438,7 +438,7 @@
     blocks = cells // LANES
     per = blocks * nodes
     slots = ffd_index.shape[1]
-    far_slots = max(1, slots * 3 // 8)
+    far_slots = slots // 2
     owned = base_points.shape[1] // lax.axis_size("nodes")
     peers = lax.axis_size(CELL_AXES)
     cores = lax.axis_size("sub")

time: 30.5 us -> 30.4 us (level)
  no operation moved by 1% of the time
where the time goes in v20:
time: 30.4 us; the launch traced here: 30.3 us
  starting transfers between devices  12.3 us (40%)
  Pallas kernels  12 us (39%)
  waiting for transfers between devices  5.24 us (17%)
  between operations  0.72 us (2%)
    ppermute x6, starting transfers between devices, exchanged(): lax.ppermute(value, SUM_AXES, [(i, i ^ mask) for i in range(peers)])  5.73 us
    ppermute x6, waiting for transfers between devices, exchanged(): lax.ppermute(value, SUM_AXES, [(i, i ^ mask) for i in range(peers)])  4.93 us
    ppermute x2, starting transfers between devices, swaps(): return (lax.ppermute(array, SUM_AXES, pairs), close)  4.47 us
    pallas_call x1, Pallas kernels, body(): pl.pallas_call(functools.partial(wendland_kernel, 0), out_shape=near_shap...  2.71 us
    pallas_call x1, Pallas kernels, body(): pl.pallas_call(functools.partial(prepare_kernel, nodes), out_shape=(shape...  2.18 us
    pallas_call x1, Pallas kernels, body(): pl.pallas_call(functools.partial(far_wendland_kernel, half), out_shape=(f...  2.13 us
    pallas_call x1, Pallas kernels, body(): pl.pallas_call(functools.partial(control_kernel, scale), out_shape=shape(...  1.84 us
    ppermute x1, starting transfers between devices, body(): all_sens.append(lax.ppermute(part_sens, 'nodes', ring))  1.32 us
  transfers between devices with their start and end apart: 11, of which 5 were waited for; matrix products, arithmetic and copies ran while one was open for 0% of the time, Pallas kernels for 23%

profile of v20, /device:TPU:0, one launch (start us, length us, event | category | flops | bytes accessed | tf_op | source)
XLA Modules:
  0.0 30.3 jit_solution(10337993468085920818)
XLA Ops:
  0.6 0.5 %collective-permute-start = (f32[80,128]{1,0:T(8,128)}, f32[80,128]{1,0:T(8,128)S(1)}, u32[]{:S(2)}, u32[]{:S(2)}) collective-permute-start(f32[80,128]{1,0:T(8,128)} %bitcast.38), channel_id=1, source_target_pairs={{0,1},{1,0},{4,5},{5,4},{8,9},{9,8},{12,13},{13,12},{2,3},{3,2},{6... | collective-permute-start | bytes 122888 | tf_op jit(solution)/shard_map/ppermute | solution.py:455
  1.2 2.6 %collective-permute-start.1 = (f32[80,128]{1,0:T(8,128)}, f32[80,128]{1,0:T(8,128)S(1)}, u32[]{:S(2)}, u32[]{:S(2)}) collective-permute-start(f32[80,128]{1,0:T(8,128)} %bitcast.39), channel_id=1, source_target_pairs={{0,2},{2,0},{1,4},{3,6},{4,1},{6,3},{5,8},{7,10},{8,5},{10,7},{9,1... | collective-permute-start | bytes 122888 | tf_op jit(solution)/shard_map/ppermute | solution.py:470
  3.7 2.2 %prepare.1 = (f32[2400,128]{1,0:T(8,128)S(1)}, f32[400,128]{1,0:T(8,128)S(1)}, f32[80,128]{1,0:T(8,128)S(1)}, f32[240,128]{1,0:T(8,128)S(1)}, s32[96,128]{1,0:T(...) custom-call(bf16[2400,128]{1,0:T(8,128)(2,1)} %bitcast.32, ...), custom_call_target="tpu_custom_call" | custom-call | flops 1000000000 | bytes 10000000 | tf_op jit(solution)/shard_map/prepare/pallas_call | solution.py:474
  5.9 0.0 collective-permute-done.refs_0_
  5.9 0.0 collective-permute-done.1.refs_1_
  5.9 1.2 %sweep.1._.refs_2_ = f32[80,128]{1,0:T(8,128)S(1)} custom-call(f32[80,128]{1,0:T(8,128)S(1)} %collective-permute-done.refs_0_, f32[80,128]{1,0:T(8,128)S(1)} %collective-permute-done.1.refs_1_, f32[80,128]{1,0:T(8,128)S(1)} %get-tuple-element.21.refs_2_, f32[80,128]{1,0:T(8,128)S(1)} %get-tuple-element.22.refs_3_, ...), custom_call_target="tpu_custom_call" | custom-call | flops 716800 | bytes 1228800 | tf_op jit(solution)/shard_map/sweep/pallas_call | solution.py:529
  7.2 0.3 collective-permute-start.2
  7.4 1.9 %collective-permute-start.3 = (f32[80,128]{1,0:T(8,128)S(1)}, f32[80,128]{1,0:T(8,128)S(1)}, u32[]{:S(2)}, u32[]{:S(2)}) collective-permute-start(f32[80,128]{1,0:T(8,128)S(1)} %sweep.1._.refs_2_), channel_id=1, source_target_pairs={{0,2},{2,0},{1,4},{3,6},{4,1},{6,3},{5,8},{7,10},{8,5},{10,7},{9,1... | collective-permute-start | bytes 122888 | tf_op jit(solution)/shard_map/ppermute | solution.py:470
  9.3 2.7 %near_wendland.1.refs_9_.refs_2_ = bf16[1280,2048]{1,0:T(8,128)(2,1)S(1)} custom-call(bf16[1024,64]{1,0:T(8,128)(2,1)S(1)} %get-tuple-element.19.left_ref, bf16[64,2048]{1,0:T(8,128)(2,1)S(1)} %get-tuple-element.20.right_ref, f32[80,128]{1,0:T(8,128)S(1)} %sweep.1._.refs_2_), custom_call_target="tpu_custom_call" | custom-call | flops 1000000000 | bytes 10000000 | tf_op jit(solution)/shard_map/near_wendland/pallas_call | solution.py:545
  12.1 0.0 collective-permute-done.2.refs_0_
  12.1 0.0 collective-permute-done.3.refs_1_
  12.1 1.3 %last_sweep.1 = (f32[80,128]{1,0:T(8,128)S(1)}, f32[24,128]{1,0:T(8,128)S(1)}) custom-call(f32[80,128]{1,0:T(8,128)S(1)} %collective-permute-done.2.refs_0_, f32[80,128]{1,0:T(8,128)S(1)} %collective-permute-done.3.refs_1_, f32[80,128]{1,0:T(8,128)S(1)} %sweep.1._.refs_2_, f32[80,128]{1,0:T(8,128)S(1)} %get-tuple-element.22.refs_3_, ...), custom_call_target="tpu_custom_call" | custom-call | flops 716800 | bytes 1228800 | tf_op jit(solution)/shard_map/last_sweep/pallas_call | solution.py:554
  13.4 1.3 %collective-permute-start.4 = (f32[24,128]{1,0:T(8,128)S(1)}, f32[24,128]{1,0:T(8,128)S(1)}, u32[]{:S(2)}, u32[]{:S(2)}) collective-permute-start(f32[24,128]{1,0:T(8,128)S(1)} %get-tuple-element.28.after.refs_0_), channel_id=1, source_target_pairs={{0,2},{2,0},{1,3},{3,1},{4,6},{6,4},{5,7},{7,5},{8,10},{10,8},{9,1... | collective-permute-start | bytes 36872 | tf_op jit(solution)/shard_map/ppermute | solution.py:568
  14.7 2.1 %far_wendland.1 = (bf16[768,2048]{1,0:T(8,128)(2,1)S(1)}, bf16[8192,128]{1,0:T(8,128)(2,1)S(1)}, f32[80,128]{1,0:T(8,128)}) custom-call(bf16[1024,64]{1,0:T(8,128)(2,1)S(1)} %get-tuple-element.19.left_ref, bf16[64,2048]{1,0:T(8,128)(2,1)S(1)} %get-tuple-element.20.right_ref, f32[24,128]{1,0:T(8,128)S(1)} %get-tuple-element.28.after.refs_0_, ...), custom_call_target="tpu_custom_call" | custom-call | flops 1000000000 | bytes 10000000 | tf_op jit(solution)/shard_map/far_wendland/pallas_call | solution.py:570
  16.8 0.3 %collective-permute-done.4.refs_1_ = f32[24,128]{1,0:T(8,128)S(1)} collective-permute-done((f32[24,128]{1,0:T(8,128)S(1)}, f32[24,128]{1,0:T(8,128)S(1)}, u32[]{:S(2)}, u32[]{:S(2)}) %collective-permute-start.4) | collective-permute-done | bytes 12320 | tf_op jit(solution)/shard_map/ppermute | solution.py:568
  17.1 1.8 %control.1.refs_0_ = f32[12,128]{1,0:T(8,128)S(1)} custom-call(f32[24,128]{1,0:T(8,128)S(1)} %get-tuple-element.28.after.refs_0_, f32[24,128]{1,0:T(8,128)S(1)} %collective-permute-done.4.refs_1_, bf16[1280,2048]{1,0:T(8,128)(2,1)S(1)} %near_wendland.1.refs_9_.refs_2_, bf16[768,2048]{1,0:T(8,128)(2,1)S(1)} %get-tuple-element.32.refs_3_, ...), custom_call_target="tpu_custom_call" | custom-call | tf_op jit(solution)/shard_map/control/pallas_call | solution.py:582
  19.0 0.1 collective-permute-start.5
  19.0 1.2 %collective-permute-start.6 = (f32[12,128]{1,0:T(8,128)S(1)}, f32[12,128]{1,0:T(8,128)S(1)}, u32[]{:S(2)}, u32[]{:S(2)}) collective-permute-start(f32[12,128]{1,0:T(8,128)S(1)} %control.1.refs_0_), channel_id=1, source_target_pairs={{0,4},{1,5},{2,6},{3,7},{4,0},{5,1},{6,2},{7,3},{8,12},{9,13},{10,... | collective-permute-start | bytes 18440 | tf_op jit(solution)/shard_map/ppermute | solution.py:419
  20.2 0.7 %collective-permute-start.7 = (f32[12,128]{1,0:T(8,128)S(1)}, f32[12,128]{1,0:T(8,128)S(1)}, u32[]{:S(2)}, u32[]{:S(2)}) collective-permute-start(f32[12,128]{1,0:T(8,128)S(1)} %control.1.refs_0_), channel_id=1, source_target_pairs={{0,5},{1,4},{2,7},{3,6},{4,1},{5,0},{6,3},{7,2},{8,13},{9,12},{10,... | collective-permute-start | bytes 18440 | tf_op jit(solution)/shard_map/ppermute | solution.py:419
  20.9 0.0 collective-permute-done.5.refs_1_
  20.9 1.9 %collective-permute-done.6.refs_2_ = f32[12,128]{1,0:T(8,128)S(1)} collective-permute-done((f32[12,128]{1,0:T(8,128)S(1)}, f32[12,128]{1,0:T(8,128)S(1)}, u32[]{:S(2)}, u32[]{:S(2)}) %collective-permute-start.6) | collective-permute-done | bytes 6176 | tf_op jit(solution)/shard_map/ppermute | solution.py:419
  22.8 0.6 %collective-permute-done.7.refs_3_ = f32[12,128]{1,0:T(8,128)S(1)} collective-permute-done((f32[12,128]{1,0:T(8,128)S(1)}, f32[12,128]{1,0:T(8,128)S(1)}, u32[]{:S(2)}, u32[]{:S(2)}) %collective-permute-start.7) | collective-permute-done | bytes 6176 | tf_op jit(solution)/shard_map/ppermute | solution.py:419
  23.4 2.3 %collective-permute-start.10 = (f32[12,128]{1,0:T(8,128)S(1)}, f32[12,128]{1,0:T(8,128)S(1)}, u32[]{:S(2)}, u32[]{:S(2)}) collective-permute-start(f32[12,128]{1,0:T(8,128)S(1)} %add.1.refs_0_), channel_id=1, source_target_pairs={{0,11},{1,10},{2,9},{3,8},{4,15},{5,14},{6,13},{7,12},{8,3},{9,2},... | collective-permute-start | bytes 18440 | tf_op jit(solution)/shard_map/ppermute | solution.py:419
  25.7 0.9 %collective-permute-start.8 = (f32[12,128]{1,0:T(8,128)S(1)}, f32[12,128]{1,0:T(8,128)S(1)}, u32[]{:S(2)}, u32[]{:S(2)}) collective-permute-start(f32[12,128]{1,0:T(8,128)S(1)} %add.1.refs_0_), channel_id=1, source_target_pairs={{0,9},{1,8},{2,11},{3,10},{4,13},{5,12},{6,15},{7,14},{8,1},{9,0},... | collective-permute-start | bytes 18440 | tf_op jit(solution)/shard_map/ppermute | solution.py:419
  26.5 0.6 %collective-permute-start.9 = (f32[12,128]{1,0:T(8,128)S(1)}, f32[12,128]{1,0:T(8,128)S(1)}, u32[]{:S(2)}, u32[]{:S(2)}) collective-permute-start(f32[12,128]{1,0:T(8,128)S(1)} %add.1.refs_0_), channel_id=1, source_target_pairs={{0,3},{1,2},{2,1},{3,0},{4,7},{5,6},{6,5},{7,4},{8,11},{9,10},{10,... | collective-permute-start | bytes 18440 | tf_op jit(solution)/shard_map/ppermute | solution.py:419
  27.2 1.1 %collective-permute-done.10.refs_3_ = f32[12,128]{1,0:T(8,128)S(1)} collective-permute-done((f32[12,128]{1,0:T(8,128)S(1)}, f32[12,128]{1,0:T(8,128)S(1)}, u32[]{:S(2)}, u32[]{:S(2)}) %collective-permute-start.10) | collective-permute-done | bytes 6176 | tf_op jit(solution)/shard_map/ppermute | solution.py:419
  28.2 1.4 %collective-permute-done.8.refs_1_ = f32[12,128]{1,0:T(8,128)S(1)} collective-permute-done((f32[12,128]{1,0:T(8,128)S(1)}, f32[12,128]{1,0:T(8,128)S(1)}, u32[]{:S(2)}, u32[]{:S(2)}) %collective-permute-start.8) | collective-permute-done | bytes 6176 | tf_op jit(solution)/shard_map/ppermute | solution.py:419
  29.6 0.0 collective-permute-done.9.refs_2_
  29.6 0.6 %finish.1 = f32[3,512]{1,0:T(4,128)} custom-call(f32[12,128]{1,0:T(8,128)S(1)} %add.1.refs_0_, f32[12,128]{1,0:T(8,128)S(1)} %collective-permute-done.8.refs_1_, f32[12,128]{1,0:T(8,128)S(1)} %collective-permute-done.9.refs_2_, f32[12,128]{1,0:T(8,128)S(1)} %collective-permute-done.10.refs_3_), custom_call_target="tpu_custom_call" | custom-call | tf_op jit(solution)/shard_map/finish/pallas_call | solution.py:598
  (1 shorter events, 0.0 us)
Async XLA Ops:
  0.6 5.3 %collective-permute-start = (f32[80,128]{1,0:T(8,128)}, f32[80,128]{1,0:T(8,128)S(1)}, u32[]{:S(2)}, u32[]{:S(2)}) collective-permute-start(f32[80,128]{1,0:T(8,128)} %bitcast.38), channel_id=1, source_target_pairs={{0,1},{1,0},{4,5},{5,4},{8,9},{9,8},{12,13},{13,12},{2,3},{3,2},{6... | collective-permute-start | bytes 122888 | tf_op jit(solution)/shard_map/ppermute | solution.py:455
  1.2 4.8 %collective-permute-start.1 = (f32[80,128]{1,0:T(8,128)}, f32[80,128]{1,0:T(8,128)S(1)}, u32[]{:S(2)}, u32[]{:S(2)}) collective-permute-start(f32[80,128]{1,0:T(8,128)} %bitcast.39), channel_id=1, source_target_pairs={{0,2},{2,0},{1,4},{3,6},{4,1},{6,3},{5,8},{7,10},{8,5},{10,7},{9,1... | collective-permute-start | bytes 122888 | tf_op jit(solution)/shard_map/ppermute | solution.py:470
  7.2 4.9 %collective-permute-start.2 = (f32[80,128]{1,0:T(8,128)S(1)}, f32[80,128]{1,0:T(8,128)S(1)}, u32[]{:S(2)}, u32[]{:S(2)}) collective-permute-start(f32[80,128]{1,0:T(8,128)S(1)} %sweep.1._.refs_2_), channel_id=1, source_target_pairs={{0,1},{1,0},{4,5},{5,4},{8,9},{9,8},{12,13},{13,12},{2,3},{3,2},{6... | collective-permute-start | bytes 122888 | tf_op jit(solution)/shard_map/ppermute | solution.py:455
  7.4 4.6 %collective-permute-start.3 = (f32[80,128]{1,0:T(8,128)S(1)}, f32[80,128]{1,0:T(8,128)S(1)}, u32[]{:S(2)}, u32[]{:S(2)}) collective-permute-start(f32[80,128]{1,0:T(8,128)S(1)} %sweep.1._.refs_2_), channel_id=1, source_target_pairs={{0,2},{2,0},{1,4},{3,6},{4,1},{6,3},{5,8},{7,10},{8,5},{10,7},{9,1... | collective-permute-start | bytes 122888 | tf_op jit(solution)/shard_map/ppermute | solution.py:470
  13.4 3.8 %collective-permute-start.4 = (f32[24,128]{1,0:T(8,128)S(1)}, f32[24,128]{1,0:T(8,128)S(1)}, u32[]{:S(2)}, u32[]{:S(2)}) collective-permute-start(f32[24,128]{1,0:T(8,128)S(1)} %get-tuple-element.28.after.refs_0_), channel_id=1, source_target_pairs={{0,2},{2,0},{1,3},{3,1},{4,6},{6,4},{5,7},{7,5},{8,10},{10,8},{9,1... | collective-permute-start | bytes 36872 | tf_op jit(solution)/shard_map/ppermute | solution.py:568
  19.0 1.9 %collective-permute-start.5 = (f32[12,128]{1,0:T(8,128)S(1)}, f32[12,128]{1,0:T(8,128)S(1)}, u32[]{:S(2)}, u32[]{:S(2)}) collective-permute-start(f32[12,128]{1,0:T(8,128)S(1)} %control.1.refs_0_), channel_id=1, source_target_pairs={{0,1},{1,0},{2,3},{3,2},{4,5},{5,4},{6,7},{7,6},{8,9},{9,8},{10,11... | collective-permute-start | bytes 18440 | tf_op jit(solution)/shard_map/ppermute | solution.py:419
  19.0 3.7 %collective-permute-start.6 = (f32[12,128]{1,0:T(8,128)S(1)}, f32[12,128]{1,0:T(8,128)S(1)}, u32[]{:S(2)}, u32[]{:S(2)}) collective-permute-start(f32[12,128]{1,0:T(8,128)S(1)} %control.1.refs_0_), channel_id=1, source_target_pairs={{0,4},{1,5},{2,6},{3,7},{4,0},{5,1},{6,2},{7,3},{8,12},{9,13},{10,... | collective-permute-start | bytes 18440 | tf_op jit(solution)/shard_map/ppermute | solution.py:419
  20.2 3.1 %collective-permute-start.7 = (f32[12,128]{1,0:T(8,128)S(1)}, f32[12,128]{1,0:T(8,128)S(1)}, u32[]{:S(2)}, u32[]{:S(2)}) collective-permute-start(f32[12,128]{1,0:T(8,128)S(1)} %control.1.refs_0_), channel_id=1, source_target_pairs={{0,5},{1,4},{2,7},{3,6},{4,1},{5,0},{6,3},{7,2},{8,13},{9,12},{10,... | collective-permute-start | bytes 18440 | tf_op jit(solution)/shard_map/ppermute | solution.py:419
  23.4 4.9 %collective-permute-start.10 = (f32[12,128]{1,0:T(8,128)S(1)}, f32[12,128]{1,0:T(8,128)S(1)}, u32[]{:S(2)}, u32[]{:S(2)}) collective-permute-start(f32[12,128]{1,0:T(8,128)S(1)} %add.1.refs_0_), channel_id=1, source_target_pairs={{0,11},{1,10},{2,9},{3,8},{4,15},{5,14},{6,13},{7,12},{8,3},{9,2},... | collective-permute-start | bytes 18440 | tf_op jit(solution)/shard_map/ppermute | solution.py:419
  25.7 4.0 %collective-permute-start.8 = (f32[12,128]{1,0:T(8,128)S(1)}, f32[12,128]{1,0:T(8,128)S(1)}, u32[]{:S(2)}, u32[]{:S(2)}) collective-permute-start(f32[12,128]{1,0:T(8,128)S(1)} %add.1.refs_0_), channel_id=1, source_target_pairs={{0,9},{1,8},{2,11},{3,10},{4,13},{5,12},{6,15},{7,14},{8,1},{9,0},... | collective-permute-start | bytes 18440 | tf_op jit(solution)/shard_map/ppermute | solution.py:419
  26.5 3.1 %collective-permute-start.9 = (f32[12,128]{1,0:T(8,128)S(1)}, f32[12,128]{1,0:T(8,128)S(1)}, u32[]{:S(2)}, u32[]{:S(2)}) collective-permute-start(f32[12,128]{1,0:T(8,128)S(1)} %add.1.refs_0_), channel_id=1, source_target_pairs={{0,3},{1,2},{2,1},{3,0},{4,7},{5,6},{6,5},{7,4},{8,11},{9,10},{10,... | collective-permute-start | bytes 18440 | tf_op jit(solution)/shard_map/ppermute | solution.py:419

commit v21 on v20

--- a/solution.py
+++ b/solution.py
@@ -231,8 +231,8 @@
             out_ref[a * per + half : a * per + half + 8, :] = total
 
 
-def sweep_kernel(blocks, *refs):
-    sweep_into(blocks, *refs)
+def sweep_kernel(blocks, far_ref, close_ref, *refs):
+    sweep_into(blocks, close_ref, far_ref, *refs)
 
 
 def last_sweep_kernel(blocks, *refs):
@@ -535,7 +535,7 @@
             compiler_params=PARAMS,
             cost_estimate=sweep_cost,
             name="sweep",
-        )(close, far, adjoint, rhs, off, inverse, lane, step)
+        )(far, close, adjoint, rhs, off, inverse, lane, step)
         far, close = swaps(adjoint)
 
     half = cells * 5 // 8 // LANES * LANES

time: 30.4 us -> 30.4 us (level)
  no operation moved by 1% of the time
where the time goes in v21:
time: 30.4 us; the launch traced here: 30.2 us
  starting transfers between devices  12.2 us (40%)
  Pallas kernels  12 us (39%)
  waiting for transfers between devices  5.32 us (18%)
  between operations  0.72 us (2%)
    ppermute x6, starting transfers between devices, exchanged(): lax.ppermute(value, SUM_AXES, [(i, i ^ mask) for i in range(peers)])  5.73 us
    ppermute x6, waiting for transfers between devices, exchanged(): lax.ppermute(value, SUM_AXES, [(i, i ^ mask) for i in range(peers)])  5.01 us
    ppermute x2, starting transfers between devices, swaps(): return (lax.ppermute(array, SUM_AXES, pairs), close)  4.57 us
    pallas_call x1, Pallas kernels, body(): pl.pallas_call(functools.partial(wendland_kernel, 0), out_shape=near_shap...  2.7 us
    pallas_call x1, Pallas kernels, body(): pl.pallas_call(functools.partial(prepare_kernel, nodes), out_shape=(shape...  2.18 us
    pallas_call x1, Pallas kernels, body(): pl.pallas_call(functools.partial(far_wendland_kernel, half), out_shape=(f...  2.12 us
    pallas_call x1, Pallas kernels, body(): pl.pallas_call(functools.partial(control_kernel, scale), out_shape=shape(...  1.84 us
    ppermute x1, starting transfers between devices, body(): all_sens.append(lax.ppermute(part_sens, 'nodes', ring))  1.33 us
  transfers between devices with their start and end apart: 11, of which 5 were waited for; matrix products, arithmetic and copies ran while one was open for 0% of the time, Pallas kernels for 23%

profile of v21, /device:TPU:0, one launch (start us, length us, event | category | flops | bytes accessed | tf_op | source)
XLA Modules:
  0.0 30.2 jit_solution(2600276562387238707)
XLA Ops:
  0.6 3.0 %collective-permute-start = (f32[80,128]{1,0:T(8,128)}, f32[80,128]{1,0:T(8,128)S(1)}, u32[]{:S(2)}, u32[]{:S(2)}) collective-permute-start(f32[80,128]{1,0:T(8,128)} %bitcast.38), channel_id=1, source_target_pairs={{0,2},{2,0},{1,4},{3,6},{4,1},{6,3},{5,8},{7,10},{8,5},{10,7},{9,1... | collective-permute-start | bytes 122888 | tf_op jit(solution)/shard_map/ppermute | solution.py:470
  3.6 0.2 collective-permute-start.1
  3.8 2.2 %prepare.1 = (f32[2400,128]{1,0:T(8,128)S(1)}, f32[400,128]{1,0:T(8,128)S(1)}, f32[80,128]{1,0:T(8,128)S(1)}, f32[240,128]{1,0:T(8,128)S(1)}, s32[96,128]{1,0:T(...) custom-call(bf16[2400,128]{1,0:T(8,128)(2,1)} %bitcast.32, ...), custom_call_target="tpu_custom_call" | custom-call | flops 1000000000 | bytes 10000000 | tf_op jit(solution)/shard_map/prepare/pallas_call | solution.py:474
  6.0 0.0 collective-permute-done.far_ref
  6.0 0.0 collective-permute-done.1.close_ref
  6.0 1.2 %sweep.1._.refs_2_ = f32[80,128]{1,0:T(8,128)S(1)} custom-call(f32[80,128]{1,0:T(8,128)S(1)} %collective-permute-done.far_ref, f32[80,128]{1,0:T(8,128)S(1)} %collective-permute-done.1.close_ref, f32[80,128]{1,0:T(8,128)S(1)} %get-tuple-element.21.refs_0_, f32[80,128]{1,0:T(8,128)S(1)} %get-tuple-element.22.refs_1_.refs_3_, ...), custom_call_target="tpu_custom_call" | custom-call | flops 716800 | bytes 1228800 | tf_op jit(solution)/shard_map/sweep/pallas_call | solution.py:529
  7.3 0.4 %collective-permute-start.2 = (f32[80,128]{1,0:T(8,128)S(1)}, f32[80,128]{1,0:T(8,128)S(1)}, u32[]{:S(2)}, u32[]{:S(2)}) collective-permute-start(f32[80,128]{1,0:T(8,128)S(1)} %sweep.1._.refs_2_), channel_id=1, source_target_pairs={{0,1},{1,0},{4,5},{5,4},{8,9},{9,8},{12,13},{13,12},{2,3},{3,2},{6... | collective-permute-start | bytes 122888 | tf_op jit(solution)/shard_map/ppermute | solution.py:455
  7.7 1.6 %collective-permute-start.3 = (f32[80,128]{1,0:T(8,128)S(1)}, f32[80,128]{1,0:T(8,128)S(1)}, u32[]{:S(2)}, u32[]{:S(2)}) collective-permute-start(f32[80,128]{1,0:T(8,128)S(1)} %sweep.1._.refs_2_), channel_id=1, source_target_pairs={{0,2},{2,0},{1,4},{3,6},{4,1},{6,3},{5,8},{7,10},{8,5},{10,7},{9,1... | collective-permute-start | bytes 122888 | tf_op jit(solution)/shard_map/ppermute | solution.py:470
  9.2 2.7 %near_wendland.1.refs_9_.refs_2_ = bf16[1280,2048]{1,0:T(8,128)(2,1)S(1)} custom-call(bf16[1024,64]{1,0:T(8,128)(2,1)S(1)} %get-tuple-element.19.left_ref, bf16[64,2048]{1,0:T(8,128)(2,1)S(1)} %get-tuple-element.20.right_ref, f32[80,128]{1,0:T(8,128)S(1)} %sweep.1._.refs_2_), custom_call_target="tpu_custom_call" | custom-call | flops 1000000000 | bytes 10000000 | tf_op jit(solution)/shard_map/near_wendland/pallas_call | solution.py:545
  11.9 0.0 collective-permute-done.2.refs_0_
  12.0 0.0 collective-permute-done.3.refs_1_
  12.0 1.3 %last_sweep.1 = (f32[80,128]{1,0:T(8,128)S(1)}, f32[24,128]{1,0:T(8,128)S(1)}) custom-call(f32[80,128]{1,0:T(8,128)S(1)} %collective-permute-done.2.refs_0_, f32[80,128]{1,0:T(8,128)S(1)} %collective-permute-done.3.refs_1_, f32[80,128]{1,0:T(8,128)S(1)} %sweep.1._.refs_2_, f32[80,128]{1,0:T(8,128)S(1)} %get-tuple-element.22.refs_1_.refs_3_, ...), custom_call_target="tpu_custom_call" | custom-call | flops 716800 | bytes 1228800 | tf_op jit(solution)/shard_map/last_sweep/pallas_call | solution.py:554
  13.2 1.3 %collective-permute-start.4 = (f32[24,128]{1,0:T(8,128)S(1)}, f32[24,128]{1,0:T(8,128)S(1)}, u32[]{:S(2)}, u32[]{:S(2)}) collective-permute-start(f32[24,128]{1,0:T(8,128)S(1)} %get-tuple-element.28.after.refs_0_), channel_id=1, source_target_pairs={{0,2},{2,0},{1,3},{3,1},{4,6},{6,4},{5,7},{7,5},{8,10},{10,8},{9,1... | collective-permute-start | bytes 36872 | tf_op jit(solution)/shard_map/ppermute | solution.py:568
  14.6 2.1 %far_wendland.1 = (bf16[768,2048]{1,0:T(8,128)(2,1)S(1)}, bf16[8192,128]{1,0:T(8,128)(2,1)S(1)}, f32[80,128]{1,0:T(8,128)}) custom-call(bf16[1024,64]{1,0:T(8,128)(2,1)S(1)} %get-tuple-element.19.left_ref, bf16[64,2048]{1,0:T(8,128)(2,1)S(1)} %get-tuple-element.20.right_ref, f32[24,128]{1,0:T(8,128)S(1)} %get-tuple-element.28.after.refs_0_, ...), custom_call_target="tpu_custom_call" | custom-call | flops 1000000000 | bytes 10000000 | tf_op jit(solution)/shard_map/far_wendland/pallas_call | solution.py:570
  16.7 0.3 %collective-permute-done.4.refs_1_ = f32[24,128]{1,0:T(8,128)S(1)} collective-permute-done((f32[24,128]{1,0:T(8,128)S(1)}, f32[24,128]{1,0:T(8,128)S(1)}, u32[]{:S(2)}, u32[]{:S(2)}) %collective-permute-start.4) | collective-permute-done | bytes 12320 | tf_op jit(solution)/shard_map/ppermute | solution.py:568
  17.0 1.8 %control.1.refs_0_ = f32[12,128]{1,0:T(8,128)S(1)} custom-call(f32[24,128]{1,0:T(8,128)S(1)} %get-tuple-element.28.after.refs_0_, f32[24,128]{1,0:T(8,128)S(1)} %collective-permute-done.4.refs_1_, bf16[1280,2048]{1,0:T(8,128)(2,1)S(1)} %near_wendland.1.refs_9_.refs_2_, bf16[768,2048]{1,0:T(8,128)(2,1)S(1)} %get-tuple-element.32.refs_3_, ...), custom_call_target="tpu_custom_call" | custom-call | tf_op jit(solution)/shard_map/control/pallas_call | solution.py:582
  18.8 0.1 collective-permute-start.5
  18.9 1.1 %collective-permute-start.6 = (f32[12,128]{1,0:T(8,128)S(1)}, f32[12,128]{1,0:T(8,128)S(1)}, u32[]{:S(2)}, u32[]{:S(2)}) collective-permute-start(f32[12,128]{1,0:T(8,128)S(1)} %control.1.refs_0_), channel_id=1, source_target_pairs={{0,4},{1,5},{2,6},{3,7},{4,0},{5,1},{6,2},{7,3},{8,12},{9,13},{10,... | collective-permute-start | bytes 18440 | tf_op jit(solution)/shard_map/ppermute | solution.py:419
  20.0 0.7 %collective-permute-start.7 = (f32[12,128]{1,0:T(8,128)S(1)}, f32[12,128]{1,0:T(8,128)S(1)}, u32[]{:S(2)}, u32[]{:S(2)}) collective-permute-start(f32[12,128]{1,0:T(8,128)S(1)} %control.1.refs_0_), channel_id=1, source_target_pairs={{0,5},{1,4},{2,7},{3,6},{4,1},{5,0},{6,3},{7,2},{8,13},{9,12},{10,... | collective-permute-start | bytes 18440 | tf_op jit(solution)/shard_map/ppermute | solution.py:419
  20.8 0.0 collective-permute-done.5.refs_1_
  20.8 1.9 %collective-permute-done.6.refs_2_ = f32[12,128]{1,0:T(8,128)S(1)} collective-permute-done((f32[12,128]{1,0:T(8,128)S(1)}, f32[12,128]{1,0:T(8,128)S(1)}, u32[]{:S(2)}, u32[]{:S(2)}) %collective-permute-start.6) | collective-permute-done | bytes 6176 | tf_op jit(solution)/shard_map/ppermute | solution.py:419
  22.6 0.5 %collective-permute-done.7.refs_3_ = f32[12,128]{1,0:T(8,128)S(1)} collective-permute-done((f32[12,128]{1,0:T(8,128)S(1)}, f32[12,128]{1,0:T(8,128)S(1)}, u32[]{:S(2)}, u32[]{:S(2)}) %collective-permute-start.7) | collective-permute-done | bytes 6176 | tf_op jit(solution)/shard_map/ppermute | solution.py:419
  23.2 2.4 %collective-permute-start.10 = (f32[12,128]{1,0:T(8,128)S(1)}, f32[12,128]{1,0:T(8,128)S(1)}, u32[]{:S(2)}, u32[]{:S(2)}) collective-permute-start(f32[12,128]{1,0:T(8,128)S(1)} %add.1.refs_0_), channel_id=1, source_target_pairs={{0,11},{1,10},{2,9},{3,8},{4,15},{5,14},{6,13},{7,12},{8,3},{9,2},... | collective-permute-start | bytes 18440 | tf_op jit(solution)/shard_map/ppermute | solution.py:419
  25.6 0.7 %collective-permute-start.8 = (f32[12,128]{1,0:T(8,128)S(1)}, f32[12,128]{1,0:T(8,128)S(1)}, u32[]{:S(2)}, u32[]{:S(2)}) collective-permute-start(f32[12,128]{1,0:T(8,128)S(1)} %add.1.refs_0_), channel_id=1, source_target_pairs={{0,9},{1,8},{2,11},{3,10},{4,13},{5,12},{6,15},{7,14},{8,1},{9,0},... | collective-permute-start | bytes 18440 | tf_op jit(solution)/shard_map/ppermute | solution.py:419
  26.3 0.7 %collective-permute-start.9 = (f32[12,128]{1,0:T(8,128)S(1)}, f32[12,128]{1,0:T(8,128)S(1)}, u32[]{:S(2)}, u32[]{:S(2)}) collective-permute-start(f32[12,128]{1,0:T(8,128)S(1)} %add.1.refs_0_), channel_id=1, source_target_pairs={{0,3},{1,2},{2,1},{3,0},{4,7},{5,6},{6,5},{7,4},{8,11},{9,10},{10,... | collective-permute-start | bytes 18440 | tf_op jit(solution)/shard_map/ppermute | solution.py:419
  27.0 1.1 %collective-permute-done.10.refs_3_ = f32[12,128]{1,0:T(8,128)S(1)} collective-permute-done((f32[12,128]{1,0:T(8,128)S(1)}, f32[12,128]{1,0:T(8,128)S(1)}, u32[]{:S(2)}, u32[]{:S(2)}) %collective-permute-start.10) | collective-permute-done | bytes 6176 | tf_op jit(solution)/shard_map/ppermute | solution.py:419
  28.1 1.5 %collective-permute-done.8.refs_1_ = f32[12,128]{1,0:T(8,128)S(1)} collective-permute-done((f32[12,128]{1,0:T(8,128)S(1)}, f32[12,128]{1,0:T(8,128)S(1)}, u32[]{:S(2)}, u32[]{:S(2)}) %collective-permute-start.8) | collective-permute-done | bytes 6176 | tf_op jit(solution)/shard_map/ppermute | solution.py:419
  29.6 0.0 collective-permute-done.9.refs_2_
  29.6 0.6 %finish.1 = f32[3,512]{1,0:T(4,128)} custom-call(f32[12,128]{1,0:T(8,128)S(1)} %add.1.refs_0_, f32[12,128]{1,0:T(8,128)S(1)} %collective-permute-done.8.refs_1_, f32[12,128]{1,0:T(8,128)S(1)} %collective-permute-done.9.refs_2_, f32[12,128]{1,0:T(8,128)S(1)} %collective-permute-done.10.refs_3_), custom_call_target="tpu_custom_call" | custom-call | tf_op jit(solution)/shard_map/finish/pallas_call | solution.py:598
  (1 shorter events, 0.0 us)
Async XLA Ops:
  0.6 5.4 %collective-permute-start = (f32[80,128]{1,0:T(8,128)}, f32[80,128]{1,0:T(8,128)S(1)}, u32[]{:S(2)}, u32[]{:S(2)}) collective-permute-start(f32[80,128]{1,0:T(8,128)} %bitcast.38), channel_id=1, source_target_pairs={{0,2},{2,0},{1,4},{3,6},{4,1},{6,3},{5,8},{7,10},{8,5},{10,7},{9,1... | collective-permute-start | bytes 122888 | tf_op jit(solution)/shard_map/ppermute | solution.py:470
  3.6 2.4 %collective-permute-start.1 = (f32[80,128]{1,0:T(8,128)}, f32[80,128]{1,0:T(8,128)S(1)}, u32[]{:S(2)}, u32[]{:S(2)}) collective-permute-start(f32[80,128]{1,0:T(8,128)} %bitcast.39), channel_id=1, source_target_pairs={{0,1},{1,0},{4,5},{5,4},{8,9},{9,8},{12,13},{13,12},{2,3},{3,2},{6... | collective-permute-start | bytes 122888 | tf_op jit(solution)/shard_map/ppermute | solution.py:455
  7.3 4.7 %collective-permute-start.2 = (f32[80,128]{1,0:T(8,128)S(1)}, f32[80,128]{1,0:T(8,128)S(1)}, u32[]{:S(2)}, u32[]{:S(2)}) collective-permute-start(f32[80,128]{1,0:T(8,128)S(1)} %sweep.1._.refs_2_), channel_id=1, source_target_pairs={{0,1},{1,0},{4,5},{5,4},{8,9},{9,8},{12,13},{13,12},{2,3},{3,2},{6... | collective-permute-start | bytes 122888 | tf_op jit(solution)/shard_map/ppermute | solution.py:455
  7.7 4.3 %collective-permute-start.3 = (f32[80,128]{1,0:T(8,128)S(1)}, f32[80,128]{1,0:T(8,128)S(1)}, u32[]{:S(2)}, u32[]{:S(2)}) collective-permute-start(f32[80,128]{1,0:T(8,128)S(1)} %sweep.1._.refs_2_), channel_id=1, source_target_pairs={{0,2},{2,0},{1,4},{3,6},{4,1},{6,3},{5,8},{7,10},{8,5},{10,7},{9,1... | collective-permute-start | bytes 122888 | tf_op jit(solution)/shard_map/ppermute | solution.py:470
  13.2 3.8 %collective-permute-start.4 = (f32[24,128]{1,0:T(8,128)S(1)}, f32[24,128]{1,0:T(8,128)S(1)}, u32[]{:S(2)}, u32[]{:S(2)}) collective-permute-start(f32[24,128]{1,0:T(8,128)S(1)} %get-tuple-element.28.after.refs_0_), channel_id=1, source_target_pairs={{0,2},{2,0},{1,3},{3,1},{4,6},{6,4},{5,7},{7,5},{8,10},{10,8},{9,1... | collective-permute-start | bytes 36872 | tf_op jit(solution)/shard_map/ppermute | solution.py:568
  18.8 1.9 %collective-permute-start.5 = (f32[12,128]{1,0:T(8,128)S(1)}, f32[12,128]{1,0:T(8,128)S(1)}, u32[]{:S(2)}, u32[]{:S(2)}) collective-permute-start(f32[12,128]{1,0:T(8,128)S(1)} %control.1.refs_0_), channel_id=1, source_target_pairs={{0,1},{1,0},{2,3},{3,2},{4,5},{5,4},{6,7},{7,6},{8,9},{9,8},{10,11... | collective-permute-start | bytes 18440 | tf_op jit(solution)/shard_map/ppermute | solution.py:419
  18.9 3.7 %collective-permute-start.6 = (f32[12,128]{1,0:T(8,128)S(1)}, f32[12,128]{1,0:T(8,128)S(1)}, u32[]{:S(2)}, u32[]{:S(2)}) collective-permute-start(f32[12,128]{1,0:T(8,128)S(1)} %control.1.refs_0_), channel_id=1, source_target_pairs={{0,4},{1,5},{2,6},{3,7},{4,0},{5,1},{6,2},{7,3},{8,12},{9,13},{10,... | collective-permute-start | bytes 18440 | tf_op jit(solution)/shard_map/ppermute | solution.py:419
  20.0 3.1 %collective-permute-start.7 = (f32[12,128]{1,0:T(8,128)S(1)}, f32[12,128]{1,0:T(8,128)S(1)}, u32[]{:S(2)}, u32[]{:S(2)}) collective-permute-start(f32[12,128]{1,0:T(8,128)S(1)} %control.1.refs_0_), channel_id=1, source_target_pairs={{0,5},{1,4},{2,7},{3,6},{4,1},{5,0},{6,3},{7,2},{8,13},{9,12},{10,... | collective-permute-start | bytes 18440 | tf_op jit(solution)/shard_map/ppermute | solution.py:419
  23.2 4.9 %collective-permute-start.10 = (f32[12,128]{1,0:T(8,128)S(1)}, f32[12,128]{1,0:T(8,128)S(1)}, u32[]{:S(2)}, u32[]{:S(2)}) collective-permute-start(f32[12,128]{1,0:T(8,128)S(1)} %add.1.refs_0_), channel_id=1, source_target_pairs={{0,11},{1,10},{2,9},{3,8},{4,15},{5,14},{6,13},{7,12},{8,3},{9,2},... | collective-permute-start | bytes 18440 | tf_op jit(solution)/shard_map/ppermute | solution.py:419
  25.6 4.0 %collective-permute-start.8 = (f32[12,128]{1,0:T(8,128)S(1)}, f32[12,128]{1,0:T(8,128)S(1)}, u32[]{:S(2)}, u32[]{:S(2)}) collective-permute-start(f32[12,128]{1,0:T(8,128)S(1)} %add.1.refs_0_), channel_id=1, source_target_pairs={{0,9},{1,8},{2,11},{3,10},{4,13},{5,12},{6,15},{7,14},{8,1},{9,0},... | collective-permute-start | bytes 18440 | tf_op jit(solution)/shard_map/ppermute | solution.py:419
  26.3 3.3 %collective-permute-start.9 = (f32[12,128]{1,0:T(8,128)S(1)}, f32[12,128]{1,0:T(8,128)S(1)}, u32[]{:S(2)}, u32[]{:S(2)}) collective-permute-start(f32[12,128]{1,0:T(8,128)S(1)} %add.1.refs_0_), channel_id=1, source_target_pairs={{0,3},{1,2},{2,1},{3,0},{4,7},{5,6},{6,5},{7,4},{8,11},{9,10},{10,... | collective-permute-start | bytes 18440 | tf_op jit(solution)/shard_map/ppermute | solution.py:419

commit v22 on v21

--- a/solution.py
+++ b/solution.py
@@ -403,13 +403,13 @@
     near = [cores >> 1 >> i for i in range(cores.bit_length() - 1)]
     node_bits = [cores << i for i in range(nodes.bit_length() - 1)]
     line_bits = [cores * nodes << i for i in range(lines.bit_length() - 1)]
-    bits = near + line_bits[:2] + node_bits[:1] + line_bits[2:] + node_bits[1:]
-    rounds = []
+    bits = line_bits[1:2] + node_bits[:1] + line_bits[2:] + node_bits[1:]
+    rounds = [[bit] for bit in near] + [[bit | (cores - 1)] for bit in line_bits[:1]]
     for first in range(0, len(bits), 2):
         masks = bits[first : first + 2]
         if len(masks) == 2:
             masks = masks + [masks[0] | masks[1]]
-        rounds.append([mask | (cores - 1) for mask in masks] if first else masks)
+        rounds.append([mask | (cores - 1) for mask in masks])
     return rounds
 
 

time: 30.4 us -> 31.5 us (1.036)
  waiting for transfers between devices: 5.32 us -> 7.5 us
  starting transfers between devices: 12.2 us -> 11.2 us
    ppermute x6 -> x5, waiting for transfers between devices: 5.01 us -> 7.18 us  [exchanged(): lax.ppermute(value, SUM_AXES, [(i, i ^ mask) for i in range(peers)])]
    ppermute x6 -> x5, starting transfers between devices: 5.73 us -> 4.68 us  [exchanged(): lax.ppermute(value, SUM_AXES, [(i, i ^ mask) for i in range(peers)])]
  transfers between devices with their start and end apart: 11 -> 10, of which waited for: 5 -> 6; matrix products, arithmetic and copies ran while one was open for 0% -> 0% of each run, Pallas kernels for 23% -> 22%
where the time goes in v22:
time: 31.5 us; the launch traced here: 31.3 us
  Pallas kernels  12 us (38%)
  starting transfers between devices  11.2 us (36%)
  waiting for transfers between devices  7.5 us (24%)
  between operations  0.72 us (2%)
    ppermute x5, waiting for transfers between devices, exchanged(): lax.ppermute(value, SUM_AXES, [(i, i ^ mask) for i in range(peers)])  7.18 us
    ppermute x5, starting transfers between devices, exchanged(): lax.ppermute(value, SUM_AXES, [(i, i ^ mask) for i in range(peers)])  4.68 us
    ppermute x2, starting transfers between devices, swaps(): return (lax.ppermute(array, SUM_AXES, pairs), close)  4.57 us
    pallas_call x1, Pallas kernels, body(): pl.pallas_call(functools.partial(wendland_kernel, 0), out_shape=near_shap...  2.7 us
    pallas_call x1, Pallas kernels, body(): pl.pallas_call(functools.partial(prepare_kernel, nodes), out_shape=(shape...  2.18 us
    pallas_call x1, Pallas kernels, body(): pl.pallas_call(functools.partial(far_wendland_kernel, half), out_shape=(f...  2.12 us
    pallas_call x1, Pallas kernels, body(): pl.pallas_call(functools.partial(control_kernel, scale), out_shape=shape(...  1.84 us
    ppermute x1, starting transfers between devices, body(): all_sens.append(lax.ppermute(part_sens, 'nodes', ring))  1.33 us
  transfers between devices with their start and end apart: 10, of which 6 were waited for; matrix products, arithmetic and copies ran while one was open for 0% of the time, Pallas kernels for 22%

profile of v22, /device:TPU:0, one launch (start us, length us, event | category | flops | bytes accessed | tf_op | source)
XLA Modules:
  0.0 31.3 jit_solution(955703997833370407)
XLA Ops:
  0.6 3.0 %collective-permute-start = (f32[80,128]{1,0:T(8,128)}, f32[80,128]{1,0:T(8,128)S(1)}, u32[]{:S(2)}, u32[]{:S(2)}) collective-permute-start(f32[80,128]{1,0:T(8,128)} %bitcast.38), channel_id=1, source_target_pairs={{0,2},{2,0},{1,4},{3,6},{4,1},{6,3},{5,8},{7,10},{8,5},{10,7},{9,1... | collective-permute-start | bytes 122888 | tf_op jit(solution)/shard_map/ppermute | solution.py:470
  3.6 0.2 collective-permute-start.1
  3.8 2.2 %prepare.1 = (f32[2400,128]{1,0:T(8,128)S(1)}, f32[400,128]{1,0:T(8,128)S(1)}, f32[80,128]{1,0:T(8,128)S(1)}, f32[240,128]{1,0:T(8,128)S(1)}, s32[96,128]{1,0:T(...) custom-call(bf16[2400,128]{1,0:T(8,128)(2,1)} %bitcast.32, ...), custom_call_target="tpu_custom_call" | custom-call | flops 1000000000 | bytes 10000000 | tf_op jit(solution)/shard_map/prepare/pallas_call | solution.py:474
  6.0 0.0 collective-permute-done.far_ref
  6.0 0.0 collective-permute-done.1.close_ref
  6.0 1.2 %sweep.1._.refs_2_ = f32[80,128]{1,0:T(8,128)S(1)} custom-call(f32[80,128]{1,0:T(8,128)S(1)} %collective-permute-done.far_ref, f32[80,128]{1,0:T(8,128)S(1)} %collective-permute-done.1.close_ref, f32[80,128]{1,0:T(8,128)S(1)} %get-tuple-element.21.refs_0_, f32[80,128]{1,0:T(8,128)S(1)} %get-tuple-element.22.refs_1_.refs_3_, ...), custom_call_target="tpu_custom_call" | custom-call | flops 716800 | bytes 1228800 | tf_op jit(solution)/shard_map/sweep/pallas_call | solution.py:529
  7.3 0.4 %collective-permute-start.2 = (f32[80,128]{1,0:T(8,128)S(1)}, f32[80,128]{1,0:T(8,128)S(1)}, u32[]{:S(2)}, u32[]{:S(2)}) collective-permute-start(f32[80,128]{1,0:T(8,128)S(1)} %sweep.1._.refs_2_), channel_id=1, source_target_pairs={{0,1},{1,0},{4,5},{5,4},{8,9},{9,8},{12,13},{13,12},{2,3},{3,2},{6... | collective-permute-start | bytes 122888 | tf_op jit(solution)/shard_map/ppermute | solution.py:455
  7.7 1.6 %collective-permute-start.3 = (f32[80,128]{1,0:T(8,128)S(1)}, f32[80,128]{1,0:T(8,128)S(1)}, u32[]{:S(2)}, u32[]{:S(2)}) collective-permute-start(f32[80,128]{1,0:T(8,128)S(1)} %sweep.1._.refs_2_), channel_id=1, source_target_pairs={{0,2},{2,0},{1,4},{3,6},{4,1},{6,3},{5,8},{7,10},{8,5},{10,7},{9,1... | collective-permute-start | bytes 122888 | tf_op jit(solution)/shard_map/ppermute | solution.py:470
  9.2 2.7 %near_wendland.1.refs_9_.refs_2_ = bf16[1280,2048]{1,0:T(8,128)(2,1)S(1)} custom-call(bf16[1024,64]{1,0:T(8,128)(2,1)S(1)} %get-tuple-element.19.left_ref, bf16[64,2048]{1,0:T(8,128)(2,1)S(1)} %get-tuple-element.20.right_ref, f32[80,128]{1,0:T(8,128)S(1)} %sweep.1._.refs_2_), custom_call_target="tpu_custom_call" | custom-call | flops 1000000000 | bytes 10000000 | tf_op jit(solution)/shard_map/near_wendland/pallas_call | solution.py:545
  11.9 0.0 collective-permute-done.2.refs_0_
  12.0 0.0 collective-permute-done.3.refs_1_
  12.0 1.3 %last_sweep.1 = (f32[80,128]{1,0:T(8,128)S(1)}, f32[24,128]{1,0:T(8,128)S(1)}) custom-call(f32[80,128]{1,0:T(8,128)S(1)} %collective-permute-done.2.refs_0_, f32[80,128]{1,0:T(8,128)S(1)} %collective-permute-done.3.refs_1_, f32[80,128]{1,0:T(8,128)S(1)} %sweep.1._.refs_2_, f32[80,128]{1,0:T(8,128)S(1)} %get-tuple-element.22.refs_1_.refs_3_, ...), custom_call_target="tpu_custom_call" | custom-call | flops 716800 | bytes 1228800 | tf_op jit(solution)/shard_map/last_sweep/pallas_call | solution.py:554
  13.2 1.3 %collective-permute-start.4 = (f32[24,128]{1,0:T(8,128)S(1)}, f32[24,128]{1,0:T(8,128)S(1)}, u32[]{:S(2)}, u32[]{:S(2)}) collective-permute-start(f32[24,128]{1,0:T(8,128)S(1)} %get-tuple-element.28.after.refs_0_), channel_id=1, source_target_pairs={{0,2},{2,0},{1,3},{3,1},{4,6},{6,4},{5,7},{7,5},{8,10},{10,8},{9,1... | collective-permute-start | bytes 36872 | tf_op jit(solution)/shard_map/ppermute | solution.py:568
  14.6 2.1 %far_wendland.1 = (bf16[768,2048]{1,0:T(8,128)(2,1)S(1)}, bf16[8192,128]{1,0:T(8,128)(2,1)S(1)}, f32[80,128]{1,0:T(8,128)}) custom-call(bf16[1024,64]{1,0:T(8,128)(2,1)S(1)} %get-tuple-element.19.left_ref, bf16[64,2048]{1,0:T(8,128)(2,1)S(1)} %get-tuple-element.20.right_ref, f32[24,128]{1,0:T(8,128)S(1)} %get-tuple-element.28.after.refs_0_, ...), custom_call_target="tpu_custom_call" | custom-call | flops 1000000000 | bytes 10000000 | tf_op jit(solution)/shard_map/far_wendland/pallas_call | solution.py:570
  16.7 0.3 collective-permute-done.4.refs_1_
  17.0 1.8 %control.1.refs_0_ = f32[12,128]{1,0:T(8,128)S(1)} custom-call(f32[24,128]{1,0:T(8,128)S(1)} %get-tuple-element.28.after.refs_0_, f32[24,128]{1,0:T(8,128)S(1)} %collective-permute-done.4.refs_1_, bf16[1280,2048]{1,0:T(8,128)(2,1)S(1)} %near_wendland.1.refs_9_.refs_2_, bf16[768,2048]{1,0:T(8,128)(2,1)S(1)} %get-tuple-element.32.refs_3_, ...), custom_call_target="tpu_custom_call" | custom-call | tf_op jit(solution)/shard_map/control/pallas_call | solution.py:582
  18.8 0.1 collective-permute-start.5
  18.9 1.2 %collective-permute-done.5.refs_1_ = f32[12,128]{1,0:T(8,128)S(1)} collective-permute-done((f32[12,128]{1,0:T(8,128)S(1)}, f32[12,128]{1,0:T(8,128)S(1)}, u32[]{:S(2)}, u32[]{:S(2)}) %collective-permute-start.5) | collective-permute-done | bytes 6176 | tf_op jit(solution)/shard_map/ppermute | solution.py:419
  20.1 0.7 %collective-permute-start.6 = (f32[12,128]{1,0:T(8,128)S(1)}, f32[12,128]{1,0:T(8,128)S(1)}, u32[]{:S(2)}, u32[]{:S(2)}) collective-permute-start(f32[12,128]{1,0:T(8,128)S(1)} %add.2.refs_0_), channel_id=1, source_target_pairs={{0,5},{1,4},{2,7},{3,6},{4,1},{5,0},{6,3},{7,2},{8,13},{9,12},{10,... | collective-permute-start | bytes 18440 | tf_op jit(solution)/shard_map/ppermute | solution.py:419
  20.8 2.3 %collective-permute-done.6.refs_1_ = f32[12,128]{1,0:T(8,128)S(1)} collective-permute-done((f32[12,128]{1,0:T(8,128)S(1)}, f32[12,128]{1,0:T(8,128)S(1)}, u32[]{:S(2)}, u32[]{:S(2)}) %collective-permute-start.6) | collective-permute-done | bytes 6176 | tf_op jit(solution)/shard_map/ppermute | solution.py:419
  23.2 1.5 %collective-permute-start.7 = (f32[12,128]{1,0:T(8,128)S(1)}, f32[12,128]{1,0:T(8,128)S(1)}, u32[]{:S(2)}, u32[]{:S(2)}) collective-permute-start(f32[12,128]{1,0:T(8,128)S(1)} %add.3.refs_0_), channel_id=1, source_target_pairs={{0,9},{1,8},{2,11},{3,10},{4,13},{5,12},{6,15},{7,14},{8,1},{9,0},... | collective-permute-start | bytes 18440 | tf_op jit(solution)/shard_map/ppermute | solution.py:419
  24.6 1.2 %collective-permute-start.8 = (f32[12,128]{1,0:T(8,128)S(1)}, f32[12,128]{1,0:T(8,128)S(1)}, u32[]{:S(2)}, u32[]{:S(2)}) collective-permute-start(f32[12,128]{1,0:T(8,128)S(1)} %add.3.refs_0_), channel_id=1, source_target_pairs={{0,3},{1,2},{2,1},{3,0},{4,7},{5,6},{6,5},{7,4},{8,11},{9,10},{10,... | collective-permute-start | bytes 18440 | tf_op jit(solution)/shard_map/ppermute | solution.py:419
  25.9 1.2 %collective-permute-start.9 = (f32[12,128]{1,0:T(8,128)S(1)}, f32[12,128]{1,0:T(8,128)S(1)}, u32[]{:S(2)}, u32[]{:S(2)}) collective-permute-start(f32[12,128]{1,0:T(8,128)S(1)} %add.3.refs_0_), channel_id=1, source_target_pairs={{0,11},{1,10},{2,9},{3,8},{4,15},{5,14},{6,13},{7,12},{8,3},{9,2},... | collective-permute-start | bytes 18440 | tf_op jit(solution)/shard_map/ppermute | solution.py:419
  27.0 0.1 collective-permute-done.7.refs_1_
  27.1 0.6 %collective-permute-done.8.refs_2_ = f32[12,128]{1,0:T(8,128)S(1)} collective-permute-done((f32[12,128]{1,0:T(8,128)S(1)}, f32[12,128]{1,0:T(8,128)S(1)}, u32[]{:S(2)}, u32[]{:S(2)}) %collective-permute-start.8) | collective-permute-done | bytes 6176 | tf_op jit(solution)/shard_map/ppermute | solution.py:419
  27.7 3.0 %collective-permute-done.9.refs_3_ = f32[12,128]{1,0:T(8,128)S(1)} collective-permute-done((f32[12,128]{1,0:T(8,128)S(1)}, f32[12,128]{1,0:T(8,128)S(1)}, u32[]{:S(2)}, u32[]{:S(2)}) %collective-permute-start.9) | collective-permute-done | bytes 6176 | tf_op jit(solution)/shard_map/ppermute | solution.py:419
  30.7 0.6 %finish.1 = f32[3,512]{1,0:T(4,128)} custom-call(f32[12,128]{1,0:T(8,128)S(1)} %add.3.refs_0_, f32[12,128]{1,0:T(8,128)S(1)} %collective-permute-done.7.refs_1_, f32[12,128]{1,0:T(8,128)S(1)} %collective-permute-done.8.refs_2_, f32[12,128]{1,0:T(8,128)S(1)} %collective-permute-done.9.refs_3_), custom_call_target="tpu_custom_call" | custom-call | tf_op jit(solution)/shard_map/finish/pallas_call | solution.py:598
  (2 shorter events, 0.0 us)
Async XLA Ops:
  0.6 5.4 %collective-permute-start = (f32[80,128]{1,0:T(8,128)}, f32[80,128]{1,0:T(8,128)S(1)}, u32[]{:S(2)}, u32[]{:S(2)}) collective-permute-start(f32[80,128]{1,0:T(8,128)} %bitcast.38), channel_id=1, source_target_pairs={{0,2},{2,0},{1,4},{3,6},{4,1},{6,3},{5,8},{7,10},{8,5},{10,7},{9,1... | collective-permute-start | bytes 122888 | tf_op jit(solution)/shard_map/ppermute | solution.py:470
  3.6 2.4 %collective-permute-start.1 = (f32[80,128]{1,0:T(8,128)}, f32[80,128]{1,0:T(8,128)S(1)}, u32[]{:S(2)}, u32[]{:S(2)}) collective-permute-start(f32[80,128]{1,0:T(8,128)} %bitcast.39), channel_id=1, source_target_pairs={{0,1},{1,0},{4,5},{5,4},{8,9},{9,8},{12,13},{13,12},{2,3},{3,2},{6... | collective-permute-start | bytes 122888 | tf_op jit(solution)/shard_map/ppermute | solution.py:455
  7.3 4.7 %collective-permute-start.2 = (f32[80,128]{1,0:T(8,128)S(1)}, f32[80,128]{1,0:T(8,128)S(1)}, u32[]{:S(2)}, u32[]{:S(2)}) collective-permute-start(f32[80,128]{1,0:T(8,128)S(1)} %sweep.1._.refs_2_), channel_id=1, source_target_pairs={{0,1},{1,0},{4,5},{5,4},{8,9},{9,8},{12,13},{13,12},{2,3},{3,2},{6... | collective-permute-start | bytes 122888 | tf_op jit(solution)/shard_map/ppermute | solution.py:455
  7.7 4.3 %collective-permute-start.3 = (f32[80,128]{1,0:T(8,128)S(1)}, f32[80,128]{1,0:T(8,128)S(1)}, u32[]{:S(2)}, u32[]{:S(2)}) collective-permute-start(f32[80,128]{1,0:T(8,128)S(1)} %sweep.1._.refs_2_), channel_id=1, source_target_pairs={{0,2},{2,0},{1,4},{3,6},{4,1},{6,3},{5,8},{7,10},{8,5},{10,7},{9,1... | collective-permute-start | bytes 122888 | tf_op jit(solution)/shard_map/ppermute | solution.py:470
  13.2 3.8 %collective-permute-start.4 = (f32[24,128]{1,0:T(8,128)S(1)}, f32[24,128]{1,0:T(8,128)S(1)}, u32[]{:S(2)}, u32[]{:S(2)}) collective-permute-start(f32[24,128]{1,0:T(8,128)S(1)} %get-tuple-element.28.after.refs_0_), channel_id=1, source_target_pairs={{0,2},{2,0},{1,3},{3,1},{4,6},{6,4},{5,7},{7,5},{8,10},{10,8},{9,1... | collective-permute-start | bytes 36872 | tf_op jit(solution)/shard_map/ppermute | solution.py:568
  18.8 1.2 %collective-permute-start.5 = (f32[12,128]{1,0:T(8,128)S(1)}, f32[12,128]{1,0:T(8,128)S(1)}, u32[]{:S(2)}, u32[]{:S(2)}) collective-permute-start(f32[12,128]{1,0:T(8,128)S(1)} %control.1.refs_0_), channel_id=1, source_target_pairs={{0,1},{1,0},{2,3},{3,2},{4,5},{5,4},{6,7},{7,6},{8,9},{9,8},{10,11... | collective-permute-start | bytes 18440 | tf_op jit(solution)/shard_map/ppermute | solution.py:419
  20.1 3.1 %collective-permute-start.6 = (f32[12,128]{1,0:T(8,128)S(1)}, f32[12,128]{1,0:T(8,128)S(1)}, u32[]{:S(2)}, u32[]{:S(2)}) collective-permute-start(f32[12,128]{1,0:T(8,128)S(1)} %add.2.refs_0_), channel_id=1, source_target_pairs={{0,5},{1,4},{2,7},{3,6},{4,1},{5,0},{6,3},{7,2},{8,13},{9,12},{10,... | collective-permute-start | bytes 18440 | tf_op jit(solution)/shard_map/ppermute | solution.py:419
  23.2 4.0 %collective-permute-start.7 = (f32[12,128]{1,0:T(8,128)S(1)}, f32[12,128]{1,0:T(8,128)S(1)}, u32[]{:S(2)}, u32[]{:S(2)}) collective-permute-start(f32[12,128]{1,0:T(8,128)S(1)} %add.3.refs_0_), channel_id=1, source_target_pairs={{0,9},{1,8},{2,11},{3,10},{4,13},{5,12},{6,15},{7,14},{8,1},{9,0},... | collective-permute-start | bytes 18440 | tf_op jit(solution)/shard_map/ppermute | solution.py:419
  24.6 3.1 %collective-permute-start.8 = (f32[12,128]{1,0:T(8,128)S(1)}, f32[12,128]{1,0:T(8,128)S(1)}, u32[]{:S(2)}, u32[]{:S(2)}) collective-permute-start(f32[12,128]{1,0:T(8,128)S(1)} %add.3.refs_0_), channel_id=1, source_target_pairs={{0,3},{1,2},{2,1},{3,0},{4,7},{5,6},{6,5},{7,4},{8,11},{9,10},{10,... | collective-permute-start | bytes 18440 | tf_op jit(solution)/shard_map/ppermute | solution.py:419
  25.9 4.9 %collective-permute-start.9 = (f32[12,128]{1,0:T(8,128)S(1)}, f32[12,128]{1,0:T(8,128)S(1)}, u32[]{:S(2)}, u32[]{:S(2)}) collective-permute-start(f32[12,128]{1,0:T(8,128)S(1)} %add.3.refs_0_), channel_id=1, source_target_pairs={{0,11},{1,10},{2,9},{3,8},{4,15},{5,14},{6,13},{7,12},{8,3},{9,2},... | collective-permute-start | bytes 18440 | tf_op jit(solution)/shard_map/ppermute | solution.py:419

commit v23 on v22

--- a/solution.py
+++ b/solution.py
@@ -408,7 +408,7 @@
     for first in range(0, len(bits), 2):
         masks = bits[first : first + 2]
         if len(masks) == 2:
-            masks = masks + [masks[0] | masks[1]]
+            masks = [masks[0] | masks[1]] + masks
         rounds.append([mask | (cores - 1) for mask in masks])
     return rounds
 

time: 31.5 us -> 30.3 us (0.962)
  waiting for transfers between devices: 7.5 us -> 6.36 us
    ppermute x5, waiting for transfers between devices: 7.18 us -> 6.04 us  [exchanged(): lax.ppermute(value, SUM_AXES, [(i, i ^ mask) for i in range(peers)])]
  transfers between devices with their start and end apart: 10 -> 10, of which waited for: 6 -> 6; matrix products, arithmetic and copies ran while one was open for 0% -> 0% of each run, Pallas kernels for 22% -> 23%
where the time goes in v23:
time: 30.3 us; the launch traced here: 30.2 us
  Pallas kernels  12 us (40%)
  starting transfers between devices  11.2 us (37%)
  waiting for transfers between devices  6.36 us (21%)
  between operations  0.72 us (2%)
    ppermute x5, waiting for transfers between devices, exchanged(): lax.ppermute(value, SUM_AXES, [(i, i ^ mask) for i in range(peers)])  6.04 us
    ppermute x5, starting transfers between devices, exchanged(): lax.ppermute(value, SUM_AXES, [(i, i ^ mask) for i in range(peers)])  4.68 us
    ppermute x2, starting transfers between devices, swaps(): return (lax.ppermute(array, SUM_AXES, pairs), close)  4.57 us
    pallas_call x1, Pallas kernels, body(): pl.pallas_call(functools.partial(wendland_kernel, 0), out_shape=near_shap...  2.7 us
    pallas_call x1, Pallas kernels, body(): pl.pallas_call(functools.partial(prepare_kernel, nodes), out_shape=(shape...  2.18 us
    pallas_call x1, Pallas kernels, body(): pl.pallas_call(functools.partial(far_wendland_kernel, half), out_shape=(f...  2.12 us
    pallas_call x1, Pallas kernels, body(): pl.pallas_call(functools.partial(control_kernel, scale), out_shape=shape(...  1.84 us
    ppermute x1, starting transfers between devices, body(): all_sens.append(lax.ppermute(part_sens, 'nodes', ring))  1.33 us
  transfers between devices with their start and end apart: 10, of which 6 were waited for; matrix products, arithmetic and copies ran while one was open for 0% of the time, Pallas kernels for 23%

profile of v23, /device:TPU:0, one launch (start us, length us, event | category | flops | bytes accessed | tf_op | source)
XLA Modules:
  0.0 30.2 jit_solution(865981121790377995)
XLA Ops:
  0.6 3.0 %collective-permute-start = (f32[80,128]{1,0:T(8,128)}, f32[80,128]{1,0:T(8,128)S(1)}, u32[]{:S(2)}, u32[]{:S(2)}) collective-permute-start(f32[80,128]{1,0:T(8,128)} %bitcast.38), channel_id=1, source_target_pairs={{0,2},{2,0},{1,4},{3,6},{4,1},{6,3},{5,8},{7,10},{8,5},{10,7},{9,1... | collective-permute-start | bytes 122888 | tf_op jit(solution)/shard_map/ppermute | solution.py:470
  3.6 0.2 collective-permute-start.1
  3.8 2.2 %prepare.1 = (f32[2400,128]{1,0:T(8,128)S(1)}, f32[400,128]{1,0:T(8,128)S(1)}, f32[80,128]{1,0:T(8,128)S(1)}, f32[240,128]{1,0:T(8,128)S(1)}, s32[96,128]{1,0:T(...) custom-call(bf16[2400,128]{1,0:T(8,128)(2,1)} %bitcast.32, ...), custom_call_target="tpu_custom_call" | custom-call | flops 1000000000 | bytes 10000000 | tf_op jit(solution)/shard_map/prepare/pallas_call | solution.py:474
  6.0 0.0 collective-permute-done.far_ref
  6.0 0.0 collective-permute-done.1.close_ref
  6.0 1.2 %sweep.1._.refs_2_ = f32[80,128]{1,0:T(8,128)S(1)} custom-call(f32[80,128]{1,0:T(8,128)S(1)} %collective-permute-done.far_ref, f32[80,128]{1,0:T(8,128)S(1)} %collective-permute-done.1.close_ref, f32[80,128]{1,0:T(8,128)S(1)} %get-tuple-element.21.refs_0_, f32[80,128]{1,0:T(8,128)S(1)} %get-tuple-element.22.refs_1_.refs_3_, ...), custom_call_target="tpu_custom_call" | custom-call | flops 716800 | bytes 1228800 | tf_op jit(solution)/shard_map/sweep/pallas_call | solution.py:529
  7.3 0.4 %collective-permute-start.2 = (f32[80,128]{1,0:T(8,128)S(1)}, f32[80,128]{1,0:T(8,128)S(1)}, u32[]{:S(2)}, u32[]{:S(2)}) collective-permute-start(f32[80,128]{1,0:T(8,128)S(1)} %sweep.1._.refs_2_), channel_id=1, source_target_pairs={{0,1},{1,0},{4,5},{5,4},{8,9},{9,8},{12,13},{13,12},{2,3},{3,2},{6... | collective-permute-start | bytes 122888 | tf_op jit(solution)/shard_map/ppermute | solution.py:455
  7.7 1.6 %collective-permute-start.3 = (f32[80,128]{1,0:T(8,128)S(1)}, f32[80,128]{1,0:T(8,128)S(1)}, u32[]{:S(2)}, u32[]{:S(2)}) collective-permute-start(f32[80,128]{1,0:T(8,128)S(1)} %sweep.1._.refs_2_), channel_id=1, source_target_pairs={{0,2},{2,0},{1,4},{3,6},{4,1},{6,3},{5,8},{7,10},{8,5},{10,7},{9,1... | collective-permute-start | bytes 122888 | tf_op jit(solution)/shard_map/ppermute | solution.py:470
  9.2 2.7 %near_wendland.1.refs_9_.refs_2_ = bf16[1280,2048]{1,0:T(8,128)(2,1)S(1)} custom-call(bf16[1024,64]{1,0:T(8,128)(2,1)S(1)} %get-tuple-element.19.left_ref, bf16[64,2048]{1,0:T(8,128)(2,1)S(1)} %get-tuple-element.20.right_ref, f32[80,128]{1,0:T(8,128)S(1)} %sweep.1._.refs_2_), custom_call_target="tpu_custom_call" | custom-call | flops 1000000000 | bytes 10000000 | tf_op jit(solution)/shard_map/near_wendland/pallas_call | solution.py:545
  11.9 0.0 collective-permute-done.2.refs_0_
  12.0 0.0 collective-permute-done.3.refs_1_
  12.0 1.3 %last_sweep.1 = (f32[80,128]{1,0:T(8,128)S(1)}, f32[24,128]{1,0:T(8,128)S(1)}) custom-call(f32[80,128]{1,0:T(8,128)S(1)} %collective-permute-done.2.refs_0_, f32[80,128]{1,0:T(8,128)S(1)} %collective-permute-done.3.refs_1_, f32[80,128]{1,0:T(8,128)S(1)} %sweep.1._.refs_2_, f32[80,128]{1,0:T(8,128)S(1)} %get-tuple-element.22.refs_1_.refs_3_, ...), custom_call_target="tpu_custom_call" | custom-call | flops 716800 | bytes 1228800 | tf_op jit(solution)/shard_map/last_sweep/pallas_call | solution.py:554
  13.2 1.3 %collective-permute-start.4 = (f32[24,128]{1,0:T(8,128)S(1)}, f32[24,128]{1,0:T(8,128)S(1)}, u32[]{:S(2)}, u32[]{:S(2)}) collective-permute-start(f32[24,128]{1,0:T(8,128)S(1)} %get-tuple-element.28.after.refs_0_), channel_id=1, source_target_pairs={{0,2},{2,0},{1,3},{3,1},{4,6},{6,4},{5,7},{7,5},{8,10},{10,8},{9,1... | collective-permute-start | bytes 36872 | tf_op jit(solution)/shard_map/ppermute | solution.py:568
  14.6 2.1 %far_wendland.1 = (bf16[768,2048]{1,0:T(8,128)(2,1)S(1)}, bf16[8192,128]{1,0:T(8,128)(2,1)S(1)}, f32[80,128]{1,0:T(8,128)}) custom-call(bf16[1024,64]{1,0:T(8,128)(2,1)S(1)} %get-tuple-element.19.left_ref, bf16[64,2048]{1,0:T(8,128)(2,1)S(1)} %get-tuple-element.20.right_ref, f32[24,128]{1,0:T(8,128)S(1)} %get-tuple-element.28.after.refs_0_, ...), custom_call_target="tpu_custom_call" | custom-call | flops 1000000000 | bytes 10000000 | tf_op jit(solution)/shard_map/far_wendland/pallas_call | solution.py:570
  16.7 0.3 %collective-permute-done.4.refs_1_ = f32[24,128]{1,0:T(8,128)S(1)} collective-permute-done((f32[24,128]{1,0:T(8,128)S(1)}, f32[24,128]{1,0:T(8,128)S(1)}, u32[]{:S(2)}, u32[]{:S(2)}) %collective-permute-start.4) | collective-permute-done | bytes 12320 | tf_op jit(solution)/shard_map/ppermute | solution.py:568
  17.0 1.8 %control.1.refs_0_ = f32[12,128]{1,0:T(8,128)S(1)} custom-call(f32[24,128]{1,0:T(8,128)S(1)} %get-tuple-element.28.after.refs_0_, f32[24,128]{1,0:T(8,128)S(1)} %collective-permute-done.4.refs_1_, bf16[1280,2048]{1,0:T(8,128)(2,1)S(1)} %near_wendland.1.refs_9_.refs_2_, bf16[768,2048]{1,0:T(8,128)(2,1)S(1)} %get-tuple-element.32.refs_3_, ...), custom_call_target="tpu_custom_call" | custom-call | tf_op jit(solution)/shard_map/control/pallas_call | solution.py:582
  18.8 0.1 collective-permute-start.5
  18.9 1.2 %collective-permute-done.5.refs_1_ = f32[12,128]{1,0:T(8,128)S(1)} collective-permute-done((f32[12,128]{1,0:T(8,128)S(1)}, f32[12,128]{1,0:T(8,128)S(1)}, u32[]{:S(2)}, u32[]{:S(2)}) %collective-permute-start.5) | collective-permute-done | bytes 6176 | tf_op jit(solution)/shard_map/ppermute | solution.py:419
  20.1 0.7 %collective-permute-start.6 = (f32[12,128]{1,0:T(8,128)S(1)}, f32[12,128]{1,0:T(8,128)S(1)}, u32[]{:S(2)}, u32[]{:S(2)}) collective-permute-start(f32[12,128]{1,0:T(8,128)S(1)} %add.2.refs_0_), channel_id=1, source_target_pairs={{0,5},{1,4},{2,7},{3,6},{4,1},{5,0},{6,3},{7,2},{8,13},{9,12},{10,... | collective-permute-start | bytes 18440 | tf_op jit(solution)/shard_map/ppermute | solution.py:419
  20.8 2.3 %collective-permute-done.6.refs_1_ = f32[12,128]{1,0:T(8,128)S(1)} collective-permute-done((f32[12,128]{1,0:T(8,128)S(1)}, f32[12,128]{1,0:T(8,128)S(1)}, u32[]{:S(2)}, u32[]{:S(2)}) %collective-permute-start.6) | collective-permute-done | bytes 6176 | tf_op jit(solution)/shard_map/ppermute | solution.py:419
  23.2 2.2 %collective-permute-start.7 = (f32[12,128]{1,0:T(8,128)S(1)}, f32[12,128]{1,0:T(8,128)S(1)}, u32[]{:S(2)}, u32[]{:S(2)}) collective-permute-start(f32[12,128]{1,0:T(8,128)S(1)} %add.3.refs_0_), channel_id=1, source_target_pairs={{0,11},{1,10},{2,9},{3,8},{4,15},{5,14},{6,13},{7,12},{8,3},{9,2},... | collective-permute-start | bytes 18440 | tf_op jit(solution)/shard_map/ppermute | solution.py:419
  25.3 1.2 %collective-permute-start.8 = (f32[12,128]{1,0:T(8,128)S(1)}, f32[12,128]{1,0:T(8,128)S(1)}, u32[]{:S(2)}, u32[]{:S(2)}) collective-permute-start(f32[12,128]{1,0:T(8,128)S(1)} %add.3.refs_0_), channel_id=1, source_target_pairs={{0,9},{1,8},{2,11},{3,10},{4,13},{5,12},{6,15},{7,14},{8,1},{9,0},... | collective-permute-start | bytes 18440 | tf_op jit(solution)/shard_map/ppermute | solution.py:419
  26.5 0.5 %collective-permute-start.9 = (f32[12,128]{1,0:T(8,128)S(1)}, f32[12,128]{1,0:T(8,128)S(1)}, u32[]{:S(2)}, u32[]{:S(2)}) collective-permute-start(f32[12,128]{1,0:T(8,128)S(1)} %add.3.refs_0_), channel_id=1, source_target_pairs={{0,3},{1,2},{2,1},{3,0},{4,7},{5,6},{6,5},{7,4},{8,11},{9,10},{10,... | collective-permute-start | bytes 18440 | tf_op jit(solution)/shard_map/ppermute | solution.py:419
  27.0 1.0 %collective-permute-done.7.refs_1_ = f32[12,128]{1,0:T(8,128)S(1)} collective-permute-done((f32[12,128]{1,0:T(8,128)S(1)}, f32[12,128]{1,0:T(8,128)S(1)}, u32[]{:S(2)}, u32[]{:S(2)}) %collective-permute-start.7) | collective-permute-done | bytes 6176 | tf_op jit(solution)/shard_map/ppermute | solution.py:419
  28.0 1.3 %collective-permute-done.8.refs_2_ = f32[12,128]{1,0:T(8,128)S(1)} collective-permute-done((f32[12,128]{1,0:T(8,128)S(1)}, f32[12,128]{1,0:T(8,128)S(1)}, u32[]{:S(2)}, u32[]{:S(2)}) %collective-permute-start.8) | collective-permute-done | bytes 6176 | tf_op jit(solution)/shard_map/ppermute | solution.py:419
  29.3 0.3 collective-permute-done.9.refs_3_
  29.6 0.6 %finish.1 = f32[3,512]{1,0:T(4,128)} custom-call(f32[12,128]{1,0:T(8,128)S(1)} %add.3.refs_0_, f32[12,128]{1,0:T(8,128)S(1)} %collective-permute-done.7.refs_1_, f32[12,128]{1,0:T(8,128)S(1)} %collective-permute-done.8.refs_2_, f32[12,128]{1,0:T(8,128)S(1)} %collective-permute-done.9.refs_3_), custom_call_target="tpu_custom_call" | custom-call | tf_op jit(solution)/shard_map/finish/pallas_call | solution.py:598
  (2 shorter events, 0.0 us)
Async XLA Ops:
  0.6 5.4 %collective-permute-start = (f32[80,128]{1,0:T(8,128)}, f32[80,128]{1,0:T(8,128)S(1)}, u32[]{:S(2)}, u32[]{:S(2)}) collective-permute-start(f32[80,128]{1,0:T(8,128)} %bitcast.38), channel_id=1, source_target_pairs={{0,2},{2,0},{1,4},{3,6},{4,1},{6,3},{5,8},{7,10},{8,5},{10,7},{9,1... | collective-permute-start | bytes 122888 | tf_op jit(solution)/shard_map/ppermute | solution.py:470
  3.6 2.4 %collective-permute-start.1 = (f32[80,128]{1,0:T(8,128)}, f32[80,128]{1,0:T(8,128)S(1)}, u32[]{:S(2)}, u32[]{:S(2)}) collective-permute-start(f32[80,128]{1,0:T(8,128)} %bitcast.39), channel_id=1, source_target_pairs={{0,1},{1,0},{4,5},{5,4},{8,9},{9,8},{12,13},{13,12},{2,3},{3,2},{6... | collective-permute-start | bytes 122888 | tf_op jit(solution)/shard_map/ppermute | solution.py:455
  7.3 4.7 %collective-permute-start.2 = (f32[80,128]{1,0:T(8,128)S(1)}, f32[80,128]{1,0:T(8,128)S(1)}, u32[]{:S(2)}, u32[]{:S(2)}) collective-permute-start(f32[80,128]{1,0:T(8,128)S(1)} %sweep.1._.refs_2_), channel_id=1, source_target_pairs={{0,1},{1,0},{4,5},{5,4},{8,9},{9,8},{12,13},{13,12},{2,3},{3,2},{6... | collective-permute-start | bytes 122888 | tf_op jit(solution)/shard_map/ppermute | solution.py:455
  7.7 4.3 %collective-permute-start.3 = (f32[80,128]{1,0:T(8,128)S(1)}, f32[80,128]{1,0:T(8,128)S(1)}, u32[]{:S(2)}, u32[]{:S(2)}) collective-permute-start(f32[80,128]{1,0:T(8,128)S(1)} %sweep.1._.refs_2_), channel_id=1, source_target_pairs={{0,2},{2,0},{1,4},{3,6},{4,1},{6,3},{5,8},{7,10},{8,5},{10,7},{9,1... | collective-permute-start | bytes 122888 | tf_op jit(solution)/shard_map/ppermute | solution.py:470
  13.2 3.8 %collective-permute-start.4 = (f32[24,128]{1,0:T(8,128)S(1)}, f32[24,128]{1,0:T(8,128)S(1)}, u32[]{:S(2)}, u32[]{:S(2)}) collective-permute-start(f32[24,128]{1,0:T(8,128)S(1)} %get-tuple-element.28.after.refs_0_), channel_id=1, source_target_pairs={{0,2},{2,0},{1,3},{3,1},{4,6},{6,4},{5,7},{7,5},{8,10},{10,8},{9,1... | collective-permute-start | bytes 36872 | tf_op jit(solution)/shard_map/ppermute | solution.py:568
  18.8 1.2 %collective-permute-start.5 = (f32[12,128]{1,0:T(8,128)S(1)}, f32[12,128]{1,0:T(8,128)S(1)}, u32[]{:S(2)}, u32[]{:S(2)}) collective-permute-start(f32[12,128]{1,0:T(8,128)S(1)} %control.1.refs_0_), channel_id=1, source_target_pairs={{0,1},{1,0},{2,3},{3,2},{4,5},{5,4},{6,7},{7,6},{8,9},{9,8},{10,11... | collective-permute-start | bytes 18440 | tf_op jit(solution)/shard_map/ppermute | solution.py:419
  20.1 3.1 %collective-permute-start.6 = (f32[12,128]{1,0:T(8,128)S(1)}, f32[12,128]{1,0:T(8,128)S(1)}, u32[]{:S(2)}, u32[]{:S(2)}) collective-permute-start(f32[12,128]{1,0:T(8,128)S(1)} %add.2.refs_0_), channel_id=1, source_target_pairs={{0,5},{1,4},{2,7},{3,6},{4,1},{5,0},{6,3},{7,2},{8,13},{9,12},{10,... | collective-permute-start | bytes 18440 | tf_op jit(solution)/shard_map/ppermute | solution.py:419
  23.2 4.9 %collective-permute-start.7 = (f32[12,128]{1,0:T(8,128)S(1)}, f32[12,128]{1,0:T(8,128)S(1)}, u32[]{:S(2)}, u32[]{:S(2)}) collective-permute-start(f32[12,128]{1,0:T(8,128)S(1)} %add.3.refs_0_), channel_id=1, source_target_pairs={{0,11},{1,10},{2,9},{3,8},{4,15},{5,14},{6,13},{7,12},{8,3},{9,2},... | collective-permute-start | bytes 18440 | tf_op jit(solution)/shard_map/ppermute | solution.py:419
  25.3 4.0 %collective-permute-start.8 = (f32[12,128]{1,0:T(8,128)S(1)}, f32[12,128]{1,0:T(8,128)S(1)}, u32[]{:S(2)}, u32[]{:S(2)}) collective-permute-start(f32[12,128]{1,0:T(8,128)S(1)} %add.3.refs_0_), channel_id=1, source_target_pairs={{0,9},{1,8},{2,11},{3,10},{4,13},{5,12},{6,15},{7,14},{8,1},{9,0},... | collective-permute-start | bytes 18440 | tf_op jit(solution)/shard_map/ppermute | solution.py:419
  26.5 3.1 %collective-permute-start.9 = (f32[12,128]{1,0:T(8,128)S(1)}, f32[12,128]{1,0:T(8,128)S(1)}, u32[]{:S(2)}, u32[]{:S(2)}) collective-permute-start(f32[12,128]{1,0:T(8,128)S(1)} %add.3.refs_0_), channel_id=1, source_target_pairs={{0,3},{1,2},{2,1},{3,0},{4,7},{5,6},{6,5},{7,4},{8,11},{9,10},{10,... | collective-permute-start | bytes 18440 | tf_op jit(solution)/shard_map/ppermute | solution.py:419

commit v24 on v23

--- a/solution.py
+++ b/solution.py
@@ -438,7 +438,7 @@
     blocks = cells // LANES
     per = blocks * nodes
     slots = ffd_index.shape[1]
-    far_slots = slots // 2
+    far_slots = slots * 5 // 8
     owned = base_points.shape[1] // lax.axis_size("nodes")
     peers = lax.axis_size(CELL_AXES)
     cores = lax.axis_size("sub")

time: 30.3 us -> 30.4 us (level)
  no operation moved by 1% of the time
where the time goes in v24:
time: 30.4 us; the launch traced here: 30.2 us
  Pallas kernels  12.1 us (40%)
  starting transfers between devices  11.3 us (37%)
  waiting for transfers between devices  6.18 us (20%)
  between operations  0.72 us (2%)
    ppermute x5, waiting for transfers between devices, exchanged(): lax.ppermute(value, SUM_AXES, [(i, i ^ mask) for i in range(peers)])  5.99 us
    ppermute x2, starting transfers between devices, swaps(): return (lax.ppermute(array, SUM_AXES, pairs), close)  4.7 us
    ppermute x5, starting transfers between devices, exchanged(): lax.ppermute(value, SUM_AXES, [(i, i ^ mask) for i in range(peers)])  4.7 us
    pallas_call x1, Pallas kernels, body(): pl.pallas_call(functools.partial(wendland_kernel, 0), out_shape=near_shap...  2.73 us
    pallas_call x1, Pallas kernels, body(): pl.pallas_call(functools.partial(far_wendland_kernel, half), out_shape=(f...  2.28 us
    pallas_call x1, Pallas kernels, body(): pl.pallas_call(functools.partial(prepare_kernel, nodes), out_shape=(shape...  2.05 us
    pallas_call x1, Pallas kernels, body(): pl.pallas_call(functools.partial(control_kernel, scale), out_shape=shape(...  1.88 us
    ppermute x1, starting transfers between devices, body(): all_sens.append(lax.ppermute(part_sens, 'nodes', ring))  1.3 us
  transfers between devices with their start and end apart: 10, of which 6 were waited for; matrix products, arithmetic and copies ran while one was open for 0% of the time, Pallas kernels for 23%

profile of v24, /device:TPU:0, one launch (start us, length us, event | category | flops | bytes accessed | tf_op | source)
XLA Modules:
  0.0 30.2 jit_solution(5155000479274828650)
XLA Ops:
  0.6 3.0 %collective-permute-start = (f32[80,128]{1,0:T(8,128)}, f32[80,128]{1,0:T(8,128)S(1)}, u32[]{:S(2)}, u32[]{:S(2)}) collective-permute-start(f32[80,128]{1,0:T(8,128)} %bitcast.38), channel_id=1, source_target_pairs={{0,2},{2,0},{1,4},{3,6},{4,1},{6,3},{5,8},{7,10},{8,5},{10,7},{9,1... | collective-permute-start | bytes 122888 | tf_op jit(solution)/shard_map/ppermute | solution.py:470
  3.6 0.2 collective-permute-start.1
  3.8 2.0 %prepare.1 = (f32[2400,128]{1,0:T(8,128)S(1)}, f32[400,128]{1,0:T(8,128)S(1)}, f32[80,128]{1,0:T(8,128)S(1)}, f32[240,128]{1,0:T(8,128)S(1)}, s32[96,128]{1,0:T(...) custom-call(bf16[2400,128]{1,0:T(8,128)(2,1)} %bitcast.32, ...), custom_call_target="tpu_custom_call" | custom-call | flops 1000000000 | bytes 10000000 | tf_op jit(solution)/shard_map/prepare/pallas_call | solution.py:474
  5.9 0.0 collective-permute-done.far_ref
  5.9 0.0 collective-permute-done.1.close_ref
  5.9 1.2 %sweep.1._.refs_2_ = f32[80,128]{1,0:T(8,128)S(1)} custom-call(f32[80,128]{1,0:T(8,128)S(1)} %collective-permute-done.far_ref, f32[80,128]{1,0:T(8,128)S(1)} %collective-permute-done.1.close_ref, f32[80,128]{1,0:T(8,128)S(1)} %get-tuple-element.21.refs_0_, f32[80,128]{1,0:T(8,128)S(1)} %get-tuple-element.22.refs_1_.refs_3_, ...), custom_call_target="tpu_custom_call" | custom-call | flops 716800 | bytes 1228800 | tf_op jit(solution)/shard_map/sweep/pallas_call | solution.py:529
  7.2 0.4 %collective-permute-start.2 = (f32[80,128]{1,0:T(8,128)S(1)}, f32[80,128]{1,0:T(8,128)S(1)}, u32[]{:S(2)}, u32[]{:S(2)}) collective-permute-start(f32[80,128]{1,0:T(8,128)S(1)} %sweep.1._.refs_2_), channel_id=1, source_target_pairs={{0,1},{1,0},{4,5},{5,4},{8,9},{9,8},{12,13},{13,12},{2,3},{3,2},{6... | collective-permute-start | bytes 122888 | tf_op jit(solution)/shard_map/ppermute | solution.py:455
  7.5 1.7 %collective-permute-start.3 = (f32[80,128]{1,0:T(8,128)S(1)}, f32[80,128]{1,0:T(8,128)S(1)}, u32[]{:S(2)}, u32[]{:S(2)}) collective-permute-start(f32[80,128]{1,0:T(8,128)S(1)} %sweep.1._.refs_2_), channel_id=1, source_target_pairs={{0,2},{2,0},{1,4},{3,6},{4,1},{6,3},{5,8},{7,10},{8,5},{10,7},{9,1... | collective-permute-start | bytes 122888 | tf_op jit(solution)/shard_map/ppermute | solution.py:470
  9.2 2.7 %near_wendland.1.refs_9_.refs_2_ = bf16[1280,2048]{1,0:T(8,128)(2,1)S(1)} custom-call(bf16[1024,64]{1,0:T(8,128)(2,1)S(1)} %get-tuple-element.19.left_ref, bf16[64,2048]{1,0:T(8,128)(2,1)S(1)} %get-tuple-element.20.right_ref, f32[80,128]{1,0:T(8,128)S(1)} %sweep.1._.refs_2_), custom_call_target="tpu_custom_call" | custom-call | flops 1000000000 | bytes 10000000 | tf_op jit(solution)/shard_map/near_wendland/pallas_call | solution.py:545
  12.0 0.0 collective-permute-done.2.refs_0_
  12.0 0.0 collective-permute-done.3.refs_1_
  12.0 1.3 %last_sweep.1 = (f32[80,128]{1,0:T(8,128)S(1)}, f32[24,128]{1,0:T(8,128)S(1)}) custom-call(f32[80,128]{1,0:T(8,128)S(1)} %collective-permute-done.2.refs_0_, f32[80,128]{1,0:T(8,128)S(1)} %collective-permute-done.3.refs_1_, f32[80,128]{1,0:T(8,128)S(1)} %sweep.1._.refs_2_, f32[80,128]{1,0:T(8,128)S(1)} %get-tuple-element.22.refs_1_.refs_3_, ...), custom_call_target="tpu_custom_call" | custom-call | flops 716800 | bytes 1228800 | tf_op jit(solution)/shard_map/last_sweep/pallas_call | solution.py:554
  13.3 1.3 %collective-permute-start.4 = (f32[24,128]{1,0:T(8,128)S(1)}, f32[24,128]{1,0:T(8,128)S(1)}, u32[]{:S(2)}, u32[]{:S(2)}) collective-permute-start(f32[24,128]{1,0:T(8,128)S(1)} %get-tuple-element.28.after.refs_0_), channel_id=1, source_target_pairs={{0,2},{2,0},{1,3},{3,1},{4,6},{6,4},{5,7},{7,5},{8,10},{10,8},{9,1... | collective-permute-start | bytes 36872 | tf_op jit(solution)/shard_map/ppermute | solution.py:568
  14.6 2.3 %far_wendland.1 = (bf16[768,2048]{1,0:T(8,128)(2,1)S(1)}, bf16[10240,128]{1,0:T(8,128)(2,1)S(1)}, f32[80,128]{1,0:T(8,128)}) custom-call(bf16[1024,64]{1,0:T(8,128)(2,1)S(1)} %get-tuple-element.19.left_ref, bf16[64,2048]{1,0:T(8,128)(2,1)S(1)} %get-tuple-element.20.right_ref, f32[24,128]{1,0:T(8,128)S(1)} %get-tuple-element.28.after.refs_0_, ...), custom_call_target="tpu_custom_call" | custom-call | flops 1000000000 | bytes 10000000 | tf_op jit(solution)/shard_map/far_wendland/pallas_call | solution.py:570
  16.9 0.2 collective-permute-done.4.refs_1_
  17.0 1.9 %control.1.refs_0_ = f32[12,128]{1,0:T(8,128)S(1)} custom-call(f32[24,128]{1,0:T(8,128)S(1)} %get-tuple-element.28.after.refs_0_, f32[24,128]{1,0:T(8,128)S(1)} %collective-permute-done.4.refs_1_, bf16[1280,2048]{1,0:T(8,128)(2,1)S(1)} %near_wendland.1.refs_9_.refs_2_, bf16[768,2048]{1,0:T(8,128)(2,1)S(1)} %get-tuple-element.32.refs_3_, ...), custom_call_target="tpu_custom_call" | custom-call | tf_op jit(solution)/shard_map/control/pallas_call | solution.py:582
  18.9 0.1 collective-permute-start.5
  19.0 1.2 %collective-permute-done.5.refs_1_ = f32[12,128]{1,0:T(8,128)S(1)} collective-permute-done((f32[12,128]{1,0:T(8,128)S(1)}, f32[12,128]{1,0:T(8,128)S(1)}, u32[]{:S(2)}, u32[]{:S(2)}) %collective-permute-start.5) | collective-permute-done | bytes 6176 | tf_op jit(solution)/shard_map/ppermute | solution.py:419
  20.2 0.8 %collective-permute-start.6 = (f32[12,128]{1,0:T(8,128)S(1)}, f32[12,128]{1,0:T(8,128)S(1)}, u32[]{:S(2)}, u32[]{:S(2)}) collective-permute-start(f32[12,128]{1,0:T(8,128)S(1)} %add.2.refs_0_), channel_id=1, source_target_pairs={{0,5},{1,4},{2,7},{3,6},{4,1},{5,0},{6,3},{7,2},{8,13},{9,12},{10,... | collective-permute-start | bytes 18440 | tf_op jit(solution)/shard_map/ppermute | solution.py:419
  20.9 2.3 %collective-permute-done.6.refs_1_ = f32[12,128]{1,0:T(8,128)S(1)} collective-permute-done((f32[12,128]{1,0:T(8,128)S(1)}, f32[12,128]{1,0:T(8,128)S(1)}, u32[]{:S(2)}, u32[]{:S(2)}) %collective-permute-start.6) | collective-permute-done | bytes 6176 | tf_op jit(solution)/shard_map/ppermute | solution.py:419
  23.2 2.1 %collective-permute-start.7 = (f32[12,128]{1,0:T(8,128)S(1)}, f32[12,128]{1,0:T(8,128)S(1)}, u32[]{:S(2)}, u32[]{:S(2)}) collective-permute-start(f32[12,128]{1,0:T(8,128)S(1)} %add.3.refs_0_), channel_id=1, source_target_pairs={{0,11},{1,10},{2,9},{3,8},{4,15},{5,14},{6,13},{7,12},{8,3},{9,2},... | collective-permute-start | bytes 18440 | tf_op jit(solution)/shard_map/ppermute | solution.py:419
  25.3 1.2 %collective-permute-start.8 = (f32[12,128]{1,0:T(8,128)S(1)}, f32[12,128]{1,0:T(8,128)S(1)}, u32[]{:S(2)}, u32[]{:S(2)}) collective-permute-start(f32[12,128]{1,0:T(8,128)S(1)} %add.3.refs_0_), channel_id=1, source_target_pairs={{0,9},{1,8},{2,11},{3,10},{4,13},{5,12},{6,15},{7,14},{8,1},{9,0},... | collective-permute-start | bytes 18440 | tf_op jit(solution)/shard_map/ppermute | solution.py:419
  26.6 0.6 %collective-permute-start.9 = (f32[12,128]{1,0:T(8,128)S(1)}, f32[12,128]{1,0:T(8,128)S(1)}, u32[]{:S(2)}, u32[]{:S(2)}) collective-permute-start(f32[12,128]{1,0:T(8,128)S(1)} %add.3.refs_0_), channel_id=1, source_target_pairs={{0,3},{1,2},{2,1},{3,0},{4,7},{5,6},{6,5},{7,4},{8,11},{9,10},{10,... | collective-permute-start | bytes 18440 | tf_op jit(solution)/shard_map/ppermute | solution.py:419
  27.1 1.0 %collective-permute-done.7.refs_1_ = f32[12,128]{1,0:T(8,128)S(1)} collective-permute-done((f32[12,128]{1,0:T(8,128)S(1)}, f32[12,128]{1,0:T(8,128)S(1)}, u32[]{:S(2)}, u32[]{:S(2)}) %collective-permute-start.7) | collective-permute-done | bytes 6176 | tf_op jit(solution)/shard_map/ppermute | solution.py:419
  28.1 1.2 %collective-permute-done.8.refs_2_ = f32[12,128]{1,0:T(8,128)S(1)} collective-permute-done((f32[12,128]{1,0:T(8,128)S(1)}, f32[12,128]{1,0:T(8,128)S(1)}, u32[]{:S(2)}, u32[]{:S(2)}) %collective-permute-start.8) | collective-permute-done | bytes 6176 | tf_op jit(solution)/shard_map/ppermute | solution.py:419
  29.3 0.3 %collective-permute-done.9.refs_3_ = f32[12,128]{1,0:T(8,128)S(1)} collective-permute-done((f32[12,128]{1,0:T(8,128)S(1)}, f32[12,128]{1,0:T(8,128)S(1)}, u32[]{:S(2)}, u32[]{:S(2)}) %collective-permute-start.9) | collective-permute-done | bytes 6176 | tf_op jit(solution)/shard_map/ppermute | solution.py:419
  29.6 0.6 %finish.1 = f32[3,512]{1,0:T(4,128)} custom-call(f32[12,128]{1,0:T(8,128)S(1)} %add.3.refs_0_, f32[12,128]{1,0:T(8,128)S(1)} %collective-permute-done.7.refs_1_, f32[12,128]{1,0:T(8,128)S(1)} %collective-permute-done.8.refs_2_, f32[12,128]{1,0:T(8,128)S(1)} %collective-permute-done.9.refs_3_), custom_call_target="tpu_custom_call" | custom-call | tf_op jit(solution)/shard_map/finish/pallas_call | solution.py:598
  (2 shorter events, 0.0 us)
Async XLA Ops:
  0.6 5.3 %collective-permute-start = (f32[80,128]{1,0:T(8,128)}, f32[80,128]{1,0:T(8,128)S(1)}, u32[]{:S(2)}, u32[]{:S(2)}) collective-permute-start(f32[80,128]{1,0:T(8,128)} %bitcast.38), channel_id=1, source_target_pairs={{0,2},{2,0},{1,4},{3,6},{4,1},{6,3},{5,8},{7,10},{8,5},{10,7},{9,1... | collective-permute-start | bytes 122888 | tf_op jit(solution)/shard_map/ppermute | solution.py:470
  3.6 2.3 %collective-permute-start.1 = (f32[80,128]{1,0:T(8,128)}, f32[80,128]{1,0:T(8,128)S(1)}, u32[]{:S(2)}, u32[]{:S(2)}) collective-permute-start(f32[80,128]{1,0:T(8,128)} %bitcast.39), channel_id=1, source_target_pairs={{0,1},{1,0},{4,5},{5,4},{8,9},{9,8},{12,13},{13,12},{2,3},{3,2},{6... | collective-permute-start | bytes 122888 | tf_op jit(solution)/shard_map/ppermute | solution.py:455
  7.2 4.8 %collective-permute-start.2 = (f32[80,128]{1,0:T(8,128)S(1)}, f32[80,128]{1,0:T(8,128)S(1)}, u32[]{:S(2)}, u32[]{:S(2)}) collective-permute-start(f32[80,128]{1,0:T(8,128)S(1)} %sweep.1._.refs_2_), channel_id=1, source_target_pairs={{0,1},{1,0},{4,5},{5,4},{8,9},{9,8},{12,13},{13,12},{2,3},{3,2},{6... | collective-permute-start | bytes 122888 | tf_op jit(solution)/shard_map/ppermute | solution.py:455
  7.5 4.5 %collective-permute-start.3 = (f32[80,128]{1,0:T(8,128)S(1)}, f32[80,128]{1,0:T(8,128)S(1)}, u32[]{:S(2)}, u32[]{:S(2)}) collective-permute-start(f32[80,128]{1,0:T(8,128)S(1)} %sweep.1._.refs_2_), channel_id=1, source_target_pairs={{0,2},{2,0},{1,4},{3,6},{4,1},{6,3},{5,8},{7,10},{8,5},{10,7},{9,1... | collective-permute-start | bytes 122888 | tf_op jit(solution)/shard_map/ppermute | solution.py:470
  13.3 3.8 %collective-permute-start.4 = (f32[24,128]{1,0:T(8,128)S(1)}, f32[24,128]{1,0:T(8,128)S(1)}, u32[]{:S(2)}, u32[]{:S(2)}) collective-permute-start(f32[24,128]{1,0:T(8,128)S(1)} %get-tuple-element.28.after.refs_0_), channel_id=1, source_target_pairs={{0,2},{2,0},{1,3},{3,1},{4,6},{6,4},{5,7},{7,5},{8,10},{10,8},{9,1... | collective-permute-start | bytes 36872 | tf_op jit(solution)/shard_map/ppermute | solution.py:568
  18.9 1.2 %collective-permute-start.5 = (f32[12,128]{1,0:T(8,128)S(1)}, f32[12,128]{1,0:T(8,128)S(1)}, u32[]{:S(2)}, u32[]{:S(2)}) collective-permute-start(f32[12,128]{1,0:T(8,128)S(1)} %control.1.refs_0_), channel_id=1, source_target_pairs={{0,1},{1,0},{2,3},{3,2},{4,5},{5,4},{6,7},{7,6},{8,9},{9,8},{10,11... | collective-permute-start | bytes 18440 | tf_op jit(solution)/shard_map/ppermute | solution.py:419
  20.2 3.1 %collective-permute-start.6 = (f32[12,128]{1,0:T(8,128)S(1)}, f32[12,128]{1,0:T(8,128)S(1)}, u32[]{:S(2)}, u32[]{:S(2)}) collective-permute-start(f32[12,128]{1,0:T(8,128)S(1)} %add.2.refs_0_), channel_id=1, source_target_pairs={{0,5},{1,4},{2,7},{3,6},{4,1},{5,0},{6,3},{7,2},{8,13},{9,12},{10,... | collective-permute-start | bytes 18440 | tf_op jit(solution)/shard_map/ppermute | solution.py:419
  23.2 4.9 %collective-permute-start.7 = (f32[12,128]{1,0:T(8,128)S(1)}, f32[12,128]{1,0:T(8,128)S(1)}, u32[]{:S(2)}, u32[]{:S(2)}) collective-permute-start(f32[12,128]{1,0:T(8,128)S(1)} %add.3.refs_0_), channel_id=1, source_target_pairs={{0,11},{1,10},{2,9},{3,8},{4,15},{5,14},{6,13},{7,12},{8,3},{9,2},... | collective-permute-start | bytes 18440 | tf_op jit(solution)/shard_map/ppermute | solution.py:419
  25.3 4.0 %collective-permute-start.8 = (f32[12,128]{1,0:T(8,128)S(1)}, f32[12,128]{1,0:T(8,128)S(1)}, u32[]{:S(2)}, u32[]{:S(2)}) collective-permute-start(f32[12,128]{1,0:T(8,128)S(1)} %add.3.refs_0_), channel_id=1, source_target_pairs={{0,9},{1,8},{2,11},{3,10},{4,13},{5,12},{6,15},{7,14},{8,1},{9,0},... | collective-permute-start | bytes 18440 | tf_op jit(solution)/shard_map/ppermute | solution.py:419
  26.6 3.1 %collective-permute-start.9 = (f32[12,128]{1,0:T(8,128)S(1)}, f32[12,128]{1,0:T(8,128)S(1)}, u32[]{:S(2)}, u32[]{:S(2)}) collective-permute-start(f32[12,128]{1,0:T(8,128)S(1)} %add.3.refs_0_), channel_id=1, source_target_pairs={{0,3},{1,2},{2,1},{3,0},{4,7},{5,6},{6,5},{7,4},{8,11},{9,10},{10,... | collective-permute-start | bytes 18440 | tf_op jit(solution)/shard_map/ppermute | solution.py:419

commit v25 on v24

--- a/solution.py
+++ b/solution.py
@@ -349,30 +349,42 @@
         first = sens.astype(jnp.bfloat16).astype(jnp.float32)
         wide.append(jnp.concatenate([first, sens - first], axis=0))
     sens = jnp.concatenate(wide, axis=1).astype(jnp.bfloat16)
-    grad = None
-    for part, ref in ((sens[:, :half], near_ref), (sens[:, half:], far_ref)):
-        both = jnp.concatenate([part, part], axis=1)
-        term = jnp.dot(both, ref[...], preferred_element_type=jnp.float32)
-        grad = term if grad is None else grad + term
-    grad = grad[:8] + grad[8:]
-    row = lax.broadcasted_iota(jnp.int32, (16, grad.shape[1]), 0)
-    wide = jnp.zeros(row.shape, jnp.float32)
-    for k in range(3):
-        mine = jnp.logical_and(row >= k * groups, row < (k + 1) * groups)
-        wide = jnp.where(mine, grad[k : k + 1], wide)
-    grad = wide
-    owned = grad.shape[1]
-    result = None
+    operands = [
+        (jnp.concatenate([part, part], axis=1), ref)
+        for part, ref in ((sens[:, :half], near_ref), (sens[:, half:], far_ref))
+    ]
+    owned = near_ref.shape[1]
+    span = min(256, owned)
+
+    def gradient(here):
+        grad = None
+        for both, ref in operands:
+            term = jnp.dot(both, ref[:, here], preferred_element_type=jnp.float32)
+            grad = term if grad is None else grad + term
+        return grad[:8] + grad[8:]
+
     places = [
         (ref, first) for ref in (near_hot, far_hot) for first in range(0, ref.shape[0], owned)
     ]
-    for j, (ref, first) in enumerate(places):
-        term = jnp.dot(
-            jnp.concatenate(halves(grad * spread_ref[j * 16 : (j + 1) * 16, :]), axis=0),
-            ref[first : first + owned, :],
-            preferred_element_type=jnp.float32,
-        )
-        result = term if result is None else result + term
+    row = lax.broadcasted_iota(jnp.int32, (16, span), 0)
+    spans = [slice(first, first + span) for first in range(0, owned, span)]
+    following = gradient(spans[0])
+    result = None
+    for at, here in enumerate(spans):
+        grad = following
+        if at + 1 < len(spans):
+            following = gradient(spans[at + 1])
+        wide = jnp.zeros((16, span), jnp.float32)
+        for k in range(3):
+            mine = jnp.logical_and(row >= k * groups, row < (k + 1) * groups)
+            wide = jnp.where(mine, grad[k : k + 1], wide)
+        for j, (ref, first) in enumerate(places):
+            term = jnp.dot(
+                jnp.concatenate(halves(wide * spread_ref[j * 16 : (j + 1) * 16, here]), axis=0),
+                ref[first + here.start : first + here.stop, :],
+                preferred_element_type=jnp.float32,
+            )
+            result = term if result is None else result + term
     result = result[:16] + result[16:]
     out_ref[...] = result[: 3 * groups]
 

time: 30.4 us -> 30.8 us (1.013)
  Pallas kernels: 12.1 us -> 12.5 us
    pallas_call x1, Pallas kernels: 1.88 us -> 2.3 us  [body(): pl.pallas_call(functools.partial(control_kernel, scale), out_shape=shape(...]
where the time goes in v25:
time: 30.8 us; the launch traced here: 30.7 us
  Pallas kernels  12.5 us (41%)
  starting transfers between devices  11.3 us (37%)
  waiting for transfers between devices  6.18 us (20%)
  between operations  0.72 us (2%)
    ppermute x5, waiting for transfers between devices, exchanged(): lax.ppermute(value, SUM_AXES, [(i, i ^ mask) for i in range(peers)])  5.99 us
    ppermute x2, starting transfers between devices, swaps(): return (lax.ppermute(array, SUM_AXES, pairs), close)  4.7 us
    ppermute x5, starting transfers between devices, exchanged(): lax.ppermute(value, SUM_AXES, [(i, i ^ mask) for i in range(peers)])  4.7 us
    pallas_call x1, Pallas kernels, body(): pl.pallas_call(functools.partial(wendland_kernel, 0), out_shape=near_shap...  2.73 us
    pallas_call x1, Pallas kernels, body(): pl.pallas_call(functools.partial(control_kernel, scale), out_shape=shape(...  2.3 us
    pallas_call x1, Pallas kernels, body(): pl.pallas_call(functools.partial(far_wendland_kernel, half), out_shape=(f...  2.28 us
    pallas_call x1, Pallas kernels, body(): pl.pallas_call(functools.partial(prepare_kernel, nodes), out_shape=(shape...  2.05 us
    ppermute x1, starting transfers between devices, body(): all_sens.append(lax.ppermute(part_sens, 'nodes', ring))  1.3 us
  transfers between devices with their start and end apart: 10, of which 6 were waited for; matrix products, arithmetic and copies ran while one was open for 0% of the time, Pallas kernels for 23%

profile of v25, /device:TPU:0, one launch (start us, length us, event | category | flops | bytes accessed | tf_op | source)
XLA Modules:
  0.0 30.7 jit_solution(11842572873256844511)
XLA Ops:
  0.6 3.0 %collective-permute-start = (f32[80,128]{1,0:T(8,128)}, f32[80,128]{1,0:T(8,128)S(1)}, u32[]{:S(2)}, u32[]{:S(2)}) collective-permute-start(f32[80,128]{1,0:T(8,128)} %bitcast.38), channel_id=1, source_target_pairs={{0,2},{2,0},{1,4},{3,6},{4,1},{6,3},{5,8},{7,10},{8,5},{10,7},{9,1... | collective-permute-start | bytes 122888 | tf_op jit(solution)/shard_map/ppermute | solution.py:482
  3.6 0.2 collective-permute-start.1
  3.8 2.0 %prepare.1 = (f32[2400,128]{1,0:T(8,128)S(1)}, f32[400,128]{1,0:T(8,128)S(1)}, f32[80,128]{1,0:T(8,128)S(1)}, f32[240,128]{1,0:T(8,128)S(1)}, s32[96,128]{1,0:T(...) custom-call(bf16[2400,128]{1,0:T(8,128)(2,1)} %bitcast.32, ...), custom_call_target="tpu_custom_call" | custom-call | flops 1000000000 | bytes 10000000 | tf_op jit(solution)/shard_map/prepare/pallas_call | solution.py:486
  5.9 0.0 collective-permute-done.far_ref
  5.9 0.0 collective-permute-done.1.close_ref
  5.9 1.2 %sweep.1._.refs_2_ = f32[80,128]{1,0:T(8,128)S(1)} custom-call(f32[80,128]{1,0:T(8,128)S(1)} %collective-permute-done.far_ref, f32[80,128]{1,0:T(8,128)S(1)} %collective-permute-done.1.close_ref, f32[80,128]{1,0:T(8,128)S(1)} %get-tuple-element.21.refs_0_, f32[80,128]{1,0:T(8,128)S(1)} %get-tuple-element.22.refs_1_.refs_3_, ...), custom_call_target="tpu_custom_call" | custom-call | flops 716800 | bytes 1228800 | tf_op jit(solution)/shard_map/sweep/pallas_call | solution.py:541
  7.2 0.4 %collective-permute-start.2 = (f32[80,128]{1,0:T(8,128)S(1)}, f32[80,128]{1,0:T(8,128)S(1)}, u32[]{:S(2)}, u32[]{:S(2)}) collective-permute-start(f32[80,128]{1,0:T(8,128)S(1)} %sweep.1._.refs_2_), channel_id=1, source_target_pairs={{0,1},{1,0},{4,5},{5,4},{8,9},{9,8},{12,13},{13,12},{2,3},{3,2},{6... | collective-permute-start | bytes 122888 | tf_op jit(solution)/shard_map/ppermute | solution.py:467
  7.5 1.7 %collective-permute-start.3 = (f32[80,128]{1,0:T(8,128)S(1)}, f32[80,128]{1,0:T(8,128)S(1)}, u32[]{:S(2)}, u32[]{:S(2)}) collective-permute-start(f32[80,128]{1,0:T(8,128)S(1)} %sweep.1._.refs_2_), channel_id=1, source_target_pairs={{0,2},{2,0},{1,4},{3,6},{4,1},{6,3},{5,8},{7,10},{8,5},{10,7},{9,1... | collective-permute-start | bytes 122888 | tf_op jit(solution)/shard_map/ppermute | solution.py:482
  9.2 2.7 %near_wendland.1.refs_9_.refs_2_ = bf16[1280,2048]{1,0:T(8,128)(2,1)S(1)} custom-call(bf16[1024,64]{1,0:T(8,128)(2,1)S(1)} %get-tuple-element.19.left_ref, bf16[64,2048]{1,0:T(8,128)(2,1)S(1)} %get-tuple-element.20.right_ref, f32[80,128]{1,0:T(8,128)S(1)} %sweep.1._.refs_2_), custom_call_target="tpu_custom_call" | custom-call | flops 1000000000 | bytes 10000000 | tf_op jit(solution)/shard_map/near_wendland/pallas_call | solution.py:557
  12.0 0.0 collective-permute-done.2.refs_0_
  12.0 0.0 collective-permute-done.3.refs_1_
  12.0 1.3 %last_sweep.1 = (f32[80,128]{1,0:T(8,128)S(1)}, f32[24,128]{1,0:T(8,128)S(1)}) custom-call(f32[80,128]{1,0:T(8,128)S(1)} %collective-permute-done.2.refs_0_, f32[80,128]{1,0:T(8,128)S(1)} %collective-permute-done.3.refs_1_, f32[80,128]{1,0:T(8,128)S(1)} %sweep.1._.refs_2_, f32[80,128]{1,0:T(8,128)S(1)} %get-tuple-element.22.refs_1_.refs_3_, ...), custom_call_target="tpu_custom_call" | custom-call | flops 716800 | bytes 1228800 | tf_op jit(solution)/shard_map/last_sweep/pallas_call | solution.py:566
  13.3 1.3 %collective-permute-start.4 = (f32[24,128]{1,0:T(8,128)S(1)}, f32[24,128]{1,0:T(8,128)S(1)}, u32[]{:S(2)}, u32[]{:S(2)}) collective-permute-start(f32[24,128]{1,0:T(8,128)S(1)} %get-tuple-element.28.after.refs_0_), channel_id=1, source_target_pairs={{0,2},{2,0},{1,3},{3,1},{4,6},{6,4},{5,7},{7,5},{8,10},{10,8},{9,1... | collective-permute-start | bytes 36872 | tf_op jit(solution)/shard_map/ppermute | solution.py:580
  14.6 2.3 %far_wendland.1 = (bf16[768,2048]{1,0:T(8,128)(2,1)S(1)}, bf16[10240,128]{1,0:T(8,128)(2,1)S(1)}, f32[80,128]{1,0:T(8,128)}) custom-call(bf16[1024,64]{1,0:T(8,128)(2,1)S(1)} %get-tuple-element.19.left_ref, bf16[64,2048]{1,0:T(8,128)(2,1)S(1)} %get-tuple-element.20.right_ref, f32[24,128]{1,0:T(8,128)S(1)} %get-tuple-element.28.after.refs_0_, ...), custom_call_target="tpu_custom_call" | custom-call | flops 1000000000 | bytes 10000000 | tf_op jit(solution)/shard_map/far_wendland/pallas_call | solution.py:582
  16.9 0.2 collective-permute-done.4.refs_1_
  17.0 2.3 %control.1.refs_0_ = f32[12,128]{1,0:T(8,128)S(1)} custom-call(f32[24,128]{1,0:T(8,128)S(1)} %get-tuple-element.28.after.refs_0_, f32[24,128]{1,0:T(8,128)S(1)} %collective-permute-done.4.refs_1_, bf16[1280,2048]{1,0:T(8,128)(2,1)S(1)} %near_wendland.1.refs_9_.refs_2_, bf16[768,2048]{1,0:T(8,128)(2,1)S(1)} %get-tuple-element.32.refs_3_, ...), custom_call_target="tpu_custom_call" | custom-call | tf_op jit(solution)/shard_map/control/pallas_call | solution.py:594
  19.3 0.1 collective-permute-start.5
  19.4 1.2 %collective-permute-done.5.refs_1_ = f32[12,128]{1,0:T(8,128)S(1)} collective-permute-done((f32[12,128]{1,0:T(8,128)S(1)}, f32[12,128]{1,0:T(8,128)S(1)}, u32[]{:S(2)}, u32[]{:S(2)}) %collective-permute-start.5) | collective-permute-done | bytes 6176 | tf_op jit(solution)/shard_map/ppermute | solution.py:431
  20.6 0.8 %collective-permute-start.6 = (f32[12,128]{1,0:T(8,128)S(1)}, f32[12,128]{1,0:T(8,128)S(1)}, u32[]{:S(2)}, u32[]{:S(2)}) collective-permute-start(f32[12,128]{1,0:T(8,128)S(1)} %add.2.refs_0_), channel_id=1, source_target_pairs={{0,5},{1,4},{2,7},{3,6},{4,1},{5,0},{6,3},{7,2},{8,13},{9,12},{10,... | collective-permute-start | bytes 18440 | tf_op jit(solution)/shard_map/ppermute | solution.py:431
  21.3 2.3 %collective-permute-done.6.refs_1_ = f32[12,128]{1,0:T(8,128)S(1)} collective-permute-done((f32[12,128]{1,0:T(8,128)S(1)}, f32[12,128]{1,0:T(8,128)S(1)}, u32[]{:S(2)}, u32[]{:S(2)}) %collective-permute-start.6) | collective-permute-done | bytes 6176 | tf_op jit(solution)/shard_map/ppermute | solution.py:431
  23.7 2.1 %collective-permute-start.7 = (f32[12,128]{1,0:T(8,128)S(1)}, f32[12,128]{1,0:T(8,128)S(1)}, u32[]{:S(2)}, u32[]{:S(2)}) collective-permute-start(f32[12,128]{1,0:T(8,128)S(1)} %add.3.refs_0_), channel_id=1, source_target_pairs={{0,11},{1,10},{2,9},{3,8},{4,15},{5,14},{6,13},{7,12},{8,3},{9,2},... | collective-permute-start | bytes 18440 | tf_op jit(solution)/shard_map/ppermute | solution.py:431
  25.7 1.2 %collective-permute-start.8 = (f32[12,128]{1,0:T(8,128)S(1)}, f32[12,128]{1,0:T(8,128)S(1)}, u32[]{:S(2)}, u32[]{:S(2)}) collective-permute-start(f32[12,128]{1,0:T(8,128)S(1)} %add.3.refs_0_), channel_id=1, source_target_pairs={{0,9},{1,8},{2,11},{3,10},{4,13},{5,12},{6,15},{7,14},{8,1},{9,0},... | collective-permute-start | bytes 18440 | tf_op jit(solution)/shard_map/ppermute | solution.py:431
  27.0 0.6 %collective-permute-start.9 = (f32[12,128]{1,0:T(8,128)S(1)}, f32[12,128]{1,0:T(8,128)S(1)}, u32[]{:S(2)}, u32[]{:S(2)}) collective-permute-start(f32[12,128]{1,0:T(8,128)S(1)} %add.3.refs_0_), channel_id=1, source_target_pairs={{0,3},{1,2},{2,1},{3,0},{4,7},{5,6},{6,5},{7,4},{8,11},{9,10},{10,... | collective-permute-start | bytes 18440 | tf_op jit(solution)/shard_map/ppermute | solution.py:431
  27.5 1.0 %collective-permute-done.7.refs_1_ = f32[12,128]{1,0:T(8,128)S(1)} collective-permute-done((f32[12,128]{1,0:T(8,128)S(1)}, f32[12,128]{1,0:T(8,128)S(1)}, u32[]{:S(2)}, u32[]{:S(2)}) %collective-permute-start.7) | collective-permute-done | bytes 6176 | tf_op jit(solution)/shard_map/ppermute | solution.py:431
  28.5 1.2 %collective-permute-done.8.refs_2_ = f32[12,128]{1,0:T(8,128)S(1)} collective-permute-done((f32[12,128]{1,0:T(8,128)S(1)}, f32[12,128]{1,0:T(8,128)S(1)}, u32[]{:S(2)}, u32[]{:S(2)}) %collective-permute-start.8) | collective-permute-done | bytes 6176 | tf_op jit(solution)/shard_map/ppermute | solution.py:431
  29.7 0.3 %collective-permute-done.9.refs_3_ = f32[12,128]{1,0:T(8,128)S(1)} collective-permute-done((f32[12,128]{1,0:T(8,128)S(1)}, f32[12,128]{1,0:T(8,128)S(1)}, u32[]{:S(2)}, u32[]{:S(2)}) %collective-permute-start.9) | collective-permute-done | bytes 6176 | tf_op jit(solution)/shard_map/ppermute | solution.py:431
  30.0 0.6 %finish.1 = f32[3,512]{1,0:T(4,128)} custom-call(f32[12,128]{1,0:T(8,128)S(1)} %add.3.refs_0_, f32[12,128]{1,0:T(8,128)S(1)} %collective-permute-done.7.refs_1_, f32[12,128]{1,0:T(8,128)S(1)} %collective-permute-done.8.refs_2_, f32[12,128]{1,0:T(8,128)S(1)} %collective-permute-done.9.refs_3_), custom_call_target="tpu_custom_call" | custom-call | tf_op jit(solution)/shard_map/finish/pallas_call | solution.py:610
  (2 shorter events, 0.0 us)
Async XLA Ops:
  0.6 5.3 %collective-permute-start = (f32[80,128]{1,0:T(8,128)}, f32[80,128]{1,0:T(8,128)S(1)}, u32[]{:S(2)}, u32[]{:S(2)}) collective-permute-start(f32[80,128]{1,0:T(8,128)} %bitcast.38), channel_id=1, source_target_pairs={{0,2},{2,0},{1,4},{3,6},{4,1},{6,3},{5,8},{7,10},{8,5},{10,7},{9,1... | collective-permute-start | bytes 122888 | tf_op jit(solution)/shard_map/ppermute | solution.py:482
  3.6 2.3 %collective-permute-start.1 = (f32[80,128]{1,0:T(8,128)}, f32[80,128]{1,0:T(8,128)S(1)}, u32[]{:S(2)}, u32[]{:S(2)}) collective-permute-start(f32[80,128]{1,0:T(8,128)} %bitcast.39), channel_id=1, source_target_pairs={{0,1},{1,0},{4,5},{5,4},{8,9},{9,8},{12,13},{13,12},{2,3},{3,2},{6... | collective-permute-start | bytes 122888 | tf_op jit(solution)/shard_map/ppermute | solution.py:467
  7.2 4.8 %collective-permute-start.2 = (f32[80,128]{1,0:T(8,128)S(1)}, f32[80,128]{1,0:T(8,128)S(1)}, u32[]{:S(2)}, u32[]{:S(2)}) collective-permute-start(f32[80,128]{1,0:T(8,128)S(1)} %sweep.1._.refs_2_), channel_id=1, source_target_pairs={{0,1},{1,0},{4,5},{5,4},{8,9},{9,8},{12,13},{13,12},{2,3},{3,2},{6... | collective-permute-start | bytes 122888 | tf_op jit(solution)/shard_map/ppermute | solution.py:467
  7.5 4.5 %collective-permute-start.3 = (f32[80,128]{1,0:T(8,128)S(1)}, f32[80,128]{1,0:T(8,128)S(1)}, u32[]{:S(2)}, u32[]{:S(2)}) collective-permute-start(f32[80,128]{1,0:T(8,128)S(1)} %sweep.1._.refs_2_), channel_id=1, source_target_pairs={{0,2},{2,0},{1,4},{3,6},{4,1},{6,3},{5,8},{7,10},{8,5},{10,7},{9,1... | collective-permute-start | bytes 122888 | tf_op jit(solution)/shard_map/ppermute | solution.py:482
  13.3 3.8 %collective-permute-start.4 = (f32[24,128]{1,0:T(8,128)S(1)}, f32[24,128]{1,0:T(8,128)S(1)}, u32[]{:S(2)}, u32[]{:S(2)}) collective-permute-start(f32[24,128]{1,0:T(8,128)S(1)} %get-tuple-element.28.after.refs_0_), channel_id=1, source_target_pairs={{0,2},{2,0},{1,3},{3,1},{4,6},{6,4},{5,7},{7,5},{8,10},{10,8},{9,1... | collective-permute-start | bytes 36872 | tf_op jit(solution)/shard_map/ppermute | solution.py:580
  19.3 1.2 %collective-permute-start.5 = (f32[12,128]{1,0:T(8,128)S(1)}, f32[12,128]{1,0:T(8,128)S(1)}, u32[]{:S(2)}, u32[]{:S(2)}) collective-permute-start(f32[12,128]{1,0:T(8,128)S(1)} %control.1.refs_0_), channel_id=1, source_target_pairs={{0,1},{1,0},{2,3},{3,2},{4,5},{5,4},{6,7},{7,6},{8,9},{9,8},{10,11... | collective-permute-start | bytes 18440 | tf_op jit(solution)/shard_map/ppermute | solution.py:431
  20.6 3.1 %collective-permute-start.6 = (f32[12,128]{1,0:T(8,128)S(1)}, f32[12,128]{1,0:T(8,128)S(1)}, u32[]{:S(2)}, u32[]{:S(2)}) collective-permute-start(f32[12,128]{1,0:T(8,128)S(1)} %add.2.refs_0_), channel_id=1, source_target_pairs={{0,5},{1,4},{2,7},{3,6},{4,1},{5,0},{6,3},{7,2},{8,13},{9,12},{10,... | collective-permute-start | bytes 18440 | tf_op jit(solution)/shard_map/ppermute | solution.py:431
  23.7 4.9 %collective-permute-start.7 = (f32[12,128]{1,0:T(8,128)S(1)}, f32[12,128]{1,0:T(8,128)S(1)}, u32[]{:S(2)}, u32[]{:S(2)}) collective-permute-start(f32[12,128]{1,0:T(8,128)S(1)} %add.3.refs_0_), channel_id=1, source_target_pairs={{0,11},{1,10},{2,9},{3,8},{4,15},{5,14},{6,13},{7,12},{8,3},{9,2},... | collective-permute-start | bytes 18440 | tf_op jit(solution)/shard_map/ppermute | solution.py:431
  25.7 4.0 %collective-permute-start.8 = (f32[12,128]{1,0:T(8,128)S(1)}, f32[12,128]{1,0:T(8,128)S(1)}, u32[]{:S(2)}, u32[]{:S(2)}) collective-permute-start(f32[12,128]{1,0:T(8,128)S(1)} %add.3.refs_0_), channel_id=1, source_target_pairs={{0,9},{1,8},{2,11},{3,10},{4,13},{5,12},{6,15},{7,14},{8,1},{9,0},... | collective-permute-start | bytes 18440 | tf_op jit(solution)/shard_map/ppermute | solution.py:431
  27.0 3.1 %collective-permute-start.9 = (f32[12,128]{1,0:T(8,128)S(1)}, f32[12,128]{1,0:T(8,128)S(1)}, u32[]{:S(2)}, u32[]{:S(2)}) collective-permute-start(f32[12,128]{1,0:T(8,128)S(1)} %add.3.refs_0_), channel_id=1, source_target_pairs={{0,3},{1,2},{2,1},{3,0},{4,7},{5,6},{6,5},{7,4},{8,11},{9,10},{10,... | collective-permute-start | bytes 18440 | tf_op jit(solution)/shard_map/ppermute | solution.py:431

commit v26 on v24

--- a/solution.py
+++ b/solution.py
@@ -362,15 +362,15 @@
         wide = jnp.where(mine, grad[k : k + 1], wide)
     grad = wide
     owned = grad.shape[1]
-    result = None
-    places = [
-        (ref, first) for ref in (near_hot, far_hot) for first in range(0, ref.shape[0], owned)
-    ]
-    for j, (ref, first) in enumerate(places):
+    result, slot = None, 0
+    for ref in (near_hot, far_hot):
+        parts = []
+        for _ in range(ref.shape[0] // owned):
+            parts.append(halves(grad * spread_ref[slot * 16 : (slot + 1) * 16, :]))
+            slot += 1
+        parts = [jnp.concatenate(both, axis=1) for both in zip(*parts)]
         term = jnp.dot(
-            jnp.concatenate(halves(grad * spread_ref[j * 16 : (j + 1) * 16, :]), axis=0),
-            ref[first : first + owned, :],
-            preferred_element_type=jnp.float32,
+            jnp.concatenate(parts, axis=0), ref[...], preferred_element_type=jnp.float32
         )
         result = term if result is None else result + term
     result = result[:16] + result[16:]

time: 30.4 us -> 30.3 us (level)
  no operation moved by 1% of the time
where the time goes in v26:
time: 30.3 us; the launch traced here: 30.2 us
  Pallas kernels  12 us (40%)
  starting transfers between devices  11.3 us (37%)
  waiting for transfers between devices  6.18 us (20%)
  between operations  0.72 us (2%)
    ppermute x5, waiting for transfers between devices, exchanged(): lax.ppermute(value, SUM_AXES, [(i, i ^ mask) for i in range(peers)])  5.99 us
    ppermute x2, starting transfers between devices, swaps(): return (lax.ppermute(array, SUM_AXES, pairs), close)  4.7 us
    ppermute x5, starting transfers between devices, exchanged(): lax.ppermute(value, SUM_AXES, [(i, i ^ mask) for i in range(peers)])  4.7 us
    pallas_call x1, Pallas kernels, body(): pl.pallas_call(functools.partial(wendland_kernel, 0), out_shape=near_shap...  2.73 us
    pallas_call x1, Pallas kernels, body(): pl.pallas_call(functools.partial(far_wendland_kernel, half), out_shape=(f...  2.28 us
    pallas_call x1, Pallas kernels, body(): pl.pallas_call(functools.partial(prepare_kernel, nodes), out_shape=(shape...  2.05 us
    pallas_call x1, Pallas kernels, body(): pl.pallas_call(functools.partial(control_kernel, scale), out_shape=shape(...  1.84 us
    ppermute x1, starting transfers between devices, body(): all_sens.append(lax.ppermute(part_sens, 'nodes', ring))  1.3 us
  transfers between devices with their start and end apart: 10, of which 6 were waited for; matrix products, arithmetic and copies ran while one was open for 0% of the time, Pallas kernels for 23%

profile of v26, /device:TPU:0, one launch (start us, length us, event | category | flops | bytes accessed | tf_op | source)
XLA Modules:
  0.0 30.2 jit_solution(12810246157708882500)
XLA Ops:
  0.6 3.0 %collective-permute-start = (f32[80,128]{1,0:T(8,128)}, f32[80,128]{1,0:T(8,128)S(1)}, u32[]{:S(2)}, u32[]{:S(2)}) collective-permute-start(f32[80,128]{1,0:T(8,128)} %bitcast.38), channel_id=1, source_target_pairs={{0,2},{2,0},{1,4},{3,6},{4,1},{6,3},{5,8},{7,10},{8,5},{10,7},{9,1... | collective-permute-start | bytes 122888 | tf_op jit(solution)/shard_map/ppermute | solution.py:470
  3.6 0.2 collective-permute-start.1
  3.8 2.0 %prepare.1 = (f32[2400,128]{1,0:T(8,128)S(1)}, f32[400,128]{1,0:T(8,128)S(1)}, f32[80,128]{1,0:T(8,128)S(1)}, f32[240,128]{1,0:T(8,128)S(1)}, s32[96,128]{1,0:T(...) custom-call(bf16[2400,128]{1,0:T(8,128)(2,1)} %bitcast.32, ...), custom_call_target="tpu_custom_call" | custom-call | flops 1000000000 | bytes 10000000 | tf_op jit(solution)/shard_map/prepare/pallas_call | solution.py:474
  5.9 0.0 collective-permute-done.far_ref
  5.9 0.0 collective-permute-done.1.close_ref
  5.9 1.2 %sweep.1._.refs_2_ = f32[80,128]{1,0:T(8,128)S(1)} custom-call(f32[80,128]{1,0:T(8,128)S(1)} %collective-permute-done.far_ref, f32[80,128]{1,0:T(8,128)S(1)} %collective-permute-done.1.close_ref, f32[80,128]{1,0:T(8,128)S(1)} %get-tuple-element.21.refs_0_, f32[80,128]{1,0:T(8,128)S(1)} %get-tuple-element.22.refs_1_.refs_3_, ...), custom_call_target="tpu_custom_call" | custom-call | flops 716800 | bytes 1228800 | tf_op jit(solution)/shard_map/sweep/pallas_call | solution.py:529
  7.2 0.4 %collective-permute-start.2 = (f32[80,128]{1,0:T(8,128)S(1)}, f32[80,128]{1,0:T(8,128)S(1)}, u32[]{:S(2)}, u32[]{:S(2)}) collective-permute-start(f32[80,128]{1,0:T(8,128)S(1)} %sweep.1._.refs_2_), channel_id=1, source_target_pairs={{0,1},{1,0},{4,5},{5,4},{8,9},{9,8},{12,13},{13,12},{2,3},{3,2},{6... | collective-permute-start | bytes 122888 | tf_op jit(solution)/shard_map/ppermute | solution.py:455
  7.5 1.7 %collective-permute-start.3 = (f32[80,128]{1,0:T(8,128)S(1)}, f32[80,128]{1,0:T(8,128)S(1)}, u32[]{:S(2)}, u32[]{:S(2)}) collective-permute-start(f32[80,128]{1,0:T(8,128)S(1)} %sweep.1._.refs_2_), channel_id=1, source_target_pairs={{0,2},{2,0},{1,4},{3,6},{4,1},{6,3},{5,8},{7,10},{8,5},{10,7},{9,1... | collective-permute-start | bytes 122888 | tf_op jit(solution)/shard_map/ppermute | solution.py:470
  9.2 2.7 %near_wendland.1.refs_9_.refs_2_ = bf16[1280,2048]{1,0:T(8,128)(2,1)S(1)} custom-call(bf16[1024,64]{1,0:T(8,128)(2,1)S(1)} %get-tuple-element.19.left_ref, bf16[64,2048]{1,0:T(8,128)(2,1)S(1)} %get-tuple-element.20.right_ref, f32[80,128]{1,0:T(8,128)S(1)} %sweep.1._.refs_2_), custom_call_target="tpu_custom_call" | custom-call | flops 1000000000 | bytes 10000000 | tf_op jit(solution)/shard_map/near_wendland/pallas_call | solution.py:545
  12.0 0.0 collective-permute-done.2.refs_0_
  12.0 0.0 collective-permute-done.3.refs_1_
  12.0 1.3 %last_sweep.1 = (f32[80,128]{1,0:T(8,128)S(1)}, f32[24,128]{1,0:T(8,128)S(1)}) custom-call(f32[80,128]{1,0:T(8,128)S(1)} %collective-permute-done.2.refs_0_, f32[80,128]{1,0:T(8,128)S(1)} %collective-permute-done.3.refs_1_, f32[80,128]{1,0:T(8,128)S(1)} %sweep.1._.refs_2_, f32[80,128]{1,0:T(8,128)S(1)} %get-tuple-element.22.refs_1_.refs_3_, ...), custom_call_target="tpu_custom_call" | custom-call | flops 716800 | bytes 1228800 | tf_op jit(solution)/shard_map/last_sweep/pallas_call | solution.py:554
  13.3 1.3 %collective-permute-start.4 = (f32[24,128]{1,0:T(8,128)S(1)}, f32[24,128]{1,0:T(8,128)S(1)}, u32[]{:S(2)}, u32[]{:S(2)}) collective-permute-start(f32[24,128]{1,0:T(8,128)S(1)} %get-tuple-element.28.after.refs_0_), channel_id=1, source_target_pairs={{0,2},{2,0},{1,3},{3,1},{4,6},{6,4},{5,7},{7,5},{8,10},{10,8},{9,1... | collective-permute-start | bytes 36872 | tf_op jit(solution)/shard_map/ppermute | solution.py:568
  14.6 2.3 %far_wendland.1 = (bf16[768,2048]{1,0:T(8,128)(2,1)S(1)}, bf16[10240,128]{1,0:T(8,128)(2,1)S(1)}, f32[80,128]{1,0:T(8,128)}) custom-call(bf16[1024,64]{1,0:T(8,128)(2,1)S(1)} %get-tuple-element.19.left_ref, bf16[64,2048]{1,0:T(8,128)(2,1)S(1)} %get-tuple-element.20.right_ref, f32[24,128]{1,0:T(8,128)S(1)} %get-tuple-element.28.after.refs_0_, ...), custom_call_target="tpu_custom_call" | custom-call | flops 1000000000 | bytes 10000000 | tf_op jit(solution)/shard_map/far_wendland/pallas_call | solution.py:570
  16.9 0.2 collective-permute-done.4.refs_1_
  17.0 1.8 %control.1.refs_0_ = f32[12,128]{1,0:T(8,128)S(1)} custom-call(f32[24,128]{1,0:T(8,128)S(1)} %get-tuple-element.28.after.refs_0_, f32[24,128]{1,0:T(8,128)S(1)} %collective-permute-done.4.refs_1_, bf16[1280,2048]{1,0:T(8,128)(2,1)S(1)} %near_wendland.1.refs_9_.refs_2_, bf16[768,2048]{1,0:T(8,128)(2,1)S(1)} %get-tuple-element.32.refs_3_, ...), custom_call_target="tpu_custom_call" | custom-call | tf_op jit(solution)/shard_map/control/pallas_call | solution.py:582
  18.9 0.1 collective-permute-start.5
  19.0 1.2 %collective-permute-done.5.refs_1_ = f32[12,128]{1,0:T(8,128)S(1)} collective-permute-done((f32[12,128]{1,0:T(8,128)S(1)}, f32[12,128]{1,0:T(8,128)S(1)}, u32[]{:S(2)}, u32[]{:S(2)}) %collective-permute-start.5) | collective-permute-done | bytes 6176 | tf_op jit(solution)/shard_map/ppermute | solution.py:419
  20.1 0.8 %collective-permute-start.6 = (f32[12,128]{1,0:T(8,128)S(1)}, f32[12,128]{1,0:T(8,128)S(1)}, u32[]{:S(2)}, u32[]{:S(2)}) collective-permute-start(f32[12,128]{1,0:T(8,128)S(1)} %add.2.refs_0_), channel_id=1, source_target_pairs={{0,5},{1,4},{2,7},{3,6},{4,1},{5,0},{6,3},{7,2},{8,13},{9,12},{10,... | collective-permute-start | bytes 18440 | tf_op jit(solution)/shard_map/ppermute | solution.py:419
  20.9 2.3 %collective-permute-done.6.refs_1_ = f32[12,128]{1,0:T(8,128)S(1)} collective-permute-done((f32[12,128]{1,0:T(8,128)S(1)}, f32[12,128]{1,0:T(8,128)S(1)}, u32[]{:S(2)}, u32[]{:S(2)}) %collective-permute-start.6) | collective-permute-done | bytes 6176 | tf_op jit(solution)/shard_map/ppermute | solution.py:419
  23.2 2.1 %collective-permute-start.7 = (f32[12,128]{1,0:T(8,128)S(1)}, f32[12,128]{1,0:T(8,128)S(1)}, u32[]{:S(2)}, u32[]{:S(2)}) collective-permute-start(f32[12,128]{1,0:T(8,128)S(1)} %add.3.refs_0_), channel_id=1, source_target_pairs={{0,11},{1,10},{2,9},{3,8},{4,15},{5,14},{6,13},{7,12},{8,3},{9,2},... | collective-permute-start | bytes 18440 | tf_op jit(solution)/shard_map/ppermute | solution.py:419
  25.3 1.2 %collective-permute-start.8 = (f32[12,128]{1,0:T(8,128)S(1)}, f32[12,128]{1,0:T(8,128)S(1)}, u32[]{:S(2)}, u32[]{:S(2)}) collective-permute-start(f32[12,128]{1,0:T(8,128)S(1)} %add.3.refs_0_), channel_id=1, source_target_pairs={{0,9},{1,8},{2,11},{3,10},{4,13},{5,12},{6,15},{7,14},{8,1},{9,0},... | collective-permute-start | bytes 18440 | tf_op jit(solution)/shard_map/ppermute | solution.py:419
  26.5 0.6 %collective-permute-start.9 = (f32[12,128]{1,0:T(8,128)S(1)}, f32[12,128]{1,0:T(8,128)S(1)}, u32[]{:S(2)}, u32[]{:S(2)}) collective-permute-start(f32[12,128]{1,0:T(8,128)S(1)} %add.3.refs_0_), channel_id=1, source_target_pairs={{0,3},{1,2},{2,1},{3,0},{4,7},{5,6},{6,5},{7,4},{8,11},{9,10},{10,... | collective-permute-start | bytes 18440 | tf_op jit(solution)/shard_map/ppermute | solution.py:419
  27.1 1.0 %collective-permute-done.7.refs_1_ = f32[12,128]{1,0:T(8,128)S(1)} collective-permute-done((f32[12,128]{1,0:T(8,128)S(1)}, f32[12,128]{1,0:T(8,128)S(1)}, u32[]{:S(2)}, u32[]{:S(2)}) %collective-permute-start.7) | collective-permute-done | bytes 6176 | tf_op jit(solution)/shard_map/ppermute | solution.py:419
  28.1 1.2 %collective-permute-done.8.refs_2_ = f32[12,128]{1,0:T(8,128)S(1)} collective-permute-done((f32[12,128]{1,0:T(8,128)S(1)}, f32[12,128]{1,0:T(8,128)S(1)}, u32[]{:S(2)}, u32[]{:S(2)}) %collective-permute-start.8) | collective-permute-done | bytes 6176 | tf_op jit(solution)/shard_map/ppermute | solution.py:419
  29.2 0.3 %collective-permute-done.9.refs_3_ = f32[12,128]{1,0:T(8,128)S(1)} collective-permute-done((f32[12,128]{1,0:T(8,128)S(1)}, f32[12,128]{1,0:T(8,128)S(1)}, u32[]{:S(2)}, u32[]{:S(2)}) %collective-permute-start.9) | collective-permute-done | bytes 6176 | tf_op jit(solution)/shard_map/ppermute | solution.py:419
  29.6 0.6 %finish.1 = f32[3,512]{1,0:T(4,128)} custom-call(f32[12,128]{1,0:T(8,128)S(1)} %add.3.refs_0_, f32[12,128]{1,0:T(8,128)S(1)} %collective-permute-done.7.refs_1_, f32[12,128]{1,0:T(8,128)S(1)} %collective-permute-done.8.refs_2_, f32[12,128]{1,0:T(8,128)S(1)} %collective-permute-done.9.refs_3_), custom_call_target="tpu_custom_call" | custom-call | tf_op jit(solution)/shard_map/finish/pallas_call | solution.py:598
  (2 shorter events, 0.0 us)
Async XLA Ops:
  0.6 5.3 %collective-permute-start = (f32[80,128]{1,0:T(8,128)}, f32[80,128]{1,0:T(8,128)S(1)}, u32[]{:S(2)}, u32[]{:S(2)}) collective-permute-start(f32[80,128]{1,0:T(8,128)} %bitcast.38), channel_id=1, source_target_pairs={{0,2},{2,0},{1,4},{3,6},{4,1},{6,3},{5,8},{7,10},{8,5},{10,7},{9,1... | collective-permute-start | bytes 122888 | tf_op jit(solution)/shard_map/ppermute | solution.py:470
  3.6 2.3 %collective-permute-start.1 = (f32[80,128]{1,0:T(8,128)}, f32[80,128]{1,0:T(8,128)S(1)}, u32[]{:S(2)}, u32[]{:S(2)}) collective-permute-start(f32[80,128]{1,0:T(8,128)} %bitcast.39), channel_id=1, source_target_pairs={{0,1},{1,0},{4,5},{5,4},{8,9},{9,8},{12,13},{13,12},{2,3},{3,2},{6... | collective-permute-start | bytes 122888 | tf_op jit(solution)/shard_map/ppermute | solution.py:455
  7.2 4.8 %collective-permute-start.2 = (f32[80,128]{1,0:T(8,128)S(1)}, f32[80,128]{1,0:T(8,128)S(1)}, u32[]{:S(2)}, u32[]{:S(2)}) collective-permute-start(f32[80,128]{1,0:T(8,128)S(1)} %sweep.1._.refs_2_), channel_id=1, source_target_pairs={{0,1},{1,0},{4,5},{5,4},{8,9},{9,8},{12,13},{13,12},{2,3},{3,2},{6... | collective-permute-start | bytes 122888 | tf_op jit(solution)/shard_map/ppermute | solution.py:455
  7.5 4.5 %collective-permute-start.3 = (f32[80,128]{1,0:T(8,128)S(1)}, f32[80,128]{1,0:T(8,128)S(1)}, u32[]{:S(2)}, u32[]{:S(2)}) collective-permute-start(f32[80,128]{1,0:T(8,128)S(1)} %sweep.1._.refs_2_), channel_id=1, source_target_pairs={{0,2},{2,0},{1,4},{3,6},{4,1},{6,3},{5,8},{7,10},{8,5},{10,7},{9,1... | collective-permute-start | bytes 122888 | tf_op jit(solution)/shard_map/ppermute | solution.py:470
  13.3 3.8 %collective-permute-start.4 = (f32[24,128]{1,0:T(8,128)S(1)}, f32[24,128]{1,0:T(8,128)S(1)}, u32[]{:S(2)}, u32[]{:S(2)}) collective-permute-start(f32[24,128]{1,0:T(8,128)S(1)} %get-tuple-element.28.after.refs_0_), channel_id=1, source_target_pairs={{0,2},{2,0},{1,3},{3,1},{4,6},{6,4},{5,7},{7,5},{8,10},{10,8},{9,1... | collective-permute-start | bytes 36872 | tf_op jit(solution)/shard_map/ppermute | solution.py:568
  18.9 1.2 %collective-permute-start.5 = (f32[12,128]{1,0:T(8,128)S(1)}, f32[12,128]{1,0:T(8,128)S(1)}, u32[]{:S(2)}, u32[]{:S(2)}) collective-permute-start(f32[12,128]{1,0:T(8,128)S(1)} %control.1.refs_0_), channel_id=1, source_target_pairs={{0,1},{1,0},{2,3},{3,2},{4,5},{5,4},{6,7},{7,6},{8,9},{9,8},{10,11... | collective-permute-start | bytes 18440 | tf_op jit(solution)/shard_map/ppermute | solution.py:419
  20.1 3.1 %collective-permute-start.6 = (f32[12,128]{1,0:T(8,128)S(1)}, f32[12,128]{1,0:T(8,128)S(1)}, u32[]{:S(2)}, u32[]{:S(2)}) collective-permute-start(f32[12,128]{1,0:T(8,128)S(1)} %add.2.refs_0_), channel_id=1, source_target_pairs={{0,5},{1,4},{2,7},{3,6},{4,1},{5,0},{6,3},{7,2},{8,13},{9,12},{10,... | collective-permute-start | bytes 18440 | tf_op jit(solution)/shard_map/ppermute | solution.py:419
  23.2 4.9 %collective-permute-start.7 = (f32[12,128]{1,0:T(8,128)S(1)}, f32[12,128]{1,0:T(8,128)S(1)}, u32[]{:S(2)}, u32[]{:S(2)}) collective-permute-start(f32[12,128]{1,0:T(8,128)S(1)} %add.3.refs_0_), channel_id=1, source_target_pairs={{0,11},{1,10},{2,9},{3,8},{4,15},{5,14},{6,13},{7,12},{8,3},{9,2},... | collective-permute-start | bytes 18440 | tf_op jit(solution)/shard_map/ppermute | solution.py:419
  25.3 4.0 %collective-permute-start.8 = (f32[12,128]{1,0:T(8,128)S(1)}, f32[12,128]{1,0:T(8,128)S(1)}, u32[]{:S(2)}, u32[]{:S(2)}) collective-permute-start(f32[12,128]{1,0:T(8,128)S(1)} %add.3.refs_0_), channel_id=1, source_target_pairs={{0,9},{1,8},{2,11},{3,10},{4,13},{5,12},{6,15},{7,14},{8,1},{9,0},... | collective-permute-start | bytes 18440 | tf_op jit(solution)/shard_map/ppermute | solution.py:419
  26.5 3.1 %collective-permute-start.9 = (f32[12,128]{1,0:T(8,128)S(1)}, f32[12,128]{1,0:T(8,128)S(1)}, u32[]{:S(2)}, u32[]{:S(2)}) collective-permute-start(f32[12,128]{1,0:T(8,128)S(1)} %add.3.refs_0_), channel_id=1, source_target_pairs={{0,3},{1,2},{2,1},{3,0},{4,7},{5,6},{6,5},{7,4},{8,11},{9,10},{10,... | collective-permute-start | bytes 18440 | tf_op jit(solution)/shard_map/ppermute | solution.py:419

commit v27 on v24

--- a/solution.py
+++ b/solution.py
@@ -77,7 +77,6 @@
     start_ref,
     left_ref,
     right_ref,
-    off_buf,
     sens_buf,
     neigh_buf,
     weight_buf,
@@ -96,7 +95,7 @@
         (spread_in.at[:, mine], spread_buf),
         (cell_in, cell_buf),
         (base_in.at[:, mine], base_buf),
-        (off_in, off_buf),
+        (off_in, off_ref),
         (weight_in, weight_buf),
         (sens_in, sens_buf),
         (inverse_in, inverse_ref),
@@ -146,7 +145,6 @@
     right_ref[...] = distance_factors(base_buf[...], False).astype(jnp.bfloat16)
 
     copies[5].wait()
-    off_ref[...] = off_buf[...].astype(jnp.float32)
     copies[6].wait()
     copies[7].wait()
     row_node = lax.rem(lax.broadcasted_iota(jnp.int32, (per, LANES), 0), nodes)
@@ -201,12 +199,16 @@
                 table_ref[to : to + 8, :] = window_ref[
                     pl.ds(b * width + tile + shift * nodes, 8), :
                 ]
-    for half in range(0, per, 8):
-        remaining = [rhs_ref[a * per + half : a * per + half + 8, :] for a in range(5)]
-        for f in range(faces):
+    halves = range(0, per, 8)
+    remaining = [
+        [rhs_ref[a * per + half : a * per + half + 8, :] for a in range(5)] for half in halves
+    ]
+    for f in range(faces):
+        beside = []
+        for half in halves:
             lanes = lane_ref[f * per + half : f * per + half + 8, :]
             dist = step_ref[f * per + half : f * per + half + 8, :]
-            beside = [jnp.zeros((8, LANES), jnp.float32)] * 5
+            found = [jnp.zeros((8, LANES), jnp.float32)] * 5
             for d in range(2 * blocks + 1):
                 here = dist == d
                 first = half + d * nodes
@@ -217,16 +219,20 @@
                         table = table_ref[at : at + 8, :]
                     else:
                         table = window_ref[at : at + 8, :]
-                    beside[b] = jnp.where(here, take_lanes(table, lanes), beside[b])
-            for a in range(5):
-                for b in range(5):
-                    row = (f * 25 + 5 * a + b) * per + half
-                    remaining[a] = remaining[a] - off_ref[row : row + 8, :] * beside[b]
+                    found[b] = jnp.where(here, take_lanes(table, lanes), found[b])
+            beside.append(found)
+        for a in range(5):
+            for b in range(5):
+                row = (f * 25 + 5 * a + b) * per
+                block = off_ref[row : row + per, :].astype(jnp.float32)
+                for i, half in enumerate(halves):
+                    remaining[i][a] = remaining[i][a] - block[half : half + 8] * beside[i][b]
+    for i, half in enumerate(halves):
         for a in range(5):
             total = None
             for b in range(5):
                 row = (5 * a + b) * per + half
-                term = inverse_ref[row : row + 8, :] * remaining[b]
+                term = inverse_ref[row : row + 8, :] * remaining[i][b]
                 total = term if total is None else total + term
             out_ref[a * per + half : a * per + half + 8, :] = total
 
@@ -474,7 +480,7 @@
     prepared = pl.pallas_call(
         functools.partial(prepare_kernel, nodes),
         out_shape=(
-            shape((faces * 25 * per, LANES)),
+            shape((faces * 25 * per, LANES), bf16),
             shape((25 * per, LANES)),
             shape((5 * per, LANES)),
             shape((15 * per, LANES)),
@@ -490,7 +496,6 @@
         in_specs=[HBM] * 11,
         out_specs=(VMEM,) * 12,
         scratch_shapes=[
-            pltpu.VMEM((faces * 25 * per, LANES), bf16),
             pltpu.VMEM((15 * per, LANES), bf16),
             pltpu.VMEM((faces, cells), i32),
             pltpu.SMEM((nodes,), f32),

time: 30.4 us -> 30.5 us (level)
  no operation moved by 1% of the time
where the time goes in v27:
time: 30.5 us; the launch traced here: 30.3 us
  Pallas kernels  12.1 us (40%)
  starting transfers between devices  11.3 us (37%)
  waiting for transfers between devices  6.27 us (21%)
  between operations  0.71 us (2%)
    ppermute x5, waiting for transfers between devices, exchanged(): lax.ppermute(value, SUM_AXES, [(i, i ^ mask) for i in range(peers)])  6.08 us
    ppermute x2, starting transfers between devices, swaps(): return (lax.ppermute(array, SUM_AXES, pairs), close)  4.79 us
    ppermute x5, starting transfers between devices, exchanged(): lax.ppermute(value, SUM_AXES, [(i, i ^ mask) for i in range(peers)])  4.62 us
    pallas_call x1, Pallas kernels, body(): pl.pallas_call(functools.partial(wendland_kernel, 0), out_shape=near_shap...  2.73 us
    pallas_call x1, Pallas kernels, body(): pl.pallas_call(functools.partial(far_wendland_kernel, half), out_shape=(f...  2.28 us
    pallas_call x1, Pallas kernels, body(): pl.pallas_call(functools.partial(prepare_kernel, nodes), out_shape=(shape...  1.97 us
    pallas_call x1, Pallas kernels, body(): pl.pallas_call(functools.partial(control_kernel, scale), out_shape=shape(...  1.87 us
    pallas_call x1, Pallas kernels, body(): pl.pallas_call(functools.partial(last_sweep_kernel, blocks), out_shape=(s...  1.33 us
  transfers between devices with their start and end apart: 10, of which 6 were waited for; matrix products, arithmetic and copies ran while one was open for 0% of the time, Pallas kernels for 23%

profile of v27, /device:TPU:0, one launch (start us, length us, event | category | flops | bytes accessed | tf_op | source)
XLA Modules:
  0.0 30.3 jit_solution(4469843434672856628)
XLA Ops:
  0.6 3.0 %collective-permute-start = (f32[80,128]{1,0:T(8,128)}, f32[80,128]{1,0:T(8,128)S(1)}, u32[]{:S(2)}, u32[]{:S(2)}) collective-permute-start(f32[80,128]{1,0:T(8,128)} %bitcast.38), channel_id=1, source_target_pairs={{0,2},{2,0},{1,4},{3,6},{4,1},{6,3},{5,8},{7,10},{8,5},{10,7},{9,1... | collective-permute-start | bytes 122888 | tf_op jit(solution)/shard_map/ppermute | solution.py:476
  3.6 0.2 collective-permute-start.1
  3.8 2.0 %prepare.1 = (bf16[2400,128]{1,0:T(8,128)(2,1)S(1)}, f32[400,128]{1,0:T(8,128)S(1)}, f32[80,128]{1,0:T(8,128)S(1)}, f32[240,128]{1,0:T(8,128)S(1)}, s32[96,128]{...) custom-call(bf16[2400,128]{1,0:T(8,128)(2,1)} %bitcast.32, ...), custom_call_target="tpu_custom_call" | custom-call | flops 1000000000 | bytes 10000000 | tf_op jit(solution)/shard_map/prepare/pallas_call | solution.py:480
  5.8 0.0 collective-permute-done.far_ref
  5.8 0.0 collective-permute-done.1.close_ref
  5.8 1.3 %sweep.1._.refs_2_ = f32[80,128]{1,0:T(8,128)S(1)} custom-call(f32[80,128]{1,0:T(8,128)S(1)} %collective-permute-done.far_ref, f32[80,128]{1,0:T(8,128)S(1)} %collective-permute-done.1.close_ref, f32[80,128]{1,0:T(8,128)S(1)} %get-tuple-element.21.refs_0_, f32[80,128]{1,0:T(8,128)S(1)} %get-tuple-element.22.refs_1_.refs_3_, ...), custom_call_target="tpu_custom_call" | custom-call | flops 716800 | bytes 1228800 | tf_op jit(solution)/shard_map/sweep/pallas_call | solution.py:534
  7.1 0.4 %collective-permute-start.2 = (f32[80,128]{1,0:T(8,128)S(1)}, f32[80,128]{1,0:T(8,128)S(1)}, u32[]{:S(2)}, u32[]{:S(2)}) collective-permute-start(f32[80,128]{1,0:T(8,128)S(1)} %sweep.1._.refs_2_), channel_id=1, source_target_pairs={{0,1},{1,0},{4,5},{5,4},{8,9},{9,8},{12,13},{13,12},{2,3},{3,2},{6... | collective-permute-start | bytes 122888 | tf_op jit(solution)/shard_map/ppermute | solution.py:461
  7.5 1.8 %collective-permute-start.3 = (f32[80,128]{1,0:T(8,128)S(1)}, f32[80,128]{1,0:T(8,128)S(1)}, u32[]{:S(2)}, u32[]{:S(2)}) collective-permute-start(f32[80,128]{1,0:T(8,128)S(1)} %sweep.1._.refs_2_), channel_id=1, source_target_pairs={{0,2},{2,0},{1,4},{3,6},{4,1},{6,3},{5,8},{7,10},{8,5},{10,7},{9,1... | collective-permute-start | bytes 122888 | tf_op jit(solution)/shard_map/ppermute | solution.py:476
  9.3 2.7 %near_wendland.1.refs_9_.refs_2_ = bf16[1280,2048]{1,0:T(8,128)(2,1)S(1)} custom-call(bf16[1024,64]{1,0:T(8,128)(2,1)S(1)} %get-tuple-element.19.left_ref, bf16[64,2048]{1,0:T(8,128)(2,1)S(1)} %get-tuple-element.20.right_ref, f32[80,128]{1,0:T(8,128)S(1)} %sweep.1._.refs_2_), custom_call_target="tpu_custom_call" | custom-call | flops 1000000000 | bytes 10000000 | tf_op jit(solution)/shard_map/near_wendland/pallas_call | solution.py:550
  12.0 0.0 collective-permute-done.2.refs_0_
  12.0 0.0 collective-permute-done.3.refs_1_
  12.1 1.3 %last_sweep.1 = (f32[80,128]{1,0:T(8,128)S(1)}, f32[24,128]{1,0:T(8,128)S(1)}) custom-call(f32[80,128]{1,0:T(8,128)S(1)} %collective-permute-done.2.refs_0_, f32[80,128]{1,0:T(8,128)S(1)} %collective-permute-done.3.refs_1_, f32[80,128]{1,0:T(8,128)S(1)} %sweep.1._.refs_2_, f32[80,128]{1,0:T(8,128)S(1)} %get-tuple-element.22.refs_1_.refs_3_, ...), custom_call_target="tpu_custom_call" | custom-call | flops 716800 | bytes 1228800 | tf_op jit(solution)/shard_map/last_sweep/pallas_call | solution.py:559
  13.4 1.3 %collective-permute-start.4 = (f32[24,128]{1,0:T(8,128)S(1)}, f32[24,128]{1,0:T(8,128)S(1)}, u32[]{:S(2)}, u32[]{:S(2)}) collective-permute-start(f32[24,128]{1,0:T(8,128)S(1)} %get-tuple-element.28.after.refs_0_), channel_id=1, source_target_pairs={{0,2},{2,0},{1,3},{3,1},{4,6},{6,4},{5,7},{7,5},{8,10},{10,8},{9,1... | collective-permute-start | bytes 36872 | tf_op jit(solution)/shard_map/ppermute | solution.py:573
  14.7 2.3 %far_wendland.1 = (bf16[768,2048]{1,0:T(8,128)(2,1)S(1)}, bf16[10240,128]{1,0:T(8,128)(2,1)S(1)}, f32[80,128]{1,0:T(8,128)}) custom-call(bf16[1024,64]{1,0:T(8,128)(2,1)S(1)} %get-tuple-element.19.left_ref, bf16[64,2048]{1,0:T(8,128)(2,1)S(1)} %get-tuple-element.20.right_ref, f32[24,128]{1,0:T(8,128)S(1)} %get-tuple-element.28.after.refs_0_, ...), custom_call_target="tpu_custom_call" | custom-call | flops 1000000000 | bytes 10000000 | tf_op jit(solution)/shard_map/far_wendland/pallas_call | solution.py:575
  17.0 0.2 collective-permute-done.4.refs_1_
  17.1 1.9 %control.1.refs_0_ = f32[12,128]{1,0:T(8,128)S(1)} custom-call(f32[24,128]{1,0:T(8,128)S(1)} %get-tuple-element.28.after.refs_0_, f32[24,128]{1,0:T(8,128)S(1)} %collective-permute-done.4.refs_1_, bf16[1280,2048]{1,0:T(8,128)(2,1)S(1)} %near_wendland.1.refs_9_.refs_2_, bf16[768,2048]{1,0:T(8,128)(2,1)S(1)} %get-tuple-element.32.refs_3_, ...), custom_call_target="tpu_custom_call" | custom-call | tf_op jit(solution)/shard_map/control/pallas_call | solution.py:587
  19.0 0.1 collective-permute-start.5
  19.1 1.2 %collective-permute-done.5.refs_1_ = f32[12,128]{1,0:T(8,128)S(1)} collective-permute-done((f32[12,128]{1,0:T(8,128)S(1)}, f32[12,128]{1,0:T(8,128)S(1)}, u32[]{:S(2)}, u32[]{:S(2)}) %collective-permute-start.5) | collective-permute-done | bytes 6176 | tf_op jit(solution)/shard_map/ppermute | solution.py:425
  20.3 0.7 %collective-permute-start.6 = (f32[12,128]{1,0:T(8,128)S(1)}, f32[12,128]{1,0:T(8,128)S(1)}, u32[]{:S(2)}, u32[]{:S(2)}) collective-permute-start(f32[12,128]{1,0:T(8,128)S(1)} %add.2.refs_0_), channel_id=1, source_target_pairs={{0,5},{1,4},{2,7},{3,6},{4,1},{5,0},{6,3},{7,2},{8,13},{9,12},{10,... | collective-permute-start | bytes 18440 | tf_op jit(solution)/shard_map/ppermute | solution.py:425
  20.9 2.4 %collective-permute-done.6.refs_1_ = f32[12,128]{1,0:T(8,128)S(1)} collective-permute-done((f32[12,128]{1,0:T(8,128)S(1)}, f32[12,128]{1,0:T(8,128)S(1)}, u32[]{:S(2)}, u32[]{:S(2)}) %collective-permute-start.6) | collective-permute-done | bytes 6176 | tf_op jit(solution)/shard_map/ppermute | solution.py:425
  23.3 2.1 %collective-permute-start.7 = (f32[12,128]{1,0:T(8,128)S(1)}, f32[12,128]{1,0:T(8,128)S(1)}, u32[]{:S(2)}, u32[]{:S(2)}) collective-permute-start(f32[12,128]{1,0:T(8,128)S(1)} %add.3.refs_0_), channel_id=1, source_target_pairs={{0,11},{1,10},{2,9},{3,8},{4,15},{5,14},{6,13},{7,12},{8,3},{9,2},... | collective-permute-start | bytes 18440 | tf_op jit(solution)/shard_map/ppermute | solution.py:425
  25.4 1.3 %collective-permute-start.8 = (f32[12,128]{1,0:T(8,128)S(1)}, f32[12,128]{1,0:T(8,128)S(1)}, u32[]{:S(2)}, u32[]{:S(2)}) collective-permute-start(f32[12,128]{1,0:T(8,128)S(1)} %add.3.refs_0_), channel_id=1, source_target_pairs={{0,9},{1,8},{2,11},{3,10},{4,13},{5,12},{6,15},{7,14},{8,1},{9,0},... | collective-permute-start | bytes 18440 | tf_op jit(solution)/shard_map/ppermute | solution.py:425
  26.7 0.6 %collective-permute-start.9 = (f32[12,128]{1,0:T(8,128)S(1)}, f32[12,128]{1,0:T(8,128)S(1)}, u32[]{:S(2)}, u32[]{:S(2)}) collective-permute-start(f32[12,128]{1,0:T(8,128)S(1)} %add.3.refs_0_), channel_id=1, source_target_pairs={{0,3},{1,2},{2,1},{3,0},{4,7},{5,6},{6,5},{7,4},{8,11},{9,10},{10,... | collective-permute-start | bytes 18440 | tf_op jit(solution)/shard_map/ppermute | solution.py:425
  27.2 1.0 %collective-permute-done.7.refs_1_ = f32[12,128]{1,0:T(8,128)S(1)} collective-permute-done((f32[12,128]{1,0:T(8,128)S(1)}, f32[12,128]{1,0:T(8,128)S(1)}, u32[]{:S(2)}, u32[]{:S(2)}) %collective-permute-start.7) | collective-permute-done | bytes 6176 | tf_op jit(solution)/shard_map/ppermute | solution.py:425
  28.2 1.2 %collective-permute-done.8.refs_2_ = f32[12,128]{1,0:T(8,128)S(1)} collective-permute-done((f32[12,128]{1,0:T(8,128)S(1)}, f32[12,128]{1,0:T(8,128)S(1)}, u32[]{:S(2)}, u32[]{:S(2)}) %collective-permute-start.8) | collective-permute-done | bytes 6176 | tf_op jit(solution)/shard_map/ppermute | solution.py:425
  29.4 0.4 %collective-permute-done.9.refs_3_ = f32[12,128]{1,0:T(8,128)S(1)} collective-permute-done((f32[12,128]{1,0:T(8,128)S(1)}, f32[12,128]{1,0:T(8,128)S(1)}, u32[]{:S(2)}, u32[]{:S(2)}) %collective-permute-start.9) | collective-permute-done | bytes 6176 | tf_op jit(solution)/shard_map/ppermute | solution.py:425
  29.7 0.6 %finish.1 = f32[3,512]{1,0:T(4,128)} custom-call(f32[12,128]{1,0:T(8,128)S(1)} %add.3.refs_0_, f32[12,128]{1,0:T(8,128)S(1)} %collective-permute-done.7.refs_1_, f32[12,128]{1,0:T(8,128)S(1)} %collective-permute-done.8.refs_2_, f32[12,128]{1,0:T(8,128)S(1)} %collective-permute-done.9.refs_3_), custom_call_target="tpu_custom_call" | custom-call | tf_op jit(solution)/shard_map/finish/pallas_call | solution.py:603
  (2 shorter events, 0.0 us)
Async XLA Ops:
  0.6 5.2 %collective-permute-start = (f32[80,128]{1,0:T(8,128)}, f32[80,128]{1,0:T(8,128)S(1)}, u32[]{:S(2)}, u32[]{:S(2)}) collective-permute-start(f32[80,128]{1,0:T(8,128)} %bitcast.38), channel_id=1, source_target_pairs={{0,2},{2,0},{1,4},{3,6},{4,1},{6,3},{5,8},{7,10},{8,5},{10,7},{9,1... | collective-permute-start | bytes 122888 | tf_op jit(solution)/shard_map/ppermute | solution.py:476
  3.6 2.2 %collective-permute-start.1 = (f32[80,128]{1,0:T(8,128)}, f32[80,128]{1,0:T(8,128)S(1)}, u32[]{:S(2)}, u32[]{:S(2)}) collective-permute-start(f32[80,128]{1,0:T(8,128)} %bitcast.39), channel_id=1, source_target_pairs={{0,1},{1,0},{4,5},{5,4},{8,9},{9,8},{12,13},{13,12},{2,3},{3,2},{6... | collective-permute-start | bytes 122888 | tf_op jit(solution)/shard_map/ppermute | solution.py:461
  7.1 4.9 %collective-permute-start.2 = (f32[80,128]{1,0:T(8,128)S(1)}, f32[80,128]{1,0:T(8,128)S(1)}, u32[]{:S(2)}, u32[]{:S(2)}) collective-permute-start(f32[80,128]{1,0:T(8,128)S(1)} %sweep.1._.refs_2_), channel_id=1, source_target_pairs={{0,1},{1,0},{4,5},{5,4},{8,9},{9,8},{12,13},{13,12},{2,3},{3,2},{6... | collective-permute-start | bytes 122888 | tf_op jit(solution)/shard_map/ppermute | solution.py:461
  7.5 4.5 %collective-permute-start.3 = (f32[80,128]{1,0:T(8,128)S(1)}, f32[80,128]{1,0:T(8,128)S(1)}, u32[]{:S(2)}, u32[]{:S(2)}) collective-permute-start(f32[80,128]{1,0:T(8,128)S(1)} %sweep.1._.refs_2_), channel_id=1, source_target_pairs={{0,2},{2,0},{1,4},{3,6},{4,1},{6,3},{5,8},{7,10},{8,5},{10,7},{9,1... | collective-permute-start | bytes 122888 | tf_op jit(solution)/shard_map/ppermute | solution.py:476
  13.4 3.8 %collective-permute-start.4 = (f32[24,128]{1,0:T(8,128)S(1)}, f32[24,128]{1,0:T(8,128)S(1)}, u32[]{:S(2)}, u32[]{:S(2)}) collective-permute-start(f32[24,128]{1,0:T(8,128)S(1)} %get-tuple-element.28.after.refs_0_), channel_id=1, source_target_pairs={{0,2},{2,0},{1,3},{3,1},{4,6},{6,4},{5,7},{7,5},{8,10},{10,8},{9,1... | collective-permute-start | bytes 36872 | tf_op jit(solution)/shard_map/ppermute | solution.py:573
  19.0 1.2 %collective-permute-start.5 = (f32[12,128]{1,0:T(8,128)S(1)}, f32[12,128]{1,0:T(8,128)S(1)}, u32[]{:S(2)}, u32[]{:S(2)}) collective-permute-start(f32[12,128]{1,0:T(8,128)S(1)} %control.1.refs_0_), channel_id=1, source_target_pairs={{0,1},{1,0},{2,3},{3,2},{4,5},{5,4},{6,7},{7,6},{8,9},{9,8},{10,11... | collective-permute-start | bytes 18440 | tf_op jit(solution)/shard_map/ppermute | solution.py:425
  20.3 3.1 %collective-permute-start.6 = (f32[12,128]{1,0:T(8,128)S(1)}, f32[12,128]{1,0:T(8,128)S(1)}, u32[]{:S(2)}, u32[]{:S(2)}) collective-permute-start(f32[12,128]{1,0:T(8,128)S(1)} %add.2.refs_0_), channel_id=1, source_target_pairs={{0,5},{1,4},{2,7},{3,6},{4,1},{5,0},{6,3},{7,2},{8,13},{9,12},{10,... | collective-permute-start | bytes 18440 | tf_op jit(solution)/shard_map/ppermute | solution.py:425
  23.3 4.9 %collective-permute-start.7 = (f32[12,128]{1,0:T(8,128)S(1)}, f32[12,128]{1,0:T(8,128)S(1)}, u32[]{:S(2)}, u32[]{:S(2)}) collective-permute-start(f32[12,128]{1,0:T(8,128)S(1)} %add.3.refs_0_), channel_id=1, source_target_pairs={{0,11},{1,10},{2,9},{3,8},{4,15},{5,14},{6,13},{7,12},{8,3},{9,2},... | collective-permute-start | bytes 18440 | tf_op jit(solution)/shard_map/ppermute | solution.py:425
  25.4 4.0 %collective-permute-start.8 = (f32[12,128]{1,0:T(8,128)S(1)}, f32[12,128]{1,0:T(8,128)S(1)}, u32[]{:S(2)}, u32[]{:S(2)}) collective-permute-start(f32[12,128]{1,0:T(8,128)S(1)} %add.3.refs_0_), channel_id=1, source_target_pairs={{0,9},{1,8},{2,11},{3,10},{4,13},{5,12},{6,15},{7,14},{8,1},{9,0},... | collective-permute-start | bytes 18440 | tf_op jit(solution)/shard_map/ppermute | solution.py:425
  26.7 3.1 %collective-permute-start.9 = (f32[12,128]{1,0:T(8,128)S(1)}, f32[12,128]{1,0:T(8,128)S(1)}, u32[]{:S(2)}, u32[]{:S(2)}) collective-permute-start(f32[12,128]{1,0:T(8,128)S(1)} %add.3.refs_0_), channel_id=1, source_target_pairs={{0,3},{1,2},{2,1},{3,0},{4,7},{5,6},{6,5},{7,4},{8,11},{9,10},{10,... | collective-permute-start | bytes 18440 | tf_op jit(solution)/shard_map/ppermute | solution.py:425

commit v28 on v24

--- a/solution.py
+++ b/solution.py
@@ -403,8 +403,8 @@
     near = [cores >> 1 >> i for i in range(cores.bit_length() - 1)]
     node_bits = [cores << i for i in range(nodes.bit_length() - 1)]
     line_bits = [cores * nodes << i for i in range(lines.bit_length() - 1)]
-    bits = line_bits[1:2] + node_bits[:1] + line_bits[2:] + node_bits[1:]
-    rounds = [[bit] for bit in near] + [[bit | (cores - 1)] for bit in line_bits[:1]]
+    bits = line_bits[:1] + node_bits[:1] + line_bits[2:] + node_bits[1:]
+    rounds = [[bit] for bit in near] + [[bit | (cores - 1)] for bit in line_bits[1:2]]
     for first in range(0, len(bits), 2):
         masks = bits[first : first + 2]
         if len(masks) == 2:

time: 30.4 us -> 30.4 us (level)
  no operation moved by 1% of the time
where the time goes in v28:
time: 30.4 us; the launch traced here: 30.2 us
  Pallas kernels  12.1 us (40%)
  starting transfers between devices  11.3 us (37%)
  waiting for transfers between devices  6.2 us (20%)
  between operations  0.72 us (2%)
    ppermute x5, waiting for transfers between devices, exchanged(): lax.ppermute(value, SUM_AXES, [(i, i ^ mask) for i in range(peers)])  6.01 us
    ppermute x2, starting transfers between devices, swaps(): return (lax.ppermute(array, SUM_AXES, pairs), close)  4.7 us
    ppermute x5, starting transfers between devices, exchanged(): lax.ppermute(value, SUM_AXES, [(i, i ^ mask) for i in range(peers)])  4.68 us
    pallas_call x1, Pallas kernels, body(): pl.pallas_call(functools.partial(wendland_kernel, 0), out_shape=near_shap...  2.73 us
    pallas_call x1, Pallas kernels, body(): pl.pallas_call(functools.partial(far_wendland_kernel, half), out_shape=(f...  2.28 us
    pallas_call x1, Pallas kernels, body(): pl.pallas_call(functools.partial(prepare_kernel, nodes), out_shape=(shape...  2.05 us
    pallas_call x1, Pallas kernels, body(): pl.pallas_call(functools.partial(control_kernel, scale), out_shape=shape(...  1.88 us
    ppermute x1, starting transfers between devices, body(): all_sens.append(lax.ppermute(part_sens, 'nodes', ring))  1.3 us
  transfers between devices with their start and end apart: 10, of which 6 were waited for; matrix products, arithmetic and copies ran while one was open for 0% of the time, Pallas kernels for 23%

profile of v28, /device:TPU:0, one launch (start us, length us, event | category | flops | bytes accessed | tf_op | source)
XLA Modules:
  0.0 30.2 jit_solution(10328722230532319775)
XLA Ops:
  0.6 3.0 %collective-permute-start = (f32[80,128]{1,0:T(8,128)}, f32[80,128]{1,0:T(8,128)S(1)}, u32[]{:S(2)}, u32[]{:S(2)}) collective-permute-start(f32[80,128]{1,0:T(8,128)} %bitcast.38), channel_id=1, source_target_pairs={{0,2},{2,0},{1,4},{3,6},{4,1},{6,3},{5,8},{7,10},{8,5},{10,7},{9,1... | collective-permute-start | bytes 122888 | tf_op jit(solution)/shard_map/ppermute | solution.py:470
  3.6 0.2 collective-permute-start.1
  3.8 2.0 %prepare.1 = (f32[2400,128]{1,0:T(8,128)S(1)}, f32[400,128]{1,0:T(8,128)S(1)}, f32[80,128]{1,0:T(8,128)S(1)}, f32[240,128]{1,0:T(8,128)S(1)}, s32[96,128]{1,0:T(...) custom-call(bf16[2400,128]{1,0:T(8,128)(2,1)} %bitcast.32, ...), custom_call_target="tpu_custom_call" | custom-call | flops 1000000000 | bytes 10000000 | tf_op jit(solution)/shard_map/prepare/pallas_call | solution.py:474
  5.9 0.0 collective-permute-done.far_ref
  5.9 0.0 collective-permute-done.1.close_ref
  5.9 1.2 %sweep.1._.refs_2_ = f32[80,128]{1,0:T(8,128)S(1)} custom-call(f32[80,128]{1,0:T(8,128)S(1)} %collective-permute-done.far_ref, f32[80,128]{1,0:T(8,128)S(1)} %collective-permute-done.1.close_ref, f32[80,128]{1,0:T(8,128)S(1)} %get-tuple-element.21.refs_0_, f32[80,128]{1,0:T(8,128)S(1)} %get-tuple-element.22.refs_1_.refs_3_, ...), custom_call_target="tpu_custom_call" | custom-call | flops 716800 | bytes 1228800 | tf_op jit(solution)/shard_map/sweep/pallas_call | solution.py:529
  7.2 0.4 %collective-permute-start.2 = (f32[80,128]{1,0:T(8,128)S(1)}, f32[80,128]{1,0:T(8,128)S(1)}, u32[]{:S(2)}, u32[]{:S(2)}) collective-permute-start(f32[80,128]{1,0:T(8,128)S(1)} %sweep.1._.refs_2_), channel_id=1, source_target_pairs={{0,1},{1,0},{4,5},{5,4},{8,9},{9,8},{12,13},{13,12},{2,3},{3,2},{6... | collective-permute-start | bytes 122888 | tf_op jit(solution)/shard_map/ppermute | solution.py:455
  7.5 1.7 %collective-permute-start.3 = (f32[80,128]{1,0:T(8,128)S(1)}, f32[80,128]{1,0:T(8,128)S(1)}, u32[]{:S(2)}, u32[]{:S(2)}) collective-permute-start(f32[80,128]{1,0:T(8,128)S(1)} %sweep.1._.refs_2_), channel_id=1, source_target_pairs={{0,2},{2,0},{1,4},{3,6},{4,1},{6,3},{5,8},{7,10},{8,5},{10,7},{9,1... | collective-permute-start | bytes 122888 | tf_op jit(solution)/shard_map/ppermute | solution.py:470
  9.2 2.7 %near_wendland.1.refs_9_.refs_2_ = bf16[1280,2048]{1,0:T(8,128)(2,1)S(1)} custom-call(bf16[1024,64]{1,0:T(8,128)(2,1)S(1)} %get-tuple-element.19.left_ref, bf16[64,2048]{1,0:T(8,128)(2,1)S(1)} %get-tuple-element.20.right_ref, f32[80,128]{1,0:T(8,128)S(1)} %sweep.1._.refs_2_), custom_call_target="tpu_custom_call" | custom-call | flops 1000000000 | bytes 10000000 | tf_op jit(solution)/shard_map/near_wendland/pallas_call | solution.py:545
  12.0 0.0 collective-permute-done.2.refs_0_
  12.0 0.0 collective-permute-done.3.refs_1_
  12.0 1.3 %last_sweep.1 = (f32[80,128]{1,0:T(8,128)S(1)}, f32[24,128]{1,0:T(8,128)S(1)}) custom-call(f32[80,128]{1,0:T(8,128)S(1)} %collective-permute-done.2.refs_0_, f32[80,128]{1,0:T(8,128)S(1)} %collective-permute-done.3.refs_1_, f32[80,128]{1,0:T(8,128)S(1)} %sweep.1._.refs_2_, f32[80,128]{1,0:T(8,128)S(1)} %get-tuple-element.22.refs_1_.refs_3_, ...), custom_call_target="tpu_custom_call" | custom-call | flops 716800 | bytes 1228800 | tf_op jit(solution)/shard_map/last_sweep/pallas_call | solution.py:554
  13.3 1.3 %collective-permute-start.4 = (f32[24,128]{1,0:T(8,128)S(1)}, f32[24,128]{1,0:T(8,128)S(1)}, u32[]{:S(2)}, u32[]{:S(2)}) collective-permute-start(f32[24,128]{1,0:T(8,128)S(1)} %get-tuple-element.28.after.refs_0_), channel_id=1, source_target_pairs={{0,2},{2,0},{1,3},{3,1},{4,6},{6,4},{5,7},{7,5},{8,10},{10,8},{9,1... | collective-permute-start | bytes 36872 | tf_op jit(solution)/shard_map/ppermute | solution.py:568
  14.6 2.3 %far_wendland.1 = (bf16[768,2048]{1,0:T(8,128)(2,1)S(1)}, bf16[10240,128]{1,0:T(8,128)(2,1)S(1)}, f32[80,128]{1,0:T(8,128)}) custom-call(bf16[1024,64]{1,0:T(8,128)(2,1)S(1)} %get-tuple-element.19.left_ref, bf16[64,2048]{1,0:T(8,128)(2,1)S(1)} %get-tuple-element.20.right_ref, f32[24,128]{1,0:T(8,128)S(1)} %get-tuple-element.28.after.refs_0_, ...), custom_call_target="tpu_custom_call" | custom-call | flops 1000000000 | bytes 10000000 | tf_op jit(solution)/shard_map/far_wendland/pallas_call | solution.py:570
  16.9 0.2 collective-permute-done.4.refs_1_
  17.0 1.9 %control.1.refs_0_ = f32[12,128]{1,0:T(8,128)S(1)} custom-call(f32[24,128]{1,0:T(8,128)S(1)} %get-tuple-element.28.after.refs_0_, f32[24,128]{1,0:T(8,128)S(1)} %collective-permute-done.4.refs_1_, bf16[1280,2048]{1,0:T(8,128)(2,1)S(1)} %near_wendland.1.refs_9_.refs_2_, bf16[768,2048]{1,0:T(8,128)(2,1)S(1)} %get-tuple-element.32.refs_3_, ...), custom_call_target="tpu_custom_call" | custom-call | tf_op jit(solution)/shard_map/control/pallas_call | solution.py:582
  18.9 0.1 collective-permute-start.5
  19.0 1.2 %collective-permute-done.5.refs_1_ = f32[12,128]{1,0:T(8,128)S(1)} collective-permute-done((f32[12,128]{1,0:T(8,128)S(1)}, f32[12,128]{1,0:T(8,128)S(1)}, u32[]{:S(2)}, u32[]{:S(2)}) %collective-permute-start.5) | collective-permute-done | bytes 6176 | tf_op jit(solution)/shard_map/ppermute | solution.py:419
  20.2 1.6 %collective-permute-start.6 = (f32[12,128]{1,0:T(8,128)S(1)}, f32[12,128]{1,0:T(8,128)S(1)}, u32[]{:S(2)}, u32[]{:S(2)}) collective-permute-start(f32[12,128]{1,0:T(8,128)S(1)} %add.2.refs_0_), channel_id=1, source_target_pairs={{0,9},{1,8},{2,11},{3,10},{4,13},{5,12},{6,15},{7,14},{8,1},{9,0},... | collective-permute-start | bytes 18440 | tf_op jit(solution)/shard_map/ppermute | solution.py:419
  21.8 2.3 %collective-permute-done.6.refs_1_ = f32[12,128]{1,0:T(8,128)S(1)} collective-permute-done((f32[12,128]{1,0:T(8,128)S(1)}, f32[12,128]{1,0:T(8,128)S(1)}, u32[]{:S(2)}, u32[]{:S(2)}) %collective-permute-start.6) | collective-permute-done | bytes 6176 | tf_op jit(solution)/shard_map/ppermute | solution.py:419
  24.1 1.3 %collective-permute-start.7 = (f32[12,128]{1,0:T(8,128)S(1)}, f32[12,128]{1,0:T(8,128)S(1)}, u32[]{:S(2)}, u32[]{:S(2)}) collective-permute-start(f32[12,128]{1,0:T(8,128)S(1)} %add.3.refs_0_), channel_id=1, source_target_pairs={{0,7},{1,6},{2,5},{3,4},{4,3},{5,2},{6,1},{7,0},{8,15},{9,14},{10,... | collective-permute-start | bytes 18440 | tf_op jit(solution)/shard_map/ppermute | solution.py:419
  25.4 1.2 %collective-permute-start.8 = (f32[12,128]{1,0:T(8,128)S(1)}, f32[12,128]{1,0:T(8,128)S(1)}, u32[]{:S(2)}, u32[]{:S(2)}) collective-permute-start(f32[12,128]{1,0:T(8,128)S(1)} %add.3.refs_0_), channel_id=1, source_target_pairs={{0,5},{1,4},{2,7},{3,6},{4,1},{5,0},{6,3},{7,2},{8,13},{9,12},{10,... | collective-permute-start | bytes 18440 | tf_op jit(solution)/shard_map/ppermute | solution.py:419
  26.6 0.6 %collective-permute-start.9 = (f32[12,128]{1,0:T(8,128)S(1)}, f32[12,128]{1,0:T(8,128)S(1)}, u32[]{:S(2)}, u32[]{:S(2)}) collective-permute-start(f32[12,128]{1,0:T(8,128)S(1)} %add.3.refs_0_), channel_id=1, source_target_pairs={{0,3},{1,2},{2,1},{3,0},{4,7},{5,6},{6,5},{7,4},{8,11},{9,10},{10,... | collective-permute-start | bytes 18440 | tf_op jit(solution)/shard_map/ppermute | solution.py:419
  27.1 1.0 %collective-permute-done.7.refs_1_ = f32[12,128]{1,0:T(8,128)S(1)} collective-permute-done((f32[12,128]{1,0:T(8,128)S(1)}, f32[12,128]{1,0:T(8,128)S(1)}, u32[]{:S(2)}, u32[]{:S(2)}) %collective-permute-start.7) | collective-permute-done | bytes 6176 | tf_op jit(solution)/shard_map/ppermute | solution.py:419
  28.1 0.4 %collective-permute-done.8.refs_2_ = f32[12,128]{1,0:T(8,128)S(1)} collective-permute-done((f32[12,128]{1,0:T(8,128)S(1)}, f32[12,128]{1,0:T(8,128)S(1)}, u32[]{:S(2)}, u32[]{:S(2)}) %collective-permute-start.8) | collective-permute-done | bytes 6176 | tf_op jit(solution)/shard_map/ppermute | solution.py:419
  28.5 1.2 %collective-permute-done.9.refs_3_ = f32[12,128]{1,0:T(8,128)S(1)} collective-permute-done((f32[12,128]{1,0:T(8,128)S(1)}, f32[12,128]{1,0:T(8,128)S(1)}, u32[]{:S(2)}, u32[]{:S(2)}) %collective-permute-start.9) | collective-permute-done | bytes 6176 | tf_op jit(solution)/shard_map/ppermute | solution.py:419
  29.6 0.6 %finish.1 = f32[3,512]{1,0:T(4,128)} custom-call(f32[12,128]{1,0:T(8,128)S(1)} %add.3.refs_0_, f32[12,128]{1,0:T(8,128)S(1)} %collective-permute-done.7.refs_1_, f32[12,128]{1,0:T(8,128)S(1)} %collective-permute-done.8.refs_2_, f32[12,128]{1,0:T(8,128)S(1)} %collective-permute-done.9.refs_3_), custom_call_target="tpu_custom_call" | custom-call | tf_op jit(solution)/shard_map/finish/pallas_call | solution.py:598
  (2 shorter events, 0.0 us)
Async XLA Ops:
  0.6 5.3 %collective-permute-start = (f32[80,128]{1,0:T(8,128)}, f32[80,128]{1,0:T(8,128)S(1)}, u32[]{:S(2)}, u32[]{:S(2)}) collective-permute-start(f32[80,128]{1,0:T(8,128)} %bitcast.38), channel_id=1, source_target_pairs={{0,2},{2,0},{1,4},{3,6},{4,1},{6,3},{5,8},{7,10},{8,5},{10,7},{9,1... | collective-permute-start | bytes 122888 | tf_op jit(solution)/shard_map/ppermute | solution.py:470
  3.6 2.3 %collective-permute-start.1 = (f32[80,128]{1,0:T(8,128)}, f32[80,128]{1,0:T(8,128)S(1)}, u32[]{:S(2)}, u32[]{:S(2)}) collective-permute-start(f32[80,128]{1,0:T(8,128)} %bitcast.39), channel_id=1, source_target_pairs={{0,1},{1,0},{4,5},{5,4},{8,9},{9,8},{12,13},{13,12},{2,3},{3,2},{6... | collective-permute-start | bytes 122888 | tf_op jit(solution)/shard_map/ppermute | solution.py:455
  7.2 4.8 %collective-permute-start.2 = (f32[80,128]{1,0:T(8,128)S(1)}, f32[80,128]{1,0:T(8,128)S(1)}, u32[]{:S(2)}, u32[]{:S(2)}) collective-permute-start(f32[80,128]{1,0:T(8,128)S(1)} %sweep.1._.refs_2_), channel_id=1, source_target_pairs={{0,1},{1,0},{4,5},{5,4},{8,9},{9,8},{12,13},{13,12},{2,3},{3,2},{6... | collective-permute-start | bytes 122888 | tf_op jit(solution)/shard_map/ppermute | solution.py:455
  7.5 4.5 %collective-permute-start.3 = (f32[80,128]{1,0:T(8,128)S(1)}, f32[80,128]{1,0:T(8,128)S(1)}, u32[]{:S(2)}, u32[]{:S(2)}) collective-permute-start(f32[80,128]{1,0:T(8,128)S(1)} %sweep.1._.refs_2_), channel_id=1, source_target_pairs={{0,2},{2,0},{1,4},{3,6},{4,1},{6,3},{5,8},{7,10},{8,5},{10,7},{9,1... | collective-permute-start | bytes 122888 | tf_op jit(solution)/shard_map/ppermute | solution.py:470
  13.3 3.8 %collective-permute-start.4 = (f32[24,128]{1,0:T(8,128)S(1)}, f32[24,128]{1,0:T(8,128)S(1)}, u32[]{:S(2)}, u32[]{:S(2)}) collective-permute-start(f32[24,128]{1,0:T(8,128)S(1)} %get-tuple-element.28.after.refs_0_), channel_id=1, source_target_pairs={{0,2},{2,0},{1,3},{3,1},{4,6},{6,4},{5,7},{7,5},{8,10},{10,8},{9,1... | collective-permute-start | bytes 36872 | tf_op jit(solution)/shard_map/ppermute | solution.py:568
  18.9 1.2 %collective-permute-start.5 = (f32[12,128]{1,0:T(8,128)S(1)}, f32[12,128]{1,0:T(8,128)S(1)}, u32[]{:S(2)}, u32[]{:S(2)}) collective-permute-start(f32[12,128]{1,0:T(8,128)S(1)} %control.1.refs_0_), channel_id=1, source_target_pairs={{0,1},{1,0},{2,3},{3,2},{4,5},{5,4},{6,7},{7,6},{8,9},{9,8},{10,11... | collective-permute-start | bytes 18440 | tf_op jit(solution)/shard_map/ppermute | solution.py:419
  20.2 4.0 %collective-permute-start.6 = (f32[12,128]{1,0:T(8,128)S(1)}, f32[12,128]{1,0:T(8,128)S(1)}, u32[]{:S(2)}, u32[]{:S(2)}) collective-permute-start(f32[12,128]{1,0:T(8,128)S(1)} %add.2.refs_0_), channel_id=1, source_target_pairs={{0,9},{1,8},{2,11},{3,10},{4,13},{5,12},{6,15},{7,14},{8,1},{9,0},... | collective-permute-start | bytes 18440 | tf_op jit(solution)/shard_map/ppermute | solution.py:419
  24.1 4.0 %collective-permute-start.7 = (f32[12,128]{1,0:T(8,128)S(1)}, f32[12,128]{1,0:T(8,128)S(1)}, u32[]{:S(2)}, u32[]{:S(2)}) collective-permute-start(f32[12,128]{1,0:T(8,128)S(1)} %add.3.refs_0_), channel_id=1, source_target_pairs={{0,7},{1,6},{2,5},{3,4},{4,3},{5,2},{6,1},{7,0},{8,15},{9,14},{10,... | collective-permute-start | bytes 18440 | tf_op jit(solution)/shard_map/ppermute | solution.py:419
  25.4 3.1 %collective-permute-start.8 = (f32[12,128]{1,0:T(8,128)S(1)}, f32[12,128]{1,0:T(8,128)S(1)}, u32[]{:S(2)}, u32[]{:S(2)}) collective-permute-start(f32[12,128]{1,0:T(8,128)S(1)} %add.3.refs_0_), channel_id=1, source_target_pairs={{0,5},{1,4},{2,7},{3,6},{4,1},{5,0},{6,3},{7,2},{8,13},{9,12},{10,... | collective-permute-start | bytes 18440 | tf_op jit(solution)/shard_map/ppermute | solution.py:419
  26.6 3.1 %collective-permute-start.9 = (f32[12,128]{1,0:T(8,128)S(1)}, f32[12,128]{1,0:T(8,128)S(1)}, u32[]{:S(2)}, u32[]{:S(2)}) collective-permute-start(f32[12,128]{1,0:T(8,128)S(1)} %add.3.refs_0_), channel_id=1, source_target_pairs={{0,3},{1,2},{2,1},{3,0},{4,7},{5,6},{6,5},{7,4},{8,11},{9,10},{10,... | collective-permute-start | bytes 18440 | tf_op jit(solution)/shard_map/ppermute | solution.py:419

commit v29 on v24

--- a/solution.py
+++ b/solution.py
@@ -289,7 +289,7 @@
 
 def wendland_kernel(first_cell, left_ref, right_ref, _, kernel_ref):
     cells, owned = kernel_ref.shape[0] // 2, kernel_ref.shape[1]
-    tile, wide = min(128, cells), min(256, owned)
+    tile, wide = min(128, cells), min(512, owned)
 
     def squares(row, lane):
         left = left_ref[first_cell + row : first_cell + row + tile, :]

time: 30.4 us -> 30.4 us (level)
  transfers between devices with their start and end apart: 10 -> 10, of which waited for: 6 -> 6; matrix products, arithmetic and copies ran while one was open for 0% -> 0% of each run, Pallas kernels for 23% -> 24%
where the time goes in v29:
time: 30.4 us; the launch traced here: 30.2 us
  Pallas kernels  12.3 us (40%)
  starting transfers between devices  11.1 us (37%)
  waiting for transfers between devices  6.2 us (20%)
  between operations  0.72 us (2%)
    ppermute x5, waiting for transfers between devices, exchanged(): lax.ppermute(value, SUM_AXES, [(i, i ^ mask) for i in range(peers)])  5.79 us
    ppermute x2, starting transfers between devices, swaps(): return (lax.ppermute(array, SUM_AXES, pairs), close)  4.7 us
    ppermute x5, starting transfers between devices, exchanged(): lax.ppermute(value, SUM_AXES, [(i, i ^ mask) for i in range(peers)])  4.69 us
    pallas_call x1, Pallas kernels, body(): pl.pallas_call(functools.partial(wendland_kernel, 0), out_shape=near_shap...  2.94 us
    pallas_call x1, Pallas kernels, body(): pl.pallas_call(functools.partial(far_wendland_kernel, half), out_shape=(f...  2.26 us
    pallas_call x1, Pallas kernels, body(): pl.pallas_call(functools.partial(prepare_kernel, nodes), out_shape=(shape...  2.05 us
    pallas_call x1, Pallas kernels, body(): pl.pallas_call(functools.partial(control_kernel, scale), out_shape=shape(...  1.88 us
    pallas_call x1, Pallas kernels, body(): pl.pallas_call(functools.partial(last_sweep_kernel, blocks), out_shape=(s...  1.27 us
  transfers between devices with their start and end apart: 10, of which 6 were waited for; matrix products, arithmetic and copies ran while one was open for 0% of the time, Pallas kernels for 24%

profile of v29, /device:TPU:0, one launch (start us, length us, event | category | flops | bytes accessed | tf_op | source)
XLA Modules:
  0.0 30.2 jit_solution(12020187519874941544)
XLA Ops:
  0.6 3.0 %collective-permute-start = (f32[80,128]{1,0:T(8,128)}, f32[80,128]{1,0:T(8,128)S(1)}, u32[]{:S(2)}, u32[]{:S(2)}) collective-permute-start(f32[80,128]{1,0:T(8,128)} %bitcast.38), channel_id=1, source_target_pairs={{0,2},{2,0},{1,4},{3,6},{4,1},{6,3},{5,8},{7,10},{8,5},{10,7},{9,1... | collective-permute-start | bytes 122888 | tf_op jit(solution)/shard_map/ppermute | solution.py:470
  3.6 0.2 collective-permute-start.1
  3.8 2.0 %prepare.1 = (f32[2400,128]{1,0:T(8,128)S(1)}, f32[400,128]{1,0:T(8,128)S(1)}, f32[80,128]{1,0:T(8,128)S(1)}, f32[240,128]{1,0:T(8,128)S(1)}, s32[96,128]{1,0:T(...) custom-call(bf16[2400,128]{1,0:T(8,128)(2,1)} %bitcast.32, ...), custom_call_target="tpu_custom_call" | custom-call | flops 1000000000 | bytes 10000000 | tf_op jit(solution)/shard_map/prepare/pallas_call | solution.py:474
  5.9 0.0 collective-permute-done.far_ref
  5.9 0.0 collective-permute-done.1.close_ref
  5.9 1.2 %sweep.1._.refs_2_ = f32[80,128]{1,0:T(8,128)S(1)} custom-call(f32[80,128]{1,0:T(8,128)S(1)} %collective-permute-done.far_ref, f32[80,128]{1,0:T(8,128)S(1)} %collective-permute-done.1.close_ref, f32[80,128]{1,0:T(8,128)S(1)} %get-tuple-element.21.refs_0_, f32[80,128]{1,0:T(8,128)S(1)} %get-tuple-element.22.refs_1_.refs_3_, ...), custom_call_target="tpu_custom_call" | custom-call | flops 716800 | bytes 1228800 | tf_op jit(solution)/shard_map/sweep/pallas_call | solution.py:529
  7.2 0.4 %collective-permute-start.2 = (f32[80,128]{1,0:T(8,128)S(1)}, f32[80,128]{1,0:T(8,128)S(1)}, u32[]{:S(2)}, u32[]{:S(2)}) collective-permute-start(f32[80,128]{1,0:T(8,128)S(1)} %sweep.1._.refs_2_), channel_id=1, source_target_pairs={{0,1},{1,0},{4,5},{5,4},{8,9},{9,8},{12,13},{13,12},{2,3},{3,2},{6... | collective-permute-start | bytes 122888 | tf_op jit(solution)/shard_map/ppermute | solution.py:455
  7.5 1.7 %collective-permute-start.3 = (f32[80,128]{1,0:T(8,128)S(1)}, f32[80,128]{1,0:T(8,128)S(1)}, u32[]{:S(2)}, u32[]{:S(2)}) collective-permute-start(f32[80,128]{1,0:T(8,128)S(1)} %sweep.1._.refs_2_), channel_id=1, source_target_pairs={{0,2},{2,0},{1,4},{3,6},{4,1},{6,3},{5,8},{7,10},{8,5},{10,7},{9,1... | collective-permute-start | bytes 122888 | tf_op jit(solution)/shard_map/ppermute | solution.py:470
  9.2 2.9 %near_wendland.1.refs_9_.refs_2_ = bf16[1280,2048]{1,0:T(8,128)(2,1)S(1)} custom-call(bf16[1024,64]{1,0:T(8,128)(2,1)S(1)} %get-tuple-element.19.left_ref, bf16[64,2048]{1,0:T(8,128)(2,1)S(1)} %get-tuple-element.20.right_ref, f32[80,128]{1,0:T(8,128)S(1)} %sweep.1._.refs_2_), custom_call_target="tpu_custom_call" | custom-call | flops 1000000000 | bytes 10000000 | tf_op jit(solution)/shard_map/near_wendland/pallas_call | solution.py:545
  12.2 0.0 collective-permute-done.2.refs_0_
  12.2 0.0 collective-permute-done.3.refs_1_
  12.2 1.3 %last_sweep.1 = (f32[80,128]{1,0:T(8,128)S(1)}, f32[24,128]{1,0:T(8,128)S(1)}) custom-call(f32[80,128]{1,0:T(8,128)S(1)} %collective-permute-done.2.refs_0_, f32[80,128]{1,0:T(8,128)S(1)} %collective-permute-done.3.refs_1_, f32[80,128]{1,0:T(8,128)S(1)} %sweep.1._.refs_2_, f32[80,128]{1,0:T(8,128)S(1)} %get-tuple-element.22.refs_1_.refs_3_, ...), custom_call_target="tpu_custom_call" | custom-call | flops 716800 | bytes 1228800 | tf_op jit(solution)/shard_map/last_sweep/pallas_call | solution.py:554
  13.5 1.1 %collective-permute-start.4 = (f32[24,128]{1,0:T(8,128)S(1)}, f32[24,128]{1,0:T(8,128)S(1)}, u32[]{:S(2)}, u32[]{:S(2)}) collective-permute-start(f32[24,128]{1,0:T(8,128)S(1)} %get-tuple-element.28.after.refs_0_), channel_id=1, source_target_pairs={{0,2},{2,0},{1,3},{3,1},{4,6},{6,4},{5,7},{7,5},{8,10},{10,8},{9,1... | collective-permute-start | bytes 36872 | tf_op jit(solution)/shard_map/ppermute | solution.py:568
  14.6 2.3 %far_wendland.1 = (bf16[768,2048]{1,0:T(8,128)(2,1)S(1)}, bf16[10240,128]{1,0:T(8,128)(2,1)S(1)}, f32[80,128]{1,0:T(8,128)}) custom-call(bf16[1024,64]{1,0:T(8,128)(2,1)S(1)} %get-tuple-element.19.left_ref, bf16[64,2048]{1,0:T(8,128)(2,1)S(1)} %get-tuple-element.20.right_ref, f32[24,128]{1,0:T(8,128)S(1)} %get-tuple-element.28.after.refs_0_, ...), custom_call_target="tpu_custom_call" | custom-call | flops 1000000000 | bytes 10000000 | tf_op jit(solution)/shard_map/far_wendland/pallas_call | solution.py:570
  16.8 0.4 %collective-permute-done.4.refs_1_ = f32[24,128]{1,0:T(8,128)S(1)} collective-permute-done((f32[24,128]{1,0:T(8,128)S(1)}, f32[24,128]{1,0:T(8,128)S(1)}, u32[]{:S(2)}, u32[]{:S(2)}) %collective-permute-start.4) | collective-permute-done | bytes 12320 | tf_op jit(solution)/shard_map/ppermute | solution.py:568
  17.2 1.9 %control.1.refs_0_ = f32[12,128]{1,0:T(8,128)S(1)} custom-call(f32[24,128]{1,0:T(8,128)S(1)} %get-tuple-element.28.after.refs_0_, f32[24,128]{1,0:T(8,128)S(1)} %collective-permute-done.4.refs_1_, bf16[1280,2048]{1,0:T(8,128)(2,1)S(1)} %near_wendland.1.refs_9_.refs_2_, bf16[768,2048]{1,0:T(8,128)(2,1)S(1)} %get-tuple-element.32.refs_3_, ...), custom_call_target="tpu_custom_call" | custom-call | tf_op jit(solution)/shard_map/control/pallas_call | solution.py:582
  19.1 0.1 collective-permute-start.5
  19.2 1.2 %collective-permute-done.5.refs_1_ = f32[12,128]{1,0:T(8,128)S(1)} collective-permute-done((f32[12,128]{1,0:T(8,128)S(1)}, f32[12,128]{1,0:T(8,128)S(1)}, u32[]{:S(2)}, u32[]{:S(2)}) %collective-permute-start.5) | collective-permute-done | bytes 6176 | tf_op jit(solution)/shard_map/ppermute | solution.py:419
  20.4 0.7 %collective-permute-start.6 = (f32[12,128]{1,0:T(8,128)S(1)}, f32[12,128]{1,0:T(8,128)S(1)}, u32[]{:S(2)}, u32[]{:S(2)}) collective-permute-start(f32[12,128]{1,0:T(8,128)S(1)} %add.2.refs_0_), channel_id=1, source_target_pairs={{0,5},{1,4},{2,7},{3,6},{4,1},{5,0},{6,3},{7,2},{8,13},{9,12},{10,... | collective-permute-start | bytes 18440 | tf_op jit(solution)/shard_map/ppermute | solution.py:419
  21.1 2.3 %collective-permute-done.6.refs_1_ = f32[12,128]{1,0:T(8,128)S(1)} collective-permute-done((f32[12,128]{1,0:T(8,128)S(1)}, f32[12,128]{1,0:T(8,128)S(1)}, u32[]{:S(2)}, u32[]{:S(2)}) %collective-permute-start.6) | collective-permute-done | bytes 6176 | tf_op jit(solution)/shard_map/ppermute | solution.py:419
  23.4 1.9 %collective-permute-start.7 = (f32[12,128]{1,0:T(8,128)S(1)}, f32[12,128]{1,0:T(8,128)S(1)}, u32[]{:S(2)}, u32[]{:S(2)}) collective-permute-start(f32[12,128]{1,0:T(8,128)S(1)} %add.3.refs_0_), channel_id=1, source_target_pairs={{0,11},{1,10},{2,9},{3,8},{4,15},{5,14},{6,13},{7,12},{8,3},{9,2},... | collective-permute-start | bytes 18440 | tf_op jit(solution)/shard_map/ppermute | solution.py:419
  25.3 1.2 %collective-permute-start.8 = (f32[12,128]{1,0:T(8,128)S(1)}, f32[12,128]{1,0:T(8,128)S(1)}, u32[]{:S(2)}, u32[]{:S(2)}) collective-permute-start(f32[12,128]{1,0:T(8,128)S(1)} %add.3.refs_0_), channel_id=1, source_target_pairs={{0,9},{1,8},{2,11},{3,10},{4,13},{5,12},{6,15},{7,14},{8,1},{9,0},... | collective-permute-start | bytes 18440 | tf_op jit(solution)/shard_map/ppermute | solution.py:419
  26.6 0.8 %collective-permute-start.9 = (f32[12,128]{1,0:T(8,128)S(1)}, f32[12,128]{1,0:T(8,128)S(1)}, u32[]{:S(2)}, u32[]{:S(2)}) collective-permute-start(f32[12,128]{1,0:T(8,128)S(1)} %add.3.refs_0_), channel_id=1, source_target_pairs={{0,3},{1,2},{2,1},{3,0},{4,7},{5,6},{6,5},{7,4},{8,11},{9,10},{10,... | collective-permute-start | bytes 18440 | tf_op jit(solution)/shard_map/ppermute | solution.py:419
  27.3 1.0 %collective-permute-done.7.refs_1_ = f32[12,128]{1,0:T(8,128)S(1)} collective-permute-done((f32[12,128]{1,0:T(8,128)S(1)}, f32[12,128]{1,0:T(8,128)S(1)}, u32[]{:S(2)}, u32[]{:S(2)}) %collective-permute-start.7) | collective-permute-done | bytes 6176 | tf_op jit(solution)/shard_map/ppermute | solution.py:419
  28.3 1.0 %collective-permute-done.8.refs_2_ = f32[12,128]{1,0:T(8,128)S(1)} collective-permute-done((f32[12,128]{1,0:T(8,128)S(1)}, f32[12,128]{1,0:T(8,128)S(1)}, u32[]{:S(2)}, u32[]{:S(2)}) %collective-permute-start.8) | collective-permute-done | bytes 6176 | tf_op jit(solution)/shard_map/ppermute | solution.py:419
  29.3 0.3 %collective-permute-done.9.refs_3_ = f32[12,128]{1,0:T(8,128)S(1)} collective-permute-done((f32[12,128]{1,0:T(8,128)S(1)}, f32[12,128]{1,0:T(8,128)S(1)}, u32[]{:S(2)}, u32[]{:S(2)}) %collective-permute-start.9) | collective-permute-done | bytes 6176 | tf_op jit(solution)/shard_map/ppermute | solution.py:419
  29.6 0.6 %finish.1 = f32[3,512]{1,0:T(4,128)} custom-call(f32[12,128]{1,0:T(8,128)S(1)} %add.3.refs_0_, f32[12,128]{1,0:T(8,128)S(1)} %collective-permute-done.7.refs_1_, f32[12,128]{1,0:T(8,128)S(1)} %collective-permute-done.8.refs_2_, f32[12,128]{1,0:T(8,128)S(1)} %collective-permute-done.9.refs_3_), custom_call_target="tpu_custom_call" | custom-call | tf_op jit(solution)/shard_map/finish/pallas_call | solution.py:598
  (2 shorter events, 0.0 us)
Async XLA Ops:
  0.6 5.3 %collective-permute-start = (f32[80,128]{1,0:T(8,128)}, f32[80,128]{1,0:T(8,128)S(1)}, u32[]{:S(2)}, u32[]{:S(2)}) collective-permute-start(f32[80,128]{1,0:T(8,128)} %bitcast.38), channel_id=1, source_target_pairs={{0,2},{2,0},{1,4},{3,6},{4,1},{6,3},{5,8},{7,10},{8,5},{10,7},{9,1... | collective-permute-start | bytes 122888 | tf_op jit(solution)/shard_map/ppermute | solution.py:470
  3.6 2.3 %collective-permute-start.1 = (f32[80,128]{1,0:T(8,128)}, f32[80,128]{1,0:T(8,128)S(1)}, u32[]{:S(2)}, u32[]{:S(2)}) collective-permute-start(f32[80,128]{1,0:T(8,128)} %bitcast.39), channel_id=1, source_target_pairs={{0,1},{1,0},{4,5},{5,4},{8,9},{9,8},{12,13},{13,12},{2,3},{3,2},{6... | collective-permute-start | bytes 122888 | tf_op jit(solution)/shard_map/ppermute | solution.py:455
  7.2 5.0 %collective-permute-start.2 = (f32[80,128]{1,0:T(8,128)S(1)}, f32[80,128]{1,0:T(8,128)S(1)}, u32[]{:S(2)}, u32[]{:S(2)}) collective-permute-start(f32[80,128]{1,0:T(8,128)S(1)} %sweep.1._.refs_2_), channel_id=1, source_target_pairs={{0,1},{1,0},{4,5},{5,4},{8,9},{9,8},{12,13},{13,12},{2,3},{3,2},{6... | collective-permute-start | bytes 122888 | tf_op jit(solution)/shard_map/ppermute | solution.py:455
  7.5 4.7 %collective-permute-start.3 = (f32[80,128]{1,0:T(8,128)S(1)}, f32[80,128]{1,0:T(8,128)S(1)}, u32[]{:S(2)}, u32[]{:S(2)}) collective-permute-start(f32[80,128]{1,0:T(8,128)S(1)} %sweep.1._.refs_2_), channel_id=1, source_target_pairs={{0,2},{2,0},{1,4},{3,6},{4,1},{6,3},{5,8},{7,10},{8,5},{10,7},{9,1... | collective-permute-start | bytes 122888 | tf_op jit(solution)/shard_map/ppermute | solution.py:470
  13.5 3.8 %collective-permute-start.4 = (f32[24,128]{1,0:T(8,128)S(1)}, f32[24,128]{1,0:T(8,128)S(1)}, u32[]{:S(2)}, u32[]{:S(2)}) collective-permute-start(f32[24,128]{1,0:T(8,128)S(1)} %get-tuple-element.28.after.refs_0_), channel_id=1, source_target_pairs={{0,2},{2,0},{1,3},{3,1},{4,6},{6,4},{5,7},{7,5},{8,10},{10,8},{9,1... | collective-permute-start | bytes 36872 | tf_op jit(solution)/shard_map/ppermute | solution.py:568
  19.1 1.2 %collective-permute-start.5 = (f32[12,128]{1,0:T(8,128)S(1)}, f32[12,128]{1,0:T(8,128)S(1)}, u32[]{:S(2)}, u32[]{:S(2)}) collective-permute-start(f32[12,128]{1,0:T(8,128)S(1)} %control.1.refs_0_), channel_id=1, source_target_pairs={{0,1},{1,0},{2,3},{3,2},{4,5},{5,4},{6,7},{7,6},{8,9},{9,8},{10,11... | collective-permute-start | bytes 18440 | tf_op jit(solution)/shard_map/ppermute | solution.py:419
  20.4 3.1 %collective-permute-start.6 = (f32[12,128]{1,0:T(8,128)S(1)}, f32[12,128]{1,0:T(8,128)S(1)}, u32[]{:S(2)}, u32[]{:S(2)}) collective-permute-start(f32[12,128]{1,0:T(8,128)S(1)} %add.2.refs_0_), channel_id=1, source_target_pairs={{0,5},{1,4},{2,7},{3,6},{4,1},{5,0},{6,3},{7,2},{8,13},{9,12},{10,... | collective-permute-start | bytes 18440 | tf_op jit(solution)/shard_map/ppermute | solution.py:419
  23.4 4.9 %collective-permute-start.7 = (f32[12,128]{1,0:T(8,128)S(1)}, f32[12,128]{1,0:T(8,128)S(1)}, u32[]{:S(2)}, u32[]{:S(2)}) collective-permute-start(f32[12,128]{1,0:T(8,128)S(1)} %add.3.refs_0_), channel_id=1, source_target_pairs={{0,11},{1,10},{2,9},{3,8},{4,15},{5,14},{6,13},{7,12},{8,3},{9,2},... | collective-permute-start | bytes 18440 | tf_op jit(solution)/shard_map/ppermute | solution.py:419
  25.3 4.0 %collective-permute-start.8 = (f32[12,128]{1,0:T(8,128)S(1)}, f32[12,128]{1,0:T(8,128)S(1)}, u32[]{:S(2)}, u32[]{:S(2)}) collective-permute-start(f32[12,128]{1,0:T(8,128)S(1)} %add.3.refs_0_), channel_id=1, source_target_pairs={{0,9},{1,8},{2,11},{3,10},{4,13},{5,12},{6,15},{7,14},{8,1},{9,0},... | collective-permute-start | bytes 18440 | tf_op jit(solution)/shard_map/ppermute | solution.py:419
  26.6 3.1 %collective-permute-start.9 = (f32[12,128]{1,0:T(8,128)S(1)}, f32[12,128]{1,0:T(8,128)S(1)}, u32[]{:S(2)}, u32[]{:S(2)}) collective-permute-start(f32[12,128]{1,0:T(8,128)S(1)} %add.3.refs_0_), channel_id=1, source_target_pairs={{0,3},{1,2},{2,1},{3,0},{4,7},{5,6},{6,5},{7,4},{8,11},{9,10},{10,... | collective-permute-start | bytes 18440 | tf_op jit(solution)/shard_map/ppermute | solution.py:419
